TPU v7x, 32 devices: a whole 2x2x4 slice. The times are simulated.
32 devices in a mesh: blk: 8 (over z, x), head: 4 (over y, core).
Axes of the slice: x: 2, y: 2, z: 4, core: 2. Of those that a mesh axis runs over, the one named last changes fastest.
Arguments:
- hidden_in: bfloat16 [2, 2048, 2048], P(None, ('blk', 'head')), may hold values from -6 to 6
- lengths: int32 [2, 9], replicated, may hold values from 1 to 1920, as said below
- query_weight: bfloat16 [2048, 2048], P('blk', 'head'), may hold values from -0.125 to 0.125
- key_matrix: bfloat16 [2048, 1024], P('blk', 'head'), may hold values from -0.125 to 0.125
- value_matrix: bfloat16 [2048, 1024], P('blk', 'head'), may hold values from -0.125 to 0.125
- out_weight: bfloat16 [2048, 2048], P('blk', 'head'), may hold values from -1 to 1
- gate_weight: bfloat16 [2048, 6144], P('blk', 'head'), may hold values from -0.125 to 0.125
- up_weight: bfloat16 [2048, 6144], P('blk', 'head'), may hold values from -0.125 to 0.125
- down_weight: bfloat16 [2048, 6144], P('blk', 'head'), may hold values from -0.078125 to 0.078125
- attn_gain: bfloat16 [2048], replicated, may hold values from 0.25 to 1.75
- query_gain: bfloat16 [128], replicated, may hold values from 0.25 to 1.75
- key_gain: bfloat16 [128], replicated, may hold values from 0.25 to 1.75
- mlp_gain: bfloat16 [2048], replicated, may hold values from 0.25 to 1.75
- cotangent: bfloat16 [2, 2048, 2048], P(None, ('blk', 'head')), may hold values from -6 to 6
Outputs:
- mixed: bfloat16 [2, 2048, 2048], P(None, ('blk', 'head'))
- input_grad: float32 [2, 2048, 2048], P(None, ('blk', 'head'))
- query_weight_grad: float32 [2048, 2048], P('blk', 'head')
- key_weight_grad: float32 [2048, 1024], P('blk', 'head')
- value_weight_grad: float32 [2048, 1024], P('blk', 'head')
- out_weight_grad: float32 [2048, 2048], P('blk', 'head')
- gate_weight_grad: float32 [2048, 6144], P('blk', 'head')
- up_weight_grad: float32 [2048, 6144], P('blk', 'head')
- down_weight_grad: float32 [2048, 6144], P('blk', 'head')
- attn_gain_grad: float32 [2048], replicated
- query_gain_grad: float32 [128], replicated
- key_gain_grad: float32 [128], replicated
- mlp_gain_grad: float32 [2048], replicated
Inputs may be any that keep to these rules, and one draw needn't show every extreme that they name: In each micro-batch the lengths sum to 2048; one document, at a place drawn from the seed, has exactly 1920 tokens, and the others together have 128.
All inputs are finite; a program needn't handle non-finite values.
Results may differ from a plain program's by a relative error of at most 0.023.
Values may be sent and summed in bfloat16 or wider, within the bound.
A program may use at most 448 MiB of HBM per device.

v0:
```python
import jax
import jax.numpy as jnp
from jax import lax
from jax.sharding import PartitionSpec as P

EPS = 1e-06
THETA = 1000000.0
NEG = -1e30


def passed_along(value, axis, steps):
    count = lax.axis_size(axis)
    initial, last = (max(0, -steps), min(count, count - steps))
    return lax.ppermute(value, axis, [(source, source + steps) for source in range(initial, last)])


def from_behind(value, axis, steps):
    count = lax.axis_size(axis)
    pairs = [(source, (source + steps) % count) for source in range(count)]
    return lax.ppermute(value, axis, pairs)


def doc_layout(length_row, offset, token_count):
    doc_ends = jnp.cumsum(length_row)
    token_index = offset + jnp.arange(token_count, dtype=jnp.int32)
    passed = doc_ends[None, :] <= token_index[:, None]
    segment = jnp.sum(passed.astype(jnp.int32), axis=1)
    doc_start = jnp.max(jnp.where(passed, doc_ends[None, :], 0), axis=1)
    return (segment, token_index - doc_start)


def rms_scale(values, weight):
    return values * lax.rsqrt(jnp.mean(values * values, axis=-1, keepdims=True) + EPS) * weight


def rotary(values, position):
    half_dim = values.shape[-1] // 2
    inverse = THETA ** (-jnp.arange(half_dim, dtype=jnp.float32) / half_dim)
    angles = position.astype(jnp.float32)[:, None] * inverse[None, :]
    cosine = jnp.cos(angles)[:, None, :]
    sine_of = jnp.sin(angles)[:, None, :]
    leading = values[..., :half_dim]
    trailing = values[..., half_dim:]
    return jnp.concatenate(
        [leading * cosine - trailing * sine_of, trailing * cosine + leading * sine_of], axis=-1
    )


def norm_back(grad_rows, normed, inverse, weight):
    scaled = grad_rows * weight
    return inverse * (scaled - normed * jnp.mean(scaled * normed, axis=-1, keepdims=True))


def contract_last(first_op, second_op):
    return lax.dot_general(
        first_op, second_op, (((1,), (1,)), ((), ())), preferred_element_type=jnp.float32
    )


def column_term(first_op, second_op):
    return lax.dot_general(
        first_op, second_op, (((0,), (0,)), ((), ())), preferred_element_type=jnp.float32
    )


def local(
    hidden_in,
    lengths,
    query_weight,
    key_matrix,
    value_matrix,
    out_weight,
    gate_weight,
    up_weight,
    down_weight,
    attn_gain,
    query_gain,
    key_gain,
    mlp_gain,
    cotangent,
):
    cycle_size = lax.axis_size("blk")
    head_ways = lax.axis_size("head")
    cycle_place = lax.axis_index("blk")
    micro_count = hidden_in.shape[0]
    local_rows = hidden_in.shape[1]
    block_rows = local_rows * head_ways
    head_size = query_gain.shape[0]
    query_heads = query_weight.shape[1] // head_size
    value_heads = key_matrix.shape[1] // head_size
    grouping = query_heads // value_heads
    scaling = head_size ** (-0.5)
    owned = (
        query_weight,
        key_matrix,
        value_matrix,
        out_weight,
        gate_weight,
        up_weight,
        down_weight,
    )
    column_widths = [weight_arr.shape[1] for weight_arr in owned]
    gain_attn = attn_gain.astype(jnp.float32)
    gain_query = query_gain.astype(jnp.float32)
    gain_key = key_gain.astype(jnp.float32)
    gain_mlp = mlp_gain.astype(jnp.float32)
    block_first = cycle_place * block_rows
    query_index = block_first + jnp.arange(block_rows, dtype=jnp.int32)

    def fetch_weights():
        return (
            lax.all_gather(owned[0], "blk", axis=0, tiled=True),
            lax.all_gather(owned[1], "blk", axis=0, tiled=True),
            lax.all_gather(owned[2], "blk", axis=0, tiled=True),
            lax.all_gather(owned[3], "blk", axis=0, tiled=True),
            lax.all_gather(owned[4], "blk", axis=0, tiled=True),
            lax.all_gather(owned[5], "blk", axis=0, tiled=True),
            lax.all_gather(owned[6], "blk", axis=0, tiled=True),
        )

    def spread_rows(values):
        return lax.all_gather(values, "head", axis=0, tiled=True)

    def spread_grads(values):
        return lax.all_gather(values, "head", axis=0, tiled=True)

    def head_total(partial_value):
        return lax.psum_scatter(
            partial_value.astype(jnp.bfloat16), "head", scatter_dimension=0, tiled=True
        ).astype(jnp.float32)

    def grad_total(partial_value):
        return lax.psum_scatter(
            partial_value.astype(jnp.bfloat16), "head", scatter_dimension=0, tiled=True
        ).astype(jnp.float32)

    def rotate_pair(key_block, value_block):
        return passed_along((key_block, value_block), "blk", 1)

    def rotate_grads(key_grad, value_grad):
        return (
            from_behind(key_grad.astype(jnp.bfloat16), "blk", 1).astype(key_grad.dtype),
            from_behind(value_grad.astype(jnp.bfloat16), "blk", 1).astype(value_grad.dtype),
        )

    mixed_list = []
    input_grads = []
    grads_summed = None
    gain_a_grad = jnp.zeros(gain_attn.shape, jnp.float32)
    gain_q_grad = jnp.zeros(gain_query.shape, jnp.float32)
    gain_k_grad = jnp.zeros(gain_key.shape, jnp.float32)
    gain_m_grad = jnp.zeros(gain_mlp.shape, jnp.float32)
    for micro_idx in range(micro_count):
        length_row = lengths[micro_idx]
        query_seg, query_pos = doc_layout(length_row, block_first, block_rows)
        weights_fwd = fetch_weights()
        query_full, key_full, value_full, out_full, gate_full, up_full, down_full = weights_fwd
        rows_in = hidden_in[micro_idx].astype(jnp.float32)
        inverse_a = lax.rsqrt(jnp.mean(rows_in * rows_in, axis=-1, keepdims=True) + EPS)
        normal_a = rows_in * inverse_a
        normalized_attention_input = spread_rows((normal_a * gain_attn).astype(jnp.bfloat16))
        query_raw = jnp.dot(
            normalized_attention_input, query_full, preferred_element_type=jnp.float32
        ).reshape(block_rows, query_heads, head_size)
        key_unrotated = jnp.dot(
            normalized_attention_input, key_full, preferred_element_type=jnp.float32
        ).reshape(block_rows, value_heads, head_size)
        value_matrix_rows = (
            jnp.dot(normalized_attention_input, value_full, preferred_element_type=jnp.float32)
            .astype(jnp.bfloat16)
            .reshape(block_rows, value_heads, head_size)
        )

        def query_prep(raw_rows, weight, position=query_pos):
            return rotary(rms_scale(raw_rows, weight), position)

        query_rot, query_pull = jax.vjp(query_prep, query_raw, gain_query)
        key_rot, key_pull = jax.vjp(query_prep, key_unrotated, gain_key)
        query_low = query_rot.astype(jnp.bfloat16).reshape(
            block_rows, value_heads, grouping, head_size
        )
        key_low = key_rot.astype(jnp.bfloat16)

        def scores_for(
            key_block, key_place, length_row=length_row, query_seg=query_seg, query_low=query_low
        ):
            key_seg, key_pos = doc_layout(length_row, key_place * block_rows, block_rows)
            key_index = key_place * block_rows + jnp.arange(block_rows, dtype=jnp.int32)
            allowed = (query_seg[:, None] == key_seg[None, :]) & (
                query_index[:, None] >= key_index[None, :]
            )
            raw_scores = (
                jnp.einsum(
                    "qkgd,skd->kgqs", query_low, key_block, preferred_element_type=jnp.float32
                )
                * scaling
            )
            return (jnp.where(allowed[None, None], raw_scores, NEG), allowed)

        def forward_step(cycle_state, key_block, value_block, key_place):
            highest, totals, accumulated = cycle_state
            masked, allowed = scores_for(key_block, key_place)
            new_high = jnp.maximum(highest, jnp.max(masked, axis=-1, keepdims=True))
            exponent = jnp.where(allowed[None, None], jnp.exp(masked - new_high), 0.0)
            fade_factor = jnp.exp(highest - new_high)
            totals = totals * fade_factor + jnp.sum(exponent, axis=-1, keepdims=True)
            accumulated = accumulated * fade_factor + jnp.einsum(
                "kgqs,skd->kgqd",
                exponent.astype(jnp.bfloat16),
                value_block,
                preferred_element_type=jnp.float32,
            )
            return (new_high, totals, accumulated)

        start_state = (
            jnp.full((value_heads, grouping, block_rows, 1), NEG, jnp.float32),
            jnp.zeros((value_heads, grouping, block_rows, 1), jnp.float32),
            jnp.zeros((value_heads, grouping, block_rows, head_size), jnp.float32),
        )
        cycle_state = forward_step(start_state, key_low, value_matrix_rows, cycle_place)

        def cycle_turn(step_idx, loop_carry):
            state_in, key_block, value_block = loop_carry
            key_block, value_block = rotate_pair(key_block, value_block)
            return (
                forward_step(
                    state_in, key_block, value_block, (cycle_place - step_idx) % cycle_size
                ),
                key_block,
                value_block,
            )

        cycle_state, key_last, value_last = lax.fori_loop(
            1, cycle_size, cycle_turn, (cycle_state, key_low, value_matrix_rows)
        )
        highest, totals, accumulated = cycle_state
        attn_heads = accumulated / totals
        attn_low = (
            jnp.transpose(attn_heads, (2, 0, 1, 3))
            .reshape(block_rows, query_heads * head_size)
            .astype(jnp.bfloat16)
        )
        middle = rows_in + head_total(contract_last(attn_low, out_full))
        inverse_m = lax.rsqrt(jnp.mean(middle * middle, axis=-1, keepdims=True) + EPS)
        normal_m = middle * inverse_m
        normed_m = spread_rows((normal_m * gain_mlp).astype(jnp.bfloat16))
        gate_rows = jnp.dot(normed_m, gate_full, preferred_element_type=jnp.float32)
        up_rows = jnp.dot(normed_m, up_full, preferred_element_type=jnp.float32)
        sigmoid_g = jax.nn.sigmoid(gate_rows)
        silu_g = gate_rows * sigmoid_g
        active = (silu_g * up_rows).astype(jnp.bfloat16)
        result_rows = middle + head_total(contract_last(active, down_full))
        mixed_list.append(result_rows.astype(jnp.bfloat16))
        weights_back = fetch_weights()
        query_full, key_full, value_full, out_full, gate_full, up_full, down_full = weights_back
        cot_rows = cotangent[micro_idx]
        cot_all = spread_grads(cot_rows)
        d_active = jnp.dot(cot_all, down_full, preferred_element_type=jnp.float32)
        d_gate = (d_active * up_rows * sigmoid_g * (1.0 + gate_rows * (1.0 - sigmoid_g))).astype(
            jnp.bfloat16
        )
        d_up = (d_active * silu_g).astype(jnp.bfloat16)
        d_normed_m = grad_total(contract_last(d_gate, gate_full) + contract_last(d_up, up_full))
        gain_m_grad = gain_m_grad + jnp.sum(d_normed_m * normal_m, axis=0)
        d_middle = cot_rows.astype(jnp.float32) + norm_back(
            d_normed_m, normal_m, inverse_m, gain_mlp
        )
        d_mid_all = spread_grads(d_middle.astype(jnp.bfloat16))
        d_attn_low = jnp.dot(d_mid_all, out_full, preferred_element_type=jnp.float32).astype(
            jnp.bfloat16
        )
        d_attn_heads = jnp.transpose(
            d_attn_low.reshape(block_rows, value_heads, grouping, head_size), (1, 2, 0, 3)
        )
        d_attn_wide = d_attn_heads.astype(jnp.float32)
        row_delta = jnp.sum(d_attn_wide * attn_heads, axis=-1, keepdims=True)
        weighted_d = d_attn_wide / totals
        weighted_high = weighted_d.astype(jnp.bfloat16)
        weighted_rest = (weighted_d - weighted_high.astype(jnp.float32)).astype(jnp.bfloat16)

        def backward_step(
            d_query,
            key_block,
            value_block,
            key_place,
            highest=highest,
            totals=totals,
            d_attn_heads=d_attn_heads,
            row_delta=row_delta,
            weighted_high=weighted_high,
            weighted_rest=weighted_rest,
            query_low=query_low,
        ):
            masked, allowed = scores_for(key_block, key_place)
            exponent = jnp.where(allowed[None, None], jnp.exp(masked - highest), 0.0)
            probability = exponent / totals
            d_prob = jnp.einsum(
                "kgqd,skd->kgqs", d_attn_heads, value_block, preferred_element_type=jnp.float32
            )
            d_score = (probability * (d_prob - row_delta)).astype(jnp.bfloat16)
            d_query = (
                d_query
                + jnp.einsum(
                    "kgqs,skd->kgqd", d_score, key_block, preferred_element_type=jnp.float32
                )
                * scaling
            )
            d_key = (
                jnp.einsum("kgqs,qkgd->skd", d_score, query_low, preferred_element_type=jnp.float32)
                * scaling
            )
            exponent_low = exponent.astype(jnp.bfloat16)
            d_value = jnp.einsum(
                "kgqs,kgqd->skd", exponent_low, weighted_high, preferred_element_type=jnp.float32
            ) + jnp.einsum(
                "kgqs,kgqd->skd", exponent_low, weighted_rest, preferred_element_type=jnp.float32
            )
            return (d_query, d_key, d_value)

        zero_query = jnp.zeros((value_heads, grouping, block_rows, head_size), jnp.float32)
        d_query, d_key_own, d_value_own = backward_step(
            zero_query, key_low, value_matrix_rows, cycle_place
        )

        def back_turn(step_idx, loop_carry):
            dq_in, key_block, value_block, key_grad, value_grad = loop_carry
            key_block, value_block = rotate_pair(key_block, value_block)
            key_grad, value_grad = rotate_grads(key_grad, value_grad)
            dq_out, key_add, value_add = backward_step(
                dq_in, key_block, value_block, (cycle_place - step_idx) % cycle_size
            )
            return (dq_out, key_block, value_block, key_grad + key_add, value_grad + value_add)

        loop_carry = lax.fori_loop(
            1, cycle_size, back_turn, (d_query, key_low, value_matrix_rows, d_key_own, d_value_own)
        )
        d_query = loop_carry[0]
        key_grad, value_grad = rotate_grads(loop_carry[3], loop_carry[4])
        d_query_rot = jnp.transpose(d_query, (2, 0, 1, 3)).reshape(
            block_rows, query_heads, head_size
        )
        d_query_raw, gain_q_part = query_pull(d_query_rot)
        d_key_raw, gain_k_part = key_pull(key_grad)
        gain_q_grad = gain_q_grad + gain_q_part
        gain_k_grad = gain_k_grad + gain_k_part
        d_query_low = d_query_raw.astype(jnp.bfloat16).reshape(block_rows, query_heads * head_size)
        d_key_low = d_key_raw.astype(jnp.bfloat16).reshape(block_rows, value_heads * head_size)
        d_value_low = value_grad.astype(jnp.bfloat16).reshape(block_rows, value_heads * head_size)
        d_normed_a = grad_total(
            contract_last(d_query_low, query_full)
            + contract_last(d_key_low, key_full)
            + contract_last(d_value_low, value_full)
        )
        gain_a_grad = gain_a_grad + jnp.sum(d_normed_a * normal_a, axis=0)
        input_grads.append(d_middle + norm_back(d_normed_a, normal_a, inverse_a, gain_attn))
        pieces = (
            normalized_attention_input,
            d_query_low,
            d_key_low,
            d_value_low,
            d_mid_all,
            attn_low,
            normed_m,
            d_gate,
            d_up,
            cot_all,
            active,
        )
        stored = [pieces]
        summed_term = None
        for term_pieces in stored:
            (
                term_normalized_attention_input,
                term_d_query_low,
                term_d_key_low,
                term_d_value_low,
                term_d_mid_all,
                term_attn_low,
                term_normed_m,
                term_d_gate,
                term_d_up,
                term_cot_all,
                term_active,
            ) = term_pieces
            parts = [
                column_term(term_normalized_attention_input, term_d_query_low),
                column_term(term_normalized_attention_input, term_d_key_low),
                column_term(term_normalized_attention_input, term_d_value_low),
                column_term(term_d_mid_all, term_attn_low),
                column_term(term_normed_m, term_d_gate),
                column_term(term_normed_m, term_d_up),
                column_term(term_cot_all, term_active),
            ]
            joined = jnp.concatenate(parts, axis=1)
            summed_term = joined
        got_terms = lax.psum_scatter(
            summed_term.astype(jnp.bfloat16), "blk", scatter_dimension=0, tiled=True
        ).astype(jnp.float32)
        grads_summed = got_terms if grads_summed is None else grads_summed + got_terms
    gains_out = lax.psum((gain_a_grad, gain_q_grad, gain_k_grad, gain_m_grad), ("blk", "head"))
    split_grads = []
    column_start = 0
    for column_width in column_widths:
        split_grads.append(grads_summed[:, column_start : column_start + column_width])
        column_start = column_start + column_width
    return (
        jnp.stack(mixed_list),
        jnp.stack(input_grads),
        split_grads[0],
        split_grads[1],
        split_grads[2],
        split_grads[3],
        split_grads[4],
        split_grads[5],
        split_grads[6],
        gains_out[0],
        gains_out[1],
        gains_out[2],
        gains_out[3],
    )


def solution(mesh):
    placed = (
        P(None, ("blk", "head"), None),
        P(),
        P("blk", "head"),
        P("blk", "head"),
        P("blk", "head"),
        P("blk", "head"),
        P("blk", "head"),
        P("blk", "head"),
        P("blk", "head"),
        P(),
        P(),
        P(),
        P(),
        P(None, ("blk", "head"), None),
    )
    return jax.shard_map(
        local,
        mesh=mesh,
        in_specs=placed,
        out_specs=(
            P(None, ("blk", "head"), None),
            P(None, ("blk", "head"), None),
            P("blk", "head"),
            P("blk", "head"),
            P("blk", "head"),
            P("blk", "head"),
            P("blk", "head"),
            P("blk", "head"),
            P("blk", "head"),
            P(),
            P(),
            P(),
            P(),
        ),
        check_vma=False,
    )
```

profile of v0, /device:TPU:0, one launch (start us, length us, event | category | flops | bytes accessed | tf_op | source)
XLA Modules:
  0.0 2183.5 jit_solution(13905567213408090804)
XLA Ops:
  18.3 12.6 all-gather.36.cloned.1.call-done
  30.8 42.3 %all-gather.24.cloned.1.call-done = bf16[2048,256]{1,0:T(8,128)(2,1)} async-done(((bf16[256,256]{1,0:T(8,128)(2,1)}), bf16[2048,256]{1,0:T(8,128)(2,1)}) %all-gather.24.cloned.1.call-update) | async-done | bytes 1048592 | tf_op jit(solution)/shard_map/all_gather | solution.py:114
  76.1 14.7 all-gather.18.cloned.1.call-done
  95.0 38.0 %all-gather.20.cloned.1.call-done = bf16[2048,256]{1,0:T(8,128)(2,1)} async-done(((bf16[256,256]{1,0:T(8,128)(2,1)}), bf16[2048,256]{1,0:T(8,128)(2,1)}) %all-gather.20.cloned.1.call-update) | async-done | bytes 1048592 | tf_op jit(solution)/shard_map/all_gather | solution.py:113
  139.6 43.4 %all-gather.22.cloned.1.call-done = bf16[2048,512]{1,0:T(8,128)(2,1)} async-done(((bf16[256,512]{1,0:T(8,128)(2,1)}), bf16[2048,512]{1,0:T(8,128)(2,1)}) %all-gather.22.cloned.1.call-update) | async-done | bytes 2097168 | tf_op jit(solution)/shard_map/all_gather | solution.py:112
  198.1 95.8 %while.96 = (s32[]{:T(128)}, f32[2,2,256,1]{2,1,0,3:T(2,128)S(1)}, f32[2,2,256,1]{2,1,0,3:T(2,128)S(1)}, f32[2,2,256,128]{3,2,1,0:T(8,128)S(1)}, bf16[256,2,128]...) while((s32[]{:T(128)}, f32[2,2,256,1]{2,1,0,3:T(2,128)S(1)}, ...), condition=%wide.region_13.14_spmd.clone, body=%wide.region_9.13_spmd.clone.sunk | while | flops 137046032 | bytes 6627734 | solution.py:233
  301.7 86.7 %while.97 = (s32[]{:T(128)}, f32[2,2,256,1]{2,1,0,3:T(2,128)S(1)}, f32[2,2,256,1]{2,1,0,3:T(2,128)S(1)}, f32[2,2,256,128]{3,2,1,0:T(8,128)S(1)}, bf16[256,2,128]...) while((s32[]{:T(128)}, f32[2,2,256,1]{2,1,0,3:T(2,128)S(1)}, ...), condition=%wide.region_30.31_spmd.clone, body=%wide.region_26.30_spmd.clone.sunk | while | flops 137046032 | bytes 6627734 | solution.py:233
  394.7 23.8 %reduce-scatter.15.cloned.1.call-done = bf16[64,2048]{1,0:T(8,128)(2,1)} async-done(((bf16[256,2048]{1,0:T(8,128)(2,1)}), bf16[64,2048]{1,0:T(8,128)(2,1)}) %reduce-scatter.15.cloned.1.call-update) | async-done | bytes 262160 | tf_op jit(solution)/shard_map/reduce_scatter | solution.py:128
  427.1 11.7 all-gather.28.cloned.1.call-done
  438.8 101.1 %all-gather.32.cloned.1.call-done = bf16[2048,1536]{1,0:T(8,128)(2,1)} async-done(((bf16[256,1536]{1,0:T(8,128)(2,1)}), bf16[2048,1536]{1,0:T(8,128)(2,1)}) %all-gather.32.cloned.1.call-update) | async-done | bytes 6291472 | tf_op jit(solution)/shard_map/all_gather | solution.py:117
  545.9 93.4 %all-gather.30.cloned.1.call-done = bf16[2048,1536]{1,0:T(8,128)(2,1)} async-done(((bf16[256,1536]{1,0:T(8,128)(2,1)}), bf16[2048,1536]{1,0:T(8,128)(2,1)}) %all-gather.30.cloned.1.call-update) | async-done | bytes 6291472 | tf_op jit(solution)/shard_map/all_gather | solution.py:116
  645.4 10.9 all-gather.44.cloned.1.call-done
  656.2 101.2 %all-gather.34.cloned.1.call-done = bf16[2048,1536]{1,0:T(8,128)(2,1)} async-done(((bf16[256,1536]{1,0:T(8,128)(2,1)}), bf16[2048,1536]{1,0:T(8,128)(2,1)}) %all-gather.34.cloned.1.call-update) | async-done | bytes 6291472 | tf_op jit(solution)/shard_map/all_gather | solution.py:118
  757.5 7.2 multiply_convert_fusion.2
  792.6 7.1 multiply_convert_fusion
  820.5 28.0 %reduce-scatter.23.cloned.1.call-done = bf16[64,2048]{1,0:T(8,128)(2,1)} async-done(((bf16[256,2048]{1,0:T(8,128)(2,1)}), bf16[64,2048]{1,0:T(8,128)(2,1)}) %reduce-scatter.23.cloned.1.call-update) | async-done | bytes 262160 | tf_op jit(solution)/shard_map/reduce_scatter | solution.py:133
  850.7 25.7 %reduce-scatter.17.cloned.1.call-done = bf16[64,2048]{1,0:T(8,128)(2,1)} async-done(((bf16[256,2048]{1,0:T(8,128)(2,1)}), bf16[64,2048]{1,0:T(8,128)(2,1)}) %reduce-scatter.17.cloned.1.call-update) | async-done | bytes 262160 | tf_op jit(solution)/shard_map/reduce_scatter | solution.py:128
  880.1 15.9 all-gather.40.cloned.1.call-done
  908.0 6.8 all-gather.42.cloned.1.call-done
  935.7 154.8 %while.98 = (s32[]{:T(128)}, f32[2,2,256,128]{3,2,1,0:T(8,128)S(1)}, bf16[256,2,128]{2,0,1:T(8,128)(2,1)}, bf16[256,2,128]{2,0,1:T(8,128)(2,1)}, bf16[256,2,128]...) while((s32[]{:T(128)}, ...), condition=%wide.region_39.40_spmd.clone, body=%wide.region_37.39_spmd.clone.sunk | while | flops 406264832 | bytes 15520426 | solution.py:334
  1096.1 131.1 %while.99 = (s32[]{:T(128)}, f32[2,2,256,128]{3,2,1,0:T(8,128)S(1)}, bf16[256,2,128]{2,0,1:T(8,128)(2,1)}, bf16[256,2,128]{2,0,1:T(8,128)(2,1)}, bf16[256,2,128]...) while((s32[]{:T(128)}, ...), condition=%wide.region_49.50_spmd.clone, body=%wide.region_47.49_spmd.clone.sunk | while | flops 406264832 | bytes 14455402 | solution.py:334
  1323.0 39.3 %all-reduce.8 = (f32[2048]{0:T(1024)}, f32[128]{0:T(128)}, f32[128]{0:T(128)}, f32[2048]{0:T(1024)}) all-reduce(f32[2048]{0:T(1024)S(1)} %add.685, f32[128]{0:T(128)S(1)} %add.686, f32[128]{0:T(128)S(1)} %add.687, f32[2048]{0:T(1024)S(1)} %add.688), channel_id=1, replica_groups=mesh['blk'=8,'head'=4] {'blk','head'}, use_global_device_ids=true, to_apply=%region_58.59 | all-reduce | flops 4352 | bytes 34816 | tf_op jit(solution)/shard_map/psum | solution.py:400
  1366.3 382.9 %reduce-scatter.27.cloned.1.call-done = bf16[256,6144]{0,1:T(8,128)(2,1)} async-done(((bf16[2048,6144]{0,1:T(8,128)(2,1)}), bf16[256,6144]{0,1:T(8,128)(2,1)}) %reduce-scatter.27.cloned.1.call-update) | async-done | bytes 3145744 | tf_op jit(solution)/shard_map/reduce_scatter | solution.py:396
  1749.2 407.5 %reduce-scatter.29.cloned.1.call-done = bf16[256,6144]{0,1:T(8,128)(2,1)} async-done(((bf16[2048,6144]{0,1:T(8,128)(2,1)}), bf16[256,6144]{0,1:T(8,128)(2,1)}) %reduce-scatter.29.cloned.1.call-update) | async-done | bytes 3145744 | tf_op jit(solution)/shard_map/reduce_scatter | solution.py:396
  (1137 shorter events, 749.8 us)
Async XLA Ops:
  11.3 61.9 %all-gather.24.cloned.1.call-start = ((), (), s32[]{:S(2)}) async-start(), calls=%async_computation.13 | async-start | bytes 1179648 | tf_op jit(solution)/shard_map/all_gather | solution.py:114
  12.0 78.8 %all-gather.18.cloned.1.call-start = ((), (), s32[]{:S(2)}) async-start(), calls=%async_computation.10 | async-start | bytes 1310720 | tf_op jit(solution)/shard_map/all_gather | solution.py:122
  12.7 120.2 %all-gather.20.cloned.1.call-start = ((), (), s32[]{:S(2)}) async-start(), calls=%async_computation.11 | async-start | bytes 1179648 | tf_op jit(solution)/shard_map/all_gather | solution.py:113
  13.3 169.7 %all-gather.22.cloned.1.call-start = ((), (), s32[]{:S(2)}) async-start(), calls=%async_computation.12 | async-start | bytes 2359296 | tf_op jit(solution)/shard_map/all_gather | solution.py:112
  13.9 282.1 %all-gather.26.cloned.1.call-start = ((), (), s32[]{:S(2)}) async-start(), calls=%async_computation.14 | async-start | bytes 2359296 | tf_op jit(solution)/shard_map/all_gather | solution.py:115
  14.5 380.2 %reduce-scatter.11.cloned.1.call-start = ((), (), s32[]{:S(2)}) async-start(), calls=%async_computation.15 | async-start | bytes 1310720 | tf_op jit(solution)/shard_map/reduce_scatter | solution.py:128
  299.5 119.0 %reduce-scatter.15.cloned.1.call-start = ((), (), s32[]{:S(2)}) async-start(), calls=%async_computation.22 | async-start | bytes 1310720 | tf_op jit(solution)/shard_map/reduce_scatter | solution.py:128
  394.6 44.2 %all-gather.28.cloned.1.call-start = ((), (), s32[]{:S(2)}) async-start(), calls=%async_computation.16 | async-start | bytes 1310720 | tf_op jit(solution)/shard_map/all_gather | solution.py:122
  421.9 118.0 %all-gather.32.cloned.1.call-start = ((), (), s32[]{:S(2)}) async-start(), calls=%async_computation.18 | async-start | bytes 7077888 | tf_op jit(solution)/shard_map/all_gather | solution.py:117
  422.5 216.8 %all-gather.30.cloned.1.call-start = ((), (), s32[]{:S(2)}) async-start(), calls=%async_computation.17 | async-start | bytes 7077888 | tf_op jit(solution)/shard_map/all_gather | solution.py:116
  423.2 233.0 %all-gather.44.cloned.1.call-start = ((), (), s32[]{:S(2)}) async-start(), calls=%async_computation.33 | async-start | bytes 1310720 | tf_op jit(solution)/shard_map/all_gather | solution.py:125
  425.2 332.3 %all-gather.34.cloned.1.call-start = ((), (), s32[]{:S(2)}) async-start(), calls=%async_computation.19 | async-start | bytes 7077888 | tf_op jit(solution)/shard_map/all_gather | solution.py:118
  425.9 348.5 %all-gather.38.cloned.1.call-start = ((), (), s32[]{:S(2)}) async-start(), calls=%async_computation.23 | async-start | bytes 1310720 | tf_op jit(solution)/shard_map/all_gather | solution.py:122
  426.5 366.1 %all-gather.46.cloned.1.call-start = ((), (), s32[]{:S(2)}) async-start(), calls=%async_computation.34 | async-start | bytes 1310720 | tf_op jit(solution)/shard_map/all_gather | solution.py:125
  427.1 393.4 %reduce-scatter.19.cloned.1.call-start = ((), (), s32[]{:S(2)}) async-start(), calls=%async_computation.25 | async-start | bytes 1310720 | tf_op jit(solution)/shard_map/reduce_scatter | solution.py:133
  772.2 76.3 %reduce-scatter.23.cloned.1.call-start = ((), (), s32[]{:S(2)}) async-start(), calls=%async_computation.28 | async-start | bytes 1310720 | tf_op jit(solution)/shard_map/reduce_scatter | solution.py:133
  810.6 65.7 %reduce-scatter.17.cloned.1.call-start = ((), (), s32[]{:S(2)}) async-start(), calls=%async_computation.24 | async-start | bytes 1310720 | tf_op jit(solution)/shard_map/reduce_scatter | solution.py:128
  816.8 79.2 %all-gather.40.cloned.1.call-start = ((), (), s32[]{:S(2)}) async-start(), calls=%async_computation.26 | async-start | bytes 1310720 | tf_op jit(solution)/shard_map/all_gather | solution.py:125
  879.6 441.7 %reduce-scatter.25.cloned.1.call-start = ((), (), s32[]{:S(2)}) async-start(), calls=%async_computation.30 | async-start | bytes 1310720 | tf_op jit(solution)/shard_map/reduce_scatter | solution.py:133
  1090.4 161.2 %collective-permute-start.12 = (bf16[256,2,128]{2,0,1:T(8,128)(2,1)}, bf16[256,2,128]{2,0,1:T(8,128)(2,1)}, u32[]{:S(2)}, u32[]{:S(2)}) collective-permute-start(bf16[256,2,128]{2,0,1:T(8,128)(2,1)} %get-tuple-element.2775), channel_id=1, source_target_pairs={{0,4},{4,8},{8,12},{12,16},{16,20},{20,24},{24,28},{28,0},{1,5},{5... | collective-permute-start | bytes 393224 | tf_op jit(solution)/shard_map/ppermute | solution.py:20
  1260.2 61.2 %reduce-scatter.21.cloned.1.call-start = ((), (), s32[]{:S(2)}) async-start(), calls=%async_computation.27 | async-start | bytes 1310720 | tf_op jit(solution)/shard_map/reduce_scatter | solution.py:133
  1271.4 91.0 %reduce-scatter.13.cloned.1.call-start = ((), (), s32[]{:S(2)}) async-start(), calls=%async_computation.20 | async-start | bytes 1310720 | tf_op jit(solution)/shard_map/reduce_scatter | solution.py:128
  1277.3 471.9 %reduce-scatter.27.cloned.1.call-start = ((), (), s32[]{:S(2)}) async-start(), calls=%async_computation.31 | async-start | bytes 28311552 | tf_op jit(solution)/shard_map/reduce_scatter | solution.py:396
  1298.0 858.7 %reduce-scatter.29.cloned.1.call-start = ((), (), s32[]{:S(2)}) async-start(), calls=%async_computation.32 | async-start | bytes 28311552 | tf_op jit(solution)/shard_map/reduce_scatter | solution.py:396
  (288 other events, 5678.2 us)
Sparse Core Ops, SparseCore 0:
  11.4 19.4 all-gather.35
  33.0 40.1 all-gather.23
  75.3 15.4 all-gather.17
  92.8 40.1 all-gather.19
  134.9 48.0 all-gather.21
  185.0 54.6 all-gather.25
  299.6 25.6 reduce-scatter.10
  394.7 23.7 reduce-scatter.14
  422.0 16.7 all-gather.27
  440.8 99.0 all-gather.31
  542.1 97.1 all-gather.29
  641.3 14.9 all-gather.43
  658.4 99.0 all-gather.33
  775.8 16.7 all-gather.45
  795.5 24.8 reduce-scatter.18
  823.6 24.8 reduce-scatter.22
  851.5 24.8 reduce-scatter.16
  879.2 16.7 all-gather.39
  898.0 16.7 all-gather.41
  1260.3 24.4 reduce-scatter.24
  1287.9 24.8 reduce-scatter.20
  1316.1 25.0 reduce-scatter.12
  1344.9 404.2 reduce-scatter.26
  1753.1 403.5 reduce-scatter.28
  (1 shorter events, 14.9 us)
where the time goes:
time: 2200 us; the launch traced here: 2180 us
  waiting for transfers between devices  1430 us (65%)
  starting transfers between devices  270 us (12%)
  matrix products  242 us (11%)
  local copies, waits for them, and re-layouts  95.8 us (4%)
  other arithmetic  86.8 us (4%)
  blocking collectives  39.3 us (2%)
    reduce_scatter x2, waiting for transfers between devices, local(): lax.psum_scatter(summed_term.astype(jnp.bfloat16), 'blk', scatter_dimensi...  790 us
    ppermute x56, starting transfers between devices, passed_along(): lax.ppermute(value, axis, [(source, source + steps) for source in range(i...  203 us
    all_gather x1, waiting for transfers between devices, fetch_weights(): lax.all_gather(owned[6], 'blk', axis=0, tiled=True)  101 us
    all_gather x1, waiting for transfers between devices, fetch_weights(): lax.all_gather(owned[5], 'blk', axis=0, tiled=True)  101 us
    all_gather x1, waiting for transfers between devices, fetch_weights(): lax.all_gather(owned[4], 'blk', axis=0, tiled=True)  93.4 us
    ppermute x32, starting transfers between devices, from_behind(): return lax.ppermute(value, axis, pairs)  64.7 us
    reduce_scatter x4, waiting for transfers between devices, head_total(): lax.psum_scatter(partial_value.astype(jnp.bfloat16), 'head', scatter_dime...  49.6 us
    ppermute x56, waiting for transfers between devices, passed_along(): lax.ppermute(value, axis, [(source, source + steps) for source in range(i...  48.1 us
  transfers between devices with their start and end apart: 113, of which 49 were waited for; matrix products, arithmetic and copies ran while one was open for 16% of the time, Pallas kernels for 0%

commit v1 on v0

v1 whole, which is shorter than its diff:
```python
import functools

import jax
import jax.numpy as jnp
from jax import lax
from jax.experimental import pallas as pl
from jax.experimental.pallas import tpu as pltpu
from jax.sharding import PartitionSpec as P

EPS = 1e-06
THETA = 1000000.0
LOG2E = 1.4426950408889634
F32 = jnp.float32
BF16 = jnp.bfloat16

TENSOR_BIT = 1


def nt(a, b):
    return lax.dot_general(a, b, (((1,), (1,)), ((), ())), preferred_element_type=F32)


def tn(a, b):
    return lax.dot_general(a, b, (((0,), (0,)), ((), ())), preferred_element_type=F32)


def nn(a, b):
    return jnp.dot(a, b, preferred_element_type=F32)


def bit_of(value, bit):
    return (value >> bit) & 1


def over_blk(value, bit):
    count = lax.axis_size("blk")
    return lax.ppermute(value, "blk", [(i, i ^ (1 << bit)) for i in range(count)])


def over_head(value, bit):
    count = lax.axis_size("head")
    return lax.ppermute(value, "head", [(i, i ^ (1 << bit)) for i in range(count)])


def in_order(flag, own, other, axis):
    return jnp.where(
        flag == 0,
        jnp.concatenate([own, other], axis=axis),
        jnp.concatenate([other, own], axis=axis),
    )


def token_offset(head_place, index, sub):
    core, upper, inner = index // (2 * sub), (index // sub) % 2, index % sub
    return (head_place ^ (upper * 2) ^ core) * sub + inner


def allowed_mask(meta_ref, start_row, q_block, k_block, rows, half, q_lanes):
    sub = half // 2
    head_place = meta_ref[0]
    k_index = lax.broadcasted_iota(jnp.int32, (2 * half, 1), 0)
    k_token = token_offset(head_place, k_index, sub) + k_block * (2 * half)
    q_index = lax.broadcasted_iota(jnp.int32, (1, q_lanes), 1) % (2 * half)
    q_token = token_offset(head_place, q_index, sub) + q_block * (2 * half)
    return (k_token <= q_token) & (k_token >= start_row)


def stacked(ref, heads, width):
    return jnp.concatenate(
        [ref[c, 0, :, h * width : (h + 1) * width] for h in range(heads) for c in range(2)], axis=0
    )


def key_rows(ref, part, block):
    return jnp.concatenate([ref[part, 0, block], ref[part, 1, block]], axis=0)


def attend_kernel(meta_ref, q_ref, k_ref, v_ref, start_ref, o_ref, ot_ref, l_ref, vt_ref, acc_ref, sum_ref, *, factor, heads):
    q_pos = pl.program_id(0)
    parts, _, blocks, half, width = k_ref.shape
    lanes = heads * 2 * half

    @pl.when(q_pos == 0)
    def _():
        for part in range(parts):
            for block in range(blocks):
                vt_ref[part * blocks + block] = key_rows(v_ref, part, block).T

    q_rows = stacked(q_ref, heads, width)
    acc_ref[...] = jnp.zeros_like(acc_ref)
    sum_ref[...] = jnp.zeros_like(sum_ref)
    start_row = start_ref[0]
    q_block = meta_ref[1 + q_pos]
    total = parts * blocks

    def add(kb, masked):
        e = jnp.exp2(nt(key_rows(k_ref, kb // blocks, kb % blocks), q_rows) * factor)
        if masked:
            k_block = meta_ref[1 + blocks + kb]
            e = jnp.where(allowed_mask(meta_ref, start_row, q_block, k_block, None, half, lanes), e, 0.0)
        sum_ref[...] += jnp.sum(e, axis=0, keepdims=True)
        acc_ref[...] += nn(vt_ref[kb], e.astype(BF16))

    def step(kb, carry):
        flag = meta_ref[1 + blocks + total + q_pos * total + kb]

        @pl.when(flag == 1)
        def _():
            add(kb, False)

        @pl.when(flag == 2)
        def _():
            add(kb, True)

        return carry

    lax.fori_loop(0, total, step, 0)
    out = acc_ref[...] / sum_ref[...]
    ot_ref[0] = out
    l_ref[0] = sum_ref[...]
    rows = out.T
    for h in range(heads):
        for c in range(2):
            at = (h * 2 + c) * half
            o_ref[c, 0, :, h * width : (h + 1) * width] = rows[at : at + half].astype(BF16)


def attend_back_kernel(
    meta_ref, q_ref, do_ref, k_ref, v_ref, start_ref, ot_ref, l_ref, dq_ref, dk_ref, dv_ref, kt_ref, acc_ref, *, factor, scaling, heads
):
    q_pos = pl.program_id(0)
    parts, _, blocks, half, width = k_ref.shape
    lanes = heads * 2 * half

    @pl.when(q_pos == 0)
    def _():
        dk_ref[...] = jnp.zeros_like(dk_ref)
        dv_ref[...] = jnp.zeros_like(dv_ref)
        for part in range(parts):
            for block in range(blocks):
                kt_ref[part * blocks + block] = key_rows(k_ref, part, block).T

    q_rows = stacked(q_ref, heads, width)
    do_rows = stacked(do_ref, heads, width)
    delta = jnp.sum(do_rows.astype(F32).T * ot_ref[0], axis=0, keepdims=True)
    inverse = 1.0 / l_ref[0]
    acc_ref[...] = jnp.zeros_like(acc_ref)
    start_row = start_ref[0]
    q_block = meta_ref[1 + q_pos]
    total = parts * blocks

    def add(kb, masked):
        part, block = kb // blocks, kb % blocks
        e = jnp.exp2(nt(key_rows(k_ref, part, block), q_rows) * factor)
        if masked:
            k_block = meta_ref[1 + blocks + kb]
            e = jnp.where(allowed_mask(meta_ref, start_row, q_block, k_block, None, half, lanes), e, 0.0)
        p = e * inverse
        dp = nt(key_rows(v_ref, part, block), do_rows)
        ds = (p * (dp - delta)).astype(BF16)
        dv = nn(p.astype(BF16), do_rows)
        dk = nn(ds, q_rows) * scaling
        for c in range(2):
            dv_ref[part, c, block] += dv[c * half : (c + 1) * half]
            dk_ref[part, c, block] += dk[c * half : (c + 1) * half]
        acc_ref[...] += nn(kt_ref[kb], ds)

    def step(kb, carry):
        flag = meta_ref[1 + blocks + total + q_pos * total + kb]

        @pl.when(flag == 1)
        def _():
            add(kb, False)

        @pl.when(flag == 2)
        def _():
            add(kb, True)

        return carry

    lax.fori_loop(0, total, step, 0)
    rows = acc_ref[...].T * scaling
    for h in range(heads):
        for c in range(2):
            at = (h * 2 + c) * half
            dq_ref[c, 0, :, h * width : (h + 1) * width] = rows[at : at + half]


def attend(meta, q, k, v, start, scaling):
    _, blocks, half, columns = q.shape
    parts, width = k.shape[0], k.shape[-1]
    heads = columns // width
    lanes = heads * 2 * half
    total = parts * blocks
    row_spec = pl.BlockSpec((2, 1, half, columns), lambda i: (0, i, 0, 0))
    key_spec = pl.BlockSpec(k.shape, lambda i: (0, 0, 0, 0, 0))
    lane_spec = pl.BlockSpec((1, 1, lanes), lambda i: (i, 0, 0))
    return pl.pallas_call(
        functools.partial(attend_kernel, factor=scaling * LOG2E, heads=heads),
        grid=(blocks,),
        in_specs=[pl.BlockSpec(memory_space=pltpu.SMEM), row_spec, key_spec, key_spec, lane_spec],
        out_specs=[row_spec, pl.BlockSpec((1, width, lanes), lambda i: (i, 0, 0)), lane_spec],
        out_shape=[
            jax.ShapeDtypeStruct(q.shape, BF16),
            jax.ShapeDtypeStruct((blocks, width, lanes), F32),
            jax.ShapeDtypeStruct((blocks, 1, lanes), F32),
        ],
        scratch_shapes=[
            pltpu.VMEM((total, width, 2 * half), BF16),
            pltpu.VMEM((width, lanes), F32),
            pltpu.VMEM((1, lanes), F32),
        ],
        compiler_params=pltpu.CompilerParams(vmem_limit_bytes=40 * 1024 * 1024),
        cost_estimate=pl.CostEstimate(
            flops=2 * 2 * lanes * 2 * half * width * blocks * total,
            bytes_accessed=8 * q.size + 8 * k.size,
            transcendentals=lanes * 2 * half * blocks * total,
        ),
    )(meta, q, k, v, start)


def attend_back(meta, q, do, k, v, start, out_t, total_e, scaling):
    _, blocks, half, columns = q.shape
    parts, width = k.shape[0], k.shape[-1]
    heads = columns // width
    lanes = heads * 2 * half
    total = parts * blocks
    row_spec = pl.BlockSpec((2, 1, half, columns), lambda i: (0, i, 0, 0))
    key_spec = pl.BlockSpec(k.shape, lambda i: (0, 0, 0, 0, 0))
    lane_spec = pl.BlockSpec((1, 1, lanes), lambda i: (i, 0, 0))
    return pl.pallas_call(
        functools.partial(attend_back_kernel, factor=scaling * LOG2E, scaling=scaling, heads=heads),
        grid=(blocks,),
        in_specs=[
            pl.BlockSpec(memory_space=pltpu.SMEM),
            row_spec,
            row_spec,
            key_spec,
            key_spec,
            lane_spec,
            pl.BlockSpec((1, width, lanes), lambda i: (i, 0, 0)),
            lane_spec,
        ],
        out_specs=[row_spec, key_spec, key_spec],
        out_shape=[
            jax.ShapeDtypeStruct(q.shape, F32),
            jax.ShapeDtypeStruct(k.shape, F32),
            jax.ShapeDtypeStruct(k.shape, F32),
        ],
        scratch_shapes=[
            pltpu.VMEM((total, width, 2 * half), BF16),
            pltpu.VMEM((width, lanes), F32),
        ],
        compiler_params=pltpu.CompilerParams(vmem_limit_bytes=48 * 1024 * 1024),
        cost_estimate=pl.CostEstimate(
            flops=5 * 2 * lanes * 2 * half * width * blocks * total,
            bytes_accessed=12 * q.size + 16 * k.size,
            transcendentals=lanes * 2 * half * blocks * total,
        ),
    )(meta, q, do, k, v, start, out_t, total_e)


def local(
    hidden_in,
    lengths,
    query_weight,
    key_matrix,
    value_matrix,
    out_weight,
    gate_weight,
    up_weight,
    down_weight,
    attn_gain,
    query_gain,
    key_gain,
    mlp_gain,
    cotangent,
):
    ring = lax.axis_size("blk")
    bits = ring.bit_length() - 1
    batch_bit = bits - 1
    seq_bits = [i for i in range(bits) if i not in (TENSOR_BIT, batch_bit)]
    data_bits = [batch_bit, *seq_bits]
    parts = 1 << len(seq_bits)
    blk, head = lax.axis_index("blk"), lax.axis_index("head")
    batch, tensor = bit_of(blk, batch_bit), bit_of(blk, TENSOR_BIT)

    local_rows, width = hidden_in.shape[1:]
    block_rows = local_rows * lax.axis_size("head")
    half = block_rows // 2
    row_features = width // ring
    head_size = query_gain.shape[0]
    scaling = head_size ** (-0.5)
    tokens = 16 * local_rows
    heads = query_weight.shape[1] // (2 * head_size)
    ff = gate_weight.shape[1] // 2

    axis_order = [*reversed(seq_bits), batch_bit, TENSOR_BIT]

    def to_group(values):
        lead = values.shape[:-1]
        n = len(lead)
        cut = values.reshape(*lead, *([2] * bits), row_features)
        for b in data_bits:
            cut = jnp.where(bit_of(blk, b) == 1, jnp.flip(cut, n + bits - 1 - b), cut)
        order = [*range(n), *[n + bits - 1 - b for b in axis_order], n + bits]
        return jnp.transpose(cut, order).reshape(*lead, width)

    def from_group(values):
        lead = values.shape[:-1]
        n = len(lead)
        cut = values.reshape(*lead, *([2] * bits), row_features)
        back = [axis_order.index(b) for b in range(bits - 1, -1, -1)]
        cut = jnp.transpose(cut, [*range(n), *[n + i for i in back], n + bits])
        for b in data_bits:
            cut = jnp.where(bit_of(blk, b) == 1, jnp.flip(cut, n + bits - 1 - b), cut)
        return cut.reshape(*lead, width)

    def cut_half(weight, which):
        return lax.dynamic_slice_in_dim(weight, which * (weight.shape[1] // 2), weight.shape[1] // 2, 1)

    def collect(weights):
        own = jnp.concatenate([cut_half(w, tensor) for w in weights], axis=1)
        other = over_blk(jnp.concatenate([cut_half(w, 1 - tensor) for w in weights], axis=1), TENSOR_BIT)
        chunks = [in_order(tensor, own, other, 0)]
        for b in data_bits:
            chunks = chunks + [over_blk(c, b) for c in chunks]
        return jnp.concatenate(chunks, axis=0)

    def settle(grad, column_widths):
        for b in reversed(data_bits):
            n = grad.shape[0] // 2
            grad = grad[:n] + over_blk(grad[n:].astype(BF16), b).astype(F32)
        own = lax.dynamic_slice_in_dim(grad, tensor * row_features, row_features, 0)
        other = over_blk(
            lax.dynamic_slice_in_dim(grad, (1 - tensor) * row_features, row_features, 0).astype(BF16), TENSOR_BIT
        ).astype(F32)
        results, at = [], 0
        for w in column_widths:
            results.append(in_order(tensor, own[:, at : at + w], other[:, at : at + w], 1))
            at += w
        return results

    def spread(rows):
        flat = rows.reshape(2 * local_rows, width)
        by_y = over_head(flat, 1)
        by_t = over_blk(flat, TENSOR_BIT)
        by_ty = over_head(by_t, 1)
        near = [flat, by_y, by_t, by_ty]
        far = [over_head(piece, 0) for piece in near]
        cut = [
            piece.reshape(2, local_rows, width)[m]
            for group in (near, far)
            for m in range(2)
            for piece in group
        ]
        return jnp.concatenate(cut, axis=0)

    def gather_sum(left, weight):
        n = tokens // 2
        away = over_head(nt(left[n:], weight).astype(BF16), 0)
        held = (nt(left[:n], weight) + away.astype(F32)).reshape(2, 2, 2, local_rows, width)
        from_y1 = over_head(held[:, 1, 1].astype(BF16), 1)
        from_y0 = over_head(held[:, 0, 1].astype(BF16), 1)
        from_t = over_blk((held[:, 1, 0] + from_y1.astype(F32)).astype(BF16), TENSOR_BIT)
        return held[:, 0, 0] + from_y0.astype(F32) + from_t.astype(F32)

    def take_batch(rows):
        mine = lax.dynamic_index_in_dim(rows, batch, 0, keepdims=False)
        theirs = lax.dynamic_index_in_dim(rows, 1 - batch, 0, keepdims=False)
        return to_group(jnp.stack([mine, over_blk(theirs, batch_bit)]))

    def give_batch(rows):
        rows = from_group(rows)
        back = over_blk(rows[1].astype(BF16), batch_bit).astype(rows.dtype)
        return in_order(batch, rows[0][None], back[None], 0)

    length_row = lax.dynamic_index_in_dim(lengths, batch, 0, keepdims=False)
    doc_ends = jnp.cumsum(length_row)
    batch_flip = jnp.arange(2, dtype=jnp.int32)[:, None] << batch_bit
    tensor_flip = jnp.arange(2, dtype=jnp.int32)[None, :] << TENSOR_BIT
    q_blocks = (blk ^ batch_flip ^ tensor_flip).reshape(4)
    index = jnp.arange(2 * half, dtype=jnp.int32)
    in_block = token_offset(head, index, local_rows).reshape(2, 1, half)
    token_index = q_blocks[None, :, None] * block_rows + in_block
    passed = doc_ends <= token_index[..., None]
    doc_start = jnp.max(jnp.where(passed, doc_ends, 0), axis=-1).astype(jnp.int32)
    position = (token_index - doc_start).reshape(tokens)
    start_lanes = jnp.tile(jnp.transpose(doc_start, (1, 0, 2)).reshape(4, 1, 2 * half), (1, 1, heads))
    k_blocks = q_blocks
    for b in seq_bits:
        k_blocks = jnp.concatenate([k_blocks, k_blocks ^ (1 << b)])
    least_start = jnp.min(doc_start, axis=(0, 2))[:, None]
    last_start = jnp.max(doc_start, axis=(0, 2))[:, None]
    k_first = (k_blocks * block_rows)[None, :]
    none = (k_blocks[None, :] > q_blocks[:, None]) | (k_first + block_rows <= least_start)
    whole = (k_blocks[None, :] < q_blocks[:, None]) & (k_first >= last_start)
    flags = jnp.where(none, 0, jnp.where(whole, 1, 2))
    meta = jnp.concatenate([head[None], q_blocks, k_blocks, flags.reshape(-1)]).astype(jnp.int32)

    inverse_freq = THETA ** (-jnp.arange(head_size // 2, dtype=F32) / (head_size // 2))
    angles = position.astype(F32)[:, None] * inverse_freq[None, :]
    cosine = jnp.cos(angles)[:, None, :]
    sine = jnp.sin(angles)[:, None, :]

    def rope(values):
        a, b = values[..., : head_size // 2], values[..., head_size // 2 :]
        return jnp.concatenate([a * cosine - b * sine, b * cosine + a * sine], axis=-1)

    def rope_back(values):
        a, b = values[..., : head_size // 2], values[..., head_size // 2 :]
        return jnp.concatenate([a * cosine + b * sine, b * cosine - a * sine], axis=-1)

    def rms(values):
        return lax.rsqrt(jnp.mean(values * values, axis=-1, keepdims=True) + EPS)

    def norm_back(grad, normed, inverse, gain):
        scaled = grad * gain
        return inverse * (scaled - normed * jnp.mean(scaled * normed, axis=-1, keepdims=True))

    gain_a = to_group(attn_gain.astype(F32))
    gain_m = to_group(mlp_gain.astype(F32))
    gain_q = query_gain.astype(F32)
    gain_k = key_gain.astype(F32)

    rows_in = take_batch(hidden_in).astype(F32)
    cot = take_batch(cotangent)
    w_qkv = collect((query_weight, key_matrix, value_matrix))
    inverse_a = rms(rows_in)
    normal_a = rows_in * inverse_a
    xa = spread((normal_a * gain_a).astype(BF16))
    w_out = collect((out_weight,))
    w_gu = collect((gate_weight, up_weight))
    w_down = collect((down_weight,))
    cot_all = spread(cot)

    qkv = nn(xa, w_qkv)
    q_columns, k_columns = heads * head_size, head_size
    q_raw = qkv[:, :q_columns].reshape(tokens, heads, head_size)
    k_raw = qkv[:, q_columns : q_columns + k_columns].reshape(tokens, 1, head_size)
    value = qkv[:, q_columns + k_columns :].astype(BF16)
    q_inverse, k_inverse = rms(q_raw), rms(k_raw)
    q_normal, k_normal = q_raw * q_inverse, k_raw * k_inverse
    query = rope(q_normal * gain_q).astype(BF16).reshape(2, 4, half, q_columns)
    key = rope(k_normal * gain_k).astype(BF16).reshape(tokens, head_size)
    key_value = [jnp.concatenate([key, value], axis=1)]
    for b in seq_bits:
        key_value = key_value + [over_blk(c, b) for c in key_value]
    key_value = jnp.stack(key_value)
    keys = key_value[..., :head_size].reshape(parts, 2, 4, half, head_size)
    values = key_value[..., head_size:].reshape(parts, 2, 4, half, head_size)
    attn, attn_t, total_e = attend(meta, query, keys, values, start_lanes, scaling)
    attn = attn.reshape(tokens, q_columns)
    middle = rows_in + gather_sum(attn, w_out)
    inverse_m = rms(middle)
    normal_m = middle * inverse_m
    xm = spread((normal_m * gain_m).astype(BF16))
    d_active = nn(cot_all, w_down)
    gate_up = nn(xm, w_gu)
    gate, up = gate_up[:, :ff], gate_up[:, ff:]
    sig = jax.nn.sigmoid(gate)
    silu = gate * sig
    active = (silu * up).astype(BF16)
    d_gate = (d_active * up * sig * (1.0 + gate * (1.0 - sig))).astype(BF16)
    d_up = (d_active * silu).astype(BF16)
    d_gu = jnp.concatenate([d_gate, d_up], axis=1)

    d_xm = gather_sum(d_gu, w_gu)
    mixed = give_batch((middle + gather_sum(active, w_down)).astype(BF16))
    g_gate, g_up = settle(tn(xm, d_gu), (ff, ff))
    (g_down,) = settle(tn(cot_all, active), (ff,))
    d_middle = cot.astype(F32) + norm_back(d_xm, normal_m, inverse_m, gain_m)
    d_mid_all = spread(d_middle.astype(BF16))
    d_attn = nn(d_mid_all, w_out).astype(BF16).reshape(2, 4, half, q_columns)
    d_query, d_key, d_value = attend_back(
        meta, query, d_attn, keys, values, start_lanes, attn_t, total_e, scaling
    )
    (g_out,) = settle(tn(d_mid_all, attn), (q_columns,))
    d_key_value = jnp.concatenate(
        [d_key.reshape(parts, tokens, head_size), d_value.reshape(parts, tokens, head_size)], axis=-1
    )
    for b in reversed(seq_bits):
        n = d_key_value.shape[0] // 2
        d_key_value = d_key_value[:n] + over_blk(d_key_value[n:].astype(BF16), b).astype(F32)
    d_key, d_value = d_key_value[0, :, :head_size], d_key_value[0, :, head_size:]
    dq_turned = rope_back(d_query.reshape(tokens, heads, head_size))
    dk_turned = rope_back(d_key.reshape(tokens, 1, head_size))
    gain_q_grad = jnp.sum(dq_turned * q_normal, axis=(0, 1))
    gain_k_grad = jnp.sum(dk_turned * k_normal, axis=(0, 1))
    dq_raw = norm_back(dq_turned, q_normal, q_inverse, gain_q).reshape(tokens, q_columns)
    dk_raw = norm_back(dk_turned, k_normal, k_inverse, gain_k).reshape(tokens, k_columns)
    d_qkv = jnp.concatenate([dq_raw, dk_raw, d_value], axis=1).astype(BF16)
    g_query, g_key, g_value = settle(tn(xa, d_qkv), (q_columns, k_columns, k_columns))
    d_xa = gather_sum(d_qkv, w_qkv)
    input_grad = give_batch(d_middle + norm_back(d_xa, normal_a, inverse_a, gain_a))
    gain_a_grad = from_group(jnp.sum(d_xa * normal_a, axis=(0, 1)))
    gain_m_grad = from_group(jnp.sum(d_xm * normal_m, axis=(0, 1)))
    gains = lax.psum((gain_a_grad, gain_q_grad, gain_k_grad, gain_m_grad), ("blk", "head"))
    return (
        mixed,
        input_grad,
        g_query,
        g_key,
        g_value,
        g_out,
        g_gate,
        g_up,
        g_down,
        *gains,
    )


def solution(mesh):
    rows = P(None, ("blk", "head"), None)
    weight = P("blk", "head")
    return jax.shard_map(
        local,
        mesh=mesh,
        in_specs=(rows, P(), *([weight] * 7), P(), P(), P(), P(), rows),
        out_specs=(rows, rows, *([weight] * 7), P(), P(), P(), P()),
        check_vma=False,
    )
```

time: 2200 us -> 824 us (0.37)
  waiting for transfers between devices: 1430 us -> 449 us
  starting transfers between devices: 270 us -> 76.8 us
  matrix products: 242 us -> 86.9 us
  other arithmetic: 86.8 us -> 52.6 us
    reduce_scatter x10 -> x0, waiting for transfers between devices: 872 us -> none  [the longest x2 790 us: local(): lax.psum_scatter(summed_term.astype(jnp.bfloat16), 'blk', scatter_dimensi...]
    all_gather x15 -> x0, waiting for transfers between devices: 500 us -> none  [the longest x1 101 us: fetch_weights(): lax.all_gather(owned[6], 'blk', axis=0, tiled=True)]
    ppermute x88 -> x78, waiting for transfers between devices: 50.6 us -> 449 us  [the longest x42 357 us: over_blk(): return lax.ppermute(value, 'blk', [(i, i ^ 1 << bit) for i in range(count)])]
    ppermute x88 -> x78, starting transfers between devices: 268 us -> 76.8 us  [the longest x42 48.3 us: over_blk(): return lax.ppermute(value, 'blk', [(i, i ^ 1 << bit) for i in range(count)])]
    dot_general x168 -> x16, matrix products: 242 us -> 86.9 us  [the longest x4 34.1 us: nn(): return jnp.dot(a, b, preferred_element_type=F32)]
    while x186 -> x0, local copies, waits for them, and re-layouts: 40.2 us -> none
    reduce_sum x53 -> x10, other arithmetic: 34.9 us -> 4.51 us  [the longest x1 1.89 us: local(): gain_a_grad = from_group(jnp.sum(d_xa * normal_a, axis=(0, 1)))]
  transfers between devices with their start and end apart: 113 -> 78, of which waited for: 49 -> 36; matrix products, arithmetic and copies ran while one was open for 16% -> 24% of each run, Pallas kernels for 0% -> 2%
where the time goes in v1:
time: 824 us; the launch traced here: 813 us
  waiting for transfers between devices  449 us (54%)
  matrix products  86.9 us (11%)
  local copies, waits for them, and re-layouts  84.3 us (10%)
  starting transfers between devices  76.8 us (9%)
  other arithmetic  52.6 us (6%)
  blocking collectives  40.4 us (5%)
  Pallas kernels  19.9 us (2%)
    ppermute x42, waiting for transfers between devices, over_blk(): return lax.ppermute(value, 'blk', [(i, i ^ 1 << bit) for i in range(count)])  357 us
    ppermute x36, waiting for transfers between devices, over_head(): lax.ppermute(value, 'head', [(i, i ^ 1 << bit) for i in range(count)])  92.2 us
    ppermute x42, starting transfers between devices, over_blk(): return lax.ppermute(value, 'blk', [(i, i ^ 1 << bit) for i in range(count)])  48.3 us
    psum x1, blocking collectives, local(): lax.psum((gain_a_grad, gain_q_grad, gain_k_grad, gain_m_grad), ('blk', 'h...  40.4 us
    dot_general x4, matrix products, nn(): return jnp.dot(a, b, preferred_element_type=F32)  34.1 us
    dot_general x8, matrix products, nt(): lax.dot_general(a, b, (((1,), (1,)), ((), ())), preferred_element_type=F32)  33.1 us
    ppermute x36, starting transfers between devices, over_head(): lax.ppermute(value, 'head', [(i, i ^ 1 << bit) for i in range(count)])  28.4 us
    unnamed x271, local copies, waits for them, and re-layouts  27.5 us
  transfers between devices with their start and end apart: 78, of which 36 were waited for; matrix products, arithmetic and copies ran while one was open for 24% of the time, Pallas kernels for 2%

profile of v1, /device:TPU:0, one launch (start us, length us, event | category | flops | bytes accessed | tf_op | source)
XLA Modules:
  0.0 813.2 jit_solution(9133636370264525777)
XLA Ops:
  24.4 9.0 %collective-permute-done.13 = bf16[256,256]{1,0:T(8,128)(2,1)S(1)} collective-permute-done((bf16[256,256]{1,0:T(8,128)(2,1)}, bf16[256,256]{1,0:T(8,128)(2,1)S(1)}, u32[]{:S(2)}, u32[]{:S(2)}) %collective-permute-start.13) | collective-permute-done | bytes 131104 | tf_op jit(solution)/shard_map/ppermute | solution.py:37
  70.7 9.2 %collective-permute-done.42 = bf16[128,2048]{1,0:T(8,128)(2,1)S(1)} collective-permute-done((bf16[128,2048]{1,0:T(8,128)(2,1)}, bf16[128,2048]{1,0:T(8,128)(2,1)S(1)}, u32[]{:S(2)}, u32[]{:S(2)}) %collective-permute-start.42) | collective-permute-done | bytes 524320 | tf_op jit(solution)/shard_map/ppermute | solution.py:42
  130.2 12.1 %collective-permute-done.10 = bf16[512,512]{1,0:T(8,128)(2,1)S(1)} collective-permute-done((bf16[512,512]{1,0:T(8,128)(2,1)S(1)}, bf16[512,512]{1,0:T(8,128)(2,1)S(1)}, u32[]{:S(2)}, u32[]{:S(2)}) %collective-permute-start.10) | collective-permute-done | bytes 524320 | tf_op jit(solution)/shard_map/ppermute | solution.py:37
  142.5 15.8 %collective-permute-done.11 = bf16[512,512]{1,0:T(8,128)(2,1)S(1)} collective-permute-done((bf16[512,512]{1,0:T(8,128)(2,1)S(1)}, bf16[512,512]{1,0:T(8,128)(2,1)S(1)}, u32[]{:S(2)}, u32[]{:S(2)}) %collective-permute-start.11) | collective-permute-done | bytes 524320 | tf_op jit(solution)/shard_map/ppermute | solution.py:37
  158.3 12.5 %fusion.74 = f32[1024,512]{0,1:T(8,128)S(1)} fusion(bf16[1024,2048]{1,0:T(8,128)(2,1)S(1)} %slice_dynamic-update-slice_fusion.42, bf16[512,512]{1,0:T(8,128)(2,1)S(1)} %collective-permute-done.11, bf16[512,512]{1,0:T(8,128)(2,1)S(1)} %collective-permute-done.10, bf16[512,512]{1,0:T(8,128)(2,1)S(1)} %collective-permute-done.9, ...), kind=kOutput, calls=%fused_computation.345 | convolution fusion | flops 2155872256 | bytes 8388608 | tf_op jit(solution)/shard_map/dot_general | solution.py:28
  175.2 11.5 %collective-permute-done.12 = bf16[1024,256]{0,1:T(8,128)(2,1)} collective-permute-done((bf16[1024,256]{0,1:T(8,128)(2,1)}, bf16[1024,256]{0,1:T(8,128)(2,1)}, u32[]{:S(2)}, u32[]{:S(2)}) %collective-permute-start.12) | collective-permute-done | bytes 524320 | tf_op jit(solution)/shard_map/ppermute | solution.py:37
  210.9 11.7 %collective-permute-done.19 = bf16[2,64,2048]{2,1,0:T(8,128)(2,1)S(1)} collective-permute-done((bf16[2,64,2048]{2,1,0:T(8,128)(2,1)S(1)}, bf16[2,64,2048]{2,1,0:T(8,128)(2,1)S(1)}, u32[]{:S(2)}, u32[]{:S(2)}) %collective-permute-start.19) | collective-permute-done | bytes 524320 | tf_op jit(solution)/shard_map/ppermute | solution.py:42
  224.5 9.0 %collective-permute-done.18 = bf16[2,64,2048]{2,1,0:T(8,128)(2,1)S(1)} collective-permute-done((bf16[2,64,2048]{2,1,0:T(8,128)(2,1)S(1)}, bf16[2,64,2048]{2,1,0:T(8,128)(2,1)S(1)}, u32[]{:S(2)}, u32[]{:S(2)}) %collective-permute-start.18) | collective-permute-done | bytes 524320 | tf_op jit(solution)/shard_map/ppermute | solution.py:42
  233.5 14.3 %collective-permute-done.20 = bf16[2,64,2048]{2,1,0:T(8,128)(2,1)S(1)} collective-permute-done((bf16[2,64,2048]{2,1,0:T(8,128)(2,1)S(1)}, bf16[2,64,2048]{2,1,0:T(8,128)(2,1)S(1)}, u32[]{:S(2)}, u32[]{:S(2)}) %collective-permute-start.20) | collective-permute-done | bytes 524320 | tf_op jit(solution)/shard_map/ppermute | solution.py:37
  261.7 22.7 %collective-permute-done.22 = bf16[128,2048]{1,0:T(8,128)(2,1)S(1)} collective-permute-done((bf16[128,2048]{1,0:T(8,128)(2,1)S(1)}, bf16[128,2048]{1,0:T(8,128)(2,1)S(1)}, u32[]{:S(2)}, u32[]{:S(2)}) %collective-permute-start.22) | collective-permute-done | bytes 524320 | tf_op jit(solution)/shard_map/ppermute | solution.py:37
  286.5 12.1 %collective-permute-done.23 = bf16[128,2048]{1,0:T(8,128)(2,1)S(1)} collective-permute-done((bf16[128,2048]{1,0:T(8,128)(2,1)S(1)}, bf16[128,2048]{1,0:T(8,128)(2,1)S(1)}, u32[]{:S(2)}, u32[]{:S(2)}) %collective-permute-start.23) | collective-permute-done | bytes 524320 | tf_op jit(solution)/shard_map/ppermute | solution.py:42
  306.5 33.0 %collective-permute-done.30 = bf16[512,1536]{1,0:T(8,128)(2,1)S(1)} collective-permute-done((bf16[512,1536]{1,0:T(8,128)(2,1)S(1)}, bf16[512,1536]{1,0:T(8,128)(2,1)S(1)}, u32[]{:S(2)}, u32[]{:S(2)}) %collective-permute-start.30) | collective-permute-done | bytes 1572896 | tf_op jit(solution)/shard_map/ppermute | solution.py:37
  339.5 50.2 %collective-permute-done.31 = bf16[512,1536]{1,0:T(8,128)(2,1)S(1)} collective-permute-done((bf16[512,1536]{1,0:T(8,128)(2,1)S(1)}, bf16[512,1536]{1,0:T(8,128)(2,1)S(1)}, u32[]{:S(2)}, u32[]{:S(2)}) %collective-permute-start.31) | collective-permute-done | bytes 1572896 | tf_op jit(solution)/shard_map/ppermute | solution.py:37
  398.4 9.9 %multiply_convert_fusion = (bf16[1024,768]{1,0:T(8,128)(2,1)S(1)}, bf16[1024,768]{1,0:T(8,128)(2,1)}, bf16[1024,768]{1,0:T(8,128)(2,1)}) fusion(f32[1024,1536]{1,0:T(8,128)} %fusion.76, bf16[1024,2048]{1,0:T(8,128)(2,1)S(1)} %slice_dynamic-update-slice_fusion.14, bf16[512,768]{1,0:T(8,128)(2,1)S(1)} %collective-permute-done.35, ...), kind=kOutput, calls=%fused_computation.18 | convolution fusion | flops 3245604864 | bytes 18350080 | tf_op jit(solution)/shard_map/dot_general | solution.py:28
  426.9 8.8 %fusion = f32[2048,1536]{0,1:T(8,128)S(1)} fusion(bf16[1024,2048]{1,0:T(8,128)(2,1)S(1)} %copy-done.67, bf16[1024,768]{1,0:T(8,128)(2,1)} %copy-done.97, bf16[1024,768]{1,0:T(8,128)(2,1)} %get-tuple-element.148), kind=kOutput, calls=%fused_computation.12 | convolution fusion | flops 6448742400 | bytes 19922944 | tf_op jit(solution)/shard_map/dot_general | solution.py:24
  438.8 18.7 %collective-permute-done.75 = bf16[1024,768]{0,1:T(8,128)(2,1)} collective-permute-done((bf16[1024,768]{0,1:T(8,128)(2,1)S(1)}, bf16[1024,768]{0,1:T(8,128)(2,1)}, u32[]{:S(2)}, u32[]{:S(2)}) %collective-permute-start.75) | collective-permute-done | bytes 1572896 | tf_op jit(solution)/shard_map/ppermute | solution.py:37
  477.5 17.8 %collective-permute-done.76 = bf16[512,768]{0,1:T(8,128)(2,1)S(1)} collective-permute-done((bf16[512,768]{0,1:T(8,128)(2,1)S(1)}, bf16[512,768]{0,1:T(8,128)(2,1)S(1)}, u32[]{:S(2)}, u32[]{:S(2)}) %collective-permute-start.76) | collective-permute-done | bytes 786464 | tf_op jit(solution)/shard_map/ppermute | solution.py:37
  514.0 10.5 %collective-permute-done.72 = bf16[1024,1536]{0,1:T(8,128)(2,1)} collective-permute-done((bf16[1024,1536]{0,1:T(8,128)(2,1)}, bf16[1024,1536]{0,1:T(8,128)(2,1)}, u32[]{:S(2)}, u32[]{:S(2)}) %collective-permute-start.72) | collective-permute-done | bytes 3145760 | tf_op jit(solution)/shard_map/ppermute | solution.py:37
  542.8 68.8 %collective-permute-done.40 = bf16[64,2048]{1,0:T(8,128)(2,1)S(1)} collective-permute-done((bf16[64,2048]{1,0:T(8,128)(2,1)S(1)}, bf16[64,2048]{1,0:T(8,128)(2,1)S(1)}, u32[]{:S(2)}, u32[]{:S(2)}) %collective-permute-start.40) | collective-permute-done | bytes 262176 | tf_op jit(solution)/shard_map/ppermute | solution.py:37
  616.7 9.9 %collective-permute-done.55 = bf16[128,2048]{1,0:T(8,128)(2,1)S(1)} collective-permute-done((bf16[128,2048]{1,0:T(8,128)(2,1)}, bf16[128,2048]{1,0:T(8,128)(2,1)S(1)}, u32[]{:S(2)}, u32[]{:S(2)}) %collective-permute-start.55) | collective-permute-done | bytes 524320 | tf_op jit(solution)/shard_map/ppermute | solution.py:42
  636.5 11.1 %shard_map.238 = (f32[2,4,128,256]{3,2,1,0:T(8,128)S(1)}, f32[2,2,4,128,128]{4,3,2,1,0:T(8,128)S(1)}, f32[2,2,4,128,128]{4,3,2,1,0:T(8,128)S(1)}) custom-call(s32[45]{0:T(128)S(1)} %concatenate.172.meta_ref, bf16[2,4,128,256]{3,2,1,0:T(8,128)(2,1)S(1)} %copy-done.5, bf16[2,4,128,256]{3,2,1,0:T(8,128)(2,1)S(1)} %bitcast.260, ...), custom_call_target="tpu_custom_call" | custom-call | flops 5368709120 | bytes 7340032 | tf_op jit(solution)/shard_map/pallas_call | solution.py:231
  707.7 9.8 %collective-permute-done.66 = bf16[1024,512]{0,1:T(8,128)(2,1)} collective-permute-done((bf16[1024,512]{0,1:T(8,128)(2,1)}, bf16[1024,512]{0,1:T(8,128)(2,1)}, u32[]{:S(2)}, u32[]{:S(2)}) %collective-permute-start.66) | collective-permute-done | bytes 1048608 | tf_op jit(solution)/shard_map/ppermute | solution.py:37
  726.6 17.6 %collective-permute-done.67 = bf16[512,512]{0,1:T(8,128)(2,1)S(1)} collective-permute-done((bf16[512,512]{0,1:T(8,128)(2,1)S(1)}, bf16[512,512]{0,1:T(8,128)(2,1)S(1)}, u32[]{:S(2)}, u32[]{:S(2)}) %collective-permute-start.67) | collective-permute-done | bytes 524320 | tf_op jit(solution)/shard_map/ppermute | solution.py:37
  771.5 40.4 %all-reduce = (f32[2048]{0:T(1024)}, f32[128]{0:T(128)}, f32[128]{0:T(128)}, f32[2048]{0:T(1024)}) all-reduce(f32[2048]{0:T(1024)S(1)} %bitcast.296, f32[128]{0:T(128)S(1)} %copy-done.79, f32[128]{0:T(128)S(1)} %get-tuple-element.133, f32[2048]{0:T(1024)S(1)} %bitcast.295), channel_id=1, replica_groups=mesh['blk'=8,'head'=4] {'blk','head'}, use_global_device_ids=true, to_apply=%region_13.14 | all-reduce | flops 4352 | bytes 34816 | tf_op jit(solution)/shard_map/psum | solution.py:498
  (617 shorter events, 363.3 us)
Async XLA Ops:
  11.1 53.7 %collective-permute-start.8 = (bf16[256,512]{1,0:T(8,128)(2,1)}, bf16[256,512]{1,0:T(8,128)(2,1)}, u32[]{:S(2)}, u32[]{:S(2)}) collective-permute-start(bf16[256,512]{1,0:T(8,128)(2,1)} %pad_maximum_fusion.14), channel_id=1, source_target_pairs={{0,8},{4,12},{8,0},{12,4},{16,24},{20,28},{24,16},{28,20},{1,9},{5... | collective-permute-start | bytes 786440 | tf_op jit(solution)/shard_map/ppermute | solution.py:37
  16.7 86.4 %collective-permute-start.28 = (bf16[256,1536]{1,0:T(8,128)(2,1)}, bf16[256,1536]{1,0:T(8,128)(2,1)}, u32[]{:S(2)}, u32[]{:S(2)}) collective-permute-start(bf16[256,1536]{1,0:T(8,128)(2,1)} %pad_maximum_fusion.9), channel_id=1, source_target_pairs={{0,8},{4,12},{8,0},{12,4},{16,24},{20,28},{24,16},{28,20},{1,9},{5... | collective-permute-start | bytes 2359304 | tf_op jit(solution)/shard_map/ppermute | solution.py:37
  34.2 93.1 %collective-permute-start.14 = (bf16[512,256]{1,0:T(8,128)(2,1)}, bf16[512,256]{1,0:T(8,128)(2,1)}, u32[]{:S(2)}, u32[]{:S(2)}) collective-permute-start(bf16[512,256]{1,0:T(8,128)(2,1)} %maximum_select_fusion.10), channel_id=1, source_target_pairs={{0,16},{4,20},{8,24},{12,28},{16,0},{20,4},{24,8},{28,12},{1,17},{... | collective-permute-start | bytes 786440 | tf_op jit(solution)/shard_map/ppermute | solution.py:37
  41.1 156.8 %collective-permute-start.15 = (bf16[512,256]{1,0:T(8,128)(2,1)}, bf16[512,256]{1,0:T(8,128)(2,1)}, u32[]{:S(2)}, u32[]{:S(2)}) collective-permute-start(bf16[512,256]{1,0:T(8,128)(2,1)} %maximum_select_fusion.10), channel_id=1, source_target_pairs={{0,4},{4,0},{8,12},{12,8},{16,20},{20,16},{24,28},{28,24},{1,5},{5... | collective-permute-start | bytes 786440 | tf_op jit(solution)/shard_map/ppermute | solution.py:37
  127.0 73.7 %collective-permute-start.45 = (bf16[128,2048]{1,0:T(8,128)(2,1)}, bf16[128,2048]{1,0:T(8,128)(2,1)}, u32[]{:S(2)}, u32[]{:S(2)}) collective-permute-start(bf16[128,2048]{1,0:T(8,128)(2,1)} %reshape_reshape.3), channel_id=1, source_target_pairs={{0,1},{1,0},{2,3},{3,2},{4,5},{5,4},{6,7},{7,6},{8,9},{9,8},{10,11... | collective-permute-start | bytes 1572872 | tf_op jit(solution)/shard_map/ppermute | solution.py:42
  128.0 70.0 %collective-permute-start.16 = (bf16[512,256]{1,0:T(8,128)(2,1)}, bf16[512,256]{1,0:T(8,128)(2,1)S(1)}, u32[]{:S(2)}, u32[]{:S(2)}) collective-permute-start(bf16[512,256]{1,0:T(8,128)(2,1)} %collective-permute-done.14), channel_id=1, source_target_pairs={{0,4},{4,0},{8,12},{12,8},{16,20},{20,16},{24,28},{28,24},{1,5},{5... | collective-permute-start | bytes 786440 | tf_op jit(solution)/shard_map/ppermute | solution.py:37
  142.2 158.4 %collective-permute-start.33 = (bf16[512,768]{1,0:T(8,128)(2,1)}, bf16[512,768]{1,0:T(8,128)(2,1)}, u32[]{:S(2)}, u32[]{:S(2)}) collective-permute-start(bf16[512,768]{1,0:T(8,128)(2,1)} %maximum_select_fusion.5), channel_id=1, source_target_pairs={{0,16},{4,20},{8,24},{12,28},{16,0},{20,4},{24,8},{28,12},{1,17},{... | collective-permute-start | bytes 2359304 | tf_op jit(solution)/shard_map/ppermute | solution.py:37
  186.7 211.7 %collective-permute-start.34 = (bf16[512,768]{1,0:T(8,128)(2,1)}, bf16[512,768]{1,0:T(8,128)(2,1)}, u32[]{:S(2)}, u32[]{:S(2)}) collective-permute-start(bf16[512,768]{1,0:T(8,128)(2,1)} %maximum_select_fusion.5), channel_id=1, source_target_pairs={{0,4},{4,0},{8,12},{12,8},{16,20},{20,16},{24,28},{28,24},{1,5},{5... | collective-permute-start | bytes 2359304 | tf_op jit(solution)/shard_map/ppermute | solution.py:37
  202.2 102.1 %collective-permute-start.29 = (bf16[512,1536]{1,0:T(8,128)(2,1)S(1)}, bf16[512,1536]{1,0:T(8,128)(2,1)S(1)}, u32[]{:S(2)}, u32[]{:S(2)}) collective-permute-start(bf16[512,1536]{1,0:T(8,128)(2,1)S(1)} %copy-done.38), channel_id=1, source_target_pairs={{0,16},{4,20},{8,24},{12,28},{16,0},{20,4},{24,8},{28,12},{1,17},{... | collective-permute-start | bytes 4718600 | tf_op jit(solution)/shard_map/ppermute | solution.py:37
  300.7 38.8 %collective-permute-start.30 = (bf16[512,1536]{1,0:T(8,128)(2,1)S(1)}, bf16[512,1536]{1,0:T(8,128)(2,1)S(1)}, u32[]{:S(2)}, u32[]{:S(2)}) collective-permute-start(bf16[512,1536]{1,0:T(8,128)(2,1)S(1)} %copy-done.38), channel_id=1, source_target_pairs={{0,4},{4,0},{8,12},{12,8},{16,20},{20,16},{24,28},{28,24},{1,5},{5... | collective-permute-start | bytes 4718600 | tf_op jit(solution)/shard_map/ppermute | solution.py:37
  304.3 94.1 %collective-permute-start.35 = (bf16[512,768]{1,0:T(8,128)(2,1)}, bf16[512,768]{1,0:T(8,128)(2,1)S(1)}, u32[]{:S(2)}, u32[]{:S(2)}) collective-permute-start(bf16[512,768]{1,0:T(8,128)(2,1)} %collective-permute-done.33), channel_id=1, source_target_pairs={{0,4},{4,0},{8,12},{12,8},{16,20},{20,16},{24,28},{28,24},{1,5},{5... | collective-permute-start | bytes 2359304 | tf_op jit(solution)/shard_map/ppermute | solution.py:37
  304.4 85.4 %collective-permute-start.31 = (bf16[512,1536]{1,0:T(8,128)(2,1)S(1)}, bf16[512,1536]{1,0:T(8,128)(2,1)S(1)}, u32[]{:S(2)}, u32[]{:S(2)}) collective-permute-start(bf16[512,1536]{1,0:T(8,128)(2,1)S(1)} %collective-permute-done.29), channel_id=1, source_target_pairs={{0,4},{4,0},{8,12},{12,8},{16,20},{20,16},{24,28},{28,24},{1,5},{5... | collective-permute-start | bytes 4718600 | tf_op jit(solution)/shard_map/ppermute | solution.py:37
  414.8 45.0 %collective-permute-start.49 = (bf16[512,2048]{1,0:T(8,128)(2,1)}, bf16[512,2048]{1,0:T(8,128)(2,1)}, u32[]{:S(2)}, u32[]{:S(2)}) collective-permute-start(bf16[512,2048]{1,0:T(8,128)(2,1)} %convolution_convert_fusion.2), channel_id=1, source_target_pairs={{0,1},{1,0},{2,3},{3,2},{4,5},{5,4},{6,7},{7,6},{8,9},{9,8},{10,11... | collective-permute-start | bytes 6291464 | tf_op jit(solution)/shard_map/ppermute | solution.py:42
  426.7 43.5 %collective-permute-start.36 = (bf16[512,2048]{1,0:T(8,128)(2,1)}, bf16[512,2048]{1,0:T(8,128)(2,1)}, u32[]{:S(2)}, u32[]{:S(2)}) collective-permute-start(bf16[512,2048]{1,0:T(8,128)(2,1)} %convolution_convert_fusion.3), channel_id=1, source_target_pairs={{0,1},{1,0},{2,3},{3,2},{4,5},{5,4},{6,7},{7,6},{8,9},{9,8},{10,11... | collective-permute-start | bytes 6291464 | tf_op jit(solution)/shard_map/ppermute | solution.py:42
  438.3 86.2 %collective-permute-start.72 = (bf16[1024,1536]{0,1:T(8,128)(2,1)}, bf16[1024,1536]{0,1:T(8,128)(2,1)}, u32[]{:S(2)}, u32[]{:S(2)}) collective-permute-start(bf16[1024,1536]{0,1:T(8,128)(2,1)} %slice.1019), channel_id=1, source_target_pairs={{0,4},{4,0},{8,12},{12,8},{16,20},{20,16},{24,28},{28,24},{1,5},{5... | collective-permute-start | bytes 9437192 | tf_op jit(solution)/shard_map/ppermute | solution.py:37
  469.9 60.7 %collective-permute-start.50 = (bf16[2,64,2048]{2,1,0:T(8,128)(2,1)}, bf16[2,64,2048]{2,1,0:T(8,128)(2,1)S(1)}, u32[]{:S(2)}, u32[]{:S(2)}) collective-permute-start(bf16[2,64,2048]{2,1,0:T(8,128)(2,1)} %get-tuple-element.156), channel_id=1, source_target_pairs={{0,2},{1,3},{2,0},{3,1},{4,6},{5,7},{6,4},{7,5},{8,10},{9,11},{10,... | collective-permute-start | bytes 1572872 | tf_op jit(solution)/shard_map/ppermute | solution.py:42
  530.6 98.2 %collective-permute-start.73 = (bf16[512,1536]{0,1:T(8,128)(2,1)}, bf16[512,1536]{0,1:T(8,128)(2,1)}, u32[]{:S(2)}, u32[]{:S(2)}) collective-permute-start(bf16[512,1536]{0,1:T(8,128)(2,1)} %slice.1021), channel_id=1, source_target_pairs={{0,16},{4,20},{8,24},{12,28},{16,0},{20,4},{24,8},{28,12},{1,17},{... | collective-permute-start | bytes 4718600 | tf_op jit(solution)/shard_map/ppermute | solution.py:37
  536.1 78.2 %collective-permute-start.53 = (bf16[128,2048]{1,0:T(8,128)(2,1)S(1)}, bf16[128,2048]{1,0:T(8,128)(2,1)}, u32[]{:S(2)}, u32[]{:S(2)}) collective-permute-start(bf16[128,2048]{1,0:T(8,128)(2,1)S(1)} %bitcast.268), channel_id=1, source_target_pairs={{0,2},{1,3},{2,0},{3,1},{4,6},{5,7},{6,4},{7,5},{8,10},{9,11},{10,... | collective-permute-start | bytes 1572872 | tf_op jit(solution)/shard_map/ppermute | solution.py:42
  537.9 74.7 %collective-permute-start.54 = (bf16[128,2048]{1,0:T(8,128)(2,1)S(1)}, bf16[128,2048]{1,0:T(8,128)(2,1)}, u32[]{:S(2)}, u32[]{:S(2)}) collective-permute-start(bf16[128,2048]{1,0:T(8,128)(2,1)S(1)} %bitcast.269), channel_id=1, source_target_pairs={{0,8},{4,12},{8,0},{12,4},{16,24},{20,28},{24,16},{28,20},{1,9},{5... | collective-permute-start | bytes 1572872 | tf_op jit(solution)/shard_map/ppermute | solution.py:37
  538.8 89.9 %collective-permute-start.56 = (bf16[128,2048]{1,0:T(8,128)(2,1)S(1)}, bf16[128,2048]{1,0:T(8,128)(2,1)S(1)}, u32[]{:S(2)}, u32[]{:S(2)}) collective-permute-start(bf16[128,2048]{1,0:T(8,128)(2,1)S(1)} %bitcast.270), channel_id=1, source_target_pairs={{0,1},{1,0},{2,3},{3,2},{4,5},{5,4},{6,7},{7,6},{8,9},{9,8},{10,11... | collective-permute-start | bytes 1572872 | tf_op jit(solution)/shard_map/ppermute | solution.py:42
  541.2 70.5 %collective-permute-start.40 = (bf16[64,2048]{1,0:T(8,128)(2,1)S(1)}, bf16[64,2048]{1,0:T(8,128)(2,1)S(1)}, u32[]{:S(2)}, u32[]{:S(2)}) collective-permute-start(bf16[64,2048]{1,0:T(8,128)(2,1)S(1)} %squeeze.57), channel_id=1, source_target_pairs={{0,16},{4,20},{8,24},{12,28},{16,0},{20,4},{24,8},{28,12},{1,17},{... | collective-permute-start | bytes 786440 | tf_op jit(solution)/shard_map/ppermute | solution.py:37
  631.9 62.6 %collective-permute-start.74 = (bf16[256,1536]{0,1:T(8,128)(2,1)}, bf16[256,1536]{0,1:T(8,128)(2,1)}, u32[]{:S(2)}, u32[]{:S(2)}) collective-permute-start(bf16[256,1536]{0,1:T(8,128)(2,1)} %dynamic-slice_convert_fusion), channel_id=1, source_target_pairs={{0,8},{4,12},{8,0},{12,4},{16,24},{20,28},{24,16},{28,20},{1,9},{5... | collective-permute-start | bytes 2359304 | tf_op jit(solution)/shard_map/ppermute | solution.py:37
  680.1 40.3 %collective-permute-start.61 = (bf16[512,2048]{1,0:T(8,128)(2,1)}, bf16[512,2048]{1,0:T(8,128)(2,1)}, u32[]{:S(2)}, u32[]{:S(2)}) collective-permute-start(bf16[512,2048]{1,0:T(8,128)(2,1)} %convolution_convert_fusion.1), channel_id=1, source_target_pairs={{0,1},{1,0},{2,3},{3,2},{4,5},{5,4},{6,7},{7,6},{8,9},{9,8},{10,11... | collective-permute-start | bytes 6291464 | tf_op jit(solution)/shard_map/ppermute | solution.py:42
  769.9 42.0 %collective-permute-start.65 = (bf16[64,2048]{1,0:T(8,128)(2,1)S(1)}, bf16[64,2048]{1,0:T(8,128)(2,1)S(1)}, u32[]{:S(2)}, u32[]{:S(2)}) collective-permute-start(bf16[64,2048]{1,0:T(8,128)(2,1)S(1)} %convert_element_type.306), channel_id=1, source_target_pairs={{0,16},{4,20},{8,24},{12,28},{16,0},{20,4},{24,8},{28,12},{1,17},{... | collective-permute-start | bytes 786440 | tf_op jit(solution)/shard_map/ppermute | solution.py:37
  (152 other events, 3522.3 us)

commit v2 on v1

--- a/solution.py
+++ b/solution.py
@@ -14,6 +14,7 @@
 BF16 = jnp.bfloat16
 
 TENSOR_BIT = 1
+SEQ_BIT = 0
 
 
 def nt(a, b):
@@ -32,14 +33,18 @@
     return (value >> bit) & 1
 
 
-def over_blk(value, bit):
+def over_blk(value, mask):
     count = lax.axis_size("blk")
-    return lax.ppermute(value, "blk", [(i, i ^ (1 << bit)) for i in range(count)])
-
-
-def over_head(value, bit):
+    return lax.ppermute(value, "blk", [(i, i ^ mask) for i in range(count)])
+
+
+def over_head(value, mask):
     count = lax.axis_size("head")
-    return lax.ppermute(value, "head", [(i, i ^ (1 << bit)) for i in range(count)])
+    return lax.ppermute(value, "head", [(i, i ^ mask) for i in range(count)])
+
+
+def pin(values):
+    return lax.optimization_barrier(values)
 
 
 def in_order(flag, own, other, axis):
@@ -260,6 +265,224 @@
     )(meta, q, do, k, v, start, out_t, total_e)
 
 
+TINY_COST = pl.CostEstimate(flops=0, bytes_accessed=0, transcendentals=0)
+
+
+def remote(src, dst, send, recv, target):
+    copy = pltpu.make_async_remote_copy(
+        src_ref=src, dst_ref=dst, send_sem=send, recv_sem=recv, device_id=target, device_id_type=pl.DeviceIdType.MESH
+    )
+    copy.start()
+    return copy
+
+
+class Plan:
+    def __init__(self):
+        self.inputs, self.shapes, self.aliases, self.jobs = [], [], {}, []
+
+    def read(self, array):
+        self.inputs.append(array)
+        return ("in", len(self.inputs) - 1)
+
+    def fresh(self, shape, dtype):
+        self.shapes.append(jax.ShapeDtypeStruct(shape, dtype))
+        return ("out", len(self.shapes) - 1)
+
+    def through(self, array):
+        self.inputs.append(array)
+        self.aliases[len(self.inputs) - 1] = len(self.shapes)
+        return self.fresh(array.shape, array.dtype)
+
+    def copy(self, src, dst, mask, after=None, point=0):
+        self.jobs.append((src, dst, mask, after, point))
+        return len(self.jobs) - 1
+
+
+def run(plan, main, collective_id):
+    inputs, in_specs, out_shapes, out_specs, scratch, body = main
+    n_in, n_out = len(inputs), len(out_shapes)
+    m_in, m_out = len(plan.inputs), len(plan.shapes)
+    jobs = plan.jobs
+    masks = sorted({job[2] for job in jobs if job[2]} - {1 << TENSOR_BIT})
+    any_spec = pl.BlockSpec(memory_space=pl.ANY)
+
+    def kernel(*refs):
+        main_in, refs = refs[:n_in], refs[n_in:]
+        plan_in, refs = refs[:m_in], refs[m_in:]
+        main_out, refs = refs[:n_out], refs[n_out:]
+        plan_out, refs = refs[:m_out], refs[m_out:]
+        send, recv, *rest = refs
+        blk, head = lax.axis_index("blk"), lax.axis_index("head")
+        core, near, across = (blk, head ^ 1), (blk, head ^ 2), (blk ^ (1 << TENSOR_BIT), head)
+        barrier = pltpu.get_barrier_semaphore()
+        partners = [core, near, across, *[(blk ^ m, head) for m in masks]]
+        for target in partners:
+            pl.semaphore_signal(barrier, inc=1, device_id=target, device_id_type=pl.DeviceIdType.MESH)
+        pl.semaphore_wait(barrier, len(partners))
+        started, arrived = {}, set()
+
+        def arrive(i):
+            if i not in arrived:
+                arrived.add(i)
+                (started[i].wait_recv if jobs[i][2] else started[i].wait)()
+
+        def part(side):
+            (kind, index), cut = side
+            return cut((plan_in if kind == "in" else plan_out)[index])
+
+        def issue(point):
+            for i, (src, dst, mask, after, at) in enumerate(jobs):
+                if i in started or (at != point and point is not None):
+                    continue
+                if after is not None:
+                    arrive(after)
+                if mask:
+                    started[i] = remote(part(src), part(dst), send.at[i], recv.at[i], (blk ^ mask, head))
+                else:
+                    started[i] = pltpu.make_async_copy(part(src), part(dst), recv.at[i])
+                    started[i].start()
+
+        point = 0
+        for _ in body((core, near, across), main_in, main_out, rest):
+            issue(point)
+            point += 1
+        issue(None)
+        for i in range(len(jobs)):
+            arrive(i)
+            if jobs[i][2]:
+                started[i].wait_send()
+
+    results = pl.pallas_call(
+        kernel,
+        out_shape=[*out_shapes, *plan.shapes],
+        in_specs=[*in_specs, *[any_spec] * m_in],
+        out_specs=[*out_specs, *[any_spec] * m_out],
+        scratch_shapes=[
+            pltpu.SemaphoreType.DMA((max(1, len(jobs)),)),
+            pltpu.SemaphoreType.DMA((max(1, len(jobs)),)),
+            *scratch,
+        ],
+        input_output_aliases={n_in + i: n_out + o for i, o in plan.aliases.items()},
+        compiler_params=pltpu.CompilerParams(
+            collective_id=collective_id, has_side_effects=True, vmem_limit_bytes=32 * 1024 * 1024
+        ),
+        cost_estimate=TINY_COST,
+    )(*inputs, *plan.inputs)
+    return results[:n_out], results[n_out:]
+
+
+def spread_main(flat, chunk):
+    rows, width = flat.shape[0] // 2, flat.shape[1]
+    pieces = width // chunk
+
+    def body(partners, ins, outs, scratch):
+        core, near, across = partners
+        (s_ref,), (o_ref,), (local_sem, send, recv) = ins, outs, scratch
+        first = remote(s_ref, o_ref.at[0, :, 0, 1], send.at[0], recv.at[0], near)
+        second = [
+            remote(
+                s_ref.at[:, :, pl.ds(i * chunk, chunk)],
+                o_ref.at[0, :, 1, 0, :, pl.ds((i ^ 1) * chunk, chunk)],
+                send.at[6 + i],
+                recv.at[6 + i],
+                across,
+            )
+            for i in range(pieces)
+        ]
+        third = remote(s_ref, o_ref.at[1, :, 0, 0], send.at[1], recv.at[1], core)
+        own = pltpu.make_async_copy(s_ref, o_ref.at[0, :, 0, 0], local_sem)
+        own.start()
+        yield
+        for copy in second:
+            copy.wait_recv()
+        fourth = remote(o_ref.at[0, :, 1, 0], o_ref.at[0, :, 1, 1], send.at[2], recv.at[2], near)
+        fifth = remote(o_ref.at[0, :, 1, 0], o_ref.at[1, :, 1, 0], send.at[3], recv.at[3], core)
+        yield
+        first.wait_recv()
+        sixth = remote(o_ref.at[0, :, 0, 1], o_ref.at[1, :, 0, 1], send.at[4], recv.at[4], core)
+        yield
+        fourth.wait_recv()
+        seventh = remote(o_ref.at[0, :, 1, 1], o_ref.at[1, :, 1, 1], send.at[5], recv.at[5], core)
+        yield
+        own.wait()
+        for copy in (first, *second, third, fourth, fifth, sixth, seventh):
+            copy.wait_send()
+        for copy in (third, fifth, sixth, seventh):
+            copy.wait_recv()
+
+    any_spec = pl.BlockSpec(memory_space=pl.ANY)
+    return (
+        [flat.reshape(2, rows, width)],
+        [any_spec],
+        [jax.ShapeDtypeStruct((2, 2, 2, 2, rows, width), flat.dtype)],
+        [any_spec],
+        [
+            pltpu.SemaphoreType.DMA,
+            pltpu.SemaphoreType.DMA((6 + pieces,)),
+            pltpu.SemaphoreType.DMA((6 + pieces,)),
+        ],
+        body,
+    )
+
+
+def gather_main(partial, chunk):
+    rows, width = partial.shape[0] // 16, partial.shape[1]
+    share = (2, rows, width)
+    pieces = width // chunk
+
+    def body(partners, ins, outs, scratch):
+        core, near, across = partners
+        (p_ref,), (o_ref,) = ins, outs
+        core_in, out_y, in_y, out_t, in_t, hold, send, recv = scratch
+        order = ((1, 1), (0, 1), (1, 0), (0, 0))
+        from_core = [
+            remote(p_ref.at[1, :, t, y], core_in.at[i], send.at[i], recv.at[i], core) for i, (t, y) in enumerate(order)
+        ]
+        from_y = []
+        for i in range(2):
+            t, y = order[i]
+            from_core[i].wait_recv()
+            out_y[i] = (p_ref[0, :, t, y].astype(F32) + core_in[i].astype(F32)).astype(BF16)
+            from_y.append(remote(out_y.at[i], in_y.at[i], send.at[4 + i], recv.at[4 + i], near))
+        yield
+        from_core[2].wait_recv()
+        hold[...] = p_ref[0, :, 1, 0].astype(F32) + core_in[2].astype(F32)
+        from_y[0].wait_recv()
+        for i in range(pieces):
+            a, b = slice(i * chunk, (i + 1) * chunk), slice((i ^ 1) * chunk, ((i ^ 1) + 1) * chunk)
+            out_t[:, :, b] = (hold[:, :, a] + in_y[0, :, :, a].astype(F32)).astype(BF16)
+        from_t = remote(out_t, in_t, send.at[6], recv.at[6], across)
+        yield
+        from_core[3].wait_recv()
+        hold[...] = p_ref[0, :, 0, 0].astype(F32) + core_in[3].astype(F32)
+        from_y[1].wait_recv()
+        hold[...] += in_y[1].astype(F32)
+        yield
+        from_t.wait_recv()
+        o_ref[...] = hold[...] + in_t[...].astype(F32)
+        for copy in (*from_core, *from_y, from_t):
+            copy.wait_send()
+
+    vmem_spec = pl.BlockSpec(memory_space=pltpu.VMEM)
+    return (
+        [partial.reshape(2, 2, 2, 2, rows, width)],
+        [vmem_spec],
+        [jax.ShapeDtypeStruct(share, F32)],
+        [vmem_spec],
+        [
+            pltpu.VMEM((4, *share), BF16),
+            pltpu.VMEM((2, *share), BF16),
+            pltpu.VMEM((2, *share), BF16),
+            pltpu.VMEM(share, BF16),
+            pltpu.VMEM(share, BF16),
+            pltpu.VMEM(share, F32),
+            pltpu.SemaphoreType.DMA((7,)),
+            pltpu.SemaphoreType.DMA((7,)),
+        ],
+        body,
+    )
+
+
 def local(
     hidden_in,
     lengths,
@@ -279,9 +502,11 @@
     ring = lax.axis_size("blk")
     bits = ring.bit_length() - 1
     batch_bit = bits - 1
-    seq_bits = [i for i in range(bits) if i not in (TENSOR_BIT, batch_bit)]
-    data_bits = [batch_bit, *seq_bits]
+    extra_bits = [i for i in range(bits) if i not in (TENSOR_BIT, SEQ_BIT, batch_bit)]
+    seq_bits = [SEQ_BIT, *extra_bits]
     parts = 1 << len(seq_bits)
+    bit_order = [batch_bit, TENSOR_BIT, SEQ_BIT, *extra_bits]
+    b_mask, t_mask, x_mask = 1 << batch_bit, 1 << TENSOR_BIT, 1 << SEQ_BIT
     blk, head = lax.axis_index("blk"), lax.axis_index("head")
     batch, tensor = bit_of(blk, batch_bit), bit_of(blk, TENSOR_BIT)
 
@@ -295,85 +520,143 @@
     heads = query_weight.shape[1] // (2 * head_size)
     ff = gate_weight.shape[1] // 2
 
-    axis_order = [*reversed(seq_bits), batch_bit, TENSOR_BIT]
-
-    def to_group(values):
-        lead = values.shape[:-1]
-        n = len(lead)
-        cut = values.reshape(*lead, *([2] * bits), row_features)
-        for b in data_bits:
-            cut = jnp.where(bit_of(blk, b) == 1, jnp.flip(cut, n + bits - 1 - b), cut)
-        order = [*range(n), *[n + bits - 1 - b for b in axis_order], n + bits]
-        return jnp.transpose(cut, order).reshape(*lead, width)
-
-    def from_group(values):
-        lead = values.shape[:-1]
-        n = len(lead)
-        cut = values.reshape(*lead, *([2] * bits), row_features)
-        back = [axis_order.index(b) for b in range(bits - 1, -1, -1)]
-        cut = jnp.transpose(cut, [*range(n), *[n + i for i in back], n + bits])
-        for b in data_bits:
-            cut = jnp.where(bit_of(blk, b) == 1, jnp.flip(cut, n + bits - 1 - b), cut)
-        return cut.reshape(*lead, width)
-
-    def cut_half(weight, which):
-        return lax.dynamic_slice_in_dim(weight, which * (weight.shape[1] // 2), weight.shape[1] // 2, 1)
-
-    def collect(weights):
-        own = jnp.concatenate([cut_half(w, tensor) for w in weights], axis=1)
-        other = over_blk(jnp.concatenate([cut_half(w, 1 - tensor) for w in weights], axis=1), TENSOR_BIT)
-        chunks = [in_order(tensor, own, other, 0)]
-        for b in data_bits:
-            chunks = chunks + [over_blk(c, b) for c in chunks]
-        return jnp.concatenate(chunks, axis=0)
-
-    def settle(grad, column_widths):
-        for b in reversed(data_bits):
+    def moved(values, place_of):
+        axis = values.ndim - 1
+        return jnp.concatenate(
+            [
+                lax.dynamic_slice_in_dim(values, place_of(i) * row_features, row_features, axis)
+                for i in range(ring)
+            ],
+            axis=axis,
+        )
+
+    def regroup(values):
+        return moved(values, lambda p: blk ^ sum(((p >> i) & 1) << b for i, b in enumerate(bit_order)))
+
+    def ungroup(values):
+        return moved(values, lambda n: sum(bit_of(blk ^ n, b) << i for i, b in enumerate(bit_order)))
+
+    def rows_at(p):
+        return lambda ref: ref.at[pl.ds(p * row_features, row_features), :]
+
+    def put(plan, weights, buffer, near, far, onward_far=True, point=0):
+        here = [plan.read(w) for w in weights]
+        at, columns = 0, []
+        for w in weights:
+            columns.append((at, w.shape[1] // 2))
+            at += w.shape[1] // 2
+
+        def half_of(k, other):
+            n = columns[k][1]
+
+            def cut(ref):
+                place = bit_of(lax.axis_index("blk"), TENSOR_BIT)
+                place = 1 - place if other else place
+                return ref.at[:, pl.ds(pl.multiple_of(place * n, n), n)]
+
+            return cut
+
+        def into(k, p):
+            start, n = columns[k]
+            return lambda ref: ref.at[pl.ds(p * row_features, row_features), pl.ds(start, n)]
+
+        def from_here(p, mask):
+            ids = [
+                plan.copy((here[k], half_of(k, mask & t_mask)), (buffer, into(k, p)), mask, point=point)
+                for k in range(len(weights))
+            ]
+            return ids
+
+        if near:
+            by_t = from_here(2, t_mask)
+            from_here(4, x_mask)
+            from_here(0, 0)
+        if far:
+            by_b = from_here(1, b_mask)
+            by_tb = from_here(3, b_mask | t_mask)
+        if near:
+            for k, i in enumerate(by_t):
+                plan.copy((buffer, into(k, 2)), (buffer, into(k, 6)), x_mask, after=i, point=point + 1)
+        if far and onward_far:
+            for p, ids in ((1, by_b), (3, by_tb)):
+                for k, i in enumerate(ids):
+                    plan.copy((buffer, into(k, p)), (buffer, into(k, p + 4)), x_mask, after=i, point=point + 3)
+
+    def put_onward(plan, buffer):
+        for p in (1, 3):
+            plan.copy((buffer, rows_at(p)), (buffer, rows_at(p + 4)), x_mask)
+
+    def buffer_shape(weights):
+        return (8 * row_features, sum(w.shape[1] for w in weights) // 2)
+
+    def whole_weight(buffer):
+        pieces = [buffer]
+        for b in extra_bits:
+            pieces = pieces + [over_blk(c, 1 << b) for c in pieces]
+        return jnp.concatenate(pieces, axis=0) if extra_bits else buffer
+
+    def split_grad(grad):
+        for b in reversed(extra_bits):
             n = grad.shape[0] // 2
-            grad = grad[:n] + over_blk(grad[n:].astype(BF16), b).astype(F32)
-        own = lax.dynamic_slice_in_dim(grad, tensor * row_features, row_features, 0)
-        other = over_blk(
-            lax.dynamic_slice_in_dim(grad, (1 - tensor) * row_features, row_features, 0).astype(BF16), TENSOR_BIT
-        ).astype(F32)
+            grad = grad[:n] + over_blk(grad[n:].astype(BF16), 1 << b).astype(F32)
+        n = grad.shape[0] // 2
+        return grad[:n], grad[n:].astype(BF16)
+
+    def everything(ref):
+        return ref
+
+    def fold(plan, away):
+        out = plan.fresh(away.shape, away.dtype)
+        plan.copy((plan.read(away), everything), (out, everything), x_mask)
+
+    def to_settle(keep, got):
+        total = keep + got.astype(F32)
+        return total[:row_features], total[row_features:].astype(BF16)
+
+    def settle(plan, away):
+        out, here = plan.fresh(away.shape, away.dtype), plan.read(away)
+        for i, mask in enumerate((b_mask, t_mask, b_mask | t_mask)):
+            plan.copy((here, rows_at(i)), (out, rows_at(i)), mask)
+
+    def settle_apart(away):
+        cut = [away[i * row_features : (i + 1) * row_features] for i in range(3)]
+        return jnp.concatenate(
+            [over_blk(c, mask) for c, mask in zip(cut, (b_mask, t_mask, b_mask | t_mask))], axis=0
+        )
+
+    def settled(own, got, column_widths):
+        f = row_features
+        own = own + got[:f].astype(F32)
+        other = got[f : 2 * f].astype(F32) + got[2 * f :].astype(F32)
         results, at = [], 0
         for w in column_widths:
             results.append(in_order(tensor, own[:, at : at + w], other[:, at : at + w], 1))
             at += w
         return results
 
-    def spread(rows):
-        flat = rows.reshape(2 * local_rows, width)
-        by_y = over_head(flat, 1)
-        by_t = over_blk(flat, TENSOR_BIT)
-        by_ty = over_head(by_t, 1)
-        near = [flat, by_y, by_t, by_ty]
-        far = [over_head(piece, 0) for piece in near]
-        cut = [
-            piece.reshape(2, local_rows, width)[m]
-            for group in (near, far)
-            for m in range(2)
-            for piece in group
-        ]
-        return jnp.concatenate(cut, axis=0)
-
-    def gather_sum(left, weight):
-        n = tokens // 2
-        away = over_head(nt(left[n:], weight).astype(BF16), 0)
-        held = (nt(left[:n], weight) + away.astype(F32)).reshape(2, 2, 2, local_rows, width)
-        from_y1 = over_head(held[:, 1, 1].astype(BF16), 1)
-        from_y0 = over_head(held[:, 0, 1].astype(BF16), 1)
-        from_t = over_blk((held[:, 1, 0] + from_y1.astype(F32)).astype(BF16), TENSOR_BIT)
-        return held[:, 0, 0] + from_y0.astype(F32) + from_t.astype(F32)
+    chunk = 2 * row_features
+    ids = iter(range(100))
+
+    def spread(flat, plan):
+        (out,), rest = run(plan, spread_main(flat, chunk), next(ids))
+        return out.reshape(tokens, width), rest
+
+    def gather_sum(partial, plan):
+        (out,), rest = run(plan, gather_main(partial, chunk), next(ids))
+        return out.reshape(2 * local_rows, width), rest
+
+    def partial_sum(left, weight):
+        return nt(left, weight).astype(BF16)
 
     def take_batch(rows):
         mine = lax.dynamic_index_in_dim(rows, batch, 0, keepdims=False)
         theirs = lax.dynamic_index_in_dim(rows, 1 - batch, 0, keepdims=False)
-        return to_group(jnp.stack([mine, over_blk(theirs, batch_bit)]))
+        return regroup(jnp.concatenate([mine, over_blk(theirs, b_mask)], axis=0))
 
     def give_batch(rows):
-        rows = from_group(rows)
-        back = over_blk(rows[1].astype(BF16), batch_bit).astype(rows.dtype)
-        return in_order(batch, rows[0][None], back[None], 0)
+        rows = ungroup(rows)
+        back = over_blk(rows[local_rows:].astype(BF16), b_mask).astype(rows.dtype)
+        return in_order(batch, rows[None, :local_rows], back[None], 0)
 
     length_row = lax.dynamic_index_in_dim(lengths, batch, 0, keepdims=False)
     doc_ends = jnp.cumsum(length_row)
@@ -418,21 +701,34 @@
         scaled = grad * gain
         return inverse * (scaled - normed * jnp.mean(scaled * normed, axis=-1, keepdims=True))
 
-    gain_a = to_group(attn_gain.astype(F32))
-    gain_m = to_group(mlp_gain.astype(F32))
+    gain_a = regroup(attn_gain.astype(F32))
+    gain_m = regroup(mlp_gain.astype(F32))
     gain_q = query_gain.astype(F32)
     gain_k = key_gain.astype(F32)
 
-    rows_in = take_batch(hidden_in).astype(F32)
-    cot = take_batch(cotangent)
-    w_qkv = collect((query_weight, key_matrix, value_matrix))
+    a_weights, o_weights = (query_weight, key_matrix, value_matrix), (out_weight,)
+    x_low = take_batch(hidden_in)
+    rows_in = x_low.astype(F32)
     inverse_a = rms(rows_in)
     normal_a = rows_in * inverse_a
-    xa = spread((normal_a * gain_a).astype(BF16))
-    w_out = collect((out_weight,))
-    w_gu = collect((gate_weight, up_weight))
-    w_down = collect((down_weight,))
-    cot_all = spread(cot)
+
+    plan = Plan()
+    a_buffer = plan.fresh(buffer_shape(a_weights), BF16)
+    put(plan, a_weights, a_buffer, True, True)
+    here, cot_out = plan.read(cotangent), plan.fresh((2, local_rows, width), BF16)
+    plan.copy((here, lambda ref: ref.at[bit_of(lax.axis_index("blk"), batch_bit)]), (cot_out, lambda ref: ref.at[0]), 0)
+    plan.copy(
+        (here, lambda ref: ref.at[1 - bit_of(lax.axis_index("blk"), batch_bit)]), (cot_out, lambda ref: ref.at[1]), b_mask
+    )
+    put(plan, (down_weight,), plan.fresh(buffer_shape((down_weight,)), BF16), True, False)
+    xa, (w_qkv, cot, w_down) = spread((normal_a * gain_a).astype(BF16), plan)
+    w_qkv = whole_weight(w_qkv)
+    cot = regroup(cot.reshape(2 * local_rows, width))
+
+    (xa, up_in) = pin((xa, up_weight))
+    up_half = lax.dynamic_slice_in_dim(up_in, tensor * ff, ff, 1)
+    up_other = lax.dynamic_slice_in_dim(up_in, (1 - tensor) * ff, ff, 1)
+    up_b, up_tb = over_blk(up_half, b_mask), over_blk(up_other, b_mask | t_mask)
 
     qkv = nn(xa, w_qkv)
     q_columns, k_columns = heads * head_size, head_size
@@ -443,46 +739,90 @@
     q_normal, k_normal = q_raw * q_inverse, k_raw * k_inverse
     query = rope(q_normal * gain_q).astype(BF16).reshape(2, 4, half, q_columns)
     key = rope(k_normal * gain_k).astype(BF16).reshape(tokens, head_size)
-    key_value = [jnp.concatenate([key, value], axis=1)]
-    for b in seq_bits:
-        key_value = key_value + [over_blk(c, b) for c in key_value]
+    key_value = jnp.concatenate([key, value], axis=1)
+
+    plan = Plan()
+    put(plan, o_weights, plan.fresh(buffer_shape(o_weights), BF16), True, True)
+    kv_out = plan.fresh(key_value.shape, BF16)
+    plan.copy((plan.read(key_value), everything), (kv_out, everything), x_mask)
+    put(plan, (down_weight,), plan.through(w_down), False, True, onward_far=False)
+    put(plan, (gate_weight,), plan.fresh(buffer_shape((gate_weight,)), BF16), True, False)
+    cot_all, (w_out, kv_x, w_down, w_gate) = spread(cot, plan)
+    w_out = whole_weight(w_out)
+    key_value = [key_value, kv_x]
+    for b in extra_bits:
+        key_value = key_value + [over_blk(c, 1 << b) for c in key_value]
     key_value = jnp.stack(key_value)
     keys = key_value[..., :head_size].reshape(parts, 2, 4, half, head_size)
     values = key_value[..., head_size:].reshape(parts, 2, 4, half, head_size)
     attn, attn_t, total_e = attend(meta, query, keys, values, start_lanes, scaling)
     attn = attn.reshape(tokens, q_columns)
-    middle = rows_in + gather_sum(attn, w_out)
+
+    plan = Plan()
+    put_onward(plan, plan.through(w_down))
+    put(plan, (gate_weight,), plan.through(w_gate), False, True, onward_far=False)
+    put(plan, (up_weight,), plan.fresh(buffer_shape((up_weight,)), BF16), True, False)
+    out_sum, (w_down, w_gate, w_up) = gather_sum(partial_sum(attn, w_out), plan)
+    w_down = whole_weight(w_down)
+    middle = x_low.astype(F32) + out_sum
     inverse_m = rms(middle)
     normal_m = middle * inverse_m
-    xm = spread((normal_m * gain_m).astype(BF16))
+
+    plan = Plan()
+    put_onward(plan, plan.through(w_gate))
+    u_buffer = plan.through(w_up)
+    for p, got in ((1, up_b), (3, up_tb)):
+        here = plan.read(got)
+        plan.copy((here, everything), (u_buffer, rows_at(p + 4)), x_mask)
+        plan.copy((here, everything), (u_buffer, rows_at(p)), 0)
+    xm, (w_gate, w_up) = spread((normal_m * gain_m).astype(BF16), plan)
+    w_gate, w_up = whole_weight(w_gate), whole_weight(w_up)
     d_active = nn(cot_all, w_down)
-    gate_up = nn(xm, w_gu)
-    gate, up = gate_up[:, :ff], gate_up[:, ff:]
+    gate = nn(xm, w_gate)
+    up = nn(xm, w_up)
     sig = jax.nn.sigmoid(gate)
     silu = gate * sig
     active = (silu * up).astype(BF16)
     d_gate = (d_active * up * sig * (1.0 + gate * (1.0 - sig))).astype(BF16)
     d_up = (d_active * silu).astype(BF16)
-    d_gu = jnp.concatenate([d_gate, d_up], axis=1)
-
-    d_xm = gather_sum(d_gu, w_gu)
-    mixed = give_batch((middle + gather_sum(active, w_down)).astype(BF16))
-    g_gate, g_up = settle(tn(xm, d_gu), (ff, ff))
-    (g_down,) = settle(tn(cot_all, active), (ff,))
+
+    keep_down, away_down = split_grad(tn(cot_all, active))
+    plan = Plan()
+    fold(plan, away_down)
+    d_xm, (got,) = gather_sum((nt(d_gate, w_gate) + nt(d_up, w_up)).astype(BF16), plan)
+    own_down, away_down = to_settle(keep_down, got)
+    keep_gate, away_gate = split_grad(tn(xm, d_gate))
     d_middle = cot.astype(F32) + norm_back(d_xm, normal_m, inverse_m, gain_m)
-    d_mid_all = spread(d_middle.astype(BF16))
+
+    plan = Plan()
+    settle(plan, away_down)
+    fold(plan, away_gate)
+    d_mid_all, (got_down, got) = spread(d_middle.astype(BF16), plan)
+    (g_down,) = settled(own_down, got_down, (ff,))
+    own_gate, away_gate = to_settle(keep_gate, got)
+    keep_up, away_up = split_grad(tn(xm, d_up))
+    keep_out, away_out = split_grad(tn(d_mid_all, attn))
     d_attn = nn(d_mid_all, w_out).astype(BF16).reshape(2, 4, half, q_columns)
     d_query, d_key, d_value = attend_back(
         meta, query, d_attn, keys, values, start_lanes, attn_t, total_e, scaling
     )
-    (g_out,) = settle(tn(d_mid_all, attn), (q_columns,))
     d_key_value = jnp.concatenate(
         [d_key.reshape(parts, tokens, head_size), d_value.reshape(parts, tokens, head_size)], axis=-1
     )
-    for b in reversed(seq_bits):
+    for b in reversed(extra_bits):
         n = d_key_value.shape[0] // 2
-        d_key_value = d_key_value[:n] + over_blk(d_key_value[n:].astype(BF16), b).astype(F32)
-    d_key, d_value = d_key_value[0, :, :head_size], d_key_value[0, :, head_size:]
+        d_key_value = d_key_value[:n] + over_blk(d_key_value[n:].astype(BF16), 1 << b).astype(F32)
+
+    plan = Plan()
+    fold(plan, d_key_value[1].astype(BF16))
+    fold(plan, away_up)
+    settle(plan, away_gate)
+    mixed_sum, (got_kv, got, got_gate) = gather_sum(partial_sum(active, w_down), plan)
+    (g_gate,) = settled(own_gate, got_gate, (ff,))
+    own_up, away_up = to_settle(keep_up, got)
+    mixed = give_batch((middle + mixed_sum).astype(BF16))
+    d_key_value = d_key_value[0] + got_kv.astype(F32)
+    d_key, d_value = d_key_value[:, :head_size], d_key_value[:, head_size:]
     dq_turned = rope_back(d_query.reshape(tokens, heads, head_size))
     dk_turned = rope_back(d_key.reshape(tokens, 1, head_size))
     gain_q_grad = jnp.sum(dq_turned * q_normal, axis=(0, 1))
@@ -490,12 +830,34 @@
     dq_raw = norm_back(dq_turned, q_normal, q_inverse, gain_q).reshape(tokens, q_columns)
     dk_raw = norm_back(dk_turned, k_normal, k_inverse, gain_k).reshape(tokens, k_columns)
     d_qkv = jnp.concatenate([dq_raw, dk_raw, d_value], axis=1).astype(BF16)
-    g_query, g_key, g_value = settle(tn(xa, d_qkv), (q_columns, k_columns, k_columns))
-    d_xa = gather_sum(d_qkv, w_qkv)
+    keep_qkv, away_qkv = split_grad(tn(xa, d_qkv))
+
+    plan = Plan()
+    settle(plan, away_up)
+    fold(plan, away_qkv)
+    fold(plan, away_out)
+    d_xa, (got_up, got, got_o) = gather_sum(partial_sum(d_qkv, w_qkv), plan)
+    (g_up,) = settled(own_up, got_up, (ff,))
+    own_qkv, away_qkv = to_settle(keep_qkv, got)
+    own_out, away_out = to_settle(keep_out, got_o)
+    got = settle_apart(jnp.concatenate([away_qkv, away_out], axis=1))
+    own = jnp.concatenate([own_qkv, own_out], axis=1)
+    g_query, g_key, g_value, g_out = settled(own, got, (q_columns, k_columns, k_columns, q_columns))
     input_grad = give_batch(d_middle + norm_back(d_xa, normal_a, inverse_a, gain_a))
-    gain_a_grad = from_group(jnp.sum(d_xa * normal_a, axis=(0, 1)))
-    gain_m_grad = from_group(jnp.sum(d_xm * normal_m, axis=(0, 1)))
-    gains = lax.psum((gain_a_grad, gain_q_grad, gain_k_grad, gain_m_grad), ("blk", "head"))
+    sums = jnp.concatenate(
+        [
+            ungroup(jnp.sum(d_xa * normal_a, axis=0)),
+            gain_q_grad,
+            gain_k_grad,
+            ungroup(jnp.sum(d_xm * normal_m, axis=0)),
+        ]
+    )
+    for b in range(2):
+        sums = sums + over_head(sums, 1 << b)
+    for b in range(bits):
+        sums = sums + over_blk(sums, 1 << b)
+    at = [width, width + head_size, width + 2 * head_size]
+    gains = jnp.split(sums, at)
     return (
         mixed,
         input_grad,

time: 824 us -> 714 us (0.87)
  Pallas kernels: 19.9 us -> 418 us
  waiting for transfers between devices: 449 us -> 64.5 us
  starting transfers between devices: 76.8 us -> 17 us
  blocking collectives: 40.4 us -> 0 us
  matrix products: 86.9 us -> 76.7 us
    pallas_call x0 -> x8, Pallas kernels: none -> 398 us  [run(): pl.pallas_call(kernel, out_shape=[*out_shapes, *plan.shapes], in_specs=[*...]
    ppermute x78 -> x13, waiting for transfers between devices: 449 us -> 64.5 us  [the longest x11 64 us: over_blk(): return lax.ppermute(value, 'blk', [(i, i ^ mask) for i in range(count)])]
    ppermute x78 -> x13, starting transfers between devices: 76.8 us -> 17 us  [the longest x11 14.7 us: over_blk(): return lax.ppermute(value, 'blk', [(i, i ^ mask) for i in range(count)])]
    psum x1 -> x0, blocking collectives: 40.4 us -> none  [local(): lax.psum((gain_a_grad, gain_q_grad, gain_k_grad, gain_m_grad), ('blk', 'h...]
    unnamed x271 -> x287, local copies, waits for them, and re-layouts: 27.5 us -> 48 us
    dot_general x4 -> x5, matrix products: 19.8 us -> 35 us  [tn(): lax.dot_general(a, b, (((0,), (0,)), ((), ())), preferred_element_type=F32)]
    dot_general x4 -> x5, matrix products: 34.1 us -> 19.3 us  [nn(): return jnp.dot(a, b, preferred_element_type=F32)]
    dot_general x8 -> x5, matrix products: 33.1 us -> 22.4 us  [nt(): lax.dot_general(a, b, (((1,), (1,)), ((), ())), preferred_element_type=F32)]
  transfers between devices with their start and end apart: 78 -> 13, of which waited for: 36 -> 8; matrix products, arithmetic and copies ran while one was open for 24% -> 4% of each run, Pallas kernels for 2% -> 0%
where the time goes in v2:
time: 714 us; the launch traced here: 703 us
  Pallas kernels  418 us (59%)
  local copies, waits for them, and re-layouts  77.6 us (11%)
  matrix products  76.7 us (11%)
  waiting for transfers between devices  64.5 us (9%)
  other arithmetic  46.7 us (7%)
  starting transfers between devices  17 us (2%)
    pallas_call x8, Pallas kernels, run(): pl.pallas_call(kernel, out_shape=[*out_shapes, *plan.shapes], in_specs=[*...  398 us
    ppermute x11, waiting for transfers between devices, over_blk(): return lax.ppermute(value, 'blk', [(i, i ^ mask) for i in range(count)])  64 us
    unnamed x287, local copies, waits for them, and re-layouts  48 us
    dot_general x5, matrix products, tn(): lax.dot_general(a, b, (((0,), (0,)), ((), ())), preferred_element_type=F32)  35 us
    dot_general x5, matrix products, nt(): lax.dot_general(a, b, (((1,), (1,)), ((), ())), preferred_element_type=F32)  22.4 us
    dot_general x5, matrix products, nn(): return jnp.dot(a, b, preferred_element_type=F32)  19.3 us
    ppermute x11, starting transfers between devices, over_blk(): return lax.ppermute(value, 'blk', [(i, i ^ mask) for i in range(count)])  14.7 us
  transfers between devices with their start and end apart: 13, of which 8 were waited for; matrix products, arithmetic and copies ran while one was open for 4% of the time, Pallas kernels for 0%

profile of v2, /device:TPU:0, one launch (start us, length us, event | category | flops | bytes accessed | tf_op | source)
XLA Modules:
  0.0 703.4 jit_solution(4727652830615227758)
XLA Ops:
  23.0 69.4 %shard_map.237 = (bf16[2,2,2,2,64,2048]{5,4,3,2,1,0:T(8,128)(2,1)S(1)}, bf16[2048,512]{1,0:T(8,128)(2,1)S(1)}, bf16[2,64,2048]{2,1,0:T(8,128)(2,1)S(1)}, bf16[2048,768]{1,0:T(8,128)(2,1)S(1)}) custom-call(bf16[2,64,2048]{2,1,0:T(8,128)(2,1)S(1)} %fusion.4.refs_0_, bf16[256,512]{1,0:T(8,128)(2,1)S(1)} %copy-done.42, bf16[256,256]{1,0:T(8,128)(2,1)S(1)} %copy-done.44, ...), custom_call_target="tpu_custom_call" | custom-call | tf_op jit(solution)/shard_map/pallas_call | solution.py:355
  128.1 62.1 %shard_map.238 = (bf16[2,2,2,2,64,2048]{5,4,3,2,1,0:T(8,128)(2,1)S(1)}, bf16[2048,256]{1,0:T(8,128)(2,1)S(1)}, bf16[1024,256]{1,0:T(8,128)(2,1)S(1)}, bf16[2048,768]{1,0:T(8,128)(2,1)S(1)}, bf16[2048,768]{1,0:T(8,128)(2,1)S(1)}) custom-call(bf16[2,64,2048]{2,1,0:T(8,128)(2,1)S(1)} %bitcast.167, ...), custom_call_target="tpu_custom_call", output_to_operand_aliasing={{3}: (3, {})} | custom-call | tf_op jit(solution)/shard_map/pallas_call | solution.py:355
  192.5 8.8 %shard_map.239 = (bf16[2,4,128,256]{3,2,1,0:T(8,128)(2,1)S(1)}, f32[4,128,512]{2,1,0:T(8,128)S(1)}, f32[4,1,512]{2,1,0:T(1,128)S(1)}) custom-call(s32[45]{0:T(128)S(1)} %concatenate.184.meta_ref, bf16[2,4,128,256]{3,2,1,0:T(8,128)(2,1)S(1)} %copy-done.35, bf16[2,2,4,128,128]{4,3,2,1,0:T(8,128)(2,1)S(1)} %bitcast.180, ...), custom_call_target="tpu_custom_call" | custom-call | flops 2147483648 | bytes 4194304 | tf_op jit(solution)/shard_map/pallas_call | solution.py:203
  204.8 43.9 %shard_map.240 = (f32[2,64,2048]{2,1,0:T(8,128)S(1)}, bf16[2048,768]{1,0:T(8,128)(2,1)S(1)}, bf16[2048,768]{1,0:T(8,128)(2,1)S(1)}, bf16[2048,768]{1,0:T(8,128)(2,1)S(1)}) custom-call(bf16[2,2,2,2,64,2048]{5,4,3,2,1,0:T(8,128)(2,1)S(1)} %bitcast.159, bf16[2048,768]{1,0:T(8,128)(2,1)S(1)} %copy-done.3, ...), custom_call_target="tpu_custom_call", output_to_operand_aliasing={{1}: (1, {}), {2}: (2, {})} | custom-call | tf_op jit(solution)/shard_map/pallas_call | solution.py:355
  258.1 6.5 fusion.79
  264.8 19.1 %collective-permute-done.1.refs_3_ = bf16[256,768]{1,0:T(8,128)(2,1)S(1)} collective-permute-done((bf16[256,768]{1,0:T(8,128)(2,1)}, bf16[256,768]{1,0:T(8,128)(2,1)S(1)}, u32[]{:S(2)}, u32[]{:S(2)}) %collective-permute-start.1) | collective-permute-done | bytes 393248 | tf_op jit(solution)/shard_map/ppermute | solution.py:38
  283.9 44.8 %shard_map.241 = (bf16[2,2,2,2,64,2048]{5,4,3,2,1,0:T(8,128)(2,1)S(1)}, bf16[2048,768]{1,0:T(8,128)(2,1)S(1)}, bf16[2048,768]{1,0:T(8,128)(2,1)S(1)}) custom-call(bf16[2,64,2048]{2,1,0:T(8,128)(2,1)S(1)} %multiply_convert_fusion.3.refs_0_, bf16[2048,768]{1,0:T(8,128)(2,1)S(1)} %copy-done.7, ...), custom_call_target="tpu_custom_call", output_to_operand_aliasing={{1}: (1, {}), {2}: (2, {})} | custom-call | tf_op jit(solution)/shard_map/pallas_call | solution.py:355
  332.1 5.7 multiply_convert_fusion.1
  339.0 5.5 fusion.81
  344.5 5.1 convolution_convert_fusion.2
  349.5 5.8 fusion.80
  355.3 16.7 %fusion.83 = f32[2048,768]{1,0:T(8,128)} fusion(bf16[1024,2048]{1,0:T(8,128)(2,1)S(1)} %bitcast.191, bf16[1024,768]{1,0:T(8,128)(2,1)S(1)} %get-tuple-element.130), kind=kOutput, calls=%fused_computation.318 | convolution fusion | flops 3221225472 | bytes 12058624 | tf_op jit(solution)/shard_map/dot_general | solution.py:25
  372.0 5.5 fusion.82
  377.5 5.9 add_convert_fusion
  385.5 36.9 %shard_map.242 = (f32[2,64,2048]{2,1,0:T(8,128)S(1)}, bf16[1024,768]{1,0:T(8,128)(2,1)S(1)}) custom-call(bf16[2,2,2,2,64,2048]{5,4,3,2,1,0:T(8,128)(2,1)S(1)} %bitcast.166, bf16[1024,768]{1,0:T(8,128)(2,1)S(1)} %slice.400.refs_1_), custom_call_target="tpu_custom_call" | custom-call | tf_op jit(solution)/shard_map/pallas_call | solution.py:355
  427.7 43.7 %shard_map.243 = (bf16[2,2,2,2,64,2048]{5,4,3,2,1,0:T(8,128)(2,1)S(1)}, bf16[768,768]{1,0:T(8,128)(2,1)S(1)}, bf16[1024,768]{1,0:T(8,128)(2,1)S(1)}) custom-call(bf16[2,64,2048]{2,1,0:T(8,128)(2,1)S(1)} %add_convert_fusion.1.refs_0_, bf16[768,768]{1,0:T(8,128)(2,1)S(1)} %slice.403.refs_1_, bf16[1024,768]{1,0:T(8,128)(2,1)S(1)} %slice.399.refs_2_), custom_call_target="tpu_custom_call" | custom-call | tf_op jit(solution)/shard_map/pallas_call | solution.py:355
  477.9 11.1 %shard_map.244 = (f32[2,4,128,256]{3,2,1,0:T(8,128)S(1)}, f32[2,2,4,128,128]{4,3,2,1,0:T(8,128)S(1)}, f32[2,2,4,128,128]{4,3,2,1,0:T(8,128)S(1)}) custom-call(s32[45]{0:T(128)S(1)} %concatenate.184.meta_ref, bf16[2,4,128,256]{3,2,1,0:T(8,128)(2,1)S(1)} %copy-done.36, bf16[2,4,128,256]{3,2,1,0:T(8,128)(2,1)S(1)} %bitcast.193, ...), custom_call_target="tpu_custom_call" | custom-call | flops 5368709120 | bytes 7340032 | tf_op jit(solution)/shard_map/pallas_call | solution.py:236
  489.1 53.9 %shard_map.245 = (f32[2,64,2048]{2,1,0:T(8,128)S(1)}, bf16[1024,256]{1,0:T(8,128)(2,1)S(1)}, bf16[1024,768]{1,0:T(8,128)(2,1)S(1)}, bf16[768,768]{1,0:T(8,128)(2,1)S(1)}) custom-call(bf16[2,2,2,2,64,2048]{5,4,3,2,1,0:T(8,128)(2,1)S(1)} %bitcast.160, bf16[1024,256]{1,0:T(8,128)(2,1)S(1)} %fusion.40.refs_1_, bf16[1024,768]{1,0:T(8,128)(2,1)S(1)} %slice.398.refs_2_, ...), custom_call_target="tpu_custom_call" | custom-call | tf_op jit(solution)/shard_map/pallas_call | solution.py:355
  565.5 4.3 convolution_convert_fusion
  569.8 4.5 fusion.41
  584.3 43.5 %shard_map.246 = (f32[2,64,2048]{2,1,0:T(8,128)S(1)}, bf16[768,768]{1,0:T(8,128)(2,1)S(1)}, bf16[1024,512]{1,0:T(8,128)(2,1)S(1)}, bf16[1024,256]{1,0:T(8,128)(2,1)S(1)}) custom-call(bf16[2,2,2,2,64,2048]{5,4,3,2,1,0:T(8,128)(2,1)S(1)} %bitcast.165, bf16[768,768]{1,0:T(8,128)(2,1)S(1)} %slice.401.refs_1_, bf16[1024,512]{1,0:T(8,128)(2,1)S(1)} %slice.404.refs_2_, ...), custom_call_target="tpu_custom_call" | custom-call | tf_op jit(solution)/shard_map/pallas_call | solution.py:355
  654.2 16.2 %collective-permute-done.11 = f32[4352]{0:T(1024)S(1)} collective-permute-done((f32[4352]{0:T(1024)S(1)}, f32[4352]{0:T(1024)S(1)}, u32[]{:S(2)}, u32[]{:S(2)}) %collective-permute-start.11) | collective-permute-done | bytes 17440 | tf_op jit(solution)/shard_map/ppermute | solution.py:38
  673.8 5.7 collective-permute-done.12
  684.7 15.1 %collective-permute-done.5 = bf16[256,768]{1,0:T(8,128)(2,1)S(1)} collective-permute-done((bf16[256,768]{1,0:T(8,128)(2,1)S(1)}, bf16[256,768]{1,0:T(8,128)(2,1)S(1)}, u32[]{:S(2)}, u32[]{:S(2)}) %collective-permute-start.5) | collective-permute-done | bytes 393248 | tf_op jit(solution)/shard_map/ppermute | solution.py:38
  (458 shorter events, 160.7 us)
Async XLA Ops:
  1.7 16.0 %collective-permute-start = (bf16[64,2048]{1,0:T(8,128)(2,1)S(1)}, bf16[64,2048]{1,0:T(8,128)(2,1)S(1)}, u32[]{:S(2)}, u32[]{:S(2)}) collective-permute-start(bf16[64,2048]{1,0:T(8,128)(2,1)S(1)} %get-tuple-element.172), channel_id=1, source_target_pairs={{0,16},{4,20},{8,24},{12,28},{16,0},{20,4},{24,8},{28,12},{1,17},{... | collective-permute-start | bytes 786440 | tf_op jit(solution)/shard_map/ppermute | solution.py:38
  120.1 72.1 %copy-start.72 = (bf16[1,1024,256]{2,1,0:T(8,128)(2,1)S(1)}, bf16[1,1024,256]{2,1,0:T(8,128)(2,1)}, u32[]{:S(2)}) copy-start(bf16[1,1024,256]{2,1,0:T(8,128)(2,1)} %fusion.113) | copy-start | bytes 1572868
  124.6 67.8 %copy-start.16 = (bf16[128,2048]{1,0:T(8,128)(2,1)}, bf16[128,2048]{1,0:T(8,128)(2,1)S(1)}, u32[]{:S(2)}) copy-start(bf16[128,2048]{1,0:T(8,128)(2,1)S(1)} %get-tuple-element.95) | copy-start | bytes 1572868
  128.1 64.4 %copy-start.35 = (bf16[2,4,128,256]{3,2,1,0:T(8,128)(2,1)S(1)}, bf16[2,4,128,256]{3,2,1,0:T(8,128)(2,1)}, u32[]{:S(2)}) copy-start(bf16[2,4,128,256]{3,2,1,0:T(8,128)(2,1)} %copy.108.q_ref) | copy-start | bytes 1572868
  204.8 47.3 %copy-start.56 = (bf16[2,64,2048]{2,1,0:T(8,128)(2,1)S(1)}, bf16[2,64,2048]{2,1,0:T(8,128)(2,1)}, u32[]{:S(2)}) copy-start(bf16[2,64,2048]{2,1,0:T(8,128)(2,1)} %copy-done.55) | copy-start | bytes 1572868
  254.0 29.9 %collective-permute-start.1 = (bf16[256,768]{1,0:T(8,128)(2,1)}, bf16[256,768]{1,0:T(8,128)(2,1)S(1)}, u32[]{:S(2)}, u32[]{:S(2)}) collective-permute-start(bf16[256,768]{1,0:T(8,128)(2,1)} %get-tuple-element.164), channel_id=1, source_target_pairs={{0,16},{4,20},{8,24},{12,28},{16,0},{20,4},{24,8},{28,12},{1,17},{... | collective-permute-start | bytes 1179656 | tf_op jit(solution)/shard_map/ppermute | solution.py:38
  256.0 27.9 %collective-permute-start.2 = (bf16[256,768]{1,0:T(8,128)(2,1)}, bf16[256,768]{1,0:T(8,128)(2,1)S(1)}, u32[]{:S(2)}, u32[]{:S(2)}) collective-permute-start(bf16[256,768]{1,0:T(8,128)(2,1)} %get-tuple-element.163), channel_id=1, source_target_pairs={{0,24},{4,28},{8,16},{12,20},{16,8},{20,12},{24,0},{28,4},{1,25},{... | collective-permute-start | bytes 1179656 | tf_op jit(solution)/shard_map/ppermute | solution.py:38
  427.3 44.2 %copy-start.28 = (bf16[2048,256]{1,0:T(8,128)(2,1)S(1)}, bf16[2048,256]{1,0:T(8,128)(2,1)}, u32[]{:S(2)}) copy-start(bf16[2048,256]{1,0:T(8,128)(2,1)} %copy-done.27) | copy-start | bytes 3145732
  584.3 46.3 %copy-start.57 = (bf16[2,64,2048]{2,1,0:T(8,128)(2,1)S(1)}, bf16[2,64,2048]{2,1,0:T(8,128)(2,1)}, u32[]{:S(2)}) copy-start(bf16[2,64,2048]{2,1,0:T(8,128)(2,1)} %copy-done.55) | copy-start | bytes 1572868
  584.3 46.3 %copy-start.87 = (f32[2048]{0:T(1024)S(1)}, f32[2048]{0:T(1024)}, u32[]{:S(2)}) copy-start(f32[2048]{0:T(1024)} %copy-done.86) | copy-start | bytes 24580
  584.3 46.3 %copy-start.97 = (f32[2,64]{1,0:T(2,128)S(1)}, f32[2,64]{1,0:T(2,128)}, u32[]{:S(2)}) copy-start(f32[2,64]{1,0:T(2,128)} %copy-done.96) | copy-start | bytes 1540
  584.3 46.8 %copy-start.103 = (f32[128]{0:T(128)S(1)}, f32[128]{0:T(128)}, u32[]{:S(2)}) copy-start(f32[128]{0:T(128)} %copy-done.102) | copy-start | bytes 1540
  584.3 46.8 %copy-start.104 = (f32[128]{0:T(128)S(1)}, f32[128]{0:T(128)}, u32[]{:S(2)}) copy-start(f32[128]{0:T(128)} %rsqrt.45) | copy-start | bytes 1540
  635.8 44.9 %collective-permute-start.3 = (bf16[64,2048]{1,0:T(8,128)(2,1)S(1)}, bf16[64,2048]{1,0:T(8,128)(2,1)S(1)}, u32[]{:S(2)}, u32[]{:S(2)}) collective-permute-start(bf16[64,2048]{1,0:T(8,128)(2,1)S(1)} %get-tuple-element.170), channel_id=1, source_target_pairs={{0,16},{4,20},{8,24},{12,28},{16,0},{20,4},{24,8},{28,12},{1,17},{... | collective-permute-start | bytes 786440 | tf_op jit(solution)/shard_map/ppermute | solution.py:38
  637.4 43.2 %collective-permute-start.4 = (bf16[64,2048]{1,0:T(8,128)(2,1)S(1)}, bf16[64,2048]{1,0:T(8,128)(2,1)S(1)}, u32[]{:S(2)}, u32[]{:S(2)}) collective-permute-start(bf16[64,2048]{1,0:T(8,128)(2,1)S(1)} %slice.408), channel_id=1, source_target_pairs={{0,16},{4,20},{8,24},{12,28},{16,0},{20,4},{24,8},{28,12},{1,17},{... | collective-permute-start | bytes 786440 | tf_op jit(solution)/shard_map/ppermute | solution.py:38
  638.9 33.0 %copy-start.66 = (f32[1024,256]{1,0:T(8,128)}, f32[1024,256]{1,0:T(8,128)S(1)}, u32[]{:S(2)}) copy-start(f32[1024,256]{1,0:T(8,128)S(1)} %slice_add_fusion.4) | copy-start | bytes 3145732
  639.1 43.6 %collective-permute-start.7 = (bf16[256,768]{1,0:T(8,128)(2,1)S(1)}, bf16[256,768]{1,0:T(8,128)(2,1)S(1)}, u32[]{:S(2)}, u32[]{:S(2)}) collective-permute-start(bf16[256,768]{1,0:T(8,128)(2,1)S(1)} %get-tuple-element.147), channel_id=1, source_target_pairs={{0,24},{4,28},{8,16},{12,20},{16,8},{20,12},{24,0},{28,4},{1,25},{... | collective-permute-start | bytes 1179656 | tf_op jit(solution)/shard_map/ppermute | solution.py:38
  643.3 1.3 collective-permute-start.8
  644.6 4.0 collective-permute-start.9
  648.7 3.8 collective-permute-start.10
  652.5 18.0 %collective-permute-start.11 = (f32[4352]{0:T(1024)S(1)}, f32[4352]{0:T(1024)S(1)}, u32[]{:S(2)}, u32[]{:S(2)}) collective-permute-start(f32[4352]{0:T(1024)S(1)} %add.525), channel_id=1, source_target_pairs={{0,8},{4,12},{8,0},{12,4},{16,24},{20,28},{24,16},{28,20},{1,9},{5... | collective-permute-start | bytes 52232 | tf_op jit(solution)/shard_map/ppermute | solution.py:38
  670.5 9.0 %collective-permute-start.12 = (f32[4352]{0:T(1024)S(1)}, f32[4352]{0:T(1024)S(1)}, u32[]{:S(2)}, u32[]{:S(2)}) collective-permute-start(f32[4352]{0:T(1024)S(1)} %add.526), channel_id=1, source_target_pairs={{0,16},{4,20},{8,24},{12,28},{16,0},{20,4},{24,8},{28,12},{1,17},{... | collective-permute-start | bytes 52232 | tf_op jit(solution)/shard_map/ppermute | solution.py:38
  671.8 12.6 %collective-permute-start.6 = (bf16[256,768]{1,0:T(8,128)(2,1)S(1)}, bf16[256,768]{1,0:T(8,128)(2,1)S(1)}, u32[]{:S(2)}, u32[]{:S(2)}) collective-permute-start(bf16[256,768]{1,0:T(8,128)(2,1)S(1)} %get-tuple-element.148), channel_id=1, source_target_pairs={{0,8},{4,12},{8,0},{12,4},{16,24},{20,28},{24,16},{28,20},{1,9},{5... | collective-permute-start | bytes 1179656 | tf_op jit(solution)/shard_map/ppermute | solution.py:38
  679.5 20.3 %collective-permute-start.5 = (bf16[256,768]{1,0:T(8,128)(2,1)S(1)}, bf16[256,768]{1,0:T(8,128)(2,1)S(1)}, u32[]{:S(2)}, u32[]{:S(2)}) collective-permute-start(bf16[256,768]{1,0:T(8,128)(2,1)S(1)} %get-tuple-element.146), channel_id=1, source_target_pairs={{0,16},{4,20},{8,24},{12,28},{16,0},{20,4},{24,8},{28,12},{1,17},{... | collective-permute-start | bytes 1179656 | tf_op jit(solution)/shard_map/ppermute | solution.py:38
  (100 other events, 493.4 us)

commit v3 on v2

--- a/solution.py
+++ b/solution.py
@@ -13,6 +13,9 @@
 F32 = jnp.float32
 BF16 = jnp.bfloat16
 
+MIB = 1024 * 1024
+TINY_COST = pl.CostEstimate(flops=0, bytes_accessed=0, transcendentals=0)
+VMEM_LIMIT = 32 * MIB
 TENSOR_BIT = 1
 SEQ_BIT = 0
 
@@ -215,7 +218,7 @@
             pltpu.VMEM((width, lanes), F32),
             pltpu.VMEM((1, lanes), F32),
         ],
-        compiler_params=pltpu.CompilerParams(vmem_limit_bytes=40 * 1024 * 1024),
+        compiler_params=pltpu.CompilerParams(vmem_limit_bytes=VMEM_LIMIT),
         cost_estimate=pl.CostEstimate(
             flops=2 * 2 * lanes * 2 * half * width * blocks * total,
             bytes_accessed=8 * q.size + 8 * k.size,
@@ -256,7 +259,7 @@
             pltpu.VMEM((total, width, 2 * half), BF16),
             pltpu.VMEM((width, lanes), F32),
         ],
-        compiler_params=pltpu.CompilerParams(vmem_limit_bytes=48 * 1024 * 1024),
+        compiler_params=pltpu.CompilerParams(vmem_limit_bytes=VMEM_LIMIT),
         cost_estimate=pl.CostEstimate(
             flops=5 * 2 * lanes * 2 * half * width * blocks * total,
             bytes_accessed=12 * q.size + 16 * k.size,
@@ -265,7 +268,223 @@
     )(meta, q, do, k, v, start, out_t, total_e)
 
 
-TINY_COST = pl.CostEstimate(flops=0, bytes_accessed=0, transcendentals=0)
+def prepare_kernel(x_ref, w_ref, cos_ref, sin_ref, gq_ref, gk_ref, q_ref, kv_ref, raw_ref, *, heads, width):
+    acc = jnp.dot(x_ref[...], w_ref[...], preferred_element_type=F32)
+    raw_ref[...] = acc[:, : (heads + 1) * width]
+    for h in range(heads + 1):
+        part = acc[:, h * width : (h + 1) * width]
+        normed = part * lax.rsqrt(jnp.mean(part * part, axis=-1, keepdims=True) + EPS)
+        scaled = normed * (gq_ref if h < heads else gk_ref)[...]
+        turned = (scaled * cos_ref[...] + pltpu.roll(scaled, width // 2, 1) * sin_ref[...]).astype(BF16)
+        if h < heads:
+            q_ref[:, h * width : (h + 1) * width] = turned
+        else:
+            kv_ref[:, :width] = turned
+    kv_ref[:, width:] = acc[:, (heads + 1) * width :].astype(BF16)
+
+
+def prepare(x, w, cos, sin, gain_q, gain_k, heads):
+    tokens, depth = x.shape
+    width, tile = gain_q.shape[1], 256
+    row = lambda n: pl.BlockSpec((tile, n), lambda i: (i, 0))
+    fixed = lambda a: pl.BlockSpec(a.shape, lambda i: (0, 0))
+    return pl.pallas_call(
+        functools.partial(prepare_kernel, heads=heads, width=width),
+        grid=(tokens // tile,),
+        in_specs=[row(depth), fixed(w), row(width), row(width), fixed(gain_q), fixed(gain_k)],
+        out_specs=[row(heads * width), row(2 * width), row((heads + 1) * width)],
+        out_shape=[
+            jax.ShapeDtypeStruct((tokens, heads * width), BF16),
+            jax.ShapeDtypeStruct((tokens, 2 * width), BF16),
+            jax.ShapeDtypeStruct((tokens, (heads + 1) * width), F32),
+        ],
+        compiler_params=pltpu.CompilerParams(vmem_limit_bytes=VMEM_LIMIT),
+        cost_estimate=TINY_COST,
+    )(x, w, cos, sin, gain_q, gain_k)
+
+
+def prepare_back_kernel(
+    dq_ref, dk_ref, dv_ref, got_ref, raw_ref, cos_ref, sin_ref, gq_ref, gk_ref, w_ref, d_ref, p_ref, g_ref, *, heads, width
+):
+    @pl.when(pl.program_id(0) == 0)
+    def _():
+        g_ref[...] = jnp.zeros_like(g_ref)
+
+    got = got_ref[...].astype(F32)
+    for h in range(heads + 1):
+        at = slice(h * width, (h + 1) * width)
+        grad = dq_ref[:, at] if h < heads else dk_ref[0] + got[:, :width]
+        gain = (gq_ref if h < heads else gk_ref)[...]
+        raw = raw_ref[:, at]
+        inverse = lax.rsqrt(jnp.mean(raw * raw, axis=-1, keepdims=True) + EPS)
+        normed = raw * inverse
+        turned = grad * cos_ref[...] - pltpu.roll(grad, width // 2, 1) * sin_ref[...]
+        row = 0 if h < heads else 1
+        g_ref[row : row + 1, :] += jnp.sum(turned * normed, axis=0, keepdims=True)
+        scaled = turned * gain
+        d_ref[:, at] = (inverse * (scaled - normed * jnp.mean(scaled * normed, axis=-1, keepdims=True))).astype(BF16)
+    d_ref[:, (heads + 1) * width :] = (dv_ref[0] + got[:, width:]).astype(BF16)
+    p_ref[...] = nt(d_ref[...], w_ref[...]).astype(BF16)
+
+
+def prepare_back(dq, dk, dv, got, raw, cos, sin, gain_q, gain_k, w, heads):
+    tokens, width, tile = dq.shape[0], gain_q.shape[1], 256
+    row = lambda n: pl.BlockSpec((tile, n), lambda i: (i, 0))
+    part = pl.BlockSpec((1, tile, width), lambda i: (0, i, 0))
+    fixed = lambda a: pl.BlockSpec(a.shape, lambda i: (0, 0))
+    return pl.pallas_call(
+        functools.partial(prepare_back_kernel, heads=heads, width=width),
+        grid=(tokens // tile,),
+        in_specs=[
+            row(heads * width),
+            part,
+            part,
+            row(2 * width),
+            row((heads + 1) * width),
+            row(width),
+            row(width),
+            fixed(gain_q),
+            fixed(gain_k),
+            fixed(w),
+        ],
+        out_specs=[row(w.shape[1]), row(w.shape[0]), pl.BlockSpec((8, width), lambda i: (0, 0))],
+        out_shape=[
+            jax.ShapeDtypeStruct((tokens, w.shape[1]), BF16),
+            jax.ShapeDtypeStruct((tokens, w.shape[0]), BF16),
+            jax.ShapeDtypeStruct((8, width), F32),
+        ],
+        compiler_params=pltpu.CompilerParams(vmem_limit_bytes=VMEM_LIMIT),
+        cost_estimate=TINY_COST,
+    )(dq, dk, dv, got, raw, cos, sin, gain_q, gain_k, w)
+
+
+def place_of_block(blk, bit_order, p):
+    return blk ^ sum(((p >> i) & 1) << b for i, b in enumerate(bit_order))
+
+
+def enter_kernel(blk_ref, *refs, bit_order, normed):
+    if normed:
+        mine_ref, other_ref, gain_ref, low_ref, out_ref, gains_ref = refs
+    else:
+        mine_ref, low_ref = refs
+    rows, width = mine_ref.shape
+    n = width >> len(bit_order)
+    for p in range(1 << len(bit_order)):
+        at = pl.ds(pl.multiple_of(place_of_block(blk_ref[0], bit_order, p) * n, n), n)
+        low_ref[:rows, p * n : (p + 1) * n] = mine_ref[:, at]
+        if normed:
+            low_ref[rows:, p * n : (p + 1) * n] = other_ref[:, at]
+            gains_ref[:, p * n : (p + 1) * n] = gain_ref[:, at]
+    if normed:
+        values = low_ref[...].astype(F32)
+        inverse = lax.rsqrt(jnp.mean(values * values, axis=-1, keepdims=True) + EPS)
+        out_ref[...] = (values * inverse * gains_ref[:1]).astype(BF16)
+
+
+def enter(blk, bit_order, mine, other=None, gain=None):
+    rows, width = mine.shape
+    normed = gain is not None
+    total = (2 * rows if normed else rows, width)
+    vmem = pl.BlockSpec(memory_space=pltpu.VMEM)
+    operands = [mine, other, gain] if normed else [mine]
+    return pl.pallas_call(
+        functools.partial(enter_kernel, bit_order=bit_order, normed=normed),
+        in_specs=[pl.BlockSpec(memory_space=pltpu.SMEM), *[vmem] * len(operands)],
+        out_specs=[vmem] * (3 if normed else 1),
+        out_shape=[
+            *[jax.ShapeDtypeStruct(total, BF16)] * (2 if normed else 1),
+            *([jax.ShapeDtypeStruct(gain.shape, F32)] if normed else []),
+        ],
+        compiler_params=pltpu.CompilerParams(vmem_limit_bytes=VMEM_LIMIT),
+        cost_estimate=TINY_COST,
+    )(blk[None].astype(jnp.int32), *operands)
+
+
+def assemble_kernel(place_ref, *refs, sources, widths):
+    ins, outs = refs[: 2 * sources], refs[2 * sources :]
+    place, k, at = place_ref[0], 0, 0
+    for own_ref, got_ref in zip(ins[::2], ins[1::2]):
+        f, at = own_ref.shape[0], 0
+        while at < own_ref.shape[1]:
+            w, cut = widths[k], slice(at, at + widths[k])
+            mine = pl.ds(pl.multiple_of(place * w, w), w)
+            theirs = pl.ds(pl.multiple_of((1 - place) * w, w), w)
+            outs[k][:, mine] = own_ref[:, cut] + got_ref[:f, cut].astype(F32)
+            outs[k][:, theirs] = got_ref[f : 2 * f, cut].astype(F32) + got_ref[2 * f :, cut].astype(F32)
+            at += w
+            k += 1
+
+
+def assemble(place, sources, widths):
+    vmem = pl.BlockSpec(memory_space=pltpu.VMEM)
+    flat = [a for pair in sources for a in pair]
+    return pl.pallas_call(
+        functools.partial(assemble_kernel, sources=len(sources), widths=widths),
+        in_specs=[pl.BlockSpec(memory_space=pltpu.SMEM), *[vmem] * len(flat)],
+        out_specs=[vmem] * len(widths),
+        out_shape=[jax.ShapeDtypeStruct((sources[0][0].shape[0], 2 * w), F32) for w in widths],
+        compiler_params=pltpu.CompilerParams(vmem_limit_bytes=VMEM_LIMIT),
+        cost_estimate=TINY_COST,
+    )(place[None].astype(jnp.int32), *flat)
+
+
+def back_kernel(*refs):
+    *ins, out_ref = refs
+    n = len(ins) // 2
+    out_ref[...] = sum(nt(d[...], w[...]) for d, w in zip(ins[:n], ins[n:])).astype(BF16)
+
+
+def back_through(grads, weights):
+    tokens, depth, tile = grads[0].shape[0], weights[0].shape[0], 256
+    return pl.pallas_call(
+        back_kernel,
+        grid=(depth // tile,),
+        in_specs=[
+            *[pl.BlockSpec(g.shape, lambda i: (0, 0)) for g in grads],
+            *[pl.BlockSpec((tile, w.shape[1]), lambda i: (i, 0)) for w in weights],
+        ],
+        out_specs=pl.BlockSpec((tokens, tile), lambda i: (0, i)),
+        out_shape=jax.ShapeDtypeStruct((tokens, depth), BF16),
+        compiler_params=pltpu.CompilerParams(vmem_limit_bytes=VMEM_LIMIT),
+        cost_estimate=TINY_COST,
+    )(*grads, *weights)
+
+
+def weight_grad_kernel(a_ref, b_ref, keep_ref, away_ref):
+    product = tn(a_ref[...], b_ref[...])
+    first = pl.program_id(0) < pl.num_programs(0) // 2
+
+    @pl.when(first)
+    def _():
+        keep_ref[...] = product
+
+    @pl.when(jnp.logical_not(first))
+    def _():
+        away_ref[...] = product.astype(BF16)
+
+
+def weight_grad(a, b):
+    tokens, depth = a.shape
+    n, tile = b.shape[1], 256
+    steps = depth // tile
+    return pl.pallas_call(
+        weight_grad_kernel,
+        grid=(steps,),
+        in_specs=[
+            pl.BlockSpec((tokens, tile), lambda i: (0, i)),
+            pl.BlockSpec((tokens, n), lambda i: (0, 0)),
+        ],
+        out_specs=[
+            pl.BlockSpec((tile, n), lambda i: (jnp.minimum(i, steps // 2 - 1), 0)),
+            pl.BlockSpec((tile, n), lambda i: (jnp.maximum(i - steps // 2, 0), 0)),
+        ],
+        out_shape=[
+            jax.ShapeDtypeStruct((depth // 2, n), F32),
+            jax.ShapeDtypeStruct((depth // 2, n), BF16),
+        ],
+        compiler_params=pltpu.CompilerParams(vmem_limit_bytes=VMEM_LIMIT),
+        cost_estimate=TINY_COST,
+    )(a, b)
 
 
 def remote(src, dst, send, recv, target):
@@ -294,17 +513,22 @@
         return self.fresh(array.shape, array.dtype)
 
     def copy(self, src, dst, mask, after=None, point=0):
-        self.jobs.append((src, dst, mask, after, point))
+        self.jobs.append((src, dst, mask, after, point, None))
         return len(self.jobs) - 1
 
-
-def run(plan, main, collective_id):
-    inputs, in_specs, out_shapes, out_specs, scratch, body = main
+    def local(self, src, dst, shape, point=0):
+        self.jobs.append((src, dst, 0, None, point, shape))
+        return len(self.jobs) - 1
+
+
+def run(plan, main, collective_id, greeted=()):
+    inputs, in_specs, out_shapes, out_specs, scratch, body, limit = main
     n_in, n_out = len(inputs), len(out_shapes)
     m_in, m_out = len(plan.inputs), len(plan.shapes)
     jobs = plan.jobs
-    masks = sorted({job[2] for job in jobs if job[2]} - {1 << TENSOR_BIT})
-    any_spec = pl.BlockSpec(memory_space=pl.ANY)
+    local_jobs = [i for i, job in enumerate(jobs) if not job[2]]
+    masks = sorted({*greeted, *[job[2] for job in jobs if job[2]]} - {1 << TENSOR_BIT})
+    any_spec = pl.BlockSpec(memory_space=pltpu.HBM)
 
     def kernel(*refs):
         main_in, refs = refs[:n_in], refs[n_in:]
@@ -312,6 +536,8 @@
         main_out, refs = refs[:n_out], refs[n_out:]
         plan_out, refs = refs[:m_out], refs[m_out:]
         send, recv, *rest = refs
+        bounce = dict(zip(local_jobs, rest))
+        rest = rest[len(local_jobs) :]
         blk, head = lax.axis_index("blk"), lax.axis_index("head")
         core, near, across = (blk, head ^ 1), (blk, head ^ 2), (blk ^ (1 << TENSOR_BIT), head)
         barrier = pltpu.get_barrier_semaphore()
@@ -319,7 +545,7 @@
         for target in partners:
             pl.semaphore_signal(barrier, inc=1, device_id=target, device_id_type=pl.DeviceIdType.MESH)
         pl.semaphore_wait(barrier, len(partners))
-        started, arrived = {}, set()
+        started, arrived, halfway = {}, set(), []
 
         def arrive(i):
             if i not in arrived:
@@ -331,7 +557,12 @@
             return cut((plan_in if kind == "in" else plan_out)[index])
 
         def issue(point):
-            for i, (src, dst, mask, after, at) in enumerate(jobs):
+            for i in list(halfway):
+                started[i].wait()
+                started[i] = pltpu.make_async_copy(bounce[i], part(jobs[i][1]), recv.at[i])
+                started[i].start()
+                halfway.remove(i)
+            for i, (src, dst, mask, after, at, shape) in enumerate(jobs):
                 if i in started or (at != point and point is not None):
                     continue
                 if after is not None:
@@ -339,13 +570,15 @@
                 if mask:
                     started[i] = remote(part(src), part(dst), send.at[i], recv.at[i], (blk ^ mask, head))
                 else:
-                    started[i] = pltpu.make_async_copy(part(src), part(dst), recv.at[i])
+                    started[i] = pltpu.make_async_copy(part(src), bounce[i], send.at[i])
                     started[i].start()
+                    halfway.append(i)
 
         point = 0
         for _ in body((core, near, across), main_in, main_out, rest):
             issue(point)
             point += 1
+        issue(None)
         issue(None)
         for i in range(len(jobs)):
             arrive(i)
@@ -360,11 +593,12 @@
         scratch_shapes=[
             pltpu.SemaphoreType.DMA((max(1, len(jobs)),)),
             pltpu.SemaphoreType.DMA((max(1, len(jobs)),)),
+            *[pltpu.VMEM(jobs[i][5], BF16) for i in local_jobs],
             *scratch,
         ],
         input_output_aliases={n_in + i: n_out + o for i, o in plan.aliases.items()},
         compiler_params=pltpu.CompilerParams(
-            collective_id=collective_id, has_side_effects=True, vmem_limit_bytes=32 * 1024 * 1024
+            collective_id=collective_id, has_side_effects=True, vmem_limit_bytes=limit
         ),
         cost_estimate=TINY_COST,
     )(*inputs, *plan.inputs)
@@ -377,7 +611,7 @@
 
     def body(partners, ins, outs, scratch):
         core, near, across = partners
-        (s_ref,), (o_ref,), (local_sem, send, recv) = ins, outs, scratch
+        (s_ref,), (o_ref,), (hold, local_sem, send, recv) = ins, outs, scratch
         first = remote(s_ref, o_ref.at[0, :, 0, 1], send.at[0], recv.at[0], near)
         second = [
             remote(
@@ -390,9 +624,12 @@
             for i in range(pieces)
         ]
         third = remote(s_ref, o_ref.at[1, :, 0, 0], send.at[1], recv.at[1], core)
-        own = pltpu.make_async_copy(s_ref, o_ref.at[0, :, 0, 0], local_sem)
+        held = pltpu.make_async_copy(s_ref, hold, local_sem.at[0])
+        held.start()
+        yield
+        held.wait()
+        own = pltpu.make_async_copy(hold, o_ref.at[0, :, 0, 0], local_sem.at[1])
         own.start()
-        yield
         for copy in second:
             copy.wait_recv()
         fourth = remote(o_ref.at[0, :, 1, 0], o_ref.at[0, :, 1, 1], send.at[2], recv.at[2], near)
@@ -410,29 +647,31 @@
         for copy in (third, fifth, sixth, seventh):
             copy.wait_recv()
 
-    any_spec = pl.BlockSpec(memory_space=pl.ANY)
+    any_spec = pl.BlockSpec(memory_space=pltpu.HBM)
     return (
         [flat.reshape(2, rows, width)],
         [any_spec],
         [jax.ShapeDtypeStruct((2, 2, 2, 2, rows, width), flat.dtype)],
         [any_spec],
         [
-            pltpu.SemaphoreType.DMA,
+            pltpu.VMEM((2, rows, width), flat.dtype),
+            pltpu.SemaphoreType.DMA((2,)),
             pltpu.SemaphoreType.DMA((6 + pieces,)),
             pltpu.SemaphoreType.DMA((6 + pieces,)),
         ],
         body,
-    )
-
-
-def gather_main(partial, chunk):
+        8 * MIB,
+    )
+
+
+def gather_main(partial, chunk, extra, outs_like, finish):
     rows, width = partial.shape[0] // 16, partial.shape[1]
     share = (2, rows, width)
     pieces = width // chunk
 
     def body(partners, ins, outs, scratch):
         core, near, across = partners
-        (p_ref,), (o_ref,) = ins, outs
+        p_ref, *extra_refs = ins
         core_in, out_y, in_y, out_t, in_t, hold, send, recv = scratch
         order = ((1, 1), (0, 1), (1, 0), (0, 0))
         from_core = [
@@ -459,16 +698,17 @@
         hold[...] += in_y[1].astype(F32)
         yield
         from_t.wait_recv()
-        o_ref[...] = hold[...] + in_t[...].astype(F32)
+        hold[...] += in_t[...].astype(F32)
+        finish(hold, extra_refs, outs)
         for copy in (*from_core, *from_y, from_t):
             copy.wait_send()
 
     vmem_spec = pl.BlockSpec(memory_space=pltpu.VMEM)
     return (
-        [partial.reshape(2, 2, 2, 2, rows, width)],
-        [vmem_spec],
-        [jax.ShapeDtypeStruct(share, F32)],
-        [vmem_spec],
+        [partial.reshape(2, 2, 2, 2, rows, width), *extra],
+        [vmem_spec] * (1 + len(extra)),
+        outs_like,
+        [vmem_spec] * len(outs_like),
         [
             pltpu.VMEM((4, *share), BF16),
             pltpu.VMEM((2, *share), BF16),
@@ -480,6 +720,98 @@
             pltpu.SemaphoreType.DMA((7,)),
         ],
         body,
+        24 * MIB,
+    )
+
+
+def inverse_rms(values):
+    return lax.rsqrt(jnp.mean(values * values, axis=-1, keepdims=True) + EPS)
+
+
+def finish_middle(total, extra, outs):
+    (low_ref, gain_ref), (middle_ref, normed_ref) = extra, outs
+    for m in range(2):
+        middle = low_ref[m].astype(F32) + total[m]
+        middle_ref[m] = middle
+        normed_ref[m] = (middle * inverse_rms(middle) * gain_ref[...]).astype(BF16)
+
+
+def norm_grad(total, values, gain, gain_grad_ref, m):
+    inverse = inverse_rms(values)
+    normal = values * inverse
+    part = jnp.sum(total * normal, axis=0, keepdims=True)
+    gain_grad_ref[...] = part if m == 0 else gain_grad_ref[...] + part
+    scaled = total * gain
+    return inverse * (scaled - normal * jnp.mean(scaled * normal, axis=-1, keepdims=True))
+
+
+def finish_mlp_norm(total, extra, outs):
+    (cot_ref, middle_ref, gain_ref), (grad_ref, low_ref, gain_grad_ref) = extra, outs
+    for m in range(2):
+        grad = cot_ref[m].astype(F32) + norm_grad(total[m], middle_ref[m], gain_ref[...], gain_grad_ref, m)
+        grad_ref[m] = grad
+        low_ref[m] = grad.astype(BF16)
+
+
+def store_ungrouped(value, ref, blk, bit_order, lead=()):
+    n = value.shape[-1] >> len(bit_order)
+    for p in range(1 << len(bit_order)):
+        block = value[:, p * n : (p + 1) * n]
+        if bit_order and n % 128 == 0:
+            at = pl.ds(pl.multiple_of(place_of_block(blk, bit_order, p) * n, n), n)
+        else:
+            at = pl.ds(p * n, n)
+        ref[(*lead, slice(None), at)] = block.astype(ref.dtype)
+
+
+def finish_mixed(total, extra, outs, *, bit_order):
+    (middle_ref,), (mixed_ref,) = extra, outs
+    blk = lax.axis_index("blk")
+    for m in range(2):
+        store_ungrouped(middle_ref[m] + total[m], mixed_ref, blk, bit_order, (m,))
+
+
+def finish_input(total, extra, outs, *, bit_order):
+    (low_ref, mid_ref, gain_ref), (own_ref, away_ref, gain_grad_ref) = extra, outs
+    blk = lax.axis_index("blk")
+    for m in range(2):
+        grad = mid_ref[m] + norm_grad(total[m], low_ref[m].astype(F32), gain_ref[...], gain_grad_ref, m)
+        store_ungrouped(grad, own_ref if m == 0 else away_ref, blk, bit_order)
+
+
+def total_main(values):
+    rows, width = values.shape
+    rounds = 2 + lax.axis_size("blk").bit_length() - 1
+
+    def body(partners, ins, outs, scratch):
+        (v_ref,), (o_ref,) = ins, outs
+        out_buf, in_buf, send, recv = scratch
+        blk, head = lax.axis_index("blk"), lax.axis_index("head")
+        o_ref[...] = v_ref[...]
+        yield
+        for i in range(rounds):
+            target = (blk, head ^ (1 << i)) if i < 2 else (blk ^ (1 << (i - 2)), head)
+            out_buf[i] = o_ref[...]
+            copy = remote(out_buf.at[i], in_buf.at[i], send.at[i], recv.at[i], target)
+            copy.wait_recv()
+            o_ref[...] += in_buf[i]
+            copy.wait_send()
+        yield
+
+    vmem_spec = pl.BlockSpec(memory_space=pltpu.VMEM)
+    return (
+        [values],
+        [vmem_spec],
+        [jax.ShapeDtypeStruct(values.shape, F32)],
+        [vmem_spec],
+        [
+            pltpu.VMEM((rounds, rows, width), F32),
+            pltpu.VMEM((rounds, rows, width), F32),
+            pltpu.SemaphoreType.DMA((rounds,)),
+            pltpu.SemaphoreType.DMA((rounds,)),
+        ],
+        body,
+        8 * MIB,
     )
 
 
@@ -536,55 +868,46 @@
     def ungroup(values):
         return moved(values, lambda n: sum(bit_of(blk ^ n, b) << i for i, b in enumerate(bit_order)))
 
+    def everything(ref):
+        return ref
+
+    def mask_of(p):
+        return sum(((p >> i) & 1) << b for i, b in enumerate(bit_order))
+
     def rows_at(p):
         return lambda ref: ref.at[pl.ds(p * row_features, row_features), :]
 
-    def put(plan, weights, buffer, near, far, onward_far=True, point=0):
-        here = [plan.read(w) for w in weights]
-        at, columns = 0, []
-        for w in weights:
-            columns.append((at, w.shape[1] // 2))
-            at += w.shape[1] // 2
-
-        def half_of(k, other):
-            n = columns[k][1]
-
-            def cut(ref):
-                place = bit_of(lax.axis_index("blk"), TENSOR_BIT)
-                place = 1 - place if other else place
-                return ref.at[:, pl.ds(pl.multiple_of(place * n, n), n)]
-
-            return cut
-
-        def into(k, p):
-            start, n = columns[k]
-            return lambda ref: ref.at[pl.ds(p * row_features, row_features), pl.ds(start, n)]
-
-        def from_here(p, mask):
-            ids = [
-                plan.copy((here[k], half_of(k, mask & t_mask)), (buffer, into(k, p)), mask, point=point)
-                for k in range(len(weights))
-            ]
-            return ids
-
-        if near:
-            by_t = from_here(2, t_mask)
-            from_here(4, x_mask)
-            from_here(0, 0)
-        if far:
-            by_b = from_here(1, b_mask)
-            by_tb = from_here(3, b_mask | t_mask)
-        if near:
-            for k, i in enumerate(by_t):
-                plan.copy((buffer, into(k, 2)), (buffer, into(k, 6)), x_mask, after=i, point=point + 1)
-        if far and onward_far:
-            for p, ids in ((1, by_b), (3, by_tb)):
-                for k, i in enumerate(ids):
-                    plan.copy((buffer, into(k, p)), (buffer, into(k, p + 4)), x_mask, after=i, point=point + 3)
-
-    def put_onward(plan, buffer):
-        for p in (1, 3):
-            plan.copy((buffer, rows_at(p)), (buffer, rows_at(p + 4)), x_mask)
+    def half_cut(n, other):
+        def cut(ref):
+            place = bit_of(lax.axis_index("blk"), TENSOR_BIT)
+            place = 1 - place if other else place
+            return ref.at[:, pl.ds(pl.multiple_of(place * n, n), n)]
+
+        return cut
+
+    def send_over(plan, weight, buffer, p, point):
+        mask, n = mask_of(p), weight.shape[1] // 2
+        plan.copy((plan.read(weight), half_cut(n, mask & t_mask)), (buffer, rows_at(p)), mask, point=point)
+
+    def keep_own(plan, weight, buffer, point, onward=True):
+        here, n = plan.read(weight), weight.shape[1] // 2
+        if onward:
+            plan.copy((here, half_cut(n, 0)), (buffer, rows_at(4)), x_mask, point=point)
+        plan.local((here, half_cut(n, 0)), (buffer, rows_at(0)), (row_features, n), point=point)
+
+    def send_on(plan, buffer, places, point, after=None):
+        for p in places:
+            plan.copy((buffer, rows_at(p)), (buffer, rows_at(p + 4)), x_mask, after=after, point=point)
+
+    def lay(plan, array, buffer, p, point=0, columns=None, onward=False):
+        here = plan.read(array)
+        cut = (lambda ref: ref.at[:, pl.ds(*columns)]) if columns else everything
+        if onward:
+            plan.copy((here, cut), (buffer, rows_at(p + 4)), x_mask, point=point)
+        plan.local((here, cut), (buffer, rows_at(p)), (row_features, columns[1] if columns else array.shape[1]), point)
+
+    def fresh_for(plan, weights):
+        return plan.fresh(buffer_shape(weights), BF16)
 
     def buffer_shape(weights):
         return (8 * row_features, sum(w.shape[1] for w in weights) // 2)
@@ -602,36 +925,41 @@
         n = grad.shape[0] // 2
         return grad[:n], grad[n:].astype(BF16)
 
-    def everything(ref):
-        return ref
+    def weight_sum(a, b):
+        return split_grad(tn(a, b)) if extra_bits else weight_grad(a, b)
 
     def fold(plan, away):
         out = plan.fresh(away.shape, away.dtype)
         plan.copy((plan.read(away), everything), (out, everything), x_mask)
 
+    def fold_part(plan, away, buffer, start, n):
+        def part(ref):
+            return ref.at[:, pl.ds(start, n)]
+
+        plan.copy((plan.read(away), part), (buffer, part), x_mask)
+
     def to_settle(keep, got):
         total = keep + got.astype(F32)
         return total[:row_features], total[row_features:].astype(BF16)
 
-    def settle(plan, away):
+    def settle(plan, away, t_point=0):
         out, here = plan.fresh(away.shape, away.dtype), plan.read(away)
-        for i, mask in enumerate((b_mask, t_mask, b_mask | t_mask)):
-            plan.copy((here, rows_at(i)), (out, rows_at(i)), mask)
-
-    def settle_apart(away):
-        cut = [away[i * row_features : (i + 1) * row_features] for i in range(3)]
-        return jnp.concatenate(
-            [over_blk(c, mask) for c, mask in zip(cut, (b_mask, t_mask, b_mask | t_mask))], axis=0
-        )
-
-    def settled(own, got, column_widths):
-        f = row_features
-        own = own + got[:f].astype(F32)
-        other = got[f : 2 * f].astype(F32) + got[2 * f :].astype(F32)
-        results, at = [], 0
-        for w in column_widths:
-            results.append(in_order(tensor, own[:, at : at + w], other[:, at : at + w], 1))
-            at += w
+        for i, mask in ((0, b_mask), (2, b_mask | t_mask), (1, t_mask)):
+            plan.copy((here, rows_at(i)), (out, rows_at(i)), mask, point=t_point if mask == t_mask else 0)
+
+    def settled(sources, column_widths):
+        if all(w % 128 == 0 for w in column_widths):
+            return assemble(tensor, sources, column_widths)
+        f, results = row_features, []
+        widths = iter(column_widths)
+        for own, got in sources:
+            own = own + got[:f].astype(F32)
+            other = got[f : 2 * f].astype(F32) + got[2 * f :].astype(F32)
+            at = 0
+            while at < own.shape[1]:
+                w = next(widths)
+                results.append(in_order(tensor, own[:, at : at + w], other[:, at : at + w], 1))
+                at += w
         return results
 
     chunk = 2 * row_features
@@ -641,22 +969,24 @@
         (out,), rest = run(plan, spread_main(flat, chunk), next(ids))
         return out.reshape(tokens, width), rest
 
-    def gather_sum(partial, plan):
-        (out,), rest = run(plan, gather_main(partial, chunk), next(ids))
-        return out.reshape(2 * local_rows, width), rest
-
-    def partial_sum(left, weight):
-        return nt(left, weight).astype(BF16)
-
-    def take_batch(rows):
+    share = (2, local_rows, width)
+
+    def gather_sum(partial, plan, extra, outs_like, finish):
+        return run(plan, gather_main(partial, chunk, extra, outs_like, finish), next(ids))
+
+    def like(shape, dtype):
+        return jax.ShapeDtypeStruct(shape, dtype)
+
+    aligned = row_features % 128 == 0
+    local_order = bit_order if aligned else []
+
+    def split_batch(rows):
         mine = lax.dynamic_index_in_dim(rows, batch, 0, keepdims=False)
         theirs = lax.dynamic_index_in_dim(rows, 1 - batch, 0, keepdims=False)
-        return regroup(jnp.concatenate([mine, over_blk(theirs, b_mask)], axis=0))
-
-    def give_batch(rows):
-        rows = ungroup(rows)
-        back = over_blk(rows[local_rows:].astype(BF16), b_mask).astype(rows.dtype)
-        return in_order(batch, rows[None, :local_rows], back[None], 0)
+        return mine, theirs
+
+    def natural(rows):
+        return rows if aligned else ungroup(rows)
 
     length_row = lax.dynamic_index_in_dim(lengths, batch, 0, keepdims=False)
     doc_ends = jnp.cumsum(length_row)
@@ -683,16 +1013,9 @@
 
     inverse_freq = THETA ** (-jnp.arange(head_size // 2, dtype=F32) / (head_size // 2))
     angles = position.astype(F32)[:, None] * inverse_freq[None, :]
-    cosine = jnp.cos(angles)[:, None, :]
-    sine = jnp.sin(angles)[:, None, :]
-
-    def rope(values):
-        a, b = values[..., : head_size // 2], values[..., head_size // 2 :]
-        return jnp.concatenate([a * cosine - b * sine, b * cosine + a * sine], axis=-1)
-
-    def rope_back(values):
-        a, b = values[..., : head_size // 2], values[..., head_size // 2 :]
-        return jnp.concatenate([a * cosine + b * sine, b * cosine - a * sine], axis=-1)
+    cosine, sine = jnp.cos(angles), jnp.sin(angles)
+    cosine = jnp.concatenate([cosine, cosine], axis=1)
+    sine = jnp.concatenate([-sine, sine], axis=1)
 
     def rms(values):
         return lax.rsqrt(jnp.mean(values * values, axis=-1, keepdims=True) + EPS)
@@ -701,53 +1024,85 @@
         scaled = grad * gain
         return inverse * (scaled - normed * jnp.mean(scaled * normed, axis=-1, keepdims=True))
 
-    gain_a = regroup(attn_gain.astype(F32))
-    gain_m = regroup(mlp_gain.astype(F32))
-    gain_q = query_gain.astype(F32)
-    gain_k = key_gain.astype(F32)
-
-    a_weights, o_weights = (query_weight, key_matrix, value_matrix), (out_weight,)
-    x_low = take_batch(hidden_in)
-    rows_in = x_low.astype(F32)
-    inverse_a = rms(rows_in)
-    normal_a = rows_in * inverse_a
+    gains_in = jnp.stack([attn_gain, mlp_gain]).astype(F32)
+    gain_q = query_gain.astype(F32)[None]
+    gain_k = key_gain.astype(F32)[None]
+
+    q_columns, k_columns = heads * head_size, head_size
+    a_weights = (query_weight, key_matrix, value_matrix)
+
+    def halves(weights, which):
+        return jnp.concatenate(
+            [lax.dynamic_slice_in_dim(w, which * (w.shape[1] // 2), w.shape[1] // 2, 1) for w in weights], axis=1
+        )
+
+    mine, theirs = split_batch(hidden_in)
+    other = over_blk(theirs, b_mask)
+    a_own, a_other = halves(a_weights, tensor), halves(a_weights, 1 - tensor)
+    a_by_t = over_blk(a_other, t_mask)
+    a_by_b = over_blk(a_own, b_mask)
+    early = over_blk(jnp.concatenate([a_own, halves((down_weight,), tensor)], axis=1), x_mask)
+    (mine, other, cosine, sine, start_lanes, meta) = pin((mine, other, cosine, sine, start_lanes, meta))
+    if aligned:
+        x_low, xa, gains_in = enter(blk, bit_order, mine, other, gains_in)
+        gain_a, gain_m = gains_in[0], gains_in[1]
+    else:
+        gains_in = regroup(gains_in)
+        gain_a, gain_m = gains_in[0], gains_in[1]
+        x_low = regroup(jnp.concatenate([mine, other], axis=0))
+        x_wide = x_low.astype(F32)
+        xa = (x_wide * rms(x_wide) * gain_a).astype(BF16)
 
     plan = Plan()
-    a_buffer = plan.fresh(buffer_shape(a_weights), BF16)
-    put(plan, a_weights, a_buffer, True, True)
+    a_columns = a_own.shape[1]
+    w_a = fresh_for(plan, a_weights)
+    by_tb = plan.copy((plan.read(a_other), everything), (w_a, rows_at(3)), b_mask | t_mask)
+    lay(plan, a_by_t, w_a, 2, onward=True)
+    lay(plan, a_by_b, w_a, 1, onward=True)
+    lay(plan, a_own, w_a, 0)
+    lay(plan, early, w_a, 4, columns=(0, a_columns))
     here, cot_out = plan.read(cotangent), plan.fresh((2, local_rows, width), BF16)
-    plan.copy((here, lambda ref: ref.at[bit_of(lax.axis_index("blk"), batch_bit)]), (cot_out, lambda ref: ref.at[0]), 0)
     plan.copy(
-        (here, lambda ref: ref.at[1 - bit_of(lax.axis_index("blk"), batch_bit)]), (cot_out, lambda ref: ref.at[1]), b_mask
-    )
-    put(plan, (down_weight,), plan.fresh(buffer_shape((down_weight,)), BF16), True, False)
-    xa, (w_qkv, cot, w_down) = spread((normal_a * gain_a).astype(BF16), plan)
+        (here, lambda ref: ref.at[1 - bit_of(lax.axis_index("blk"), batch_bit)]),
+        (cot_out, lambda ref: ref.at[1]),
+        b_mask,
+        point=1,
+    )
+    plan.local(
+        (here, lambda ref: ref.at[bit_of(lax.axis_index("blk"), batch_bit)]),
+        (cot_out, lambda ref: ref.at[0]),
+        (local_rows, width),
+    )
+    w_out = fresh_for(plan, (out_weight,))
+    send_over(plan, out_weight, w_out, 1, 1)
+    send_over(plan, out_weight, w_out, 3, 1)
+    send_over(plan, out_weight, w_out, 2, 1)
+    keep_own(plan, out_weight, w_out, 0)
+    w_down = fresh_for(plan, (down_weight,))
+    send_over(plan, down_weight, w_down, 2, 1)
+    keep_own(plan, down_weight, w_down, 0, onward=False)
+    lay(plan, early, w_down, 4, columns=(a_columns, ff))
+    w_gate = fresh_for(plan, (gate_weight,))
+    keep_own(plan, gate_weight, w_gate, 1)
+    send_on(plan, w_a, (3,), 2, after=by_tb)
+    xa, (w_qkv, cot, w_out, w_down, w_gate) = spread(xa, plan)
     w_qkv = whole_weight(w_qkv)
-    cot = regroup(cot.reshape(2 * local_rows, width))
-
-    (xa, up_in) = pin((xa, up_weight))
-    up_half = lax.dynamic_slice_in_dim(up_in, tensor * ff, ff, 1)
-    up_other = lax.dynamic_slice_in_dim(up_in, (1 - tensor) * ff, ff, 1)
-    up_b, up_tb = over_blk(up_half, b_mask), over_blk(up_other, b_mask | t_mask)
-
-    qkv = nn(xa, w_qkv)
-    q_columns, k_columns = heads * head_size, head_size
-    q_raw = qkv[:, :q_columns].reshape(tokens, heads, head_size)
-    k_raw = qkv[:, q_columns : q_columns + k_columns].reshape(tokens, 1, head_size)
-    value = qkv[:, q_columns + k_columns :].astype(BF16)
-    q_inverse, k_inverse = rms(q_raw), rms(k_raw)
-    q_normal, k_normal = q_raw * q_inverse, k_raw * k_inverse
-    query = rope(q_normal * gain_q).astype(BF16).reshape(2, 4, half, q_columns)
-    key = rope(k_normal * gain_k).astype(BF16).reshape(tokens, head_size)
-    key_value = jnp.concatenate([key, value], axis=1)
+    cot = cot.reshape(2 * local_rows, width)
+    cot = enter(blk, bit_order, cot)[0] if aligned else regroup(cot)
+    query, key_value, raw = prepare(xa, w_qkv, cosine, sine, gain_q, gain_k, heads)
 
     plan = Plan()
-    put(plan, o_weights, plan.fresh(buffer_shape(o_weights), BF16), True, True)
     kv_out = plan.fresh(key_value.shape, BF16)
     plan.copy((plan.read(key_value), everything), (kv_out, everything), x_mask)
-    put(plan, (down_weight,), plan.through(w_down), False, True, onward_far=False)
-    put(plan, (gate_weight,), plan.fresh(buffer_shape((gate_weight,)), BF16), True, False)
-    cot_all, (w_out, kv_x, w_down, w_gate) = spread(cot, plan)
+    w_out = plan.through(w_out)
+    send_on(plan, w_out, (1, 2, 3), 0)
+    w_down = plan.through(w_down)
+    send_over(plan, down_weight, w_down, 1, 0)
+    send_over(plan, down_weight, w_down, 3, 0)
+    send_on(plan, w_down, (2,), 1)
+    w_gate = plan.through(w_gate)
+    send_over(plan, gate_weight, w_gate, 2, 1)
+    cot_all, (kv_x, w_out, w_down, w_gate) = spread(cot, plan)
     w_out = whole_weight(w_out)
     key_value = [key_value, kv_x]
     for b in extra_bits:
@@ -755,27 +1110,43 @@
     key_value = jnp.stack(key_value)
     keys = key_value[..., :head_size].reshape(parts, 2, 4, half, head_size)
     values = key_value[..., head_size:].reshape(parts, 2, 4, half, head_size)
+    query = query.reshape(2, 4, half, q_columns)
     attn, attn_t, total_e = attend(meta, query, keys, values, start_lanes, scaling)
     attn = attn.reshape(tokens, q_columns)
 
     plan = Plan()
-    put_onward(plan, plan.through(w_down))
-    put(plan, (gate_weight,), plan.through(w_gate), False, True, onward_far=False)
-    put(plan, (up_weight,), plan.fresh(buffer_shape((up_weight,)), BF16), True, False)
-    out_sum, (w_down, w_gate, w_up) = gather_sum(partial_sum(attn, w_out), plan)
+    w_down = plan.through(w_down)
+    send_on(plan, w_down, (1, 3), 0)
+    w_gate = plan.through(w_gate)
+    send_over(plan, gate_weight, w_gate, 1, 0)
+    send_over(plan, gate_weight, w_gate, 3, 0)
+    send_on(plan, w_gate, (2,), 0)
+    w_up = fresh_for(plan, (up_weight,))
+    send_over(plan, up_weight, w_up, 2, 0)
+    keep_own(plan, up_weight, w_up, 1)
+    x_low = x_low.reshape(share)
+    (middle, xm), (w_down, w_gate, w_up) = gather_sum(
+        nt(attn, w_out).astype(BF16),
+        plan,
+        [x_low, gain_m[None]],
+        [like(share, F32), like(share, BF16)],
+        finish_middle,
+    )
     w_down = whole_weight(w_down)
-    middle = x_low.astype(F32) + out_sum
-    inverse_m = rms(middle)
-    normal_m = middle * inverse_m
 
     plan = Plan()
-    put_onward(plan, plan.through(w_gate))
-    u_buffer = plan.through(w_up)
-    for p, got in ((1, up_b), (3, up_tb)):
-        here = plan.read(got)
-        plan.copy((here, everything), (u_buffer, rows_at(p + 4)), x_mask)
-        plan.copy((here, everything), (u_buffer, rows_at(p)), 0)
-    xm, (w_gate, w_up) = spread((normal_m * gain_m).astype(BF16), plan)
+    w_gate = plan.through(w_gate)
+    w_up = plan.through(w_up)
+    by_b = len(plan.jobs)
+    send_over(plan, up_weight, w_up, 1, 0)
+    send_on(plan, w_gate, (1, 3), 0)
+    send_on(plan, w_up, (2,), 1)
+    by_tb = plan.copy(
+        (plan.read(up_weight), half_cut(ff, True)), (w_up, rows_at(3)), b_mask | t_mask, after=by_b, point=2
+    )
+    send_on(plan, w_up, (1,), 2)
+    send_on(plan, w_up, (3,), 3, after=by_tb)
+    xm, (w_gate, w_up) = spread(xm.reshape(2 * local_rows, width), plan)
     w_gate, w_up = whole_weight(w_gate), whole_weight(w_up)
     d_active = nn(cot_all, w_down)
     gate = nn(xm, w_gate)
@@ -786,78 +1157,98 @@
     d_gate = (d_active * up * sig * (1.0 + gate * (1.0 - sig))).astype(BF16)
     d_up = (d_active * silu).astype(BF16)
 
-    keep_down, away_down = split_grad(tn(cot_all, active))
+    keep_down, away_down = weight_sum(cot_all, active)
+    got_x = over_blk(away_down, x_mask)
+    (d_gate, d_up, away_down) = pin((d_gate, d_up, away_down))
+    keep_gate, away_gate = weight_sum(xm, d_gate)
     plan = Plan()
-    fold(plan, away_down)
-    d_xm, (got,) = gather_sum((nt(d_gate, w_gate) + nt(d_up, w_up)).astype(BF16), plan)
-    own_down, away_down = to_settle(keep_down, got)
-    keep_gate, away_gate = split_grad(tn(xm, d_gate))
-    d_middle = cot.astype(F32) + norm_back(d_xm, normal_m, inverse_m, gain_m)
+    gate_x = plan.fresh(away_gate.shape, BF16)
+    ff_cut = ff // 2
+    fold_part(plan, away_gate, gate_x, 0, ff_cut)
+    (d_middle, d_mid, gain_m_grad), (gate_x,) = gather_sum(
+        back_through((d_gate, d_up), (w_gate, w_up)),
+        plan,
+        [cot.reshape(share), middle, gain_m[None]],
+        [like(share, F32), like(share, BF16), like((1, width), F32)],
+        finish_mlp_norm,
+    )
+    (d_mid, got_x) = pin((d_mid, got_x))
+    own_down, away_down = to_settle(keep_down, got_x)
+    keep_up, away_up = weight_sum(xm, d_up)
 
     plan = Plan()
-    settle(plan, away_down)
-    fold(plan, away_gate)
-    d_mid_all, (got_down, got) = spread(d_middle.astype(BF16), plan)
-    (g_down,) = settled(own_down, got_down, (ff,))
-    own_gate, away_gate = to_settle(keep_gate, got)
-    keep_up, away_up = split_grad(tn(xm, d_up))
-    keep_out, away_out = split_grad(tn(d_mid_all, attn))
+    settle(plan, away_down, 1)
+    gate_x = plan.through(gate_x)
+    fold_part(plan, away_gate, gate_x, ff_cut, ff - ff_cut)
+    up_x = plan.fresh(away_up.shape, BF16)
+    fold_part(plan, away_up, up_x, 0, ff_cut)
+    d_mid_all, (got_down, gate_x, up_x) = spread(d_mid.reshape(2 * local_rows, width), plan)
+    (g_down,) = settled([(own_down, got_down)], (ff,))
+    own_gate, away_gate = to_settle(keep_gate, gate_x)
+    keep_out, away_out = weight_sum(d_mid_all, attn)
     d_attn = nn(d_mid_all, w_out).astype(BF16).reshape(2, 4, half, q_columns)
     d_query, d_key, d_value = attend_back(
         meta, query, d_attn, keys, values, start_lanes, attn_t, total_e, scaling
     )
-    d_key_value = jnp.concatenate(
-        [d_key.reshape(parts, tokens, head_size), d_value.reshape(parts, tokens, head_size)], axis=-1
-    )
+    d_key = d_key.reshape(parts, tokens, head_size)
+    d_value = d_value.reshape(parts, tokens, head_size)
     for b in reversed(extra_bits):
-        n = d_key_value.shape[0] // 2
-        d_key_value = d_key_value[:n] + over_blk(d_key_value[n:].astype(BF16), 1 << b).astype(F32)
+        n = d_key.shape[0] // 2
+        d_key = d_key[:n] + over_blk(d_key[n:].astype(BF16), 1 << b).astype(F32)
+        d_value = d_value[:n] + over_blk(d_value[n:].astype(BF16), 1 << b).astype(F32)
 
     plan = Plan()
-    fold(plan, d_key_value[1].astype(BF16))
-    fold(plan, away_up)
+    fold(plan, jnp.concatenate([d_key[1], d_value[1]], axis=1).astype(BF16))
     settle(plan, away_gate)
-    mixed_sum, (got_kv, got, got_gate) = gather_sum(partial_sum(active, w_down), plan)
-    (g_gate,) = settled(own_gate, got_gate, (ff,))
-    own_up, away_up = to_settle(keep_up, got)
-    mixed = give_batch((middle + mixed_sum).astype(BF16))
-    d_key_value = d_key_value[0] + got_kv.astype(F32)
-    d_key, d_value = d_key_value[:, :head_size], d_key_value[:, head_size:]
-    dq_turned = rope_back(d_query.reshape(tokens, heads, head_size))
-    dk_turned = rope_back(d_key.reshape(tokens, 1, head_size))
-    gain_q_grad = jnp.sum(dq_turned * q_normal, axis=(0, 1))
-    gain_k_grad = jnp.sum(dk_turned * k_normal, axis=(0, 1))
-    dq_raw = norm_back(dq_turned, q_normal, q_inverse, gain_q).reshape(tokens, q_columns)
-    dk_raw = norm_back(dk_turned, k_normal, k_inverse, gain_k).reshape(tokens, k_columns)
-    d_qkv = jnp.concatenate([dq_raw, dk_raw, d_value], axis=1).astype(BF16)
-    keep_qkv, away_qkv = split_grad(tn(xa, d_qkv))
+    up_x = plan.through(up_x)
+    fold_part(plan, away_up, up_x, ff_cut, ff - ff_cut)
+    fold(plan, away_out)
+    (mixed,), (got_kv, got_gate, up_x, out_x) = gather_sum(
+        back_through((active,), (w_down,)),
+        plan,
+        [middle],
+        [like(share, BF16)],
+        functools.partial(finish_mixed, bit_order=local_order),
+    )
+    (g_gate,) = settled([(own_gate, got_gate)], (ff,))
+    own_up, away_up = to_settle(keep_up, up_x)
+    own_out, away_out = to_settle(keep_out, out_x)
+    mixed = natural(mixed)
+    mixed_got = over_blk(mixed[1], b_mask)
+    d_qkv, d_xa_partial, gains_qk = prepare_back(
+        d_query.reshape(tokens, q_columns), d_key, d_value, got_kv, raw, cosine, sine, gain_q, gain_k, w_qkv, heads
+    )
+    keep_qkv, away_qkv = weight_sum(xa, d_qkv)
+    (away_qkv, mixed_got) = pin((away_qkv, mixed_got))
 
     plan = Plan()
     settle(plan, away_up)
     fold(plan, away_qkv)
-    fold(plan, away_out)
-    d_xa, (got_up, got, got_o) = gather_sum(partial_sum(d_qkv, w_qkv), plan)
-    (g_up,) = settled(own_up, got_up, (ff,))
+    (input_own, input_away, gain_a_grad), (got_up, got) = gather_sum(
+        d_xa_partial,
+        plan,
+        [x_low, d_middle, gain_a[None]],
+        [like((local_rows, width), F32), like((local_rows, width), BF16), like((1, width), F32)],
+        functools.partial(finish_input, bit_order=local_order),
+    )
+    (g_up,) = settled([(own_up, got_up)], (ff,))
     own_qkv, away_qkv = to_settle(keep_qkv, got)
-    own_out, away_out = to_settle(keep_out, got_o)
-    got = settle_apart(jnp.concatenate([away_qkv, away_out], axis=1))
-    own = jnp.concatenate([own_qkv, own_out], axis=1)
-    g_query, g_key, g_value, g_out = settled(own, got, (q_columns, k_columns, k_columns, q_columns))
-    input_grad = give_batch(d_middle + norm_back(d_xa, normal_a, inverse_a, gain_a))
-    sums = jnp.concatenate(
-        [
-            ungroup(jnp.sum(d_xa * normal_a, axis=0)),
-            gain_q_grad,
-            gain_k_grad,
-            ungroup(jnp.sum(d_xm * normal_m, axis=0)),
-        ]
-    )
-    for b in range(2):
-        sums = sums + over_head(sums, 1 << b)
-    for b in range(bits):
-        sums = sums + over_blk(sums, 1 << b)
-    at = [width, width + head_size, width + 2 * head_size]
-    gains = jnp.split(sums, at)
+
+    plan = Plan()
+    settle(plan, away_qkv)
+    settle(plan, away_out)
+    input_got = plan.fresh((local_rows, width), BF16)
+    plan.copy((plan.read(natural(input_away)), everything), (input_got, everything), b_mask)
+    sums = jnp.concatenate([ungroup(gain_a_grad[0]), gains_qk[0], gains_qk[1], ungroup(gain_m_grad[0])])
+    (sums,), (got_a, got_o, input_got) = run(
+        plan, total_main(sums.reshape(-1, 128)), next(ids), [1 << i for i in range(bits)]
+    )
+    g_query, g_key, g_value, g_out = settled(
+        [(own_qkv, got_a), (own_out, got_o)], (q_columns, k_columns, k_columns, q_columns)
+    )
+    mixed = in_order(batch, mixed[:1], mixed_got[None], 0)
+    input_grad = in_order(batch, natural(input_own)[None], input_got.astype(F32)[None], 0)
+    gains = jnp.split(sums.reshape(-1), [width, width + head_size, width + 2 * head_size])
     return (
         mixed,
         input_grad,

time: 714 us -> 552 us (0.77); the launches traced: 703 us -> 552 us
  matrix products: 76.7 us -> 15.3 us
  Pallas kernels: 418 us -> 473 us
  waiting for transfers between devices: 64.5 us -> 11.8 us
  local copies, waits for them, and re-layouts: 77.6 us -> 29.1 us
  other arithmetic: 46.7 us -> 11.4 us
  starting transfers between devices: 17 us -> 9.75 us
    pallas_call x0 -> x15, Pallas kernels: none -> 56.8 us  [the longest x5 26.4 us: weight_grad(): pl.pallas_call(weight_grad_kernel, grid=(steps,), in_specs=[pl.BlockSpec(...]
    ppermute x11 -> x6, waiting for transfers between devices: 64 us -> 11.8 us  [over_blk(): return lax.ppermute(value, 'blk', [(i, i ^ mask) for i in range(count)])]
    dot_general x5 -> x0, matrix products: 35 us -> none  [tn(): lax.dot_general(a, b, (((0,), (0,)), ((), ())), preferred_element_type=F32)]
    unnamed x287 -> x153, local copies, waits for them, and re-layouts: 48 us -> 23 us
    dot_general x5 -> x1, matrix products: 22.4 us -> 1.29 us  [nt(): lax.dot_general(a, b, (((1,), (1,)), ((), ())), preferred_element_type=F32)]
    slice x15 -> x4, local copies, waits for them, and re-layouts: 15 us -> 0.13 us  [the longest x2 0.08 us: local(): fold(plan, jnp.concatenate([d_key[1], d_value[1]], axis=1).astype(BF16))]
    add x13 -> x0, other arithmetic: 8.39 us -> none  [the longest x4 4.01 us: settled(): own = own + got[:f].astype(F32)]
    select_n x9 -> x2, other arithmetic: 9.08 us -> 1.93 us  [in_order(): jnp.where(flag == 0, jnp.concatenate([own, other], axis=axis), jnp.concat...]
  transfers between devices with their start and end apart: 13 -> 6, of which waited for: 8 -> 1; matrix products, arithmetic and copies ran while one was open for 4% -> 2% of each run, Pallas kernels for 0% -> 13%
where the time goes in v3:
time: 552 us
  Pallas kernels  473 us (86%)
  local copies, waits for them, and re-layouts  29.1 us (5%)
  matrix products  15.3 us (3%)
  waiting for transfers between devices  11.8 us (2%)
  other arithmetic  11.4 us (2%)
  starting transfers between devices  9.75 us (2%)
    pallas_call x9, Pallas kernels, run(): pl.pallas_call(kernel, out_shape=[*out_shapes, *plan.shapes], in_specs=[*...  396 us
    pallas_call x5, Pallas kernels, weight_grad(): pl.pallas_call(weight_grad_kernel, grid=(steps,), in_specs=[pl.BlockSpec(...  26.4 us
    unnamed x153, local copies, waits for them, and re-layouts  23 us
    dot_general x4, matrix products, nn(): return jnp.dot(a, b, preferred_element_type=F32)  14 us
    pallas_call x2, Pallas kernels, back_through(): pl.pallas_call(back_kernel, grid=(depth // tile,), in_specs=[*[pl.BlockSp...  13.9 us
    ppermute x6, waiting for transfers between devices, over_blk(): return lax.ppermute(value, 'blk', [(i, i ^ mask) for i in range(count)])  11.8 us
  transfers between devices with their start and end apart: 6, of which 1 were waited for; matrix products, arithmetic and copies ran while one was open for 2% of the time, Pallas kernels for 13%

profile of v3, /device:TPU:0, one launch (start us, length us, event | category | flops | bytes accessed | tf_op | source)
XLA Modules:
  0.0 551.8 jit_solution(5899277419614023232)
XLA Ops:
  2.8 4.1 collective-permute-start.2
  18.3 11.8 %collective-permute-done.refs_1_ = bf16[64,2048]{1,0:T(8,128)(2,1)S(1)} collective-permute-done((bf16[64,2048]{1,0:T(8,128)(2,1)}, bf16[64,2048]{1,0:T(8,128)(2,1)S(1)}, u32[]{:S(2)}, u32[]{:S(2)}) %collective-permute-start) | collective-permute-done | bytes 262176 | tf_op jit(solution)/shard_map/ppermute | solution.py:41
  40.9 45.5 %shard_map.238 = (bf16[2,2,2,2,64,2048]{5,4,3,2,1,0:T(8,128)(2,1)S(1)}, bf16[2048,512]{1,0:T(8,128)(2,1)S(1)}, bf16[2,64,2048]{2,1,0:T(8,128)(2,1)S(1)}, bf16[20...) custom-call(bf16[2,64,2048]{2,1,0:T(8,128)(2,1)S(1)} %bitcast.121, ...), custom_call_target="tpu_custom_call" | custom-call | tf_op jit(solution)/shard_map/pallas_call | solution.py:588
  86.5 3.8 shard_map.239
  90.4 40.0 %shard_map.241 = (bf16[2,2,2,2,64,2048]{5,4,3,2,1,0:T(8,128)(2,1)S(1)}, bf16[1024,256]{1,0:T(8,128)(2,1)S(1)}, bf16[2048,256]{1,0:T(8,128)(2,1)S(1)}, bf16[2048,768]{1,0:T(8,128)(2,1)S(1)}, bf16[2048,768]{1,0:T(8,128)(2,1)S(1)}) custom-call(bf16[2,64,2048]{2,1,0:T(8,128)(2,1)S(1)} %bitcast.99, ...), custom_call_target="tpu_custom_call", output_to_operand_aliasing={{2}: (2, {}), {3}: (3, {}), {4}: (6, {})} | custom-call | tf_op jit(solution)/shard_map/pallas_call | solution.py:588
  130.6 8.8 %shard_map.242 = (bf16[2,4,128,256]{3,2,1,0:T(8,128)(2,1)S(1)}, f32[4,128,512]{2,1,0:T(8,128)S(1)}, f32[4,1,512]{2,1,0:T(1,128)S(1)}) custom-call(s32[45]{0:T(128)S(1)} %concatenate.52.meta_ref, bf16[2,4,128,256]{3,2,1,0:T(8,128)(2,1)S(1)} %bitcast.123, bf16[2,2,4,128,128]{4,3,2,1,0:T(8,128)(2,1)S(1)} %bitcast.118, ...), custom_call_target="tpu_custom_call" | custom-call | flops 2147483648 | bytes 4194304 | tf_op jit(solution)/shard_map/pallas_call | solution.py:206
  141.1 45.4 %shard_map.243 = (f32[2,64,2048]{2,1,0:T(8,128)S(1)}, bf16[2,64,2048]{2,1,0:T(8,128)(2,1)S(1)}, bf16[2048,768]{1,0:T(8,128)(2,1)S(1)}, bf16[2048,768]{1,0:T(8,128)(2,1)S(1)}, bf16[2048,768]{1,0:T(8,128)(2,1)S(1)}) custom-call(bf16[2,2,2,2,64,2048]{5,4,3,2,1,0:T(8,128)(2,1)S(1)} %bitcast.90, ...), custom_call_target="tpu_custom_call", output_to_operand_aliasing={{2}: (3, {}), {3}: (4, {})} | custom-call | tf_op jit(solution)/shard_map/pallas_call | solution.py:588
  187.3 3.4 fusion.13
  190.8 50.4 %shard_map.244 = (bf16[2,2,2,2,64,2048]{5,4,3,2,1,0:T(8,128)(2,1)S(1)}, bf16[2048,768]{1,0:T(8,128)(2,1)S(1)}, bf16[2048,768]{1,0:T(8,128)(2,1)S(1)}) custom-call(bf16[2,64,2048]{2,1,0:T(8,128)(2,1)S(1)} %get-tuple-element.117.refs_0_, bf16[2048,768]{1,0:T(8,128)(2,1)S(1)} %get-tuple-element.118.refs_1_, ...), custom_call_target="tpu_custom_call", output_to_operand_aliasing={{1}: (1, {}), {2}: (2, {})} | custom-call | tf_op jit(solution)/shard_map/pallas_call | solution.py:588
  244.7 5.9 %multiply_convert_fusion.2 = (bf16[1024,768]{1,0:T(8,128)(2,1)S(1)}, bf16[1024,768]{1,0:T(8,128)(2,1)}, bf16[1024,768]{1,0:T(8,128)(2,1)}) fusion(f32[1024,768]{1,0:T(8,128)S(1)} %fusion.12, f32[1024,768]{1,0:T(8,128)S(1)} %fusion.13, bf16[1024,2048]{1,0:T(8,128)(2,1)S(1)} %bitcast.94, bf16[2048,768]{1,0:T(8,128)(2,1)S(1)} %get-tuple-element.122.refs_3_), kind=kOutput, calls=%fused_computation.6 | convolution fusion | flops 3233021952 | bytes 18350080 | tf_op jit(solution)/shard_map/dot_general | solution.py:32
  250.6 6.6 %shard_map.246 = (f32[1024,768]{1,0:T(8,128)S(1)}, bf16[1024,768]{1,0:T(8,128)(2,1)}) custom-call(bf16[1024,2048]{1,0:T(8,128)(2,1)S(1)} %bitcast.105, bf16[1024,768]{1,0:T(8,128)(2,1)S(1)} %get-tuple-element.181.refs_0_.b_ref), custom_call_target="tpu_custom_call" | custom-call | tf_op jit(solution)/shard_map/pallas_call | solution.py:470
  263.5 5.3 shard_map.245
  268.9 5.9 %shard_map.250 = (f32[1024,768]{1,0:T(8,128)S(1)}, bf16[1024,768]{1,0:T(8,128)(2,1)S(1)}) custom-call(bf16[1024,2048]{1,0:T(8,128)(2,1)S(1)} %bitcast.95, bf16[1024,768]{1,0:T(8,128)(2,1)S(1)} %copy-done.19), custom_call_target="tpu_custom_call" | custom-call | tf_op jit(solution)/shard_map/pallas_call | solution.py:470
  276.5 8.6 %shard_map.247 = bf16[1024,2048]{1,0:T(8,128)(2,1)S(1)} custom-call(bf16[1024,768]{1,0:T(8,128)(2,1)S(1)} %copy-done.18, bf16[1024,768]{1,0:T(8,128)(2,1)S(1)} %copy-done.19, bf16[2048,768]{1,0:T(8,128)(2,1)S(1)} %get-tuple-element.121.refs_2_, bf16[2048,768]{1,0:T(8,128)(2,1)S(1)} %copy-done.13), custom_call_target="tpu_custom_call" | custom-call | tf_op jit(solution)/shard_map/pallas_call | solution.py:439
  285.1 5.9 %shard_map.248 = (f32[1024,768]{1,0:T(8,128)S(1)}, bf16[1024,768]{1,0:T(8,128)(2,1)S(1)}) custom-call(bf16[1024,2048]{1,0:T(8,128)(2,1)S(1)} %bitcast.96, bf16[1024,768]{1,0:T(8,128)(2,1)S(1)} %copy-done.18), custom_call_target="tpu_custom_call" | custom-call | tf_op jit(solution)/shard_map/pallas_call | solution.py:470
  291.0 31.2 %shard_map.249 = (f32[2,64,2048]{2,1,0:T(8,128)S(1)}, bf16[2,64,2048]{2,1,0:T(8,128)(2,1)S(1)}, f32[1,2048]{1,0:T(1,128)S(1)}, bf16[1024,768]{1,0:T(8,128)(2,1)S(1)}) custom-call(bf16[2,2,2,2,64,2048]{5,4,3,2,1,0:T(8,128)(2,1)S(1)} %bitcast.97, bf16[2,64,2048]{2,1,0:T(8,128)(2,1)S(1)} %bitcast.100, f32[2,64,2048]{2,1,0:T(8,128)S(1)} %copy-done.31, ...), custom_call_target="tpu_custom_call" | custom-call | tf_op jit(solution)/shard_map/pallas_call | solution.py:588
  324.7 41.0 %shard_map.251 = (bf16[2,2,2,2,64,2048]{5,4,3,2,1,0:T(8,128)(2,1)S(1)}, bf16[768,768]{1,0:T(8,128)(2,1)S(1)}, bf16[1024,768]{1,0:T(8,128)(2,1)S(1)}, bf16[1024,768]{1,0:T(8,128)(2,1)S(1)}) custom-call(bf16[2,64,2048]{2,1,0:T(8,128)(2,1)S(1)} %get-tuple-element.131.refs_0_, bf16[768,768]{1,0:T(8,128)(2,1)S(1)} %slice.125.refs_1_, ...), custom_call_target="tpu_custom_call", output_to_operand_aliasing={{2}: (2, {})} | custom-call | tf_op jit(solution)/shard_map/pallas_call | solution.py:588
  367.0 3.5 shard_map.253
  372.6 10.9 %shard_map.252 = (f32[2,4,128,256]{3,2,1,0:T(8,128)S(1)}, f32[2,2,4,128,128]{4,3,2,1,0:T(8,128)S(1)}, f32[2,2,4,128,128]{4,3,2,1,0:T(8,128)S(1)}) custom-call(s32[45]{0:T(128)S(1)} %concatenate.52.meta_ref, bf16[2,4,128,256]{3,2,1,0:T(8,128)(2,1)S(1)} %bitcast.124, bf16[2,4,128,256]{3,2,1,0:T(8,128)(2,1)S(1)} %bitcast.125, ...), custom_call_target="tpu_custom_call" | custom-call | flops 5368709120 | bytes 7340032 | tf_op jit(solution)/shard_map/pallas_call | solution.py:239
  383.7 48.5 %shard_map.254 = (bf16[2,64,2048]{2,1,0:T(8,128)(2,1)S(1)}, bf16[1024,256]{1,0:T(8,128)(2,1)S(1)}, bf16[768,768]{1,0:T(8,128)(2,1)S(1)}, bf16[1024,768]{1,0:T(8,128)(2,1)S(1)}, bf16[1024,256]{1,0:T(8,128)(2,1)S(1)}) custom-call(bf16[2,2,2,2,64,2048]{5,4,3,2,1,0:T(8,128)(2,1)S(1)} %bitcast.98, ...), custom_call_target="tpu_custom_call", output_to_operand_aliasing={{3}: (4, {})} | custom-call | tf_op jit(solution)/shard_map/pallas_call | solution.py:588
  436.9 7.2 %shard_map.255 = (bf16[1024,512]{1,0:T(8,128)(2,1)S(1)}, bf16[1024,2048]{1,0:T(8,128)(2,1)S(1)}, f32[8,128]{1,0:T(8,128)S(1)}) custom-call(f32[1024,256]{1,0:T(8,128)S(1)} %bitcast.113, f32[2,1024,128]{2,1,0:T(8,128)S(1)} %bitcast.111, f32[2,1024,128]{2,1,0:T(8,128)S(1)} %bitcast.112, bf16[1024,256]{1,0:T(8,128)(2,1)S(1)} %get-tuple-element.147.got_ref, ...), custom_call_target="tpu_custom_call" | custom-call | tf_op jit(solution)/shard_map/pallas_call | solution.py:335
  444.1 4.6 shard_map.256
  451.3 44.3 %shard_map.257 = (f32[64,2048]{1,0:T(8,128)S(1)}, bf16[64,2048]{1,0:T(8,128)(2,1)S(1)}, f32[1,2048]{1,0:T(1,128)S(1)}, bf16[768,768]{1,0:T(8,128)(2,1)S(1)}, bf16[1024,512]{1,0:T(8,128)(2,1)S(1)}) custom-call(bf16[2,2,2,2,64,2048]{5,4,3,2,1,0:T(8,128)(2,1)S(1)} %bitcast.101, bf16[2,64,2048]{2,1,0:T(8,128)(2,1)S(1)} %bitcast.109, ...), custom_call_target="tpu_custom_call" | custom-call | tf_op jit(solution)/shard_map/pallas_call | solution.py:588
  496.4 49.8 %shard_map.258 = (f32[34,128]{1,0:T(8,128)S(1)}, bf16[768,512]{1,0:T(8,128)(2,1)S(1)}, bf16[768,256]{1,0:T(8,128)(2,1)S(1)}, bf16[64,2048]{1,0:T(8,128)(2,1)S(1)}) custom-call(f32[34,128]{1,0:T(8,128)S(1)} %bitcast.122, bf16[768,512]{1,0:T(8,128)(2,1)S(1)} %slice.126.refs_1_, bf16[768,256]{1,0:T(8,128)(2,1)S(1)} %slice.127.refs_2_, ...), custom_call_target="tpu_custom_call" | custom-call | tf_op jit(solution)/shard_map/pallas_call | solution.py:588
  (234 shorter events, 57.6 us)
Async XLA Ops:
  0.6 12.5 %copy-start = (s32[2,9]{1,0:T(2,128)S(1)}, s32[2,9]{1,0:T(2,128)}, u32[]{:S(2)}) copy-start(s32[2,9]{1,0:T(2,128)} %param.15) | copy-start | bytes 220
  0.7 10.0 %copy-start.8 = (bf16[256,1536]{1,0:T(8,128)(2,1)S(1)}, bf16[256,1536]{1,0:T(8,128)(2,1)}, u32[]{:S(2)}) copy-start(bf16[256,1536]{1,0:T(8,128)(2,1)} %refs_5_.2) | copy-start | bytes 2359300
  0.7 13.3 %copy-start.64 = (bf16[2048]{0:T(1024)(128)(2,1)S(1)}, bf16[2048]{0:T(1024)(128)(2,1)}, u32[]{:S(2)}) copy-start(bf16[2048]{0:T(1024)(128)(2,1)} %param.23) | copy-start | bytes 12292
  0.7 13.3 %copy-start.65 = (bf16[2048]{0:T(1024)(128)(2,1)S(1)}, bf16[2048]{0:T(1024)(128)(2,1)}, u32[]{:S(2)}) copy-start(bf16[2048]{0:T(1024)(128)(2,1)} %param.26) | copy-start | bytes 12292
  2.8 14.2 %copy-start.47 = (bf16[256,512]{1,0:T(8,128)(2,1)}, bf16[256,512]{1,0:T(8,128)(2,1)S(1)}, u32[]{:S(2)}) copy-start(bf16[256,512]{1,0:T(8,128)(2,1)S(1)} %pad_maximum_fusion.6.refs_4_) | copy-start | bytes 786436
  2.8 27.6 %collective-permute-start.2 = (bf16[256,512]{1,0:T(8,128)(2,1)S(1)}, bf16[256,512]{1,0:T(8,128)(2,1)S(1)}, u32[]{:S(2)}, u32[]{:S(2)}) collective-permute-start(bf16[256,512]{1,0:T(8,128)(2,1)S(1)} %pad_maximum_fusion.6.refs_4_), channel_id=1, source_target_pairs={{0,16},{4,20},{8,24},{12,28},{16,0},{20,4},{24,8},{28,12},{1,17},{... | collective-permute-start | bytes 786440 | tf_op jit(solution)/shard_map/ppermute | solution.py:41
  6.9 11.2 %copy-start.49 = (bf16[256,512]{1,0:T(8,128)(2,1)}, bf16[256,512]{1,0:T(8,128)(2,1)S(1)}, u32[]{:S(2)}) copy-start(bf16[256,512]{1,0:T(8,128)(2,1)S(1)} %pad_maximum_fusion.5.refs_1_) | copy-start | bytes 786436
  6.9 24.2 %collective-permute-start.1 = (bf16[256,512]{1,0:T(8,128)(2,1)S(1)}, bf16[256,512]{1,0:T(8,128)(2,1)S(1)}, u32[]{:S(2)}, u32[]{:S(2)}) collective-permute-start(bf16[256,512]{1,0:T(8,128)(2,1)S(1)} %pad_maximum_fusion.5.refs_1_), channel_id=1, source_target_pairs={{0,8},{4,12},{8,0},{12,4},{16,24},{20,28},{24,16},{28,20},{1,9},{5... | collective-permute-start | bytes 786440 | tf_op jit(solution)/shard_map/ppermute | solution.py:41
  10.3 19.7 %collective-permute-start = (bf16[64,2048]{1,0:T(8,128)(2,1)}, bf16[64,2048]{1,0:T(8,128)(2,1)S(1)}, u32[]{:S(2)}, u32[]{:S(2)}) collective-permute-start(bf16[64,2048]{1,0:T(8,128)(2,1)} %get-tuple-element.188), channel_id=1, source_target_pairs={{0,16},{4,20},{8,24},{12,28},{16,0},{20,4},{24,8},{28,12},{1,17},{... | collective-permute-start | bytes 786440 | tf_op jit(solution)/shard_map/ppermute | solution.py:41
  10.7 21.9 %copy-start.32 = (bf16[256,512]{1,0:T(8,128)(2,1)S(1)}, bf16[256,512]{1,0:T(8,128)(2,1)}, u32[]{:S(2)}) copy-start(bf16[256,512]{1,0:T(8,128)(2,1)} %refs_10_.1) | copy-start | bytes 786436
  11.6 20.2 %collective-permute-start.3 = (bf16[256,1280]{1,0:T(8,128)(2,1)}, bf16[256,1280]{1,0:T(8,128)(2,1)S(1)}, u32[]{:S(2)}, u32[]{:S(2)}) collective-permute-start(bf16[256,1280]{1,0:T(8,128)(2,1)} %pad_maximum_fusion), channel_id=1, source_target_pairs={{0,4},{4,0},{8,12},{12,8},{16,20},{20,16},{24,28},{28,24},{1,5},{5... | collective-permute-start | bytes 1966088 | tf_op jit(solution)/shard_map/ppermute | solution.py:41
  40.9 45.6 %copy-start.22 = (f32[1024,128]{1,0:T(8,128)S(1)}, f32[1024,128]{1,0:T(8,128)}, u32[]{:S(2)}) copy-start(f32[1024,128]{1,0:T(8,128)} %pad_maximum_fusion.3.sin_ref) | copy-start | bytes 1572868
  40.9 45.6 %copy-start.24 = (f32[1024,128]{1,0:T(8,128)S(1)}, f32[1024,128]{1,0:T(8,128)}, u32[]{:S(2)}) copy-start(f32[1024,128]{1,0:T(8,128)} %pad_maximum_fusion.2.cos_ref) | copy-start | bytes 1572868
  90.3 40.0 %copy-start.43 = (f32[1024,384]{1,0:T(8,128)}, f32[1024,384]{1,0:T(8,128)S(1)}, u32[]{:S(2)}) copy-start(f32[1024,384]{1,0:T(8,128)S(1)} %get-tuple-element.148.raw_ref) | copy-start | bytes 4718596
  90.3 40.3 %copy-start.60 = (bf16[1024,256]{1,0:T(8,128)(2,1)}, bf16[1024,256]{1,0:T(8,128)(2,1)S(1)}, u32[]{:S(2)}) copy-start(bf16[1024,256]{1,0:T(8,128)(2,1)S(1)} %get-tuple-element.103) | copy-start | bytes 1572868
  130.4 9.0 %copy-start.28 = (bf16[2048,256]{1,0:T(8,128)(2,1)}, bf16[2048,256]{1,0:T(8,128)(2,1)S(1)}, u32[]{:S(2)}) copy-start(bf16[2048,256]{1,0:T(8,128)(2,1)S(1)} %get-tuple-element.112) | copy-start | bytes 3145732
  130.6 8.8 %copy-start.51 = (bf16[2,1024,128]{2,1,0:T(8,128)(2,1)}, bf16[2,1024,128]{2,1,0:T(8,128)(2,1)S(1)}, u32[]{:S(2)}) copy-start(bf16[2,1024,128]{2,1,0:T(8,128)(2,1)S(1)} %get-tuple-element.184) | copy-start | bytes 1572868
  130.6 8.8 %copy-start.53 = (bf16[2,1024,128]{2,1,0:T(8,128)(2,1)}, bf16[2,1024,128]{2,1,0:T(8,128)(2,1)S(1)}, u32[]{:S(2)}) copy-start(bf16[2,1024,128]{2,1,0:T(8,128)(2,1)S(1)} %get-tuple-element.185) | copy-start | bytes 1572868
  260.1 62.2 %collective-permute-start.4 = (bf16[1024,768]{1,0:T(8,128)(2,1)}, bf16[1024,768]{1,0:T(8,128)(2,1)}, u32[]{:S(2)}, u32[]{:S(2)}) collective-permute-start(bf16[1024,768]{1,0:T(8,128)(2,1)} %get-tuple-element.126), channel_id=1, source_target_pairs={{0,4},{4,0},{8,12},{12,8},{16,20},{20,16},{24,28},{28,24},{1,5},{5... | collective-permute-start | bytes 4718600 | tf_op jit(solution)/shard_map/ppermute | solution.py:41
  268.9 7.6 %copy-start.13 = (bf16[2048,768]{1,0:T(8,128)(2,1)S(1)}, bf16[2048,768]{1,0:T(8,128)(2,1)}, u32[]{:S(2)}) copy-start(bf16[2048,768]{1,0:T(8,128)(2,1)} %copy-done.12) | copy-start | bytes 9437188
  268.9 7.6 %copy-start.18 = (bf16[1024,768]{1,0:T(8,128)(2,1)S(1)}, bf16[1024,768]{1,0:T(8,128)(2,1)}, u32[]{:S(2)}) copy-start(bf16[1024,768]{1,0:T(8,128)(2,1)} %get-tuple-element.127.refs_0_.b_ref) | copy-start | bytes 4718596
  291.0 31.3 %copy-start.36 = (f32[1024,768]{1,0:T(8,128)S(1)}, f32[1024,768]{1,0:T(8,128)}, u32[]{:S(2)}) copy-start(f32[1024,768]{1,0:T(8,128)} %copy-done.35) | copy-start | bytes 9437188
  324.7 41.0 %copy-start.29 = (bf16[2048,256]{1,0:T(8,128)(2,1)S(1)}, bf16[2048,256]{1,0:T(8,128)(2,1)}, u32[]{:S(2)}) copy-start(bf16[2048,256]{1,0:T(8,128)(2,1)} %copy-done.28) | copy-start | bytes 3145732
  432.4 18.8 %collective-permute-start.5 = (bf16[64,2048]{1,0:T(8,128)(2,1)S(1)}, bf16[64,2048]{1,0:T(8,128)(2,1)S(1)}, u32[]{:S(2)}, u32[]{:S(2)}) collective-permute-start(bf16[64,2048]{1,0:T(8,128)(2,1)S(1)} %get-tuple-element.187), channel_id=1, source_target_pairs={{0,16},{4,20},{8,24},{12,28},{16,0},{20,4},{24,8},{28,12},{1,17},{... | collective-permute-start | bytes 786440 | tf_op jit(solution)/shard_map/ppermute | solution.py:41
  (50 other events, 128.6 us)

commit v4 on v3

--- a/solution.py
+++ b/solution.py
@@ -1,4 +1,5 @@
 import functools
+import math
 
 import jax
 import jax.numpy as jnp
@@ -521,8 +522,71 @@
         return len(self.jobs) - 1
 
 
-def run(plan, main, collective_id, greeted=()):
-    inputs, in_specs, out_shapes, out_specs, scratch, body, limit = main
+class Fill:
+    def __init__(self, inputs, outputs, step, point):
+        self.inputs, self.outputs, self.step, self.point = inputs, outputs, step, point
+
+    def scratch(self):
+        shapes = [pltpu.VMEM(a.shape, a.dtype) for a in (*self.inputs, *self.outputs)]
+        return [*shapes, pltpu.SemaphoreType.DMA((len(shapes),))]
+
+
+def fill_weight_grad(a, b, point):
+    depth, n, tile = a.shape[1], b.shape[1], 256
+    half = depth // 2
+
+    def step(ins, outs):
+        (a_ref, b_ref), (keep_ref, away_ref) = ins, outs
+
+        def one(i, carry):
+            at = pl.ds(pl.multiple_of(i * tile, tile), tile)
+            keep_ref[at, :] = tn(a_ref[:, at], b_ref[...])
+            far = pl.ds(pl.multiple_of(half + i * tile, tile), tile)
+            away_ref[at, :] = tn(a_ref[:, far], b_ref[...]).astype(BF16)
+            return carry
+
+        lax.fori_loop(0, half // tile, one, 0)
+
+    outputs = [jax.ShapeDtypeStruct((half, n), F32), jax.ShapeDtypeStruct((half, n), BF16)]
+    return Fill([a, b], outputs, step, point)
+
+
+def fill_back(grad, weight, point):
+    tokens, depth, tile = grad.shape[0], weight.shape[0], 256
+
+    def step(ins, outs):
+        (g_ref, w_ref), (out_ref,) = ins, outs
+
+        def one(i, carry):
+            at = pl.ds(pl.multiple_of(i * tile, tile), tile)
+            out_ref[:, at] = nt(g_ref[...], w_ref[at, :]).astype(BF16)
+            return carry
+
+        lax.fori_loop(0, depth // tile, one, 0)
+
+    return Fill([grad, weight], [jax.ShapeDtypeStruct((tokens, depth), BF16)], step, point)
+
+
+def fill_product(left, right, point):
+    tokens, n, tile = left.shape[0], right.shape[1], 256
+
+    def step(ins, outs):
+        (l_ref, r_ref), (out_ref,) = ins, outs
+
+        def one(i, carry):
+            at = pl.ds(pl.multiple_of(i * tile, tile), tile)
+            out_ref[at, :] = nn(l_ref[at, :], r_ref[...])
+            return carry
+
+        lax.fori_loop(0, tokens // tile, one, 0)
+
+    return Fill([left, right], [jax.ShapeDtypeStruct((tokens, n), F32)], step, point)
+
+
+def run(plan, main, collective_id, greeted=(), fills=(), limit=None):
+    inputs, in_specs, out_shapes, out_specs, scratch, body, own_limit = main
+    limit = limit or own_limit + sum(math.prod(s.shape) * s.dtype.itemsize for f in fills for s in f.scratch()[:-1])
+    f_in, f_out = [a for f in fills for a in f.inputs], [a for f in fills for a in f.outputs]
     n_in, n_out = len(inputs), len(out_shapes)
     m_in, m_out = len(plan.inputs), len(plan.shapes)
     jobs = plan.jobs
@@ -533,11 +597,33 @@
     def kernel(*refs):
         main_in, refs = refs[:n_in], refs[n_in:]
         plan_in, refs = refs[:m_in], refs[m_in:]
+        fill_in, refs = refs[: len(f_in)], refs[len(f_in) :]
         main_out, refs = refs[:n_out], refs[n_out:]
         plan_out, refs = refs[:m_out], refs[m_out:]
+        fill_out, refs = refs[: len(f_out)], refs[len(f_out) :]
         send, recv, *rest = refs
         bounce = dict(zip(local_jobs, rest))
         rest = rest[len(local_jobs) :]
+        parts = []
+        for f in fills:
+            k, m = len(f.inputs), len(f.outputs)
+            (*held, sems), rest = rest[: k + m + 1], rest[k + m + 1 :]
+            loads = [pltpu.make_async_copy(fill_in[i], held[i], sems.at[i]) for i in range(k)]
+            stores = [pltpu.make_async_copy(held[k + i], fill_out[i], sems.at[k + i]) for i in range(m)]
+            fill_in, fill_out = fill_in[k:], fill_out[m:]
+            for copy in loads:
+                copy.start()
+            parts.append((f, held[:k], held[k:], loads, stores))
+
+        def compute(point):
+            for f, ins, outs, loads, stores in parts:
+                if f.point == point:
+                    for copy in loads:
+                        copy.wait()
+                    f.step(ins, outs)
+                    for copy in stores:
+                        copy.start()
+
         blk, head = lax.axis_index("blk"), lax.axis_index("head")
         core, near, across = (blk, head ^ 1), (blk, head ^ 2), (blk ^ (1 << TENSOR_BIT), head)
         barrier = pltpu.get_barrier_semaphore()
@@ -554,6 +640,8 @@
 
         def part(side):
             (kind, index), cut = side
+            if kind == "fill":
+                return cut(parts[index[0]][2][index[1]])
             return cut((plan_in if kind == "in" else plan_out)[index])
 
         def issue(point):
@@ -577,6 +665,7 @@
         point = 0
         for _ in body((core, near, across), main_in, main_out, rest):
             issue(point)
+            compute(point)
             point += 1
         issue(None)
         issue(None)
@@ -584,16 +673,20 @@
             arrive(i)
             if jobs[i][2]:
                 started[i].wait_send()
+        for *_, stores in parts:
+            for copy in stores:
+                copy.wait()
 
     results = pl.pallas_call(
         kernel,
-        out_shape=[*out_shapes, *plan.shapes],
-        in_specs=[*in_specs, *[any_spec] * m_in],
-        out_specs=[*out_specs, *[any_spec] * m_out],
+        out_shape=[*out_shapes, *plan.shapes, *f_out],
+        in_specs=[*in_specs, *[any_spec] * (m_in + len(f_in))],
+        out_specs=[*out_specs, *[any_spec] * (m_out + len(f_out))],
         scratch_shapes=[
             pltpu.SemaphoreType.DMA((max(1, len(jobs)),)),
             pltpu.SemaphoreType.DMA((max(1, len(jobs)),)),
             *[pltpu.VMEM(jobs[i][5], BF16) for i in local_jobs],
+            *[s for f in fills for s in f.scratch()],
             *scratch,
         ],
         input_output_aliases={n_in + i: n_out + o for i, o in plan.aliases.items()},
@@ -601,7 +694,7 @@
             collective_id=collective_id, has_side_effects=True, vmem_limit_bytes=limit
         ),
         cost_estimate=TINY_COST,
-    )(*inputs, *plan.inputs)
+    )(*inputs, *plan.inputs, *f_in)
     return results[:n_out], results[n_out:]
 
 
@@ -928,15 +1021,14 @@
     def weight_sum(a, b):
         return split_grad(tn(a, b)) if extra_bits else weight_grad(a, b)
 
-    def fold(plan, away):
-        out = plan.fresh(away.shape, away.dtype)
-        plan.copy((plan.read(away), everything), (out, everything), x_mask)
-
-    def fold_part(plan, away, buffer, start, n):
+    def fold(plan, source, shape, point=0):
+        plan.copy((source, everything), (plan.fresh(shape, BF16), everything), x_mask, point=point)
+
+    def fold_part(plan, source, buffer, start, n, point=0):
         def part(ref):
             return ref.at[:, pl.ds(start, n)]
 
-        plan.copy((plan.read(away), part), (buffer, part), x_mask)
+        plan.copy((source, part), (buffer, part), x_mask, point=point)
 
     def to_settle(keep, got):
         total = keep + got.astype(F32)
@@ -965,14 +1057,14 @@
     chunk = 2 * row_features
     ids = iter(range(100))
 
-    def spread(flat, plan):
-        (out,), rest = run(plan, spread_main(flat, chunk), next(ids))
+    def spread(flat, plan, fills=(), limit=None):
+        (out,), rest = run(plan, spread_main(flat, chunk), next(ids), fills=fills, limit=limit)
         return out.reshape(tokens, width), rest
 
     share = (2, local_rows, width)
 
-    def gather_sum(partial, plan, extra, outs_like, finish):
-        return run(plan, gather_main(partial, chunk, extra, outs_like, finish), next(ids))
+    def gather_sum(partial, plan, extra, outs_like, finish, fills=()):
+        return run(plan, gather_main(partial, chunk, extra, outs_like, finish), next(ids), fills=fills)
 
     def like(shape, dtype):
         return jax.ShapeDtypeStruct(shape, dtype)
@@ -1085,7 +1177,7 @@
     w_gate = fresh_for(plan, (gate_weight,))
     keep_own(plan, gate_weight, w_gate, 1)
     send_on(plan, w_a, (3,), 2, after=by_tb)
-    xa, (w_qkv, cot, w_out, w_down, w_gate) = spread(xa, plan)
+    xa, (w_qkv, cot, w_out, w_down, w_gate) = spread(xa, plan, limit=56 * MIB)
     w_qkv = whole_weight(w_qkv)
     cot = cot.reshape(2 * local_rows, width)
     cot = enter(blk, bit_order, cot)[0] if aligned else regroup(cot)
@@ -1146,9 +1238,10 @@
     )
     send_on(plan, w_up, (1,), 2)
     send_on(plan, w_up, (3,), 3, after=by_tb)
-    xm, (w_gate, w_up) = spread(xm.reshape(2 * local_rows, width), plan)
+    xm, (w_gate, w_up, d_active) = spread(
+        xm.reshape(2 * local_rows, width), plan, [fill_product(cot_all, w_down, 0)]
+    )
     w_gate, w_up = whole_weight(w_gate), whole_weight(w_up)
-    d_active = nn(cot_all, w_down)
     gate = nn(xm, w_gate)
     up = nn(xm, w_up)
     sig = jax.nn.sigmoid(gate)
@@ -1160,32 +1253,41 @@
     keep_down, away_down = weight_sum(cot_all, active)
     got_x = over_blk(away_down, x_mask)
     (d_gate, d_up, away_down) = pin((d_gate, d_up, away_down))
-    keep_gate, away_gate = weight_sum(xm, d_gate)
-    plan = Plan()
-    gate_x = plan.fresh(away_gate.shape, BF16)
     ff_cut = ff // 2
-    fold_part(plan, away_gate, gate_x, 0, ff_cut)
-    (d_middle, d_mid, gain_m_grad), (gate_x,) = gather_sum(
+    plan, fills = Plan(), []
+    if extra_bits:
+        keep_gate, away_gate = weight_sum(xm, d_gate)
+        keep_up, away_up = weight_sum(xm, d_up)
+        source, point = plan.read(away_gate), 0
+    else:
+        fills = [fill_weight_grad(xm, d_gate, 0), fill_weight_grad(xm, d_up, 1)]
+        source, point = ("fill", (0, 1)), 1
+    gate_x = plan.fresh((4 * row_features, ff), BF16)
+    fold_part(plan, source, gate_x, 0, ff_cut, point)
+    (d_middle, d_mid, gain_m_grad), (gate_x, *filled) = gather_sum(
         back_through((d_gate, d_up), (w_gate, w_up)),
         plan,
         [cot.reshape(share), middle, gain_m[None]],
         [like(share, F32), like(share, BF16), like((1, width), F32)],
         finish_mlp_norm,
-    )
+        fills,
+    )
+    if filled:
+        keep_gate, away_gate, keep_up, away_up = filled
     (d_mid, got_x) = pin((d_mid, got_x))
     own_down, away_down = to_settle(keep_down, got_x)
-    keep_up, away_up = weight_sum(xm, d_up)
 
     plan = Plan()
     settle(plan, away_down, 1)
     gate_x = plan.through(gate_x)
-    fold_part(plan, away_gate, gate_x, ff_cut, ff - ff_cut)
+    fold_part(plan, plan.read(away_gate), gate_x, ff_cut, ff - ff_cut)
     up_x = plan.fresh(away_up.shape, BF16)
-    fold_part(plan, away_up, up_x, 0, ff_cut)
-    d_mid_all, (got_down, gate_x, up_x) = spread(d_mid.reshape(2 * local_rows, width), plan)
+    fold_part(plan, plan.read(away_up), up_x, 0, ff_cut)
+    d_mid_all, (got_down, gate_x, up_x, mixed_partial) = spread(
+        d_mid.reshape(2 * local_rows, width), plan, [fill_back(active, w_down, 0)]
+    )
     (g_down,) = settled([(own_down, got_down)], (ff,))
     own_gate, away_gate = to_settle(keep_gate, gate_x)
-    keep_out, away_out = weight_sum(d_mid_all, attn)
     d_attn = nn(d_mid_all, w_out).astype(BF16).reshape(2, 4, half, q_columns)
     d_query, d_key, d_value = attend_back(
         meta, query, d_attn, keys, values, start_lanes, attn_t, total_e, scaling
@@ -1198,39 +1300,49 @@
         d_value = d_value[:n] + over_blk(d_value[n:].astype(BF16), 1 << b).astype(F32)
 
     plan = Plan()
-    fold(plan, jnp.concatenate([d_key[1], d_value[1]], axis=1).astype(BF16))
+    away_kv = jnp.concatenate([d_key[1], d_value[1]], axis=1).astype(BF16)
+    fold(plan, plan.read(away_kv), away_kv.shape)
     settle(plan, away_gate)
     up_x = plan.through(up_x)
-    fold_part(plan, away_up, up_x, ff_cut, ff - ff_cut)
-    fold(plan, away_out)
-    (mixed,), (got_kv, got_gate, up_x, out_x) = gather_sum(
-        back_through((active,), (w_down,)),
+    fold_part(plan, plan.read(away_up), up_x, ff_cut, ff - ff_cut)
+    (mixed,), (got_kv, got_gate, up_x, *filled) = gather_sum(
+        mixed_partial,
         plan,
         [middle],
         [like(share, BF16)],
         functools.partial(finish_mixed, bit_order=local_order),
-    )
+        [] if extra_bits else [fill_weight_grad(d_mid_all, attn, 0)],
+    )
+    keep_out, away_out = filled if filled else weight_sum(d_mid_all, attn)
     (g_gate,) = settled([(own_gate, got_gate)], (ff,))
     own_up, away_up = to_settle(keep_up, up_x)
-    own_out, away_out = to_settle(keep_out, out_x)
     mixed = natural(mixed)
     mixed_got = over_blk(mixed[1], b_mask)
     d_qkv, d_xa_partial, gains_qk = prepare_back(
         d_query.reshape(tokens, q_columns), d_key, d_value, got_kv, raw, cosine, sine, gain_q, gain_k, w_qkv, heads
     )
-    keep_qkv, away_qkv = weight_sum(xa, d_qkv)
-    (away_qkv, mixed_got) = pin((away_qkv, mixed_got))
-
-    plan = Plan()
+    (d_xa_partial, mixed_got) = pin((d_xa_partial, mixed_got))
+
+    plan, fills = Plan(), []
     settle(plan, away_up)
-    fold(plan, away_qkv)
-    (input_own, input_away, gain_a_grad), (got_up, got) = gather_sum(
+    fold(plan, plan.read(away_out), away_out.shape)
+    if extra_bits:
+        keep_qkv, away_qkv = weight_sum(xa, d_qkv)
+        fold(plan, plan.read(away_qkv), away_qkv.shape)
+    else:
+        fills = [fill_weight_grad(xa, d_qkv, 0)]
+        fold(plan, ("fill", (0, 1)), (4 * row_features, a_columns), 1)
+    (input_own, input_away, gain_a_grad), (got_up, out_x, got, *filled) = gather_sum(
         d_xa_partial,
         plan,
         [x_low, d_middle, gain_a[None]],
         [like((local_rows, width), F32), like((local_rows, width), BF16), like((1, width), F32)],
         functools.partial(finish_input, bit_order=local_order),
-    )
+        fills,
+    )
+    if filled:
+        keep_qkv = filled[0]
+    own_out, away_out = to_settle(keep_out, out_x)
     (g_up,) = settled([(own_up, got_up)], (ff,))
     own_qkv, away_qkv = to_settle(keep_qkv, got)
 

time: 552 us -> 532 us (0.964)
  Pallas kernels: 473 us -> 453 us
    pallas_call x5 -> x1, Pallas kernels: 26.4 us -> 6.7 us  [weight_grad(): pl.pallas_call(weight_grad_kernel, grid=(steps,), in_specs=[pl.BlockSpec(...]
    pallas_call x9, Pallas kernels: 396 us -> 402 us  [run(): pl.pallas_call(kernel, out_shape=[*out_shapes, *plan.shapes, *f_out], in_...]
    pallas_call x2 -> x1, Pallas kernels: 13.9 us -> 8.55 us  [back_through(): pl.pallas_call(back_kernel, grid=(depth // tile,), in_specs=[*[pl.BlockSp...]
    dot_general x4 -> x3, matrix products: 14 us -> 10.4 us  [nn(): return jnp.dot(a, b, preferred_element_type=F32)]
    unnamed x153 -> x147, local copies, waits for them, and re-layouts: 23 us -> 23.6 us
  transfers between devices with their start and end apart: 6 -> 6, of which waited for: 1 -> 2; matrix products, arithmetic and copies ran while one was open for 2% -> 2% of each run, Pallas kernels for 13% -> 11%
where the time goes in v4:
time: 532 us; the launch traced here: 530 us
  Pallas kernels  453 us (85%)
  local copies, waits for them, and re-layouts  29 us (5%)
  waiting for transfers between devices  13.8 us (3%)
  other arithmetic  12.1 us (2%)
  matrix products  11.7 us (2%)
  starting transfers between devices  8.68 us (2%)
    pallas_call x9, Pallas kernels, run(): pl.pallas_call(kernel, out_shape=[*out_shapes, *plan.shapes, *f_out], in_...  402 us
    unnamed x147, local copies, waits for them, and re-layouts  23.6 us
    ppermute x6, waiting for transfers between devices, over_blk(): return lax.ppermute(value, 'blk', [(i, i ^ mask) for i in range(count)])  13.8 us
    pallas_call x1, Pallas kernels, attend_back(): pl.pallas_call(functools.partial(attend_back_kernel, factor=scaling * LOG...  10.7 us
  transfers between devices with their start and end apart: 6, of which 2 were waited for; matrix products, arithmetic and copies ran while one was open for 2% of the time, Pallas kernels for 11%

profile of v4, /device:TPU:0, one launch (start us, length us, event | category | flops | bytes accessed | tf_op | source)
XLA Modules:
  0.0 530.2 jit_solution(6063309940879174960)
XLA Ops:
  2.8 4.1 collective-permute-start.2
  16.8 13.2 %collective-permute-done.refs_1_ = bf16[64,2048]{1,0:T(8,128)(2,1)S(1)} collective-permute-done((bf16[64,2048]{1,0:T(8,128)(2,1)S(1)}, bf16[64,2048]{1,0:T(8,128)(2,1)S(1)}, u32[]{:S(2)}, u32[]{:S(2)}) %collective-permute-start) | collective-permute-done | bytes 262176 | tf_op jit(solution)/shard_map/ppermute | solution.py:42
  32.2 45.8 %shard_map.238 = (bf16[2,2,2,2,64,2048]{5,4,3,2,1,0:T(8,128)(2,1)}, bf16[2048,512]{1,0:T(8,128)(2,1)}, bf16[2,64,2048]{2,1,0:T(8,128)(2,1)}, bf16[2048,256]{1,0:...) custom-call(bf16[2,64,2048]{2,1,0:T(8,128)(2,1)} %bitcast.119, bf16[256,512]{1,0:T(8,128)(2,1)} %copy-done.59, ...), custom_call_target="tpu_custom_call" | custom-call | tf_op jit(solution)/shard_map/pallas_call | solution.py:680
  79.2 2.4 copy-done.6
  83.2 3.7 shard_map.239
  87.0 1.9 copy-done.31
  89.0 39.6 %shard_map.241 = (bf16[2,2,2,2,64,2048]{5,4,3,2,1,0:T(8,128)(2,1)S(1)}, bf16[1024,256]{1,0:T(8,128)(2,1)S(1)}, bf16[2048,256]{1,0:T(8,128)(2,1)S(1)}, bf16[2048,768]{1,0:T(8,128)(2,1)S(1)}, bf16[2048,768]{1,0:T(8,128)(2,1)S(1)}) custom-call(bf16[2,64,2048]{2,1,0:T(8,128)(2,1)S(1)} %bitcast.98, ...), custom_call_target="tpu_custom_call", output_to_operand_aliasing={{2}: (2, {}), {3}: (3, {}), {4}: (6, {})} | custom-call | tf_op jit(solution)/shard_map/pallas_call | solution.py:680
  128.8 8.8 %shard_map.242 = (bf16[2,4,128,256]{3,2,1,0:T(8,128)(2,1)S(1)}, f32[4,128,512]{2,1,0:T(8,128)S(1)}, f32[4,1,512]{2,1,0:T(1,128)S(1)}) custom-call(s32[45]{0:T(128)S(1)} %concatenate.52.meta_ref, bf16[2,4,128,256]{3,2,1,0:T(8,128)(2,1)S(1)} %bitcast.121, bf16[2,2,4,128,128]{4,3,2,1,0:T(8,128)(2,1)S(1)} %bitcast.116, ...), custom_call_target="tpu_custom_call" | custom-call | flops 2147483648 | bytes 4194304 | tf_op jit(solution)/shard_map/pallas_call | solution.py:207
  139.3 45.5 %shard_map.243 = (f32[2,64,2048]{2,1,0:T(8,128)S(1)}, bf16[2,64,2048]{2,1,0:T(8,128)(2,1)S(1)}, bf16[2048,768]{1,0:T(8,128)(2,1)S(1)}, bf16[2048,768]{1,0:T(8,128)(2,1)S(1)}, bf16[2048,768]{1,0:T(8,128)(2,1)S(1)}) custom-call(bf16[2,2,2,2,64,2048]{5,4,3,2,1,0:T(8,128)(2,1)S(1)} %bitcast.88, ...), custom_call_target="tpu_custom_call", output_to_operand_aliasing={{2}: (3, {}), {3}: (4, {})} | custom-call | tf_op jit(solution)/shard_map/pallas_call | solution.py:680
  184.8 51.6 %shard_map.244 = (bf16[2,2,2,2,64,2048]{5,4,3,2,1,0:T(8,128)(2,1)S(1)}, bf16[2048,768]{1,0:T(8,128)(2,1)S(1)}, bf16[2048,768]{1,0:T(8,128)(2,1)S(1)}, f32[1024,768]{1,0:T(8,128)S(1)}) custom-call(bf16[2,64,2048]{2,1,0:T(8,128)(2,1)S(1)} %get-tuple-element.118.refs_0_, ...), custom_call_target="tpu_custom_call", output_to_operand_aliasing={{1}: (1, {}), {2}: (2, {})} | custom-call | tf_op jit(solution)/shard_map/pallas_call | solution.py:680
  236.4 3.4 fusion.12
  240.3 5.7 %multiply_convert_fusion = (bf16[1024,768]{1,0:T(8,128)(2,1)S(1)}, bf16[1024,768]{1,0:T(8,128)(2,1)}, bf16[1024,768]{1,0:T(8,128)(2,1)}) fusion(f32[1024,768]{1,0:T(8,128)S(1)} %fusion.12, f32[1024,768]{1,0:T(8,128)S(1)} %get-tuple-element.123, bf16[1024,2048]{1,0:T(8,128)(2,1)S(1)} %bitcast.95, bf16[2048,768]{1,0:T(8,128)(2,1)S(1)} %get-tuple-element.125.refs_3_), kind=kOutput, calls=%fused_computation.4 | convolution fusion | flops 3233021952 | bytes 18350080 | tf_op jit(solution)/shard_map/dot_general | solution.py:33
  246.0 6.7 %shard_map.245 = (f32[1024,768]{1,0:T(8,128)S(1)}, bf16[1024,768]{1,0:T(8,128)(2,1)}) custom-call(bf16[1024,2048]{1,0:T(8,128)(2,1)S(1)} %bitcast.92, bf16[1024,768]{1,0:T(8,128)(2,1)S(1)} %get-tuple-element.183.b_ref.refs_5_), custom_call_target="tpu_custom_call" | custom-call | tf_op jit(solution)/shard_map/pallas_call | solution.py:471
  261.6 8.5 %shard_map.246 = bf16[1024,2048]{1,0:T(8,128)(2,1)S(1)} custom-call(bf16[1024,768]{1,0:T(8,128)(2,1)S(1)} %copy-done.20, bf16[1024,768]{1,0:T(8,128)(2,1)S(1)} %copy-done.22, bf16[2048,768]{1,0:T(8,128)(2,1)S(1)} %copy-done.5, bf16[2048,768]{1,0:T(8,128)(2,1)S(1)} %copy-done.14), custom_call_target="tpu_custom_call" | custom-call | tf_op jit(solution)/shard_map/pallas_call | solution.py:440
  270.2 2.1 copy-done.8
  272.3 38.0 %shard_map.247 = (f32[2,64,2048]{2,1,0:T(8,128)S(1)}, bf16[2,64,2048]{2,1,0:T(8,128)(2,1)S(1)}, f32[1,2048]{1,0:T(1,128)S(1)}, bf16[1024,768]{1,0:T(8,128)(2,1)S...) custom-call(bf16[2,2,2,2,64,2048]{5,4,3,2,1,0:T(8,128)(2,1)} %bitcas, ...), custom_call_target="tpu_custom_call" | custom-call | tf_op jit(solution)/shard_map/pallas_call | solution.py:680
  310.3 2.0 convert_add_fusion.2
  313.8 41.1 %shard_map.248 = (bf16[2,2,2,2,64,2048]{5,4,3,2,1,0:T(8,128)(2,1)S(1)}, bf16[768,768]{1,0:T(8,128)(2,1)S(1)}, bf16[1024,768]{1,0:T(8,128)(2,1)S(1)}, bf16[1024,768]{1,0:T(8,128)(2,1)S(1)}, bf16[1024,2048]{1,0:T(8,128)(2,1)S(1)}) custom-call(bf16[2,64,2048]{2,1,0:T(8,128)(2,1)S(1)} %get-tuple-element.132.refs_0_, ...), custom_call_target="tpu_custom_call", output_to_operand_aliasing={{2}: (2, {})} | custom-call | tf_op jit(solution)/shard_map/pallas_call | solution.py:680
  358.2 10.7 %shard_map.249 = (f32[2,4,128,256]{3,2,1,0:T(8,128)S(1)}, f32[2,2,4,128,128]{4,3,2,1,0:T(8,128)S(1)}, f32[2,2,4,128,128]{4,3,2,1,0:T(8,128)S(1)}) custom-call(s32[45]{0:T(128)S(1)} %concatenate.52.meta_ref, bf16[2,4,128,256]{3,2,1,0:T(8,128)(2,1)S(1)} %bitcast.122, bf16[2,4,128,256]{3,2,1,0:T(8,128)(2,1)S(1)} %bitcast.123, ...), custom_call_target="tpu_custom_call" | custom-call | flops 5368709120 | bytes 7340032 | tf_op jit(solution)/shard_map/pallas_call | solution.py:240
  369.0 45.5 %shard_map.250 = (bf16[2,64,2048]{2,1,0:T(8,128)(2,1)S(1)}, bf16[1024,256]{1,0:T(8,128)(2,1)S(1)}, bf16[768,768]{1,0:T(8,128)(2,1)S(1)}, bf16[1024,768]{1,0:T(8,...) custom-call(bf16[2,2,2,2,64,2048]{5,4,3,2,1,0:T(8,128)(2,1)S(1)} %bitcast.1, ...), custom_call_target="tpu_custom_call", output_to_operand_aliasing={{3}: (4, {})} | custom-call | tf_op jit(solution)/shard_map/pallas_call | solution.py:680
  414.9 2.2 convert_add_fusion
  420.8 7.3 %shard_map.251 = (bf16[1024,512]{1,0:T(8,128)(2,1)S(1)}, bf16[1024,2048]{1,0:T(8,128)(2,1)S(1)}, f32[8,128]{1,0:T(8,128)S(1)}) custom-call(f32[1024,256]{1,0:T(8,128)S(1)} %bitcast.111, f32[2,1024,128]{2,1,0:T(8,128)S(1)} %bitcast.109, f32[2,1024,128]{2,1,0:T(8,128)S(1)} %bitcast.110, bf16[1024,256]{1,0:T(8,128)(2,1)S(1)} %get-tuple-element.149.got_ref, ...), custom_call_target="tpu_custom_call" | custom-call | tf_op jit(solution)/shard_map/pallas_call | solution.py:336
  428.6 45.3 %shard_map.252 = (f32[64,2048]{1,0:T(8,128)S(1)}, bf16[64,2048]{1,0:T(8,128)(2,1)S(1)}, f32[1,2048]{1,0:T(1,128)S(1)}, bf16[768,768]{1,0:T(8,128)(2,1)S(1)}, bf1...) custom-call(bf16[2,2,2,2,64,2048]{5,4,3,2,1,0:T(8,128)(2,1)S(1)} %bi, ...), custom_call_target="tpu_custom_call" | custom-call | tf_op jit(solution)/shard_map/pallas_call | solution.py:680
  474.9 49.6 %shard_map.253 = (f32[34,128]{1,0:T(8,128)S(1)}, bf16[768,512]{1,0:T(8,128)(2,1)S(1)}, bf16[768,256]{1,0:T(8,128)(2,1)S(1)}, bf16[64,2048]{1,0:T(8,128)(2,1)S(1)}) custom-call(f32[34,128]{1,0:T(8,128)S(1)} %bitcast.120, bf16[768,512]{1,0:T(8,128)(2,1)S(1)} %slice.126.refs_1_, bf16[768,256]{1,0:T(8,128)(2,1)S(1)} %slice.127.refs_2_, ...), custom_call_target="tpu_custom_call" | custom-call | tf_op jit(solution)/shard_map/pallas_call | solution.py:680
  (222 shorter events, 43.7 us)
Async XLA Ops:
  0.6 11.1 %copy-start = (s32[2,9]{1,0:T(2,128)S(1)}, s32[2,9]{1,0:T(2,128)}, u32[]{:S(2)}) copy-start(s32[2,9]{1,0:T(2,128)} %param.15) | copy-start | bytes 220
  0.7 11.9 %copy-start.61 = (bf16[2048]{0:T(1024)(128)(2,1)S(1)}, bf16[2048]{0:T(1024)(128)(2,1)}, u32[]{:S(2)}) copy-start(bf16[2048]{0:T(1024)(128)(2,1)} %param.23) | copy-start | bytes 12292
  0.7 11.9 %copy-start.62 = (bf16[2048]{0:T(1024)(128)(2,1)S(1)}, bf16[2048]{0:T(1024)(128)(2,1)}, u32[]{:S(2)}) copy-start(bf16[2048]{0:T(1024)(128)(2,1)} %param.26) | copy-start | bytes 12292
  2.8 12.8 %copy-start.58 = (bf16[256,512]{1,0:T(8,128)(2,1)}, bf16[256,512]{1,0:T(8,128)(2,1)S(1)}, u32[]{:S(2)}) copy-start(bf16[256,512]{1,0:T(8,128)(2,1)S(1)} %pad_maximum_fusion.6.refs_4_) | copy-start | bytes 786436
  2.8 28.4 %collective-permute-start.2 = (bf16[256,512]{1,0:T(8,128)(2,1)S(1)}, bf16[256,512]{1,0:T(8,128)(2,1)S(1)}, u32[]{:S(2)}, u32[]{:S(2)}) collective-permute-start(bf16[256,512]{1,0:T(8,128)(2,1)S(1)} %pad_maximum_fusion.6.refs_4_), channel_id=1, source_target_pairs={{0,16},{4,20},{8,24},{12,28},{16,0},{20,4},{24,8},{28,12},{1,17},{... | collective-permute-start | bytes 786440 | tf_op jit(solution)/shard_map/ppermute | solution.py:42
  6.9 9.7 %copy-start.59 = (bf16[256,512]{1,0:T(8,128)(2,1)}, bf16[256,512]{1,0:T(8,128)(2,1)S(1)}, u32[]{:S(2)}) copy-start(bf16[256,512]{1,0:T(8,128)(2,1)S(1)} %pad_maximum_fusion.5.refs_1_) | copy-start | bytes 786436
  6.9 24.3 %collective-permute-start.1 = (bf16[256,512]{1,0:T(8,128)(2,1)S(1)}, bf16[256,512]{1,0:T(8,128)(2,1)}, u32[]{:S(2)}, u32[]{:S(2)}) collective-permute-start(bf16[256,512]{1,0:T(8,128)(2,1)S(1)} %pad_maximum_fusion.5.refs_1_), channel_id=1, source_target_pairs={{0,8},{4,12},{8,0},{12,4},{16,24},{20,28},{24,16},{28,20},{1,9},{5... | collective-permute-start | bytes 786440 | tf_op jit(solution)/shard_map/ppermute | solution.py:42
  9.6 20.5 %collective-permute-start = (bf16[64,2048]{1,0:T(8,128)(2,1)S(1)}, bf16[64,2048]{1,0:T(8,128)(2,1)S(1)}, u32[]{:S(2)}, u32[]{:S(2)}) collective-permute-start(bf16[64,2048]{1,0:T(8,128)(2,1)S(1)} %get-tuple-element.190), channel_id=1, source_target_pairs={{0,16},{4,20},{8,24},{12,28},{16,0},{20,4},{24,8},{28,12},{1,17},{... | collective-permute-start | bytes 786440 | tf_op jit(solution)/shard_map/ppermute | solution.py:42
  10.1 21.1 %collective-permute-start.3 = (bf16[256,1280]{1,0:T(8,128)(2,1)S(1)}, bf16[256,1280]{1,0:T(8,128)(2,1)S(1)}, u32[]{:S(2)}, u32[]{:S(2)}) collective-permute-start(bf16[256,1280]{1,0:T(8,128)(2,1)S(1)} %pad_maximum_fusion), channel_id=1, source_target_pairs={{0,4},{4,0},{8,12},{12,8},{16,20},{20,16},{24,28},{28,24},{1,5},{5... | collective-permute-start | bytes 1966088 | tf_op jit(solution)/shard_map/ppermute | solution.py:42
  31.2 107.8 %copy-start.38 = (bf16[128,2048]{1,0:T(8,128)(2,1)}, bf16[128,2048]{1,0:T(8,128)(2,1)S(1)}, u32[]{:S(2)}) copy-start(bf16[128,2048]{1,0:T(8,128)(2,1)S(1)} %get-tuple-element.114) | copy-start | bytes 1572868
  32.2 47.0 %copy-start.23 = (f32[1024,128]{1,0:T(8,128)S(1)}, f32[1024,128]{1,0:T(8,128)}, u32[]{:S(2)}) copy-start(f32[1024,128]{1,0:T(8,128)} %pad_maximum_fusion.3.sin_ref) | copy-start | bytes 1572868
  32.2 47.0 %copy-start.25 = (f32[1024,128]{1,0:T(8,128)S(1)}, f32[1024,128]{1,0:T(8,128)}, u32[]{:S(2)}) copy-start(f32[1024,128]{1,0:T(8,128)} %pad_maximum_fusion.2.cos_ref) | copy-start | bytes 1572868
  87.0 41.6 %copy-start.40 = (f32[1024,384]{1,0:T(8,128)}, f32[1024,384]{1,0:T(8,128)S(1)}, u32[]{:S(2)}) copy-start(f32[1024,384]{1,0:T(8,128)S(1)} %get-tuple-element.150.raw_ref) | copy-start | bytes 4718596
  87.0 41.8 %copy-start.52 = (bf16[1024,256]{1,0:T(8,128)(2,1)}, bf16[1024,256]{1,0:T(8,128)(2,1)S(1)}, u32[]{:S(2)}) copy-start(bf16[1024,256]{1,0:T(8,128)(2,1)S(1)} %get-tuple-element.104) | copy-start | bytes 1572868
  184.8 51.6 %copy-start.29 = (f32[2,64,2048]{2,1,0:T(8,128)}, f32[2,64,2048]{2,1,0:T(8,128)S(1)}, u32[]{:S(2)}) copy-start(f32[2,64,2048]{2,1,0:T(8,128)S(1)} %get-tuple-element.130.refs_2_.refs_1_) | copy-start | bytes 3145732
  254.3 56.0 %collective-permute-start.4 = (bf16[1024,768]{1,0:T(8,128)(2,1)}, bf16[1024,768]{1,0:T(8,128)(2,1)}, u32[]{:S(2)}, u32[]{:S(2)}) collective-permute-start(bf16[1024,768]{1,0:T(8,128)(2,1)} %get-tuple-element.127), channel_id=1, source_target_pairs={{0,4},{4,0},{8,12},{12,8},{16,20},{20,16},{24,28},{28,24},{1,5},{5... | collective-permute-start | bytes 4718600 | tf_op jit(solution)/shard_map/ppermute | solution.py:42
  261.6 10.6 %copy-start.21 = (bf16[1024,768]{1,0:T(8,128)(2,1)S(1)}, bf16[1024,768]{1,0:T(8,128)(2,1)}, u32[]{:S(2)}) copy-start(bf16[1024,768]{1,0:T(8,128)(2,1)} %get-tuple-element.128.refs_0_.refs_5_) | copy-start | bytes 4718596
  261.6 10.6 %copy-start.28 = (bf16[128,2048]{1,0:T(8,128)(2,1)S(1)}, bf16[128,2048]{1,0:T(8,128)(2,1)}, u32[]{:S(2)}) copy-start(bf16[128,2048]{1,0:T(8,128)(2,1)} %copy-done.27) | copy-start | bytes 1572868
  261.6 10.7 %copy-start.30 = (f32[2,64,2048]{2,1,0:T(8,128)S(1)}, f32[2,64,2048]{2,1,0:T(8,128)}, u32[]{:S(2)}) copy-start(f32[2,64,2048]{2,1,0:T(8,128)} %copy-done.29) | copy-start | bytes 3145732
  272.3 38.0 %copy-start.37 = (f32[1024,768]{1,0:T(8,128)S(1)}, f32[1024,768]{1,0:T(8,128)}, u32[]{:S(2)}) copy-start(f32[1024,768]{1,0:T(8,128)} %copy-done.36) | copy-start | bytes 9437188
  313.8 41.1 %copy-start.56 = (f32[1024,768]{1,0:T(8,128)S(1)}, f32[1024,768]{1,0:T(8,128)}, u32[]{:S(2)}) copy-start(f32[1024,768]{1,0:T(8,128)} %get-tuple-element.144) | copy-start | bytes 9437188
  358.2 10.8 %copy-start.35 = (bf16[2,4,128,256]{3,2,1,0:T(8,128)(2,1)S(1)}, bf16[2,4,128,256]{3,2,1,0:T(8,128)(2,1)}, u32[]{:S(2)}) copy-start(bf16[2,4,128,256]{3,2,1,0:T(8,128)(2,1)} %copy-done.34) | copy-start | bytes 1572868
  414.6 14.0 %collective-permute-start.5 = (bf16[64,2048]{1,0:T(8,128)(2,1)S(1)}, bf16[64,2048]{1,0:T(8,128)(2,1)S(1)}, u32[]{:S(2)}, u32[]{:S(2)}) collective-permute-start(bf16[64,2048]{1,0:T(8,128)(2,1)S(1)} %get-tuple-element.189), channel_id=1, source_target_pairs={{0,16},{4,20},{8,24},{12,28},{16,0},{20,4},{24,8},{28,12},{1,17},{... | collective-permute-start | bytes 786440 | tf_op jit(solution)/shard_map/ppermute | solution.py:42
  428.6 45.3 %copy-start.43 = (f32[1024,256]{1,0:T(8,128)S(1)}, f32[1024,256]{1,0:T(8,128)}, u32[]{:S(2)}) copy-start(f32[1024,256]{1,0:T(8,128)} %copy-done.42) | copy-start | bytes 3145732
  (47 other events, 170.6 us)

commit v5 on v4

--- a/solution.py
+++ b/solution.py
@@ -908,6 +908,387 @@
     )
 
 
+class Moving:
+    def __init__(self, copy, away):
+        self.copy, self.away, self.here, self.gone = copy, away, False, not away
+
+    def arrive(self):
+        if not self.here:
+            self.here = True
+            (self.copy.wait_recv if self.away else self.copy.wait)()
+
+    def sent(self):
+        if not self.gone:
+            self.gone = True
+            self.copy.wait_send()
+
+
+class Links:
+    def __init__(self, send, recv, batch_mask):
+        self.send, self.recv, self.all = send, recv, []
+        blk, head = lax.axis_index("blk"), lax.axis_index("head")
+        self.core, self.near, self.across = (blk, head ^ 1), (blk, head ^ 2), (blk ^ (1 << TENSOR_BIT), head)
+        self.seq, self.batch = (blk ^ (1 << SEQ_BIT), head), (blk ^ batch_mask, head)
+        self.both = (blk ^ (batch_mask | (1 << TENSOR_BIT)), head)
+        self.place = bit_of(blk, TENSOR_BIT)
+        self.blk = blk
+
+    def greet(self):
+        barrier = pltpu.get_barrier_semaphore()
+        partners = (self.core, self.near, self.across, self.seq, self.batch, self.both)
+        for target in partners:
+            pl.semaphore_signal(barrier, inc=1, device_id=target, device_id_type=pl.DeviceIdType.MESH)
+        pl.semaphore_wait(barrier, len(partners))
+
+    def to(self, target, src, dst):
+        i = len(self.all)
+        self.all.append(Moving(remote(src, dst, self.send.at[i], self.recv.at[i], target), True))
+        return self.all[-1]
+
+    def load(self, src, dst):
+        copy = pltpu.make_async_copy(src, dst, self.recv.at[len(self.all)])
+        copy.start()
+        self.all.append(Moving(copy, False))
+        return self.all[-1]
+
+    def finish(self):
+        for moving in self.all:
+            moving.arrive()
+            moving.sent()
+
+    def half(self, ref, other):
+        n = ref.shape[1] // 2
+        place = 1 - self.place if other else self.place
+        return ref.at[:, pl.ds(pl.multiple_of(place * n, n), n)]
+
+
+def nothing(stage):
+    pass
+
+
+def spread_in(links, s_ref, o_ref, chunk, between=nothing, in_vmem=True):
+    pieces = s_ref.shape[-1] // chunk
+    across = [
+        links.to(
+            links.across,
+            s_ref.at[:, :, pl.ds(i * chunk, chunk)],
+            o_ref.at[0, :, 1, 0, :, pl.ds((i ^ 1) * chunk, chunk)],
+        )
+        for i in range(pieces)
+    ]
+    near = links.to(links.near, s_ref, o_ref.at[0, :, 0, 1])
+    core = [links.to(links.core, s_ref, o_ref.at[1, :, 0, 0])]
+    if in_vmem:
+        o_ref[0, :, 0, 0] = s_ref[...]
+    else:
+        links.load(s_ref, o_ref.at[0, :, 0, 0])
+    between(0)
+    for copy in across:
+        copy.arrive()
+    onward = links.to(links.near, o_ref.at[0, :, 1, 0], o_ref.at[0, :, 1, 1])
+    core.append(links.to(links.core, o_ref.at[0, :, 1, 0], o_ref.at[1, :, 1, 0]))
+    near.arrive()
+    core.append(links.to(links.core, o_ref.at[0, :, 0, 1], o_ref.at[1, :, 0, 1]))
+    between(1)
+    onward.arrive()
+    core.append(links.to(links.core, o_ref.at[0, :, 1, 1], o_ref.at[1, :, 1, 1]))
+    between(2)
+    for copy in core:
+        copy.arrive()
+    for copy in (*across, near, core[0]):
+        copy.sent()
+
+
+def sum_in(links, bufs, chunk, partial, between=nothing):
+    p_ref, core_in, out_y, in_y, out_t, in_t, hold = bufs
+    order = ((1, 1), (0, 1), (1, 0), (0, 0))
+    partial(1)
+    core = [links.to(links.core, p_ref.at[1, :, t, y], core_in.at[i]) for i, (t, y) in enumerate(order)]
+    partial(0)
+    near = []
+    for i in range(2):
+        t, y = order[i]
+        core[i].arrive()
+        out_y[i] = (p_ref[0, :, t, y].astype(F32) + core_in[i].astype(F32)).astype(BF16)
+        near.append(links.to(links.near, out_y.at[i], in_y.at[i]))
+    between(0)
+    core[2].arrive()
+    hold[...] = p_ref[0, :, 1, 0].astype(F32) + core_in[2].astype(F32)
+    near[0].arrive()
+    for i in range(p_ref.shape[-1] // chunk):
+        a, b = slice(i * chunk, (i + 1) * chunk), slice((i ^ 1) * chunk, ((i ^ 1) + 1) * chunk)
+        out_t[:, :, b] = (hold[:, :, a] + in_y[0, :, :, a].astype(F32)).astype(BF16)
+    across = links.to(links.across, out_t, in_t)
+    between(1)
+    core[3].arrive()
+    hold[...] = p_ref[0, :, 0, 0].astype(F32) + core_in[3].astype(F32)
+    near[1].arrive()
+    hold[...] += in_y[1].astype(F32)
+    between(2)
+    across.arrive()
+    hold[...] += in_t[...].astype(F32)
+    for copy in (*core, *near, across):
+        copy.sent()
+
+
+def loop(count, step):
+    def one(i, carry):
+        step(i)
+        return carry
+
+    lax.fori_loop(0, count, one, 0)
+
+
+def rows_of(ref, i):
+    value = ref[i // 2, i % 2]
+    return value.reshape(-1, value.shape[-1])
+
+
+def away_rows(a_cols, b_ref, away_ref):
+    depth, tile = away_ref.shape[0], 512
+
+    def step(i):
+        product = tn(a_cols(pl.multiple_of(depth + i * tile, tile), tile), b_ref[...])
+        away_ref[pl.ds(pl.multiple_of(i * tile, tile), tile), :] = product.astype(BF16)
+
+    loop(depth // tile, step)
+
+
+def keep_rows(a_cols, b_ref, fold_ref, own_ref, send_ref):
+    f = own_ref.shape[0]
+    own_ref[...] = tn(a_cols(0, f), b_ref[...]) + fold_ref[:f, :].astype(F32)
+
+    def step(i):
+        at = pl.multiple_of(i * f, f)
+        product = tn(a_cols(pl.multiple_of(at + f, f), f), b_ref[...])
+        send_ref[pl.ds(at, f), :] = (product + fold_ref[pl.ds(pl.multiple_of(at + f, f), f), :].astype(F32)).astype(BF16)
+
+    loop(3, step)
+
+
+def middle_kernel(
+    low_ref, cot_ref, gain_ref, attn_ref, wo_ref, c_ref, wd_ref, wg_ref, gate_ref, up_ref,
+    middle_ref, dmid_ref, gain_grad_ref, dall_ref, mixed_ref, own_d_ref, got_d_ref, own_g_ref, send_g_ref, keep_u_ref, away_u_ref,
+    attn, wo, p, core_in, out_y, in_y, out_t, in_t, hold, xm_s, xm, c, wd, wg, wu, dact, gate, act, dg, du,
+    away_d, fold_d, away_g, fold_g, own_d, send_d, own_g, send_g, up_tile, send, recv, *, batch_mask, chunk,
+):
+    links = Links(send, recv, batch_mask)
+    f, ff = own_d.shape[0], act.shape[1]
+    to, load = links.to, links.load
+    loads = [load(attn_ref, attn), load(wo_ref, wo)]
+    links.greet()
+
+    def rows(ref, q):
+        return ref.at[pl.ds(q * f, f), :]
+
+    down = [to(links.seq, rows(wd_ref, q), rows(wd, q + 4)) for q in (1, 3)]
+    gate_z = [to(links.batch, links.half(gate_ref, 0), rows(wg, 1)), to(links.both, links.half(gate_ref, 1), rows(wg, 3))]
+    gates = [to(links.seq, rows(wg_ref, 2), rows(wg, 6))]
+    up_t = to(links.across, links.half(up_ref, 1), rows(wu, 2))
+    ups = []
+    for copy in loads:
+        copy.arrive()
+    down += [load(rows(wd_ref, q), rows(wd, q)) for q in (0, 1, 2, 3, 4, 6)]
+    gates += [load(rows(wg_ref, q), rows(wg, q)) for q in (0, 2, 4)]
+    c_load = load(c_ref, c)
+    up_own = load(links.half(up_ref, 0), rows(wu, 0))
+    bufs = (p, core_in, out_y, in_y, out_t, in_t, hold)
+
+    def out_partial(k):
+        for m in range(2):
+            at = (k * 2 + m) * attn.shape[0] // 4
+            p[k, m] = nt(attn[at : at + attn.shape[0] // 4], wo[...]).astype(BF16).reshape(p.shape[2:])
+
+    def while_out(stage):
+        if stage == 0:
+            ups.append(to(links.seq, links.half(up_ref, 0), rows(wu, 4)))
+        if stage == 1:
+            up_t.arrive()
+            ups.append(to(links.seq, rows(wu, 2), rows(wu, 6)))
+
+    sum_in(links, bufs, chunk, out_partial, while_out)
+    for m in range(2):
+        middle = low_ref[m].astype(F32) + hold[m]
+        middle_ref[m] = middle
+        xm_s[m] = (middle * inverse_rms(middle) * gain_ref[...]).astype(BF16)
+
+    up_z = []
+
+    def while_xm(stage):
+        if stage == 0:
+            for copy in gate_z:
+                copy.arrive()
+            up_z.append(to(links.batch, links.half(up_ref, 0), rows(wu, 1)))
+            gates.extend(to(links.seq, rows(wg, q), rows(wg, q + 4)) for q in (1, 3))
+            for copy in (*down, c_load):
+                copy.arrive()
+
+            def step(i):
+                at = pl.ds(pl.multiple_of(i * 512, 512), 512)
+                dact[at, :] = nn(c[at, :], wd[...])
+
+            loop(c.shape[0] // 512, step)
+        if stage == 2:
+            up_z[0].arrive()
+            up_z.append(to(links.both, links.half(up_ref, 1), rows(wu, 3)))
+            ups.append(to(links.seq, rows(wu, 1), rows(wu, 5)))
+
+    spread_in(links, xm_s, xm, chunk, while_xm)
+    for copy in gates:
+        copy.arrive()
+
+    def gate_step(i):
+        at = pl.ds(pl.multiple_of(i * 256, 256), 256)
+        gate[at, :] = nn(rows_of(xm, i), wg[...])
+
+    loop(4, gate_step)
+    up_z[1].arrive()
+    ups.append(to(links.seq, rows(wu, 3), rows(wu, 7)))
+    up_own.arrive()
+    for copy in ups:
+        copy.arrive()
+
+    def up_step(i):
+        base = pl.multiple_of(i * 256, 256)
+        up_tile[...] = nn(rows_of(xm, i), wu[...])
+
+        def part(j):
+            at, here = pl.ds(pl.multiple_of(base + j * 32, 32), 32), pl.ds(pl.multiple_of(j * 32, 32), 32)
+            g, u, d = gate[at, :], up_tile[here, :], dact[at, :]
+            sig = 1.0 / (1.0 + jnp.exp(-g))
+            silu = g * sig
+            act[at, :] = (silu * u).astype(BF16)
+            dg[at, :] = (d * u * sig * (1.0 + g * (1.0 - sig))).astype(BF16)
+            du[at, :] = (d * silu).astype(BF16)
+
+        loop(8, part)
+
+    loop(4, up_step)
+
+    def c_cols(at, n):
+        return c[:, pl.ds(at, n)]
+
+    def xm_cols(at, n):
+        return xm[:, :, :, :, :, pl.ds(at, n)].reshape(-1, n)
+
+    away_rows(c_cols, act, away_d)
+    fold = to(links.seq, away_d, fold_d)
+
+    def back_partial(k):
+        def step(m):
+            at = pl.ds(pl.multiple_of((k * 2 + m) * 256, 256), 256)
+            value = nt(dg[at, :], wg[...]) + nt(du[at, :], wu[...])
+            p[k, m] = value.astype(BF16).reshape(p.shape[2:])
+
+        loop(2, step)
+
+    later = []
+
+    def while_back(stage):
+        if stage == 0:
+            away_rows(xm_cols, dg, away_g)
+            later.append(to(links.seq, away_g, fold_g))
+        if stage == 1:
+            def step(i):
+                at = pl.ds(pl.multiple_of(i * 512, 512), 512)
+                dact[at, :] = tn(xm_cols(pl.multiple_of(i * 512, 512), 512), du[...])
+
+            loop(2, step)
+            later.append(load(dact, keep_u_ref))
+
+    sum_in(links, bufs, chunk, back_partial, while_back)
+    for m in range(2):
+        middle = middle_ref[m]
+        grad = cot_ref[m].astype(F32) + norm_grad(hold[m], middle, gain_ref[...], gain_grad_ref, m)
+        dmid_ref[m] = grad
+        xm_s[m] = grad.astype(BF16)
+
+    settles = []
+
+    def while_mid(stage):
+        if stage == 0:
+            fold.arrive()
+            fold.sent()
+            keep_rows(c_cols, act, fold_d, own_d, send_d)
+            for q, target in ((0, links.batch), (2, links.both), (1, links.across)):
+                settles.append(to(target, rows(send_d, q), rows(got_d_ref, q)))
+            settles.append(load(own_d, own_d_ref))
+            away_rows(xm_cols, du, away_d)
+            settles.append(load(away_d, away_u_ref))
+        if stage == 1:
+
+            def step(i):
+                at = pl.ds(pl.multiple_of(i * 256, 256), 256)
+                p[i // 2, i % 2] = nt(act[at, :], wd[...]).astype(BF16).reshape(p.shape[2:])
+
+            loop(4, step)
+            settles.append(load(p, mixed_ref))
+
+    spread_in(links, xm_s, dall_ref, chunk, while_mid, in_vmem=False)
+    later[0].arrive()
+    keep_rows(xm_cols, dg, fold_g, own_g, send_g)
+    load(own_g, own_g_ref)
+    load(send_g, send_g_ref)
+    links.finish()
+
+
+def middle_call(batch_mask, low, cot, gain, attn, w_out, cot_all, w_down, w_gate, gate_weight, up_weight, collective_id):
+    _, rows, width = low.shape
+    tokens, columns = attn.shape
+    ff = w_down.shape[1]
+    f = w_down.shape[0] // 8
+    share, full = (2, rows, width), (2, 2, 2, 2, rows, width)
+    vmem, hbm = pl.BlockSpec(memory_space=pltpu.VMEM), pl.BlockSpec(memory_space=pltpu.HBM)
+    like = jax.ShapeDtypeStruct
+    return pl.pallas_call(
+        functools.partial(middle_kernel, batch_mask=batch_mask, chunk=2 * width // 8),
+        in_specs=[vmem] * 3 + [hbm] * 7,
+        out_specs=[vmem] * 3 + [hbm] * 8,
+        out_shape=[
+            like(share, F32),
+            like(share, F32),
+            like((1, width), F32),
+            like(full, BF16),
+            like(full, BF16),
+            like((f, ff), F32),
+            like((3 * f, ff), BF16),
+            like((f, ff), F32),
+            like((3 * f, ff), BF16),
+            like((4 * f, ff), F32),
+            like((4 * f, ff), BF16),
+        ],
+        scratch_shapes=[
+            pltpu.VMEM((tokens, columns), BF16),
+            pltpu.VMEM((width, columns), BF16),
+            pltpu.VMEM(full, BF16),
+            pltpu.VMEM((4, *share), BF16),
+            pltpu.VMEM((2, *share), BF16),
+            pltpu.VMEM((2, *share), BF16),
+            pltpu.VMEM(share, BF16),
+            pltpu.VMEM(share, BF16),
+            pltpu.VMEM(share, F32),
+            pltpu.VMEM(share, BF16),
+            pltpu.VMEM(full, BF16),
+            pltpu.VMEM((tokens, width), BF16),
+            *[pltpu.VMEM((width, ff), BF16)] * 3,
+            *[pltpu.VMEM((tokens, ff), F32)] * 2,
+            *[pltpu.VMEM((tokens, ff), BF16)] * 3,
+            *[pltpu.VMEM((4 * f, ff), BF16)] * 4,
+            pltpu.VMEM((f, ff), F32),
+            pltpu.VMEM((3 * f, ff), BF16),
+            pltpu.VMEM((f, ff), F32),
+            pltpu.VMEM((3 * f, ff), BF16),
+            pltpu.VMEM((256, ff), F32),
+            pltpu.SemaphoreType.DMA((96,)),
+            pltpu.SemaphoreType.DMA((96,)),
+        ],
+        compiler_params=pltpu.CompilerParams(
+            collective_id=collective_id, has_side_effects=True, vmem_limit_bytes=60 * MIB
+        ),
+        cost_estimate=TINY_COST,
+    )(low, cot, gain, attn, w_out, cot_all, w_down, w_gate, gate_weight, up_weight)
+
+
 def local(
     hidden_in,
     lengths,
@@ -1206,88 +1587,99 @@
     attn, attn_t, total_e = attend(meta, query, keys, values, start_lanes, scaling)
     attn = attn.reshape(tokens, q_columns)
 
-    plan = Plan()
-    w_down = plan.through(w_down)
-    send_on(plan, w_down, (1, 3), 0)
-    w_gate = plan.through(w_gate)
-    send_over(plan, gate_weight, w_gate, 1, 0)
-    send_over(plan, gate_weight, w_gate, 3, 0)
-    send_on(plan, w_gate, (2,), 0)
-    w_up = fresh_for(plan, (up_weight,))
-    send_over(plan, up_weight, w_up, 2, 0)
-    keep_own(plan, up_weight, w_up, 1)
     x_low = x_low.reshape(share)
-    (middle, xm), (w_down, w_gate, w_up) = gather_sum(
-        nt(attn, w_out).astype(BF16),
-        plan,
-        [x_low, gain_m[None]],
-        [like(share, F32), like(share, BF16)],
-        finish_middle,
-    )
-    w_down = whole_weight(w_down)
-
-    plan = Plan()
-    w_gate = plan.through(w_gate)
-    w_up = plan.through(w_up)
-    by_b = len(plan.jobs)
-    send_over(plan, up_weight, w_up, 1, 0)
-    send_on(plan, w_gate, (1, 3), 0)
-    send_on(plan, w_up, (2,), 1)
-    by_tb = plan.copy(
-        (plan.read(up_weight), half_cut(ff, True)), (w_up, rows_at(3)), b_mask | t_mask, after=by_b, point=2
-    )
-    send_on(plan, w_up, (1,), 2)
-    send_on(plan, w_up, (3,), 3, after=by_tb)
-    xm, (w_gate, w_up, d_active) = spread(
-        xm.reshape(2 * local_rows, width), plan, [fill_product(cot_all, w_down, 0)]
-    )
-    w_gate, w_up = whole_weight(w_gate), whole_weight(w_up)
-    gate = nn(xm, w_gate)
-    up = nn(xm, w_up)
-    sig = jax.nn.sigmoid(gate)
-    silu = gate * sig
-    active = (silu * up).astype(BF16)
-    d_gate = (d_active * up * sig * (1.0 + gate * (1.0 - sig))).astype(BF16)
-    d_up = (d_active * silu).astype(BF16)
-
-    keep_down, away_down = weight_sum(cot_all, active)
-    got_x = over_blk(away_down, x_mask)
-    (d_gate, d_up, away_down) = pin((d_gate, d_up, away_down))
-    ff_cut = ff // 2
-    plan, fills = Plan(), []
     if extra_bits:
-        keep_gate, away_gate = weight_sum(xm, d_gate)
-        keep_up, away_up = weight_sum(xm, d_up)
-        source, point = plan.read(away_gate), 0
+        plan = Plan()
+        w_down = plan.through(w_down)
+        send_on(plan, w_down, (1, 3), 0)
+        w_gate = plan.through(w_gate)
+        send_over(plan, gate_weight, w_gate, 1, 0)
+        send_over(plan, gate_weight, w_gate, 3, 0)
+        send_on(plan, w_gate, (2,), 0)
+        w_up = fresh_for(plan, (up_weight,))
+        send_over(plan, up_weight, w_up, 2, 0)
+        keep_own(plan, up_weight, w_up, 1)
+        (middle, xm), (w_down, w_gate, w_up) = gather_sum(
+            nt(attn, w_out).astype(BF16),
+            plan,
+            [x_low, gain_m[None]],
+            [like(share, F32), like(share, BF16)],
+            finish_middle,
+        )
+        w_down = whole_weight(w_down)
+
+        plan = Plan()
+        w_gate = plan.through(w_gate)
+        w_up = plan.through(w_up)
+        by_b = len(plan.jobs)
+        send_over(plan, up_weight, w_up, 1, 0)
+        send_on(plan, w_gate, (1, 3), 0)
+        send_on(plan, w_up, (2,), 1)
+        by_tb = plan.copy(
+            (plan.read(up_weight), half_cut(ff, True)), (w_up, rows_at(3)), b_mask | t_mask, after=by_b, point=2
+        )
+        send_on(plan, w_up, (1,), 2)
+        send_on(plan, w_up, (3,), 3, after=by_tb)
+        xm, (w_gate, w_up, d_active) = spread(
+            xm.reshape(2 * local_rows, width), plan, [fill_product(cot_all, w_down, 0)]
+        )
+        w_gate, w_up = whole_weight(w_gate), whole_weight(w_up)
+        gate = nn(xm, w_gate)
+        up = nn(xm, w_up)
+        sig = jax.nn.sigmoid(gate)
+        silu = gate * sig
+        active = (silu * up).astype(BF16)
+        d_gate = (d_active * up * sig * (1.0 + gate * (1.0 - sig))).astype(BF16)
+        d_up = (d_active * silu).astype(BF16)
+
+        keep_down, away_down = weight_sum(cot_all, active)
+        got_x = over_blk(away_down, x_mask)
+        (d_gate, d_up, away_down) = pin((d_gate, d_up, away_down))
+        ff_cut = ff // 2
+        plan, fills = Plan(), []
+        if extra_bits:
+            keep_gate, away_gate = weight_sum(xm, d_gate)
+            keep_up, away_up = weight_sum(xm, d_up)
+            source, point = plan.read(away_gate), 0
+        else:
+            fills = [fill_weight_grad(xm, d_gate, 0), fill_weight_grad(xm, d_up, 1)]
+            source, point = ("fill", (0, 1)), 1
+        gate_x = plan.fresh((4 * row_features, ff), BF16)
+        fold_part(plan, source, gate_x, 0, ff_cut, point)
+        (d_middle, d_mid, gain_m_grad), (gate_x, *filled) = gather_sum(
+            back_through((d_gate, d_up), (w_gate, w_up)),
+            plan,
+            [cot.reshape(share), middle, gain_m[None]],
+            [like(share, F32), like(share, BF16), like((1, width), F32)],
+            finish_mlp_norm,
+            fills,
+        )
+        if filled:
+            keep_gate, away_gate, keep_up, away_up = filled
+        (d_mid, got_x) = pin((d_mid, got_x))
+        own_down, away_down = to_settle(keep_down, got_x)
+
+        plan = Plan()
+        settle(plan, away_down, 1)
+        gate_x = plan.through(gate_x)
+        fold_part(plan, plan.read(away_gate), gate_x, ff_cut, ff - ff_cut)
+        up_x = plan.fresh(away_up.shape, BF16)
+        fold_part(plan, plan.read(away_up), up_x, 0, ff_cut)
+        d_mid_all, (got_down, gate_x, up_x, mixed_partial) = spread(
+            d_mid.reshape(2 * local_rows, width), plan, [fill_back(active, w_down, 0)]
+        )
+        (g_down,) = settled([(own_down, got_down)], (ff,))
+        own_gate, away_gate = to_settle(keep_gate, gate_x)
     else:
-        fills = [fill_weight_grad(xm, d_gate, 0), fill_weight_grad(xm, d_up, 1)]
-        source, point = ("fill", (0, 1)), 1
-    gate_x = plan.fresh((4 * row_features, ff), BF16)
-    fold_part(plan, source, gate_x, 0, ff_cut, point)
-    (d_middle, d_mid, gain_m_grad), (gate_x, *filled) = gather_sum(
-        back_through((d_gate, d_up), (w_gate, w_up)),
-        plan,
-        [cot.reshape(share), middle, gain_m[None]],
-        [like(share, F32), like(share, BF16), like((1, width), F32)],
-        finish_mlp_norm,
-        fills,
-    )
-    if filled:
-        keep_gate, away_gate, keep_up, away_up = filled
-    (d_mid, got_x) = pin((d_mid, got_x))
-    own_down, away_down = to_settle(keep_down, got_x)
-
-    plan = Plan()
-    settle(plan, away_down, 1)
-    gate_x = plan.through(gate_x)
-    fold_part(plan, plan.read(away_gate), gate_x, ff_cut, ff - ff_cut)
-    up_x = plan.fresh(away_up.shape, BF16)
-    fold_part(plan, plan.read(away_up), up_x, 0, ff_cut)
-    d_mid_all, (got_down, gate_x, up_x, mixed_partial) = spread(
-        d_mid.reshape(2 * local_rows, width), plan, [fill_back(active, w_down, 0)]
-    )
-    (g_down,) = settled([(own_down, got_down)], (ff,))
-    own_gate, away_gate = to_settle(keep_gate, gate_x)
+        (
+            middle, d_middle, gain_m_grad, d_mid_all, mixed_partial, own_down, got_down, own_gate, away_gate, keep_up, away_up,
+        ) = middle_call(
+            b_mask, x_low, cot.reshape(share), gain_m[None], attn, w_out, cot_all, w_down, w_gate, gate_weight, up_weight, next(ids)
+        )
+        d_mid_all = d_mid_all.reshape(tokens, width)
+        mixed_partial = mixed_partial.reshape(tokens, width)
+        (g_down,) = settled([(own_down, got_down)], (ff,))
+        up_x = None
     d_attn = nn(d_mid_all, w_out).astype(BF16).reshape(2, 4, half, q_columns)
     d_query, d_key, d_value = attend_back(
         meta, query, d_attn, keys, values, start_lanes, attn_t, total_e, scaling
@@ -1303,8 +1695,11 @@
     away_kv = jnp.concatenate([d_key[1], d_value[1]], axis=1).astype(BF16)
     fold(plan, plan.read(away_kv), away_kv.shape)
     settle(plan, away_gate)
-    up_x = plan.through(up_x)
-    fold_part(plan, plan.read(away_up), up_x, ff_cut, ff - ff_cut)
+    if up_x is None:
+        fold(plan, plan.read(away_up), away_up.shape)
+    else:
+        up_x = plan.through(up_x)
+        fold_part(plan, plan.read(away_up), up_x, ff_cut, ff - ff_cut)
     (mixed,), (got_kv, got_gate, up_x, *filled) = gather_sum(
         mixed_partial,
         plan,

time: 532 us -> 504 us (0.947)
  matrix products: 11.7 us -> 3.55 us
  Pallas kernels: 453 us -> 447 us
  local copies, waits for them, and re-layouts: 29 us -> 23.6 us
    pallas_call x9 -> x5, Pallas kernels: 402 us -> 236 us  [run(): pl.pallas_call(kernel, out_shape=[*out_shapes, *plan.shapes, *f_out], in_...]
    pallas_call x2 -> x1, Pallas kernels: 15.2 us -> 175 us  [middle_call(): pl.pallas_call(functools.partial(middle_kernel, batch_mask=batch_mask, ch...]
    dot_general x3 -> x1, matrix products: 10.4 us -> 3.55 us  [nn(): return jnp.dot(a, b, preferred_element_type=F32)]
    unnamed x147 -> x127, local copies, waits for them, and re-layouts: 23.6 us -> 17.8 us
    ppermute x6 -> x5, waiting for transfers between devices: 13.8 us -> 11.6 us  [over_blk(): return lax.ppermute(value, 'blk', [(i, i ^ mask) for i in range(count)])]
  transfers between devices with their start and end apart: 6 -> 5, of which waited for: 2 -> 3; matrix products, arithmetic and copies ran while one was open for 2% -> 2% of each run, Pallas kernels for 11% -> 2%
where the time goes in v5:
time: 504 us; the launch traced here: 503 us
  Pallas kernels  447 us (89%)
  local copies, waits for them, and re-layouts  23.6 us (5%)
  waiting for transfers between devices  11.6 us (2%)
  starting transfers between devices  8.01 us (2%)
  other arithmetic  7.84 us (2%)
    pallas_call x5, Pallas kernels, run(): pl.pallas_call(kernel, out_shape=[*out_shapes, *plan.shapes, *f_out], in_...  236 us
    pallas_call x1, Pallas kernels, middle_call(): pl.pallas_call(functools.partial(middle_kernel, batch_mask=batch_mask, ch...  175 us
    unnamed x127, local copies, waits for them, and re-layouts  17.8 us
    ppermute x5, waiting for transfers between devices, over_blk(): return lax.ppermute(value, 'blk', [(i, i ^ mask) for i in range(count)])  11.6 us
    pallas_call x1, Pallas kernels, attend_back(): pl.pallas_call(functools.partial(attend_back_kernel, factor=scaling * LOG...  10.7 us
  transfers between devices with their start and end apart: 5, of which 3 were waited for; matrix products, arithmetic and copies ran while one was open for 2% of the time, Pallas kernels for 2%

profile of v5, /device:TPU:0, one launch (start us, length us, event | category | flops | bytes accessed | tf_op | source)
XLA Modules:
  0.0 503.2 jit_solution(12522808103013909958)
XLA Ops:
  1.8 4.1 collective-permute-start
  8.1 1.6 collective-permute-start.3
  10.1 1.6 collective-permute-start.1
  12.7 1.9 fusion.1
  17.0 7.3 %collective-permute-done.refs_1_ = bf16[64,2048]{1,0:T(8,128)(2,1)S(1)} collective-permute-done((bf16[64,2048]{1,0:T(8,128)(2,1)S(1)}, bf16[64,2048]{1,0:T(8,128)(2,1)S(1)}, u32[]{:S(2)}, u32[]{:S(2)}) %collective-permute-start) | collective-permute-done | bytes 262176 | tf_op jit(solution)/shard_map/ppermute | solution.py:42
  26.8 2.3 collective-permute-done.2.refs_3_
  30.1 45.9 %shard_map.238 = (bf16[2,2,2,2,64,2048]{5,4,3,2,1,0:T(8,128)(2,1)}, bf16[2048,512]{1,0:T(8,128)(2,1)}, bf16[2,64,2048]{2,1,0:T(8,128)(2,1)}, bf16[2048,256]{1,0:...) custom-call(bf16[2,64,2048]{2,1,0:T(8,128)(2,1)} %bitcast.101, bf16[256,512]{1,0:T(8,128)(2,1)} %copy-done.45, ...), custom_call_target="tpu_custom_call" | custom-call | tf_op jit(solution)/shard_map/pallas_call | solution.py:680
  77.1 2.4 copy-done.2
  79.6 1.6 copy-done.9
  81.2 3.7 shard_map.240
  84.9 1.4 copy-done.20
  86.3 39.6 %shard_map.241 = (bf16[2,2,2,2,64,2048]{5,4,3,2,1,0:T(8,128)(2,1)S(1)}, bf16[1024,256]{1,0:T(8,128)(2,1)S(1)}, bf16[2048,256]{1,0:T(8,128)(2,1)S(1)}, bf16[2048,768]{1,0:T(8,128)(2,1)S(1)}, bf16[2048,768]{1,0:T(8,128)(2,1)S(1)}) custom-call(bf16[2,64,2048]{2,1,0:T(8,128)(2,1)S(1)} %bitcast.80, ...), custom_call_target="tpu_custom_call", output_to_operand_aliasing={{2}: (2, {}), {3}: (3, {}), {4}: (6, {})} | custom-call | tf_op jit(solution)/shard_map/pallas_call | solution.py:680
  125.9 1.9 copy-done.19
  129.0 8.8 %shard_map.242 = (bf16[2,4,128,256]{3,2,1,0:T(8,128)(2,1)S(1)}, f32[4,128,512]{2,1,0:T(8,128)S(1)}, f32[4,1,512]{2,1,0:T(1,128)S(1)}) custom-call(s32[45]{0:T(128)S(1)} %concatenate.52.meta_ref, bf16[2,4,128,256]{3,2,1,0:T(8,128)(2,1)S(1)} %bitcast.103, bf16[2,2,4,128,128]{4,3,2,1,0:T(8,128)(2,1)S(1)} %bitcast.98, bf16[2,2,4,128,128]{4,3,2,1,0:T(8,128)(2,1)S(1)} %bitcast.96, ...), custom_call_target="tpu_custom_call" | custom-call | flops 2147483648 | bytes 4194304 | tf_op jit(solution)/shard_map/pallas_call | solution.py:207
  139.5 175.4 %shard_map.243 = (f32[2,64,2048]{2,1,0:T(8,128)}, f32[2,64,2048]{2,1,0:T(8,128)}, f32[1,2048]{1,0:T(1,128)}, bf16[2,2,2,2,64,2048]{5,4,3,2,1,0:T(8,128)(2,1)}, b...) custom-call(bf16[2,64,2048]{2,1,0:T(8,128)(2,1)} %bitcast.86, ...), custom_call_target="tpu_custom_call" | custom-call | tf_op jit(solution)/shard_map/pallas_call | solution.py:1243
  315.0 3.6 convolution_convert_fusion
  318.6 10.7 %shard_map.244 = (f32[2,4,128,256]{3,2,1,0:T(8,128)S(1)}, f32[2,2,4,128,128]{4,3,2,1,0:T(8,128)S(1)}, f32[2,2,4,128,128]{4,3,2,1,0:T(8,128)S(1)}) custom-call(s32[45]{0:T(128)S(1)} %concatenate.52.meta_ref, bf16[2,4,128,256]{3,2,1,0:T(8,128)(2,1)S(1)} %bitcast.104, bf16[2,4,128,256]{3,2,1,0:T(8,128)(2,1)S(1)} %bitcast.105, ...), custom_call_target="tpu_custom_call" | custom-call | flops 5368709120 | bytes 7340032 | tf_op jit(solution)/shard_map/pallas_call | solution.py:240
  330.9 54.4 %shard_map.245 = (bf16[2,64,2048]{2,1,0:T(8,128)(2,1)S(1)}, bf16[1024,256]{1,0:T(8,128)(2,1)S(1)}, bf16[768,768]{1,0:T(8,128)(2,1)S(1)}, bf16[1024,768]{1,0:T(8,...) custom-call(bf16[2,2,2,2,64,2048]{5,4,3,2,1,0:T(8,128)(2,1)S(1)} %copy-done.18, ...), custom_call_target="tpu_custom_call" | custom-call | tf_op jit(solution)/shard_map/pallas_call | solution.py:680
  388.8 1.3 shard_map.250
  391.3 7.4 %shard_map.246 = (bf16[1024,512]{1,0:T(8,128)(2,1)S(1)}, bf16[1024,2048]{1,0:T(8,128)(2,1)S(1)}, f32[8,128]{1,0:T(8,128)S(1)}) custom-call(f32[1024,256]{1,0:T(8,128)S(1)} %bitcast.93, f32[2,1024,128]{2,1,0:T(8,128)S(1)} %bitcast.91, f32[2,1024,128]{2,1,0:T(8,128)S(1)} %bitcast.92, bf16[1024,256]{1,0:T(8,128)(2,1)S(1)} %get-tuple-element.113.got_ref, ...), custom_call_target="tpu_custom_call" | custom-call | tf_op jit(solution)/shard_map/pallas_call | solution.py:336
  398.7 1.9 collective-permute-done.4
  400.7 45.0 %shard_map.247 = (f32[64,2048]{1,0:T(8,128)S(1)}, bf16[64,2048]{1,0:T(8,128)(2,1)S(1)}, f32[1,2048]{1,0:T(1,128)S(1)}, bf16[768,768]{1,0:T(8,128)(2,1)S(1)}, bf1...) custom-call(bf16[2,2,2,2,64,2048]{5,4,3,2,1,0:T(8,128)(2,1)S(1)} %bi, ...), custom_call_target="tpu_custom_call" | custom-call | tf_op jit(solution)/shard_map/pallas_call | solution.py:680
  446.6 50.9 %shard_map.248 = (f32[34,128]{1,0:T(8,128)S(1)}, bf16[768,512]{1,0:T(8,128)(2,1)S(1)}, bf16[768,256]{1,0:T(8,128)(2,1)S(1)}, bf16[64,2048]{1,0:T(8,128)(2,1)S(1)}) custom-call(f32[34,128]{1,0:T(8,128)S(1)} %bitcast.102, bf16[768,512]{1,0:T(8,128)(2,1)S(1)} %slice.100.refs_1_, bf16[768,256]{1,0:T(8,128)(2,1)S(1)} %slice.101.refs_2_, ...), custom_call_target="tpu_custom_call" | custom-call | tf_op jit(solution)/shard_map/pallas_call | solution.py:680
  498.7 1.3 shard_map.251
  (186 shorter events, 25.8 us)
Async XLA Ops:
  0.6 11.2 %copy-start = (s32[2,9]{1,0:T(2,128)S(1)}, s32[2,9]{1,0:T(2,128)}, u32[]{:S(2)}) copy-start(s32[2,9]{1,0:T(2,128)} %param.15) | copy-start | bytes 220
  1.8 22.5 %collective-permute-start = (bf16[64,2048]{1,0:T(8,128)(2,1)S(1)}, bf16[64,2048]{1,0:T(8,128)(2,1)S(1)}, u32[]{:S(2)}, u32[]{:S(2)}) collective-permute-start(bf16[64,2048]{1,0:T(8,128)(2,1)S(1)} %get-tuple-element.153), channel_id=1, source_target_pairs={{0,16},{4,20},{8,24},{12,28},{16,0},{20,4},{24,8},{28,12},{1,17},{... | collective-permute-start | bytes 786440 | tf_op jit(solution)/shard_map/ppermute | solution.py:42
  8.1 7.5 %copy-start.52 = (bf16[2048]{0:T(1024)(128)(2,1)S(1)}, bf16[2048]{0:T(1024)(128)(2,1)}, u32[]{:S(2)}) copy-start(bf16[2048]{0:T(1024)(128)(2,1)} %param.26) | copy-start | bytes 12292
  8.1 21.0 %collective-permute-start.3 = (bf16[256,1280]{1,0:T(8,128)(2,1)S(1)}, bf16[256,1280]{1,0:T(8,128)(2,1)S(1)}, u32[]{:S(2)}, u32[]{:S(2)}) collective-permute-start(bf16[256,1280]{1,0:T(8,128)(2,1)S(1)} %pad_maximum_fusion), channel_id=1, source_target_pairs={{0,4},{4,0},{8,12},{12,8},{16,20},{20,16},{24,28},{28,24},{1,5},{5... | collective-permute-start | bytes 1966088 | tf_op jit(solution)/shard_map/ppermute | solution.py:42
  9.7 19.4 %collective-permute-start.2 = (bf16[256,512]{1,0:T(8,128)(2,1)S(1)}, bf16[256,512]{1,0:T(8,128)(2,1)S(1)}, u32[]{:S(2)}, u32[]{:S(2)}) collective-permute-start(bf16[256,512]{1,0:T(8,128)(2,1)S(1)} %pad_maximum_fusion.6.refs_4_), channel_id=1, source_target_pairs={{0,16},{4,20},{8,24},{12,28},{16,0},{20,4},{24,8},{28,12},{1,17},{... | collective-permute-start | bytes 786440 | tf_op jit(solution)/shard_map/ppermute | solution.py:42
  10.1 18.9 %collective-permute-start.1 = (bf16[256,512]{1,0:T(8,128)(2,1)S(1)}, bf16[256,512]{1,0:T(8,128)(2,1)S(1)}, u32[]{:S(2)}, u32[]{:S(2)}) collective-permute-start(bf16[256,512]{1,0:T(8,128)(2,1)S(1)} %pad_maximum_fusion.5.refs_1_), channel_id=1, source_target_pairs={{0,8},{4,12},{8,0},{12,4},{16,24},{20,28},{24,16},{28,20},{1,9},{5... | collective-permute-start | bytes 786440 | tf_op jit(solution)/shard_map/ppermute | solution.py:42
  30.1 47.0 %copy-start.12 = (f32[1024,128]{1,0:T(8,128)S(1)}, f32[1024,128]{1,0:T(8,128)}, u32[]{:S(2)}) copy-start(f32[1024,128]{1,0:T(8,128)} %pad_maximum_fusion.3.sin_ref) | copy-start | bytes 1572868
  30.1 47.0 %copy-start.14 = (f32[1024,128]{1,0:T(8,128)S(1)}, f32[1024,128]{1,0:T(8,128)}, u32[]{:S(2)}) copy-start(f32[1024,128]{1,0:T(8,128)} %pad_maximum_fusion.2.cos_ref) | copy-start | bytes 1572868
  77.0 7.9 %copy-start.11 = (bf16[256,1536]{1,0:T(8,128)(2,1)S(1)}, bf16[256,1536]{1,0:T(8,128)(2,1)}, u32[]{:S(2)}) copy-start(bf16[256,1536]{1,0:T(8,128)(2,1)} %gate_ref.1) | copy-start | bytes 2359300
  77.1 7.8 %copy-start.16 = (bf16[128,2048]{1,0:T(8,128)(2,1)}, bf16[128,2048]{1,0:T(8,128)(2,1)S(1)}, u32[]{:S(2)}) copy-start(bf16[128,2048]{1,0:T(8,128)(2,1)S(1)} %shard_map.239) | copy-start | bytes 1572868
  84.9 44.1 %copy-start.38 = (bf16[1024,256]{1,0:T(8,128)(2,1)}, bf16[1024,256]{1,0:T(8,128)(2,1)S(1)}, u32[]{:S(2)}) copy-start(bf16[1024,256]{1,0:T(8,128)(2,1)S(1)} %get-tuple-element.90) | copy-start | bytes 1572868
  128.8 9.0 %copy-start.6 = (bf16[2048,768]{1,0:T(8,128)(2,1)}, bf16[2048,768]{1,0:T(8,128)(2,1)S(1)}, u32[]{:S(2)}) copy-start(bf16[2048,768]{1,0:T(8,128)(2,1)S(1)} %get-tuple-element.100.wd_ref) | copy-start | bytes 9437188
  128.8 9.0 %copy-start.8 = (bf16[2048,768]{1,0:T(8,128)(2,1)}, bf16[2048,768]{1,0:T(8,128)(2,1)S(1)}, u32[]{:S(2)}) copy-start(bf16[2048,768]{1,0:T(8,128)(2,1)S(1)} %get-tuple-element.101.wg_ref) | copy-start | bytes 9437188
  139.5 175.4 %copy-start.22 = (bf16[2048,256]{1,0:T(8,128)(2,1)S(1)}, bf16[2048,256]{1,0:T(8,128)(2,1)}, u32[]{:S(2)}) copy-start(bf16[2048,256]{1,0:T(8,128)(2,1)} %copy-done.21) | copy-start | bytes 3145732
  318.5 10.9 %copy-start.17 = (bf16[2,2,2,2,64,2048]{5,4,3,2,1,0:T(8,128)(2,1)S(1)}, bf16[2,2,2,2,64,2048]{5,4,3,2,1,0:T(8,128)(2,1)}, u32[]{:S(2)}) copy-start(bf16[2,2,2,2,64,2048]{5,4,3,2,1,0:T(8,128)(2,1)} %get-tuple-element.104) | copy-start | bytes 12582916
  318.6 10.9 %copy-start.18 = (bf16[2,2,2,2,64,2048]{5,4,3,2,1,0:T(8,128)(2,1)S(1)}, bf16[2,2,2,2,64,2048]{5,4,3,2,1,0:T(8,128)(2,1)}, u32[]{:S(2)}) copy-start(bf16[2,2,2,2,64,2048]{5,4,3,2,1,0:T(8,128)(2,1)} %get-tuple-element.102.refs_0_) | copy-start | bytes 12582916
  318.6 10.9 %copy-start.28 = (bf16[768,768]{1,0:T(8,128)(2,1)S(1)}, bf16[768,768]{1,0:T(8,128)(2,1)}, u32[]{:S(2)}) copy-start(bf16[768,768]{1,0:T(8,128)(2,1)} %get-tuple-element.109.refs_3_) | copy-start | bytes 3538948
  318.6 10.9 %copy-start.30 = (f32[2,64,2048]{2,1,0:T(8,128)S(1)}, f32[2,64,2048]{2,1,0:T(8,128)}, u32[]{:S(2)}) copy-start(f32[2,64,2048]{2,1,0:T(8,128)} %get-tuple-element.103.refs_1_) | copy-start | bytes 3145732
  330.9 54.8 %copy-start.42 = (f32[1024,768]{1,0:T(8,128)S(1)}, f32[1024,768]{1,0:T(8,128)}, u32[]{:S(2)}) copy-start(f32[1024,768]{1,0:T(8,128)} %get-tuple-element.119) | copy-start | bytes 9437188
  385.3 15.3 %collective-permute-start.4 = (bf16[64,2048]{1,0:T(8,128)(2,1)S(1)}, bf16[64,2048]{1,0:T(8,128)(2,1)S(1)}, u32[]{:S(2)}, u32[]{:S(2)}) collective-permute-start(bf16[64,2048]{1,0:T(8,128)(2,1)S(1)} %get-tuple-element.152), channel_id=1, source_target_pairs={{0,16},{4,20},{8,24},{12,28},{16,0},{20,4},{24,8},{28,12},{1,17},{... | collective-permute-start | bytes 786440 | tf_op jit(solution)/shard_map/ppermute | solution.py:42
  391.2 9.4 %copy-start.3 = (bf16[2,2,2,2,64,2048]{5,4,3,2,1,0:T(8,128)(2,1)S(1)}, bf16[2,2,2,2,64,2048]{5,4,3,2,1,0:T(8,128)(2,1)}, u32[]{:S(2)}) copy-start(bf16[2,2,2,2,64,2048]{5,4,3,2,1,0:T(8,128)(2,1)} %get-tuple-element.86) | copy-start | bytes 12582916
  391.2 9.4 %copy-start.24 = (bf16[128,2048]{1,0:T(8,128)(2,1)S(1)}, bf16[128,2048]{1,0:T(8,128)(2,1)}, u32[]{:S(2)}) copy-start(bf16[128,2048]{1,0:T(8,128)(2,1)} %copy-done.23) | copy-start | bytes 1572868
  391.2 9.4 %copy-start.31 = (f32[2,64,2048]{2,1,0:T(8,128)S(1)}, f32[2,64,2048]{2,1,0:T(8,128)}, u32[]{:S(2)}) copy-start(f32[2,64,2048]{2,1,0:T(8,128)} %get-tuple-element.118.refs_2_) | copy-start | bytes 3145732
  391.2 9.4 %copy-start.35 = (bf16[1024,256]{1,0:T(8,128)(2,1)S(1)}, bf16[1024,256]{1,0:T(8,128)(2,1)}, u32[]{:S(2)}) copy-start(bf16[1024,256]{1,0:T(8,128)(2,1)} %copy-done.34) | copy-start | bytes 1572868
  (36 other events, 104.1 us)

commit v6 on v5

--- a/solution.py
+++ b/solution.py
@@ -999,12 +999,15 @@
         copy.sent()
 
 
-def sum_in(links, bufs, chunk, partial, between=nothing):
+def sum_in(links, bufs, chunk, partial, between=nothing, far=None):
     p_ref, core_in, out_y, in_y, out_t, in_t, hold = bufs
     order = ((1, 1), (0, 1), (1, 0), (0, 0))
-    partial(1)
-    core = [links.to(links.core, p_ref.at[1, :, t, y], core_in.at[i]) for i, (t, y) in enumerate(order)]
-    partial(0)
+    if partial:
+        partial(1)
+        far = p_ref.at[1]
+    core = [links.to(links.core, far.at[:, t, y], core_in.at[i]) for i, (t, y) in enumerate(order)]
+    if partial:
+        partial(0)
     near = []
     for i in range(2):
         t, y = order[i]
@@ -1289,6 +1292,317 @@
     )(low, cot, gain, attn, w_out, cot_all, w_down, w_gate, gate_weight, up_weight)
 
 
+def block_of(n, batch_mask):
+    blk = lax.axis_index("blk")
+    return blk ^ ((n // 2) * batch_mask) ^ ((n % 2) << TENSOR_BIT)
+
+
+def key_tokens(block, half):
+    head = lax.axis_index("head")
+    index = lax.broadcasted_iota(jnp.int32, (2 * half, 1), 0)
+    return token_offset(head, index, half // 2) + block * (2 * half)
+
+
+def query_tokens(block, half, lanes):
+    head = lax.axis_index("head")
+    index = lax.broadcasted_iota(jnp.int32, (1, lanes), 1) % (2 * half)
+    return token_offset(head, index, half // 2) + block * (2 * half)
+
+
+def head_rows(ref, i, heads, width):
+    both = [ref[c, i] for c in range(2)]
+    return jnp.concatenate([b[:, h * width : (h + 1) * width] for h in range(heads) for b in both], axis=0)
+
+
+def attention_back(q, do, k, v, start, ot, l, dq, dk, dv, kt, acc, batch_mask, scaling):
+    parts, _, blocks, half, width = k.shape
+    heads = q.shape[-1] // width
+    lanes = heads * 2 * half
+    dk[...] = jnp.zeros_like(dk)
+    dv[...] = jnp.zeros_like(dv)
+
+    def turn(kb):
+        kt[kb] = key_rows(k, kb // blocks, kb % blocks).T
+
+    loop(parts * blocks, turn)
+
+    def per_query(i):
+        q_rows, do_rows = head_rows(q, i, heads, width), head_rows(do, i, heads, width)
+        delta = jnp.sum(do_rows.astype(F32).T * ot[i], axis=0, keepdims=True)
+        inverse, first = 1.0 / l[i], start[i]
+        acc[...] = jnp.zeros_like(acc)
+        q_block = block_of(i, batch_mask)
+
+        def per_key(kb):
+            part, block = kb // blocks, kb % blocks
+            k_block = block_of(block, batch_mask) ^ (part << SEQ_BIT)
+
+            def add(diagonal):
+                tokens = key_tokens(k_block, half)
+                allowed = tokens >= first
+                if diagonal:
+                    allowed = allowed & (tokens <= query_tokens(q_block, half, lanes))
+                score = nt(key_rows(k, part, block), q_rows) * (scaling * LOG2E)
+                prob = jnp.where(allowed, jnp.exp2(score), 0.0) * inverse
+                d_prob = nt(key_rows(v, part, block), do_rows)
+                d_score = (prob * (d_prob - delta)).astype(BF16)
+                d_v, d_k = nn(prob.astype(BF16), do_rows), nn(d_score, q_rows) * scaling
+                for c in range(2):
+                    dv[part, c, block] += d_v[c * half : (c + 1) * half]
+                    dk[part, c, block] += d_k[c * half : (c + 1) * half]
+                acc[...] += nn(kt[kb], d_score)
+
+            @pl.when(k_block < q_block)
+            def _():
+                add(False)
+
+            @pl.when(k_block == q_block)
+            def _():
+                add(True)
+
+        loop(parts * blocks, per_key)
+        rows = acc[...].T * scaling
+        for h in range(heads):
+            for c in range(2):
+                at = (h * 2 + c) * half
+                dq[c, i, :, h * width : (h + 1) * width] = rows[at : at + half]
+
+    loop(blocks, per_query)
+
+
+def last_kernel(
+    low_ref, middle_ref, dmid_ref, gain_ref, gain_m_grad_ref, gain_q_ref, gain_k_ref, start_ref, l_ref,
+    dall_ref, wo_ref, attn_ref, q_ref, k_ref, v_ref, ot_ref, raw_ref, cos_ref, sin_ref, wa_ref, xa_ref, mixed_ref,
+    send_g_ref, keep_u_ref, away_u_ref,
+    mixed_own_ref, mixed_got_ref, input_own_ref, input_got_ref, sums_ref,
+    got_g_ref, own_u_ref, got_u_ref, own_a_ref, got_a_ref, own_o_ref, got_o_ref,
+    dall, wo, attn, q, do, k, v, ot, raw, cos, sin, wa, xa, dq, dk, dv, kt, acc, kv_out, kv_in, d_qkv,
+    p, core_in, out_y, in_y, out_t, in_t, hold, m_near, m_core_in, m_out_y, m_in_y, m_out_t, m_in_t,
+    swap_m, swap_i, keep_u, fold_u, own_u, send_u, away_o, fold_o, own_o, send_o, away_a, fold_a, own_a, send_a,
+    gains_qk, gain_a_grad, ring_out, ring_in, send, recv, *, batch_mask, bit_order, scaling, chunk,
+):
+    links = Links(send, recv, batch_mask)
+    to, load = links.to, links.load
+    f = own_u.shape[0]
+    heads = q.shape[-1] // k.shape[-1]
+    width = k.shape[-1]
+
+    def rows(ref, i):
+        return ref.at[pl.ds(i * f, f), :]
+
+    first = [load(dall_ref, dall), load(wo_ref, wo), load(attn_ref, attn)]
+    second = [load(a, b) for a, b in ((q_ref, q), (k_ref, k), (v_ref, v), (ot_ref, ot))]
+    third = [load(a, b) for a, b in ((raw_ref, raw), (cos_ref, cos), (sin_ref, sin), (wa_ref, wa), (xa_ref, xa))]
+    mixed_near, keep_load = load(mixed_ref.at[0], m_near.at[0]), load(keep_u_ref, keep_u)
+    links.greet()
+
+    def settle(src, dst):
+        for i, target in ((0, links.batch), (2, links.both), (1, links.across)):
+            to(target, rows(src, i), rows(dst, i))
+
+    settle(send_g_ref, got_g_ref)
+    up_fold = to(links.seq, away_u_ref, fold_u)
+    for copy in (*first, *second):
+        copy.arrive()
+
+    def d_attn(i):
+        at = pl.ds(pl.multiple_of(i * 256, 256), 256)
+        value = nn(dall[at, :], wo[...]).astype(BF16)
+        do[i // 2, pl.ds((i % 2) * 2, 2)] = value.reshape(2, 128, value.shape[1])
+
+    loop(4, d_attn)
+    attention_back(q, do, k, v, start_ref, ot, l_ref, dq, dk, dv, kt, acc, batch_mask, scaling)
+    kv_out[:, :width] = dk[1].reshape(-1, width).astype(BF16)
+    kv_out[:, width:] = dv[1].reshape(-1, width).astype(BF16)
+    kv = to(links.seq, kv_out, kv_in)
+
+    def dall_cols(at, n):
+        return dall[:, pl.ds(at, n)]
+
+    def xa_cols(at, n):
+        return xa[:, pl.ds(at, n)]
+
+    folds = []
+
+    def while_mixed(stage):
+        if stage == 0:
+            away_rows(dall_cols, attn, away_o)
+        if stage == 1:
+            kv.arrive()
+            folds.append(to(links.seq, away_o, fold_o))
+        if stage == 2:
+            up_fold.arrive()
+            keep_load.arrive()
+            own_u[...] = keep_u[:f, :] + fold_u[:f, :].astype(F32)
+
+            def step(i):
+                at = pl.ds(pl.multiple_of(i * f, f), f)
+                here = pl.ds(pl.multiple_of(i * f + f, f), f)
+                send_u[at, :] = (keep_u[here, :] + fold_u[here, :].astype(F32)).astype(BF16)
+
+            loop(3, step)
+            settle(send_u, got_u_ref)
+            load(own_u, own_u_ref)
+
+    mixed_near.arrive()
+    sum_in(links, (m_near, m_core_in, m_out_y, m_in_y, m_out_t, m_in_t, hold), chunk, None, while_mixed, mixed_ref.at[1])
+    blk = lax.axis_index("blk")
+    store_ungrouped(middle_ref[0] + hold[0], mixed_own_ref, blk, bit_order)
+    store_ungrouped(middle_ref[1] + hold[1], swap_m, blk, bit_order)
+    to(links.batch, swap_m, mixed_got_ref)
+
+    for copy in third:
+        copy.arrive()
+    gains_qk[...] = jnp.zeros_like(gains_qk)
+
+    def input_partial(c):
+        def step(m):
+            at = pl.ds(pl.multiple_of((c * 2 + m) * 256, 256), 256)
+            pair = pl.ds(m * 2, 2)
+            got = kv_in[at, :].astype(F32)
+            for h in range(heads + 1):
+                cut = slice(h * width, (h + 1) * width)
+                if h < heads:
+                    grad = dq[c, pair, :, cut].reshape(256, width)
+                else:
+                    grad = dk[0, c, pair].reshape(256, width) + got[:, :width]
+                gain = (gain_q_ref if h < heads else gain_k_ref)[...]
+                values = raw[at, cut]
+                inverse = inverse_rms(values)
+                normed = values * inverse
+                turned = grad * cos[at, :] - pltpu.roll(grad, width // 2, 1) * sin[at, :]
+                row = 0 if h < heads else 1
+                gains_qk[row : row + 1, :] += jnp.sum(turned * normed, axis=0, keepdims=True)
+                scaled = turned * gain
+                mean = jnp.mean(scaled * normed, axis=-1, keepdims=True)
+                d_qkv[at, cut] = (inverse * (scaled - normed * mean)).astype(BF16)
+            d_qkv[at, (heads + 1) * width :] = (dv[0, c, pair].reshape(256, width) + got[:, width:]).astype(BF16)
+            p[c, m] = nt(d_qkv[at, :], wa[...]).astype(BF16).reshape(p.shape[2:])
+
+        loop(2, step)
+
+    def while_input(stage):
+        if stage == 0:
+            away_rows(xa_cols, d_qkv, away_a)
+            folds.append(to(links.seq, away_a, fold_a))
+            folds[0].arrive()
+            keep_rows(dall_cols, attn, fold_o, own_o, send_o)
+            settle(send_o, got_o_ref)
+            load(own_o, own_o_ref)
+        if stage == 2:
+            folds[1].arrive()
+            keep_rows(xa_cols, d_qkv, fold_a, own_a, send_a)
+            settle(send_a, got_a_ref)
+            load(own_a, own_a_ref)
+
+    sum_in(links, (p, core_in, out_y, in_y, out_t, in_t, hold), chunk, input_partial, while_input)
+    for m in range(2):
+        grad = dmid_ref[m] + norm_grad(hold[m], low_ref[m].astype(F32), gain_ref[...], gain_a_grad, m)
+        store_ungrouped(grad, input_own_ref if m == 0 else swap_i, blk, bit_order)
+    to(links.batch, swap_i, input_got_ref)
+    n = gain_a_grad.shape[1]
+    store_ungrouped(gain_a_grad[...], sums_ref.at[:, pl.ds(0, n)], blk, bit_order)
+    sums_ref[:, n : n + width] = gains_qk[0:1, :]
+    sums_ref[:, n + width : n + 2 * width] = gains_qk[1:2, :]
+    store_ungrouped(gain_m_grad_ref[...], sums_ref.at[:, pl.ds(n + 2 * width, n)], blk, bit_order)
+    for i, target in enumerate((links.core, links.near, links.seq, links.across, links.batch)):
+        ring_out[i] = sums_ref[...]
+        to(target, ring_out.at[i], ring_in.at[i]).arrive()
+        sums_ref[...] += ring_in[i]
+    links.finish()
+
+
+def last_call(batch_mask, bit_order, scaling, arrays, collective_id):
+    low, dall, attn, q, k, raw, wa, away_u = (arrays[n] for n in ("low", "dall", "attn", "q", "k", "raw", "wa", "away_u"))
+    _, rows, width = low.shape
+    tokens, columns = attn.shape
+    head_size = k.shape[-1]
+    ff, f = away_u.shape[1], away_u.shape[0] // 4
+    n_a = wa.shape[1]
+    share, full, half_full = (2, rows, width), (2, 2, 2, 2, rows, width), (1, 2, 2, 2, rows, width)
+    vmem, hbm = pl.BlockSpec(memory_space=pltpu.VMEM), pl.BlockSpec(memory_space=pltpu.HBM)
+    like, held = jax.ShapeDtypeStruct, pltpu.VMEM
+    in_vmem = ("low", "middle", "d_middle", "gain", "gain_m_grad", "gain_q", "gain_k", "start", "l")
+    in_hbm = (
+        "dall", "w_out", "attn", "q", "k", "v", "ot", "raw", "cos", "sin", "wa", "xa", "mixed", "send_g", "keep_u", "away_u",
+    )
+    total = 2 * width + 2 * head_size
+    lanes = 2 * 2 * 128
+    sums = (1, total)
+    own_and_send = lambda n: [held((f, n), F32), held((3 * f, n), BF16)]
+    sum_bufs = [
+        held((4, *share), BF16), held((2, *share), BF16), held((2, *share), BF16), held(share, BF16), held(share, BF16),
+    ]
+    return pl.pallas_call(
+        functools.partial(last_kernel, batch_mask=batch_mask, bit_order=bit_order, scaling=scaling, chunk=2 * width // 8),
+        in_specs=[vmem] * len(in_vmem) + [hbm] * len(in_hbm),
+        out_specs=[vmem, hbm, vmem, hbm, vmem] + [hbm] * 7,
+        out_shape=[
+            like((rows, width), BF16),
+            like((rows, width), BF16),
+            like((rows, width), F32),
+            like((rows, width), BF16),
+            like(sums, F32),
+            like((3 * f, ff), BF16),
+            like((f, ff), F32),
+            like((3 * f, ff), BF16),
+            like((f, n_a), F32),
+            like((3 * f, n_a), BF16),
+            like((f, columns), F32),
+            like((3 * f, columns), BF16),
+        ],
+        scratch_shapes=[
+            held((tokens, width), BF16),
+            held((width, columns), BF16),
+            held((tokens, columns), BF16),
+            held(q.shape, BF16),
+            held(q.shape, BF16),
+            held(k.shape, BF16),
+            held(k.shape, BF16),
+            held((4, head_size, lanes), F32),
+            held(raw.shape, F32),
+            held((tokens, head_size), F32),
+            held((tokens, head_size), F32),
+            held(wa.shape, BF16),
+            held((tokens, width), BF16),
+            held(q.shape, F32),
+            held(k.shape, F32),
+            held(k.shape, F32),
+            held((8, head_size, 256), BF16),
+            held((head_size, lanes), F32),
+            held((tokens, 2 * head_size), BF16),
+            held((tokens, 2 * head_size), BF16),
+            held((tokens, n_a), BF16),
+            held(full, BF16),
+            *sum_bufs,
+            held(share, F32),
+            held(half_full, BF16),
+            *sum_bufs,
+            held((rows, width), BF16),
+            held((rows, width), BF16),
+            held((4 * f, ff), F32),
+            held((4 * f, ff), BF16),
+            *own_and_send(ff),
+            held((4 * f, columns), BF16),
+            held((4 * f, columns), BF16),
+            *own_and_send(columns),
+            held((4 * f, n_a), BF16),
+            held((4 * f, n_a), BF16),
+            *own_and_send(n_a),
+            held((8, head_size), F32),
+            held((1, width), F32),
+            held((5, *sums), F32),
+            held((5, *sums), F32),
+            pltpu.SemaphoreType.DMA((96,)),
+            pltpu.SemaphoreType.DMA((96,)),
+        ],
+        compiler_params=pltpu.CompilerParams(
+            collective_id=collective_id, has_side_effects=True, vmem_limit_bytes=60 * MIB
+        ),
+        cost_estimate=TINY_COST,
+    )(*[arrays[n] for n in (*in_vmem, *in_hbm)])
+
+
 def local(
     hidden_in,
     lengths,
@@ -1680,82 +1994,126 @@
         mixed_partial = mixed_partial.reshape(tokens, width)
         (g_down,) = settled([(own_down, got_down)], (ff,))
         up_x = None
-    d_attn = nn(d_mid_all, w_out).astype(BF16).reshape(2, 4, half, q_columns)
-    d_query, d_key, d_value = attend_back(
-        meta, query, d_attn, keys, values, start_lanes, attn_t, total_e, scaling
-    )
-    d_key = d_key.reshape(parts, tokens, head_size)
-    d_value = d_value.reshape(parts, tokens, head_size)
-    for b in reversed(extra_bits):
-        n = d_key.shape[0] // 2
-        d_key = d_key[:n] + over_blk(d_key[n:].astype(BF16), 1 << b).astype(F32)
-        d_value = d_value[:n] + over_blk(d_value[n:].astype(BF16), 1 << b).astype(F32)
-
-    plan = Plan()
-    away_kv = jnp.concatenate([d_key[1], d_value[1]], axis=1).astype(BF16)
-    fold(plan, plan.read(away_kv), away_kv.shape)
-    settle(plan, away_gate)
-    if up_x is None:
-        fold(plan, plan.read(away_up), away_up.shape)
+    if extra_bits:
+        d_attn = nn(d_mid_all, w_out).astype(BF16).reshape(2, 4, half, q_columns)
+        d_query, d_key, d_value = attend_back(
+            meta, query, d_attn, keys, values, start_lanes, attn_t, total_e, scaling
+        )
+        d_key = d_key.reshape(parts, tokens, head_size)
+        d_value = d_value.reshape(parts, tokens, head_size)
+        for b in reversed(extra_bits):
+            n = d_key.shape[0] // 2
+            d_key = d_key[:n] + over_blk(d_key[n:].astype(BF16), 1 << b).astype(F32)
+            d_value = d_value[:n] + over_blk(d_value[n:].astype(BF16), 1 << b).astype(F32)
+
+        plan = Plan()
+        away_kv = jnp.concatenate([d_key[1], d_value[1]], axis=1).astype(BF16)
+        fold(plan, plan.read(away_kv), away_kv.shape)
+        settle(plan, away_gate)
+        if up_x is None:
+            fold(plan, plan.read(away_up), away_up.shape)
+        else:
+            up_x = plan.through(up_x)
+            fold_part(plan, plan.read(away_up), up_x, ff_cut, ff - ff_cut)
+        (mixed,), (got_kv, got_gate, up_x, *filled) = gather_sum(
+            mixed_partial,
+            plan,
+            [middle],
+            [like(share, BF16)],
+            functools.partial(finish_mixed, bit_order=local_order),
+            [] if extra_bits else [fill_weight_grad(d_mid_all, attn, 0)],
+        )
+        keep_out, away_out = filled if filled else weight_sum(d_mid_all, attn)
+        (g_gate,) = settled([(own_gate, got_gate)], (ff,))
+        own_up, away_up = to_settle(keep_up, up_x)
+        mixed = natural(mixed)
+        mixed_got = over_blk(mixed[1], b_mask)
+        d_qkv, d_xa_partial, gains_qk = prepare_back(
+            d_query.reshape(tokens, q_columns), d_key, d_value, got_kv, raw, cosine, sine, gain_q, gain_k, w_qkv, heads
+        )
+        (d_xa_partial, mixed_got) = pin((d_xa_partial, mixed_got))
+
+        plan, fills = Plan(), []
+        settle(plan, away_up)
+        fold(plan, plan.read(away_out), away_out.shape)
+        if extra_bits:
+            keep_qkv, away_qkv = weight_sum(xa, d_qkv)
+            fold(plan, plan.read(away_qkv), away_qkv.shape)
+        else:
+            fills = [fill_weight_grad(xa, d_qkv, 0)]
+            fold(plan, ("fill", (0, 1)), (4 * row_features, a_columns), 1)
+        (input_own, input_away, gain_a_grad), (got_up, out_x, got, *filled) = gather_sum(
+            d_xa_partial,
+            plan,
+            [x_low, d_middle, gain_a[None]],
+            [like((local_rows, width), F32), like((local_rows, width), BF16), like((1, width), F32)],
+            functools.partial(finish_input, bit_order=local_order),
+            fills,
+        )
+        if filled:
+            keep_qkv = filled[0]
+        own_out, away_out = to_settle(keep_out, out_x)
+        (g_up,) = settled([(own_up, got_up)], (ff,))
+        own_qkv, away_qkv = to_settle(keep_qkv, got)
+
+        plan = Plan()
+        settle(plan, away_qkv)
+        settle(plan, away_out)
+        input_got = plan.fresh((local_rows, width), BF16)
+        plan.copy((plan.read(natural(input_away)), everything), (input_got, everything), b_mask)
+        sums = jnp.concatenate([ungroup(gain_a_grad[0]), gains_qk[0], gains_qk[1], ungroup(gain_m_grad[0])])
+        (sums,), (got_a, got_o, input_got) = run(
+            plan, total_main(sums.reshape(-1, 128)), next(ids), [1 << i for i in range(bits)]
+        )
+        g_query, g_key, g_value, g_out = settled(
+            [(own_qkv, got_a), (own_out, got_o)], (q_columns, k_columns, k_columns, q_columns)
+        )
+        mixed = in_order(batch, mixed[:1], mixed_got[None], 0)
+        input_grad = in_order(batch, natural(input_own)[None], input_got.astype(F32)[None], 0)
+        gains = jnp.split(sums.reshape(-1), [width, width + head_size, width + 2 * head_size])
     else:
-        up_x = plan.through(up_x)
-        fold_part(plan, plan.read(away_up), up_x, ff_cut, ff - ff_cut)
-    (mixed,), (got_kv, got_gate, up_x, *filled) = gather_sum(
-        mixed_partial,
-        plan,
-        [middle],
-        [like(share, BF16)],
-        functools.partial(finish_mixed, bit_order=local_order),
-        [] if extra_bits else [fill_weight_grad(d_mid_all, attn, 0)],
-    )
-    keep_out, away_out = filled if filled else weight_sum(d_mid_all, attn)
-    (g_gate,) = settled([(own_gate, got_gate)], (ff,))
-    own_up, away_up = to_settle(keep_up, up_x)
-    mixed = natural(mixed)
-    mixed_got = over_blk(mixed[1], b_mask)
-    d_qkv, d_xa_partial, gains_qk = prepare_back(
-        d_query.reshape(tokens, q_columns), d_key, d_value, got_kv, raw, cosine, sine, gain_q, gain_k, w_qkv, heads
-    )
-    (d_xa_partial, mixed_got) = pin((d_xa_partial, mixed_got))
-
-    plan, fills = Plan(), []
-    settle(plan, away_up)
-    fold(plan, plan.read(away_out), away_out.shape)
-    if extra_bits:
-        keep_qkv, away_qkv = weight_sum(xa, d_qkv)
-        fold(plan, plan.read(away_qkv), away_qkv.shape)
-    else:
-        fills = [fill_weight_grad(xa, d_qkv, 0)]
-        fold(plan, ("fill", (0, 1)), (4 * row_features, a_columns), 1)
-    (input_own, input_away, gain_a_grad), (got_up, out_x, got, *filled) = gather_sum(
-        d_xa_partial,
-        plan,
-        [x_low, d_middle, gain_a[None]],
-        [like((local_rows, width), F32), like((local_rows, width), BF16), like((1, width), F32)],
-        functools.partial(finish_input, bit_order=local_order),
-        fills,
-    )
-    if filled:
-        keep_qkv = filled[0]
-    own_out, away_out = to_settle(keep_out, out_x)
-    (g_up,) = settled([(own_up, got_up)], (ff,))
-    own_qkv, away_qkv = to_settle(keep_qkv, got)
-
-    plan = Plan()
-    settle(plan, away_qkv)
-    settle(plan, away_out)
-    input_got = plan.fresh((local_rows, width), BF16)
-    plan.copy((plan.read(natural(input_away)), everything), (input_got, everything), b_mask)
-    sums = jnp.concatenate([ungroup(gain_a_grad[0]), gains_qk[0], gains_qk[1], ungroup(gain_m_grad[0])])
-    (sums,), (got_a, got_o, input_got) = run(
-        plan, total_main(sums.reshape(-1, 128)), next(ids), [1 << i for i in range(bits)]
-    )
-    g_query, g_key, g_value, g_out = settled(
-        [(own_qkv, got_a), (own_out, got_o)], (q_columns, k_columns, k_columns, q_columns)
-    )
-    mixed = in_order(batch, mixed[:1], mixed_got[None], 0)
-    input_grad = in_order(batch, natural(input_own)[None], input_got.astype(F32)[None], 0)
-    gains = jnp.split(sums.reshape(-1), [width, width + head_size, width + 2 * head_size])
+        (
+            mixed_own, mixed_got, input_own, input_got, sums, got_gate, own_up, got_up, own_qkv, got_a, own_out, got_o,
+        ) = last_call(
+            b_mask,
+            bit_order,
+            scaling,
+            dict(
+                low=x_low,
+                middle=middle,
+                d_middle=d_middle,
+                gain=gain_a[None],
+                gain_m_grad=gain_m_grad,
+                gain_q=gain_q,
+                gain_k=gain_k,
+                start=start_lanes,
+                l=total_e,
+                dall=d_mid_all,
+                w_out=w_out,
+                attn=attn,
+                q=query,
+                k=keys,
+                v=values,
+                ot=attn_t,
+                raw=raw,
+                cos=cosine,
+                sin=sine,
+                wa=w_qkv,
+                xa=xa,
+                mixed=mixed_partial.reshape(2, 2, 2, 2, local_rows, width),
+                send_g=away_gate,
+                keep_u=keep_up,
+                away_u=away_up,
+            ),
+            next(ids),
+        )
+        g_gate, g_up, g_query, g_key, g_value, g_out = settled(
+            [(own_gate, got_gate), (own_up, got_up), (own_qkv, got_a), (own_out, got_o)],
+            (ff, ff, q_columns, k_columns, k_columns, q_columns),
+        )
+        mixed = in_order(batch, mixed_own[None], mixed_got[None], 0)
+        input_grad = in_order(batch, input_own[None], input_got.astype(F32)[None], 0)
+        gains = jnp.split(sums.reshape(-1), [width, width + head_size, width + 2 * head_size])
     return (
         mixed,
         input_grad,

time: 504 us -> 476 us (0.944)
  Pallas kernels: 447 us -> 420 us
    pallas_call x5 -> x2, Pallas kernels: 236 us -> 85.5 us  [run(): pl.pallas_call(kernel, out_shape=[*out_shapes, *plan.shapes, *f_out], in_...]
    pallas_call x2 -> x1, Pallas kernels: 18.1 us -> 142 us  [last_call(): pl.pallas_call(functools.partial(last_kernel, batch_mask=batch_mask, bit_...]
    unnamed x127 -> x98, local copies, waits for them, and re-layouts: 17.8 us -> 13.5 us
    ppermute x5 -> x4, waiting for transfers between devices: 11.6 us -> 14.2 us  [over_blk(): return lax.ppermute(value, 'blk', [(i, i ^ mask) for i in range(count)])]
  transfers between devices with their start and end apart: 5 -> 4, of which waited for: 3 -> 1; matrix products, arithmetic and copies ran while one was open for 2% -> 1% of each run, Pallas kernels for 2% -> 0%
where the time goes in v6:
time: 476 us; the launch traced here: 473 us
  Pallas kernels  420 us (88%)
  local copies, waits for them, and re-layouts  19 us (4%)
  waiting for transfers between devices  14.2 us (3%)
  other arithmetic  10.7 us (2%)
  starting transfers between devices  7.7 us (2%)
    pallas_call x1, Pallas kernels, middle_call(): pl.pallas_call(functools.partial(middle_kernel, batch_mask=batch_mask, ch...  175 us
    pallas_call x1, Pallas kernels, last_call(): pl.pallas_call(functools.partial(last_kernel, batch_mask=batch_mask, bit_...  142 us
    pallas_call x2, Pallas kernels, run(): pl.pallas_call(kernel, out_shape=[*out_shapes, *plan.shapes, *f_out], in_...  85.5 us
    ppermute x4, waiting for transfers between devices, over_blk(): return lax.ppermute(value, 'blk', [(i, i ^ mask) for i in range(count)])  14.2 us
    unnamed x98, local copies, waits for them, and re-layouts  13.5 us
  transfers between devices with their start and end apart: 4, of which 1 were waited for; matrix products, arithmetic and copies ran while one was open for 1% of the time, Pallas kernels for 0%

profile of v6, /device:TPU:0, one launch (start us, length us, event | category | flops | bytes accessed | tf_op | source)
XLA Modules:
  0.0 472.6 jit_solution(11626193193896699946)
XLA Ops:
  0.7 1.1 constant_dynamic-slice_fusion.3
  2.8 4.1 collective-permute-start.2
  6.9 1.6 collective-permute-start.1
  9.2 1.6 collective-permute-start.3
  11.7 1.9 fusion.1
  13.6 1.0 pad_maximum_fusion.2.cos_ref
  15.9 14.2 %collective-permute-done.refs_1_ = bf16[64,2048]{1,0:T(8,128)(2,1)S(1)} collective-permute-done((bf16[64,2048]{1,0:T(8,128)(2,1)S(1)}, bf16[64,2048]{1,0:T(8,128)(2,1)S(1)}, u32[]{:S(2)}, u32[]{:S(2)}) %collective-permute-start) | collective-permute-done | bytes 262176 | tf_op jit(solution)/shard_map/ppermute | solution.py:42
  33.5 45.8 %shard_map.238 = (bf16[2,2,2,2,64,2048]{5,4,3,2,1,0:T(8,128)(2,1)}, bf16[2048,512]{1,0:T(8,128)(2,1)}, bf16[2,64,2048]{2,1,0:T(8,128)(2,1)}, bf16[2048,256]{1,0:...) custom-call(bf16[2,64,2048]{2,1,0:T(8,128)(2,1)} %bitcast.61, bf16[256,512]{1,0:T(8,128)(2,1)} %copy-done.42, ...), custom_call_target="tpu_custom_call" | custom-call | tf_op jit(solution)/shard_map/pallas_call | solution.py:680
  79.4 1.0 copy-done.31
  80.5 2.4 copy-done.2
  83.0 1.6 copy-done.11
  84.6 3.7 shard_map.240
  88.4 39.7 %shard_map.241 = (bf16[2,2,2,2,64,2048]{5,4,3,2,1,0:T(8,128)(2,1)S(1)}, bf16[1024,256]{1,0:T(8,128)(2,1)S(1)}, bf16[2048,256]{1,0:T(8,128)(2,1)S(1)}, bf16[2048,768]{1,0:T(8,128)(2,1)S(1)}, bf16[2048,768]{1,0:T(8,128)(2,1)S(1)}) custom-call(bf16[2,64,2048]{2,1,0:T(8,128)(2,1)S(1)} %bitcast.47, ...), custom_call_target="tpu_custom_call", output_to_operand_aliasing={{2}: (2, {}), {3}: (3, {}), {4}: (6, {})} | custom-call | tf_op jit(solution)/shard_map/pallas_call | solution.py:680
  128.0 1.9 copy-done.16
  130.2 8.8 %shard_map.242 = (bf16[2,4,128,256]{3,2,1,0:T(8,128)(2,1)S(1)}, f32[4,128,512]{2,1,0:T(8,128)S(1)}, f32[4,1,512]{2,1,0:T(1,128)S(1)}) custom-call(s32[45]{0:T(128)S(1)} %concatenate.45.meta_ref, bf16[2,4,128,256]{3,2,1,0:T(8,128)(2,1)S(1)} %bitcast.62, bf16[2,2,4,128,128]{4,3,2,1,0:T(8,128)(2,1)S(1)} %bitcast.57, bf16[2,2,4,128,128]{4,3,2,1,0:T(8,128)(2,1)S(1)} %bitcast.55, ...), custom_call_target="tpu_custom_call" | custom-call | flops 2147483648 | bytes 4194304 | tf_op jit(solution)/shard_map/pallas_call | solution.py:207
  140.8 175.2 %shard_map.243 = (f32[2,64,2048]{2,1,0:T(8,128)}, f32[2,64,2048]{2,1,0:T(8,128)}, f32[1,2048]{1,0:T(1,128)}, bf16[2,2,2,2,64,2048]{5,4,3,2,1,0:T(8,128)(2,1)}, b...) custom-call(bf16[2,64,2048]{2,1,0:T(8,128)(2,1)} %bitcast.51, ...), custom_call_target="tpu_custom_call" | custom-call | tf_op jit(solution)/shard_map/pallas_call | solution.py:1246
  316.0 142.3 %shard_map.244 = (bf16[64,2048]{1,0:T(8,128)(2,1)}, bf16[64,2048]{1,0:T(8,128)(2,1)}, f32[64,2048]{1,0:T(8,128)}, bf16[64,2048]{1,0:T(8,128)(2,1)}, f32[1,4352]{...) custom-call(bf16[2,64,2048]{2,1,0:T(8,128)(2,1)} %bitcast.52, ...), custom_call_target="tpu_custom_call" | custom-call | tf_op jit(solution)/shard_map/pallas_call | solution.py:1536
  458.4 1.2 slice_bitcast_fusion
  459.5 1.3 fusion.8
  460.9 1.1 bitcast_convert_fusion
  462.0 2.2 maximum_select_fusion.1
  464.2 2.4 maximum_select_fusion
  466.6 1.3 shard_map.246
  470.0 2.6 shard_map.245
  (131 shorter events, 11.3 us)
Async XLA Ops:
  0.6 10.1 %copy-start = (s32[2,9]{1,0:T(2,128)S(1)}, s32[2,9]{1,0:T(2,128)}, u32[]{:S(2)}) copy-start(s32[2,9]{1,0:T(2,128)} %param.15) | copy-start | bytes 220
  0.7 7.9 %copy-start.43 = (bf16[2,64,2048]{2,1,0:T(8,128)(2,1)S(1)}, bf16[2,64,2048]{2,1,0:T(8,128)(2,1)}, u32[]{:S(2)}) copy-start(bf16[2,64,2048]{2,1,0:T(8,128)(2,1)} %param.14) | copy-start | bytes 1572868
  0.7 8.4 %copy-start.3 = (bf16[256,1536]{1,0:T(8,128)(2,1)S(1)}, bf16[256,1536]{1,0:T(8,128)(2,1)}, u32[]{:S(2)}) copy-start(bf16[256,1536]{1,0:T(8,128)(2,1)} %refs_5_.1) | copy-start | bytes 2359300
  2.8 29.8 %collective-permute-start.2 = (bf16[256,512]{1,0:T(8,128)(2,1)S(1)}, bf16[256,512]{1,0:T(8,128)(2,1)S(1)}, u32[]{:S(2)}, u32[]{:S(2)}) collective-permute-start(bf16[256,512]{1,0:T(8,128)(2,1)S(1)} %pad_maximum_fusion.5.refs_4_), channel_id=1, source_target_pairs={{0,16},{4,20},{8,24},{12,28},{16,0},{20,4},{24,8},{28,12},{1,17},{... | collective-permute-start | bytes 786440 | tf_op jit(solution)/shard_map/ppermute | solution.py:42
  6.9 25.6 %collective-permute-start.1 = (bf16[256,512]{1,0:T(8,128)(2,1)S(1)}, bf16[256,512]{1,0:T(8,128)(2,1)}, u32[]{:S(2)}, u32[]{:S(2)}) collective-permute-start(bf16[256,512]{1,0:T(8,128)(2,1)S(1)} %pad_maximum_fusion.4.refs_1_), channel_id=1, source_target_pairs={{0,8},{4,12},{8,0},{12,4},{16,24},{20,28},{24,16},{28,20},{1,9},{5... | collective-permute-start | bytes 786440 | tf_op jit(solution)/shard_map/ppermute | solution.py:42
  8.6 21.5 %collective-permute-start = (bf16[64,2048]{1,0:T(8,128)(2,1)S(1)}, bf16[64,2048]{1,0:T(8,128)(2,1)S(1)}, u32[]{:S(2)}, u32[]{:S(2)}) collective-permute-start(bf16[64,2048]{1,0:T(8,128)(2,1)S(1)} %get-tuple-element.129), channel_id=1, source_target_pairs={{0,16},{4,20},{8,24},{12,28},{16,0},{20,4},{24,8},{28,12},{1,17},{... | collective-permute-start | bytes 786440 | tf_op jit(solution)/shard_map/ppermute | solution.py:42
  9.2 23.4 %collective-permute-start.3 = (bf16[256,1280]{1,0:T(8,128)(2,1)S(1)}, bf16[256,1280]{1,0:T(8,128)(2,1)S(1)}, u32[]{:S(2)}, u32[]{:S(2)}) collective-permute-start(bf16[256,1280]{1,0:T(8,128)(2,1)S(1)} %pad_maximum_fusion), channel_id=1, source_target_pairs={{0,4},{4,0},{8,12},{12,8},{16,20},{20,16},{24,28},{28,24},{1,5},{5... | collective-permute-start | bytes 1966088 | tf_op jit(solution)/shard_map/ppermute | solution.py:42
  15.8 114.4 %copy-start.36 = (s32[4,1,512]{2,1,0:T(1,128)}, s32[4,1,512]{2,1,0:T(1,128)S(1)}, u32[]{:S(2)}) copy-start(s32[4,1,512]{2,1,0:T(1,128)S(1)} %tile.12.start_ref) | copy-start | bytes 24580
  15.9 64.6 %copy-start.38 = (f32[1,128]{1,0:T(1,128)}, f32[1,128]{1,0:T(1,128)S(1)}, u32[]{:S(2)}) copy-start(f32[1,128]{1,0:T(1,128)S(1)} %get-tuple-element.154.gk_ref.gain_k_ref) | copy-start | bytes 1540
  15.9 64.6 %copy-start.39 = (f32[1,128]{1,0:T(1,128)}, f32[1,128]{1,0:T(1,128)S(1)}, u32[]{:S(2)}) copy-start(f32[1,128]{1,0:T(1,128)S(1)} %get-tuple-element.155.gq_ref.gain_q_ref) | copy-start | bytes 1540
  33.5 47.0 %copy-start.14 = (f32[1024,128]{1,0:T(8,128)S(1)}, f32[1024,128]{1,0:T(8,128)}, u32[]{:S(2)}) copy-start(f32[1024,128]{1,0:T(8,128)} %pad_maximum_fusion.3.sin_ref) | copy-start | bytes 1572868
  33.5 47.0 %copy-start.15 = (f32[1024,128]{1,0:T(8,128)S(1)}, f32[1024,128]{1,0:T(8,128)}, u32[]{:S(2)}) copy-start(f32[1024,128]{1,0:T(8,128)} %pad_maximum_fusion.2.cos_ref) | copy-start | bytes 1572868
  33.5 54.8 %copy-start.12 = (bf16[256,1536]{1,0:T(8,128)(2,1)S(1)}, bf16[256,1536]{1,0:T(8,128)(2,1)}, u32[]{:S(2)}) copy-start(bf16[256,1536]{1,0:T(8,128)(2,1)} %gate_ref.1) | copy-start | bytes 2359300
  80.4 7.9 %copy-start.9 = (bf16[2048,256]{1,0:T(8,128)(2,1)S(1)}, bf16[2048,256]{1,0:T(8,128)(2,1)}, u32[]{:S(2)}) copy-start(bf16[2048,256]{1,0:T(8,128)(2,1)} %get-tuple-element.81.refs_2_) | copy-start | bytes 3145732
  80.5 7.8 %copy-start.13 = (bf16[128,2048]{1,0:T(8,128)(2,1)}, bf16[128,2048]{1,0:T(8,128)(2,1)S(1)}, u32[]{:S(2)}) copy-start(bf16[128,2048]{1,0:T(8,128)(2,1)S(1)} %shard_map.239) | copy-start | bytes 1572868
  88.3 39.7 %copy-start.21 = (f32[1024,384]{1,0:T(8,128)}, f32[1024,384]{1,0:T(8,128)S(1)}, u32[]{:S(2)}) copy-start(f32[1024,384]{1,0:T(8,128)S(1)} %get-tuple-element.97.raw_ref) | copy-start | bytes 4718596
  88.3 41.9 %copy-start.33 = (bf16[1024,256]{1,0:T(8,128)(2,1)}, bf16[1024,256]{1,0:T(8,128)(2,1)S(1)}, u32[]{:S(2)}) copy-start(bf16[1024,256]{1,0:T(8,128)(2,1)S(1)} %get-tuple-element.79) | copy-start | bytes 1572868
  130.0 9.0 %copy-start.6 = (bf16[2048,768]{1,0:T(8,128)(2,1)}, bf16[2048,768]{1,0:T(8,128)(2,1)S(1)}, u32[]{:S(2)}) copy-start(bf16[2048,768]{1,0:T(8,128)(2,1)S(1)} %get-tuple-element.89.wd_ref) | copy-start | bytes 9437188
  130.0 9.0 %copy-start.8 = (bf16[2048,768]{1,0:T(8,128)(2,1)}, bf16[2048,768]{1,0:T(8,128)(2,1)S(1)}, u32[]{:S(2)}) copy-start(bf16[2048,768]{1,0:T(8,128)(2,1)S(1)} %get-tuple-element.90.wg_ref) | copy-start | bytes 9437188
  130.0 9.0 %copy-start.10 = (bf16[2048,256]{1,0:T(8,128)(2,1)}, bf16[2048,256]{1,0:T(8,128)(2,1)S(1)}, u32[]{:S(2)}) copy-start(bf16[2048,256]{1,0:T(8,128)(2,1)S(1)} %get-tuple-element.87.wo_ref) | copy-start | bytes 3145732
  130.2 8.8 %copy-start.19 = (bf16[2,1024,128]{2,1,0:T(8,128)(2,1)}, bf16[2,1024,128]{2,1,0:T(8,128)(2,1)S(1)}, u32[]{:S(2)}) copy-start(bf16[2,1024,128]{2,1,0:T(8,128)(2,1)S(1)} %get-tuple-element.127) | copy-start | bytes 1572868
  130.2 8.8 %copy-start.20 = (bf16[2,1024,128]{2,1,0:T(8,128)(2,1)}, bf16[2,1024,128]{2,1,0:T(8,128)(2,1)S(1)}, u32[]{:S(2)}) copy-start(bf16[2,1024,128]{2,1,0:T(8,128)(2,1)S(1)} %get-tuple-element.128) | copy-start | bytes 1572868
  140.8 175.2 %copy-start.37 = (f32[4,1,512]{2,1,0:T(1,128)}, f32[4,1,512]{2,1,0:T(1,128)S(1)}, u32[]{:S(2)}) copy-start(f32[4,1,512]{2,1,0:T(1,128)S(1)} %get-tuple-element.94.l_ref) | copy-start | bytes 24580
  460.9 7.0 %copy-start.35 = (f32[256,256]{1,0:T(8,128)S(1)}, f32[256,256]{1,0:T(8,128)}, u32[]{:S(2)}) copy-start(f32[256,256]{1,0:T(8,128)} %get-tuple-element.112.refs_6_) | copy-start | bytes 786436
  (29 other events, 78.3 us)

commit v7 on v6

--- a/solution.py
+++ b/solution.py
@@ -1001,36 +1001,45 @@
 
 def sum_in(links, bufs, chunk, partial, between=nothing, far=None):
     p_ref, core_in, out_y, in_y, out_t, in_t, hold = bufs
-    order = ((1, 1), (0, 1), (1, 0), (0, 0))
+    order = ((1, 1), (1, 0), (0, 1), (0, 0))
     if partial:
         partial(1)
         far = p_ref.at[1]
     core = [links.to(links.core, far.at[:, t, y], core_in.at[i]) for i, (t, y) in enumerate(order)]
     if partial:
         partial(0)
-    near = []
-    for i in range(2):
+
+    def both(i):
         t, y = order[i]
         core[i].arrive()
-        out_y[i] = (p_ref[0, :, t, y].astype(F32) + core_in[i].astype(F32)).astype(BF16)
-        near.append(links.to(links.near, out_y.at[i], in_y.at[i]))
+        return p_ref[0, :, t, y].astype(F32) + core_in[i].astype(F32)
+
+    def near(i, m):
+        return links.to(links.near, out_y.at[i, m], in_y.at[i, m])
+
+    out_y[0] = both(0).astype(BF16)
+    copies = [near(0, 0)]
+    hold[...] = both(1)
+    out_y[1] = both(2).astype(BF16)
     between(0)
-    core[2].arrive()
-    hold[...] = p_ref[0, :, 1, 0].astype(F32) + core_in[2].astype(F32)
-    near[0].arrive()
-    for i in range(p_ref.shape[-1] // chunk):
-        a, b = slice(i * chunk, (i + 1) * chunk), slice((i ^ 1) * chunk, ((i ^ 1) + 1) * chunk)
-        out_t[:, :, b] = (hold[:, :, a] + in_y[0, :, :, a].astype(F32)).astype(BF16)
-    across = links.to(links.across, out_t, in_t)
+    across = []
+    for m in range(2):
+        copies[m].arrive()
+        copies += [near(0, 1)] if m == 0 else [near(1, 0), near(1, 1)]
+        for i in range(p_ref.shape[-1] // chunk):
+            a, b = slice(i * chunk, (i + 1) * chunk), slice((i ^ 1) * chunk, ((i ^ 1) + 1) * chunk)
+            out_t[m, :, b] = (hold[m, :, a] + in_y[0, m, :, a].astype(F32)).astype(BF16)
+        across.append(links.to(links.across, out_t.at[m], in_t.at[m]))
+    hold[...] = both(3)
     between(1)
-    core[3].arrive()
-    hold[...] = p_ref[0, :, 0, 0].astype(F32) + core_in[3].astype(F32)
-    near[1].arrive()
-    hold[...] += in_y[1].astype(F32)
+    for m in range(2):
+        copies[2 + m].arrive()
+        hold[m] += in_y[1, m].astype(F32)
     between(2)
-    across.arrive()
-    hold[...] += in_t[...].astype(F32)
-    for copy in (*core, *near, across):
+    for m in range(2):
+        across[m].arrive()
+        hold[m] += in_t[m].astype(F32)
+    for copy in (*core, *copies, *across):
         copy.sent()
 
 
@@ -1070,10 +1079,10 @@
 
 
 def middle_kernel(
-    low_ref, cot_ref, gain_ref, attn_ref, wo_ref, c_ref, wd_ref, wg_ref, gate_ref, up_ref,
-    middle_ref, dmid_ref, gain_grad_ref, dall_ref, mixed_ref, own_d_ref, got_d_ref, own_g_ref, send_g_ref, keep_u_ref, away_u_ref,
+    low_ref, cot_ref, gain_ref, attn_ref, wo_ref, c_ref, wd_ref, wg_ref, down_ref, gate_ref, up_ref,
+    middle_ref, dmid_ref, gain_grad_ref, dall_ref, mixed_ref, own_d_ref, got_d_b_ref, got_d_o_ref, got_g_b_ref, send_g_ref, keep_g_ref, away_g_ref, keep_u_ref, away_u_ref,
     attn, wo, p, core_in, out_y, in_y, out_t, in_t, hold, xm_s, xm, c, wd, wg, wu, dact, gate, act, dg, du,
-    away_d, fold_d, away_g, fold_g, own_d, send_d, own_g, send_g, up_tile, send, recv, *, batch_mask, chunk,
+    away_d, fold_d, away_g, fold_g, own_d, send_d, keep_g, send_g, up_tile, send, recv, *, batch_mask, chunk,
 ):
     links = Links(send, recv, batch_mask)
     f, ff = own_d.shape[0], act.shape[1]
@@ -1091,8 +1100,10 @@
     ups = []
     for copy in loads:
         copy.arrive()
-    down += [load(rows(wd_ref, q), rows(wd, q)) for q in (0, 1, 2, 3, 4, 6)]
-    gates += [load(rows(wg_ref, q), rows(wg, q)) for q in (0, 2, 4)]
+    down += [load(rows(wd_ref, q), rows(wd, q)) for q in (1, 2, 3, 4, 6)]
+    gates += [load(rows(wg_ref, q), rows(wg, q)) for q in (2, 4)]
+    down.append(load(links.half(down_ref, 0), rows(wd, 0)))
+    gates.append(load(links.half(gate_ref, 0), rows(wg, 0)))
     c_load = load(c_ref, c)
     up_own = load(links.half(up_ref, 0), rows(wu, 0))
     bufs = (p, core_in, out_y, in_y, out_t, in_t, hold)
@@ -1108,21 +1119,18 @@
         if stage == 1:
             up_t.arrive()
             ups.append(to(links.seq, rows(wu, 2), rows(wu, 6)))
-
+            up_z.append(to(links.batch, links.half(up_ref, 0), rows(wu, 1)))
+
+    up_z = []
     sum_in(links, bufs, chunk, out_partial, while_out)
     for m in range(2):
         middle = low_ref[m].astype(F32) + hold[m]
         middle_ref[m] = middle
         xm_s[m] = (middle * inverse_rms(middle) * gain_ref[...]).astype(BF16)
 
-    up_z = []
-
     def while_xm(stage):
         if stage == 0:
-            for copy in gate_z:
-                copy.arrive()
-            up_z.append(to(links.batch, links.half(up_ref, 0), rows(wu, 1)))
-            gates.extend(to(links.seq, rows(wg, q), rows(wg, q + 4)) for q in (1, 3))
+            up_z.append(to(links.both, links.half(up_ref, 1), rows(wu, 3)))
             for copy in (*down, c_load):
                 copy.arrive()
 
@@ -1131,10 +1139,15 @@
                 dact[at, :] = nn(c[at, :], wd[...])
 
             loop(c.shape[0] // 512, step)
+            for copy in gate_z:
+                copy.arrive()
+            gates.extend(to(links.seq, rows(wg, q), rows(wg, q + 4)) for q in (1, 3))
+        if stage == 1:
+            up_z[0].arrive()
+            ups.append(to(links.seq, rows(wu, 1), rows(wu, 5)))
         if stage == 2:
-            up_z[0].arrive()
-            up_z.append(to(links.both, links.half(up_ref, 1), rows(wu, 3)))
-            ups.append(to(links.seq, rows(wu, 1), rows(wu, 5)))
+            up_z[1].arrive()
+            ups.append(to(links.seq, rows(wu, 3), rows(wu, 7)))
 
     spread_in(links, xm_s, xm, chunk, while_xm)
     for copy in gates:
@@ -1145,8 +1158,6 @@
         gate[at, :] = nn(rows_of(xm, i), wg[...])
 
     loop(4, gate_step)
-    up_z[1].arrive()
-    ups.append(to(links.seq, rows(wu, 3), rows(wu, 7)))
     up_own.arrive()
     for copy in ups:
         copy.arrive()
@@ -1174,8 +1185,20 @@
     def xm_cols(at, n):
         return xm[:, :, :, :, :, pl.ds(at, n)].reshape(-1, n)
 
-    away_rows(c_cols, act, away_d)
-    fold = to(links.seq, away_d, fold_d)
+    def fold(away, into, *places):
+        return {i: to(links.seq, rows(away, i), rows(into, i)) for i in places}
+
+    def compute_away(a_cols, b_ref, away, *places):
+        for i in places:
+            away[pl.ds(i * f, f), :] = tn(a_cols((i + 4) * f, f), b_ref[...]).astype(BF16)
+
+    def total(a_cols, b_ref, into, i):
+        return tn(a_cols(i * f, f), b_ref[...]) + into[pl.ds(i * f, f), :].astype(F32)
+
+    compute_away(c_cols, act, away_d, 1)
+    folds_d = fold(away_d, fold_d, 1)
+    folds_g = {}
+    compute_away(c_cols, act, away_d, 3)
 
     def back_partial(k):
         def step(m):
@@ -1184,20 +1207,27 @@
             p[k, m] = value.astype(BF16).reshape(p.shape[2:])
 
         loop(2, step)
-
-    later = []
+        if k == 1:
+            folds_d.update(fold(away_d, fold_d, 3))
+
+    def settle_d(i, target, dst):
+        folds_d[i].arrive()
+        send_d[pl.ds((i - 1) * f, f), :] = total(c_cols, act, fold_d, i).astype(BF16)
+        to(target, rows(send_d, i - 1), dst)
 
     def while_back(stage):
         if stage == 0:
-            away_rows(xm_cols, dg, away_g)
-            later.append(to(links.seq, away_g, fold_g))
+            compute_away(c_cols, act, away_d, 0, 2)
         if stage == 1:
-            def step(i):
-                at = pl.ds(pl.multiple_of(i * 512, 512), 512)
-                dact[at, :] = tn(xm_cols(pl.multiple_of(i * 512, 512), 512), du[...])
-
-            loop(2, step)
-            later.append(load(dact, keep_u_ref))
+            settle_d(1, links.batch, got_d_b_ref)
+            folds_d.update(fold(away_d, fold_d, 2, 0))
+            settle_d(3, links.both, rows(got_d_o_ref, 1))
+            compute_away(xm_cols, dg, away_g, 1, 3)
+            folds_g.update(fold(away_g, fold_g, 1))
+        if stage == 2:
+            compute_away(xm_cols, dg, away_g, 0, 2)
+            folds_g.update(fold(away_g, fold_g, 3))
+            load(away_g, away_g_ref)
 
     sum_in(links, bufs, chunk, back_partial, while_back)
     for m in range(2):
@@ -1206,36 +1236,47 @@
         dmid_ref[m] = grad
         xm_s[m] = grad.astype(BF16)
 
-    settles = []
-
     def while_mid(stage):
         if stage == 0:
-            fold.arrive()
-            fold.sent()
-            keep_rows(c_cols, act, fold_d, own_d, send_d)
-            for q, target in ((0, links.batch), (2, links.both), (1, links.across)):
-                settles.append(to(target, rows(send_d, q), rows(got_d_ref, q)))
-            settles.append(load(own_d, own_d_ref))
-            away_rows(xm_cols, du, away_d)
-            settles.append(load(away_d, away_u_ref))
+            folds_d[0].arrive()
+            own_d[...] = total(c_cols, act, fold_d, 0)
+            load(own_d, own_d_ref)
         if stage == 1:
+            settle_d(2, links.across, rows(got_d_o_ref, 0))
+            folds_g[1].arrive()
+            send_g[pl.ds(0, f), :] = total(xm_cols, dg, fold_g, 1).astype(BF16)
+            to(links.batch, rows(send_g, 0), got_g_b_ref)
+            keep_g[pl.ds(0, f), :] = tn(xm_cols(0, f), dg[...])
+            keep_g[pl.ds(f, f), :] = tn(xm_cols(2 * f, f), dg[...])
+            load(keep_g, keep_g_ref)
+
+            def step(i):
+                at = pl.ds(pl.multiple_of(i * 512, 512), 512)
+                dact[at, :] = tn(xm_cols(pl.multiple_of(i * 512, 512), 512), du[...])
+
+            loop(2, step)
+            load(dact, keep_u_ref)
+            for copy in folds_d.values():
+                copy.sent()
+            compute_away(xm_cols, du, away_d, 0, 1, 2, 3)
+            load(away_d, away_u_ref)
 
             def step(i):
                 at = pl.ds(pl.multiple_of(i * 256, 256), 256)
                 p[i // 2, i % 2] = nt(act[at, :], wd[...]).astype(BF16).reshape(p.shape[2:])
 
             loop(4, step)
-            settles.append(load(p, mixed_ref))
+            load(p, mixed_ref)
+        if stage == 2:
+            folds_g[3].arrive()
+            send_g[pl.ds(f, f), :] = total(xm_cols, dg, fold_g, 3).astype(BF16)
+            load(rows(send_g, 1), send_g_ref)
 
     spread_in(links, xm_s, dall_ref, chunk, while_mid, in_vmem=False)
-    later[0].arrive()
-    keep_rows(xm_cols, dg, fold_g, own_g, send_g)
-    load(own_g, own_g_ref)
-    load(send_g, send_g_ref)
     links.finish()
 
 
-def middle_call(batch_mask, low, cot, gain, attn, w_out, cot_all, w_down, w_gate, gate_weight, up_weight, collective_id):
+def middle_call(batch_mask, low, cot, gain, attn, w_out, cot_all, w_down, w_gate, params, collective_id):
     _, rows, width = low.shape
     tokens, columns = attn.shape
     ff = w_down.shape[1]
@@ -1245,8 +1286,8 @@
     like = jax.ShapeDtypeStruct
     return pl.pallas_call(
         functools.partial(middle_kernel, batch_mask=batch_mask, chunk=2 * width // 8),
-        in_specs=[vmem] * 3 + [hbm] * 7,
-        out_specs=[vmem] * 3 + [hbm] * 8,
+        in_specs=[vmem] * 3 + [hbm] * 8,
+        out_specs=[vmem] * 3 + [hbm] * 11,
         out_shape=[
             like(share, F32),
             like(share, F32),
@@ -1254,9 +1295,12 @@
             like(full, BF16),
             like(full, BF16),
             like((f, ff), F32),
-            like((3 * f, ff), BF16),
-            like((f, ff), F32),
-            like((3 * f, ff), BF16),
+            like((f, ff), BF16),
+            like((2 * f, ff), BF16),
+            like((f, ff), BF16),
+            like((f, ff), BF16),
+            like((2 * f, ff), F32),
+            like((4 * f, ff), BF16),
             like((4 * f, ff), F32),
             like((4 * f, ff), BF16),
         ],
@@ -1279,8 +1323,8 @@
             *[pltpu.VMEM((4 * f, ff), BF16)] * 4,
             pltpu.VMEM((f, ff), F32),
             pltpu.VMEM((3 * f, ff), BF16),
-            pltpu.VMEM((f, ff), F32),
-            pltpu.VMEM((3 * f, ff), BF16),
+            pltpu.VMEM((2 * f, ff), F32),
+            pltpu.VMEM((2 * f, ff), BF16),
             pltpu.VMEM((256, ff), F32),
             pltpu.SemaphoreType.DMA((96,)),
             pltpu.SemaphoreType.DMA((96,)),
@@ -1289,7 +1333,7 @@
             collective_id=collective_id, has_side_effects=True, vmem_limit_bytes=60 * MIB
         ),
         cost_estimate=TINY_COST,
-    )(low, cot, gain, attn, w_out, cot_all, w_down, w_gate, gate_weight, up_weight)
+    )(low, cot, gain, attn, w_out, cot_all, w_down, w_gate, *params)
 
 
 def block_of(n, batch_mask):
@@ -1372,13 +1416,13 @@
 
 def last_kernel(
     low_ref, middle_ref, dmid_ref, gain_ref, gain_m_grad_ref, gain_q_ref, gain_k_ref, start_ref, l_ref,
-    dall_ref, wo_ref, attn_ref, q_ref, k_ref, v_ref, ot_ref, raw_ref, cos_ref, sin_ref, wa_ref, xa_ref, mixed_ref,
-    send_g_ref, keep_u_ref, away_u_ref,
+    dall_ref, wo_ref, attn_ref, q_ref, k_ref, v_ref, ot_ref, raw_ref, table_ref, wa_ref, xa_ref, mixed_ref,
+    send_g_ref, keep_g_ref, away_g_ref, keep_u_ref, away_u_ref,
     mixed_own_ref, mixed_got_ref, input_own_ref, input_got_ref, sums_ref,
-    got_g_ref, own_u_ref, got_u_ref, own_a_ref, got_a_ref, own_o_ref, got_o_ref,
-    dall, wo, attn, q, do, k, v, ot, raw, cos, sin, wa, xa, dq, dk, dv, kt, acc, kv_out, kv_in, d_qkv,
-    p, core_in, out_y, in_y, out_t, in_t, hold, m_near, m_core_in, m_out_y, m_in_y, m_out_t, m_in_t,
-    swap_m, swap_i, keep_u, fold_u, own_u, send_u, away_o, fold_o, own_o, send_o, away_a, fold_a, own_a, send_a,
+    own_g_ref, got_g_o_ref, own_u_ref, got_u_b_ref, got_u_o_ref, own_a_ref, got_a_b_ref, got_a_o_ref, own_o_ref, got_o_b_ref, got_o_o_ref,
+    dall, wo, attn, q, do, k, v, ot, raw, table, wa, xa, dq, dk, dv, kt, acc, kv_out, kv_in, d_qkv,
+    p, core_in, out_y, in_y, out_t, in_t, hold, m_near, m_core_in, m_in_y, m_in_t,
+    swap_m, swap_i, keep_g, fold_g, own_g, send_g, keep_u, fold_u, own_u, send_u, away_o, fold_o, own_o, send_o, away_a, fold_a, own_a, send_a,
     gains_qk, gain_a_grad, ring_out, ring_in, send, recv, *, batch_mask, bit_order, scaling, chunk,
 ):
     links = Links(send, recv, batch_mask)
@@ -1392,30 +1436,34 @@
 
     first = [load(dall_ref, dall), load(wo_ref, wo), load(attn_ref, attn)]
     second = [load(a, b) for a, b in ((q_ref, q), (k_ref, k), (v_ref, v), (ot_ref, ot))]
-    third = [load(a, b) for a, b in ((raw_ref, raw), (cos_ref, cos), (sin_ref, sin), (wa_ref, wa), (xa_ref, xa))]
-    mixed_near, keep_load = load(mixed_ref.at[0], m_near.at[0]), load(keep_u_ref, keep_u)
+    third = [load(a, b) for a, b in ((raw_ref, raw), (table_ref, table), (wa_ref, wa), (xa_ref, xa))]
+    mixed_near, keep_load, keep_g_load = load(mixed_ref.at[0], m_near.at[0]), load(keep_u_ref, keep_u), load(keep_g_ref, keep_g)
     links.greet()
 
-    def settle(src, dst):
-        for i, target in ((0, links.batch), (2, links.both), (1, links.across)):
-            to(target, rows(src, i), rows(dst, i))
-
-    settle(send_g_ref, got_g_ref)
-    up_fold = to(links.seq, away_u_ref, fold_u)
+    def settle(src, dst_b, dst_o):
+        to(links.batch, rows(src, 0), dst_b)
+        to(links.both, rows(src, 2), rows(dst_o, 1))
+        to(links.across, rows(src, 1), rows(dst_o, 0))
+
+    to(links.both, send_g_ref, rows(got_g_o_ref, 1))
+    folds_u = {i: to(links.seq, rows(away_u_ref, i), rows(fold_u, i)) for i in (1, 3)}
+    folds_g = {i: to(links.seq, rows(away_g_ref, i), rows(fold_g, i // 2)) for i in (0, 2)}
     for copy in (*first, *second):
         copy.arrive()
+
+    def total_u(i):
+        return keep_u[pl.ds(i * f, f), :] + fold_u[pl.ds(i * f, f), :].astype(F32)
+
+    def settle_u(i, target, dst):
+        folds_u[i].arrive()
+        send_u[pl.ds((i - 1) * f, f), :] = total_u(i).astype(BF16)
+        to(target, rows(send_u, i - 1), dst)
 
     def d_attn(i):
         at = pl.ds(pl.multiple_of(i * 256, 256), 256)
         value = nn(dall[at, :], wo[...]).astype(BF16)
         do[i // 2, pl.ds((i % 2) * 2, 2)] = value.reshape(2, 128, value.shape[1])
 
-    loop(4, d_attn)
-    attention_back(q, do, k, v, start_ref, ot, l_ref, dq, dk, dv, kt, acc, batch_mask, scaling)
-    kv_out[:, :width] = dk[1].reshape(-1, width).astype(BF16)
-    kv_out[:, width:] = dv[1].reshape(-1, width).astype(BF16)
-    kv = to(links.seq, kv_out, kv_in)
-
     def dall_cols(at, n):
         return dall[:, pl.ds(at, n)]
 
@@ -1426,26 +1474,22 @@
 
     def while_mixed(stage):
         if stage == 0:
+            loop(4, d_attn)
+            attention_back(q, do, k, v, start_ref, ot, l_ref, dq, dk, dv, kt, acc, batch_mask, scaling)
+            kv_out[:, :width] = dk[1].reshape(-1, width).astype(BF16)
+            kv_out[:, width:] = dv[1].reshape(-1, width).astype(BF16)
+            folds.extend(to(links.seq, kv_out.at[pl.ds(i, 128), :], kv_in.at[pl.ds(i, 128), :]) for i in range(0, kv_out.shape[0], 128))
+            keep_load.arrive()
+            settle_u(1, links.batch, got_u_b_ref)
+            settle_u(3, links.both, rows(got_u_o_ref, 1))
             away_rows(dall_cols, attn, away_o)
         if stage == 1:
-            kv.arrive()
-            folds.append(to(links.seq, away_o, fold_o))
-        if stage == 2:
-            up_fold.arrive()
-            keep_load.arrive()
-            own_u[...] = keep_u[:f, :] + fold_u[:f, :].astype(F32)
-
-            def step(i):
-                at = pl.ds(pl.multiple_of(i * f, f), f)
-                here = pl.ds(pl.multiple_of(i * f + f, f), f)
-                send_u[at, :] = (keep_u[here, :] + fold_u[here, :].astype(F32)).astype(BF16)
-
-            loop(3, step)
-            settle(send_u, got_u_ref)
-            load(own_u, own_u_ref)
+            for copy in folds:
+                copy.arrive()
+            folds[:] = [to(links.seq, away_o, fold_o)]
 
     mixed_near.arrive()
-    sum_in(links, (m_near, m_core_in, m_out_y, m_in_y, m_out_t, m_in_t, hold), chunk, None, while_mixed, mixed_ref.at[1])
+    sum_in(links, (m_near, m_core_in, out_y, m_in_y, out_t, m_in_t, hold), chunk, None, while_mixed, mixed_ref.at[1])
     blk = lax.axis_index("blk")
     store_ungrouped(middle_ref[0] + hold[0], mixed_own_ref, blk, bit_order)
     store_ungrouped(middle_ref[1] + hold[1], swap_m, blk, bit_order)
@@ -1460,6 +1504,8 @@
             at = pl.ds(pl.multiple_of((c * 2 + m) * 256, 256), 256)
             pair = pl.ds(m * 2, 2)
             got = kv_in[at, :].astype(F32)
+            cos, sin = table[at, : width // 2], table[at, width // 2 :]
+            cos, sin = jnp.concatenate([cos, cos], axis=1), jnp.concatenate([-sin, sin], axis=1)
             for h in range(heads + 1):
                 cut = slice(h * width, (h + 1) * width)
                 if h < heads:
@@ -1470,7 +1516,7 @@
                 values = raw[at, cut]
                 inverse = inverse_rms(values)
                 normed = values * inverse
-                turned = grad * cos[at, :] - pltpu.roll(grad, width // 2, 1) * sin[at, :]
+                turned = grad * cos - pltpu.roll(grad, width // 2, 1) * sin
                 row = 0 if h < heads else 1
                 gains_qk[row : row + 1, :] += jnp.sum(turned * normed, axis=0, keepdims=True)
                 scaled = turned * gain
@@ -1484,16 +1530,30 @@
     def while_input(stage):
         if stage == 0:
             away_rows(xa_cols, d_qkv, away_a)
-            folds.append(to(links.seq, away_a, fold_a))
+            folds.extend(to(links.seq, rows(away_a, i), rows(fold_a, i)) for i in (1, 3, 0, 2))
             folds[0].arrive()
             keep_rows(dall_cols, attn, fold_o, own_o, send_o)
-            settle(send_o, got_o_ref)
+            settle(send_o, got_o_b_ref, got_o_o_ref)
             load(own_o, own_o_ref)
+        if stage == 1:
+            folds_u.update({i: to(links.seq, rows(away_u_ref, i), rows(fold_u, i)) for i in (2, 0)})
+            for copy in (*folds_g.values(), keep_g_load):
+                copy.arrive()
+            for i, ref in ((0, own_g), (1, send_g)):
+                here = pl.ds(i * f, f)
+                ref[...] = (keep_g[here, :] + fold_g[here, :].astype(F32)).astype(ref.dtype)
+            load(own_g, own_g_ref)
+            to(links.across, send_g, rows(got_g_o_ref, 0))
         if stage == 2:
-            folds[1].arrive()
+            for copy in folds:
+                copy.arrive()
             keep_rows(xa_cols, d_qkv, fold_a, own_a, send_a)
-            settle(send_a, got_a_ref)
+            settle(send_a, got_a_b_ref, got_a_o_ref)
             load(own_a, own_a_ref)
+            settle_u(2, links.across, rows(got_u_o_ref, 0))
+            folds_u[0].arrive()
+            own_u[...] = total_u(0)
+            load(own_u, own_u_ref)
 
     sum_in(links, (p, core_in, out_y, in_y, out_t, in_t, hold), chunk, input_partial, while_input)
     for m in range(2):
@@ -1524,7 +1584,8 @@
     like, held = jax.ShapeDtypeStruct, pltpu.VMEM
     in_vmem = ("low", "middle", "d_middle", "gain", "gain_m_grad", "gain_q", "gain_k", "start", "l")
     in_hbm = (
-        "dall", "w_out", "attn", "q", "k", "v", "ot", "raw", "cos", "sin", "wa", "xa", "mixed", "send_g", "keep_u", "away_u",
+        "dall", "w_out", "attn", "q", "k", "v", "ot", "raw", "table", "wa", "xa", "mixed", "send_g", "keep_g", "away_g", "keep_u",
+        "away_u",
     )
     total = 2 * width + 2 * head_size
     lanes = 2 * 2 * 128
@@ -1536,20 +1597,20 @@
     return pl.pallas_call(
         functools.partial(last_kernel, batch_mask=batch_mask, bit_order=bit_order, scaling=scaling, chunk=2 * width // 8),
         in_specs=[vmem] * len(in_vmem) + [hbm] * len(in_hbm),
-        out_specs=[vmem, hbm, vmem, hbm, vmem] + [hbm] * 7,
+        out_specs=[vmem, hbm, vmem, hbm, vmem] + [hbm] * 11,
         out_shape=[
             like((rows, width), BF16),
             like((rows, width), BF16),
             like((rows, width), F32),
             like((rows, width), BF16),
             like(sums, F32),
-            like((3 * f, ff), BF16),
             like((f, ff), F32),
-            like((3 * f, ff), BF16),
-            like((f, n_a), F32),
-            like((3 * f, n_a), BF16),
-            like((f, columns), F32),
-            like((3 * f, columns), BF16),
+            like((2 * f, ff), BF16),
+            *[
+                like((m * f, n), dtype)
+                for n in (ff, n_a, columns)
+                for m, dtype in ((1, F32), (1, BF16), (2, BF16))
+            ],
         ],
         scratch_shapes=[
             held((tokens, width), BF16),
@@ -1561,7 +1622,6 @@
             held(k.shape, BF16),
             held((4, head_size, lanes), F32),
             held(raw.shape, F32),
-            held((tokens, head_size), F32),
             held((tokens, head_size), F32),
             held(wa.shape, BF16),
             held((tokens, width), BF16),
@@ -1577,9 +1637,13 @@
             *sum_bufs,
             held(share, F32),
             held(half_full, BF16),
-            *sum_bufs,
+            *[sum_bufs[i] for i in (0, 2, 4)],
             held((rows, width), BF16),
             held((rows, width), BF16),
+            held((2 * f, ff), F32),
+            held((2 * f, ff), BF16),
+            held((f, ff), F32),
+            held((f, ff), BF16),
             held((4 * f, ff), F32),
             held((4 * f, ff), BF16),
             *own_and_send(ff),
@@ -1601,6 +1665,293 @@
         ),
         cost_estimate=TINY_COST,
     )(*[arrays[n] for n in (*in_vmem, *in_hbm)])
+
+
+def attention(q, k, v, start, out, ot, total_ref, vt, acc, total, batch_mask, scaling):
+    parts, _, blocks, half, width = k.shape
+    heads = q.shape[-1] // width
+    lanes = heads * 2 * half
+
+    def turn(kb):
+        vt[kb] = key_rows(v, kb // blocks, kb % blocks).T
+
+    loop(parts * blocks, turn)
+
+    def per_query(i):
+        q_rows = head_rows(q, i, heads, width)
+        first = start[i]
+        acc[...] = jnp.zeros_like(acc)
+        total[...] = jnp.zeros_like(total)
+        q_block = block_of(i, batch_mask)
+
+        def per_key(kb):
+            part, block = kb // blocks, kb % blocks
+            k_block = block_of(block, batch_mask) ^ (part << SEQ_BIT)
+
+            def add(diagonal):
+                tokens = key_tokens(k_block, half)
+                allowed = tokens >= first
+                if diagonal:
+                    allowed = allowed & (tokens <= query_tokens(q_block, half, lanes))
+                score = nt(key_rows(k, part, block), q_rows) * (scaling * LOG2E)
+                e = jnp.where(allowed, jnp.exp2(score), 0.0)
+                total[...] += jnp.sum(e, axis=0, keepdims=True)
+                acc[...] += nn(vt[kb], e.astype(BF16))
+
+            @pl.when(k_block < q_block)
+            def _():
+                add(False)
+
+            @pl.when(k_block == q_block)
+            def _():
+                add(True)
+
+        loop(parts * blocks, per_key)
+        value = acc[...] / total[...]
+        ot[i] = value
+        total_ref[i] = total[...]
+        rows = value.T
+        for h in range(heads):
+            for c in range(2):
+                at = (h * 2 + c) * half
+                out[c, i, :, h * width : (h + 1) * width] = rows[at : at + half].astype(BF16)
+
+    loop(blocks, per_query)
+
+
+def first_kernel(
+    gains_ref, gain_q_ref, gain_k_ref, table_ref, start_ref,
+    hid_ref, cot_ref, wq_ref, wk_ref, wv_ref, wo_ref, wd_ref, wg_ref,
+    low_ref, cot_low_ref, gains_out_ref, l_ref,
+    xa_ref, call_ref, wa_out, wo_out, wd_out, wg_out, q_ref, k_ref, v_ref, raw_ref, attn_ref, ot_ref,
+    x_in, c_in, xa_s, xa, wa, wb, q, k, v, raw, out, ot, vt, acc, total, send, recv, *, batch_mask, bit_order, scaling, chunk,
+):
+    links = Links(send, recv, batch_mask)
+    to, load = links.to, links.load
+    blk = lax.axis_index("blk")
+    batch = bit_of(blk, bit_order[0])
+    width = k.shape[-1]
+    heads = q.shape[-1] // width
+    f = wa.shape[0] // 8
+    a_params, at = [], 0
+    for ref in (wq_ref, wk_ref, wv_ref):
+        n = ref.shape[1] // 2
+        a_params.append((ref, at, n))
+        at += n
+
+    def rows(ref, i):
+        return ref.at[pl.ds(i * f, f), :]
+
+    x_own = load(hid_ref.at[batch], x_in.at[0])
+    c_own = load(cot_ref.at[batch], c_in.at[0])
+    a_own = [load(links.half(ref, 0), wa.at[pl.ds(0, f), pl.ds(start, n)]) for ref, start, n in a_params]
+    a_other = [load(links.half(ref, 1), wb.at[:, pl.ds(start, n)]) for ref, start, n in a_params]
+    links.greet()
+    x_far = to(links.batch, hid_ref.at[1 - batch], x_in.at[1])
+    for copy in (*a_own, *a_other):
+        copy.arrive()
+    a_t = to(links.across, wb, rows(wa, 2))
+    a_rest = [to(links.seq, rows(wa, 0), rows(wa, 4))]
+    to(links.seq, links.half(wo_ref, 0), rows(wo_out, 4))
+    load(links.half(wo_ref, 0), rows(wo_out, 0))
+    to(links.seq, links.half(wd_ref, 0), rows(wd_out, 4))
+    to(links.seq, links.half(wg_ref, 0), rows(wg_out, 4))
+    down_t = to(links.across, links.half(wd_ref, 1), rows(wd_out, 2))
+    out_rows = [to(links.across, links.half(wo_ref, 1), rows(wo_out, 2))]
+    n_blocks = 1 << len(bit_order)
+    n = x_in.shape[-1] // n_blocks
+
+    def regroup(src, dst, lead):
+        for p in range(n_blocks):
+            cut = pl.ds(pl.multiple_of(place_of_block(blk, bit_order, p) * n, n), n)
+            dst[(*lead, pl.ds(p * n, n))] = src[(*lead, cut)]
+
+    all_rows = (slice(None), slice(None))
+    regroup(gains_ref, gains_out_ref, (slice(None),))
+    x_own.arrive()
+    x_far.arrive()
+    a_far = {1: to(links.batch, rows(wa, 0), rows(wa, 1)), 3: to(links.both, wb, rows(wa, 3))}
+    c_far = to(links.batch, cot_ref.at[1 - batch], c_in.at[1])
+    to(links.batch, links.half(wd_ref, 0), rows(wd_out, 1))
+    regroup(x_in, low_ref, all_rows)
+    for m in range(2):
+        value = low_ref[m].astype(F32)
+        xa_s[m] = (value * inverse_rms(value) * gains_out_ref[0:1, :]).astype(BF16)
+
+    def while_xa(stage):
+        if stage == 0:
+            a_t.arrive()
+            a_rest.append(to(links.seq, rows(wa, 2), rows(wa, 6)))
+        if stage == 1:
+            for i, copy in a_far.items():
+                copy.arrive()
+                a_rest.append(to(links.seq, rows(wa, i), rows(wa, i + 4)))
+            out_rows.append(to(links.batch, links.half(wo_ref, 0), rows(wo_out, 1)))
+            out_rows.append(to(links.both, links.half(wo_ref, 1), rows(wo_out, 3)))
+            to(links.both, links.half(wd_ref, 1), rows(wd_out, 3))
+            c_own.arrive()
+            c_far.arrive()
+            regroup(c_in, cot_low_ref, all_rows)
+
+    spread_in(links, xa_s, xa, chunk, while_xa)
+    load(xa, xa_ref)
+
+    def prepare_rows(i):
+        c, m = i // 2, i % 2
+        pair = pl.ds(m * 2, 2)
+        at = pl.ds(pl.multiple_of(i * 256, 256), 256)
+        acc_rows = nn(rows_of(xa, i), wa[...])
+        raw[at, :] = acc_rows[:, : (heads + 1) * width]
+        cos, sin = table_ref[at, : width // 2], table_ref[at, width // 2 :]
+        cos, sin = jnp.concatenate([cos, cos], axis=1), jnp.concatenate([-sin, sin], axis=1)
+        for h in range(heads + 1):
+            part = acc_rows[:, h * width : (h + 1) * width]
+            scaled = part * inverse_rms(part) * (gain_q_ref if h < heads else gain_k_ref)[...]
+            turned = (scaled * cos + pltpu.roll(scaled, width // 2, 1) * sin).astype(BF16).reshape(2, 128, width)
+            if h < heads:
+                q[c, pair, :, h * width : (h + 1) * width] = turned
+            else:
+                k[0, c, pair] = turned
+        v[0, c, pair] = acc_rows[:, (heads + 1) * width :].astype(BF16).reshape(2, 128, width)
+
+    kv = []
+
+    def while_cot(stage):
+        if stage == 0:
+            for copy in a_rest:
+                copy.arrive()
+            loop(4, prepare_rows)
+            kv.extend(
+                to(links.seq, ref.at[0, c, i], ref.at[1, c, i]) for ref in (k, v) for c in range(2) for i in range(4)
+            )
+            load(wa, wa_out)
+            load(raw, raw_ref)
+            load(q, q_ref)
+            down_t.arrive()
+            to(links.seq, rows(wd_out, 2), rows(wd_out, 6))
+        if stage == 1:
+            to(links.across, links.half(wg_ref, 1), rows(wg_out, 2))
+            for i, copy in zip((2, 1, 3), out_rows):
+                copy.arrive()
+                to(links.seq, rows(wo_out, i), rows(wo_out, i + 4))
+            for copy in kv:
+                copy.arrive()
+            load(k, k_ref)
+            load(v, v_ref)
+            attention(q, k, v, start_ref, out, ot, l_ref, vt, acc, total, batch_mask, scaling)
+            load(out, attn_ref)
+            load(ot, ot_ref)
+
+    spread_in(links, cot_low_ref, call_ref, chunk, while_cot, in_vmem=False)
+    links.finish()
+
+
+def first_call(batch_mask, bit_order, scaling, arrays, collective_id):
+    hid, wq, wk, wv, wo, wd, wg = (arrays[n] for n in ("hidden", "wq", "wk", "wv", "wo", "wd", "wg"))
+    _, rows, width = hid.shape
+    tokens, head_size = 16 * rows, arrays["gain_q"].shape[1]
+    columns, n_a = wq.shape[1] // 2, (wq.shape[1] + wk.shape[1] + wv.shape[1]) // 2
+    heads = columns // head_size
+    half, lanes = tokens // 8, heads * tokens // 4
+    share, full = (2, rows, width), (2, 2, 2, 2, rows, width)
+    vmem, hbm = pl.BlockSpec(memory_space=pltpu.VMEM), pl.BlockSpec(memory_space=pltpu.HBM)
+    like, held = jax.ShapeDtypeStruct, pltpu.VMEM
+    in_vmem = ("gains", "gain_q", "gain_k", "table", "start")
+    in_hbm = ("hidden", "cotangent", "wq", "wk", "wv", "wo", "wd", "wg")
+    q_shape, k_shape = (2, 4, half, columns), (2, 2, 4, half, head_size)
+    ot_shape, raw_shape = (4, head_size, lanes), (tokens, (heads + 1) * head_size)
+    return pl.pallas_call(
+        functools.partial(first_kernel, batch_mask=batch_mask, bit_order=bit_order, scaling=scaling, chunk=2 * width // 8),
+        in_specs=[vmem] * len(in_vmem) + [hbm] * len(in_hbm),
+        out_specs=[vmem] * 4 + [hbm] * 12,
+        out_shape=[
+            like(share, BF16),
+            like(share, BF16),
+            like((2, width), F32),
+            like((4, 1, lanes), F32),
+            like(full, BF16),
+            like(full, BF16),
+            like((width, n_a), BF16),
+            like((width, columns), BF16),
+            like((width, wd.shape[1] // 2), BF16),
+            like((width, wg.shape[1] // 2), BF16),
+            like(q_shape, BF16),
+            like(k_shape, BF16),
+            like(k_shape, BF16),
+            like(raw_shape, F32),
+            like(q_shape, BF16),
+            like(ot_shape, F32),
+        ],
+        scratch_shapes=[
+            held(share, BF16),
+            held(share, BF16),
+            held(share, BF16),
+            held(full, BF16),
+            held((width, n_a), BF16),
+            held((width // 8, n_a), BF16),
+            held(q_shape, BF16),
+            held(k_shape, BF16),
+            held(k_shape, BF16),
+            held(raw_shape, F32),
+            held(q_shape, BF16),
+            held(ot_shape, F32),
+            held((8, head_size, 2 * half), BF16),
+            held((head_size, lanes), F32),
+            held((1, lanes), F32),
+            pltpu.SemaphoreType.DMA((96,)),
+            pltpu.SemaphoreType.DMA((96,)),
+        ],
+        compiler_params=pltpu.CompilerParams(
+            collective_id=collective_id, has_side_effects=True, vmem_limit_bytes=56 * MIB
+        ),
+        cost_estimate=TINY_COST,
+    )(*[arrays[n] for n in (*in_vmem, *in_hbm)])
+
+
+def finish_kernel(place_ref, mixed_own, mixed_got, input_own, input_got, *refs, sources, widths):
+    ins, (mixed_ref, input_ref, *outs) = refs[: 3 * sources], refs[3 * sources :]
+    place, batch, k = place_ref[0], place_ref[1], 0
+    mixed_ref[batch] = mixed_own[...]
+    mixed_ref[1 - batch] = mixed_got[...]
+    input_ref[batch] = input_own[...]
+    input_ref[1 - batch] = input_got[...].astype(F32)
+    for own, by_batch, by_other in zip(ins[::3], ins[1::3], ins[2::3]):
+        at = 0
+        while at < own.shape[1]:
+            w, cut = widths[k], slice(at, at + widths[k])
+            mine = pl.ds(pl.multiple_of(place * w, w), w)
+            theirs = pl.ds(pl.multiple_of((1 - place) * w, w), w)
+            outs[k][:, mine] = own[:, cut] + by_batch[:, cut].astype(F32)
+            outs[k][:, theirs] = by_other[0, :, cut].astype(F32) + by_other[1, :, cut].astype(F32)
+            at += w
+            k += 1
+
+
+def finish_call(places, rows, sources, widths):
+    steps = 4
+    f, (n_rows, width) = sources[0][0].shape[0], rows[0].shape
+    tile, row_tile = f // steps, n_rows // steps
+    by_rows = lambda t, n: pl.BlockSpec((t, n), lambda i: (i, 0))
+    by_pairs = lambda t, n: pl.BlockSpec((2, t, n), lambda i: (0, i, 0))
+    flat, specs = [], []
+    for own, by_batch, by_other in sources:
+        n = own.shape[1]
+        flat += [own, by_batch, by_other.reshape(2, f, n)]
+        specs += [by_rows(tile, n), by_rows(tile, n), by_pairs(tile, n)]
+    like = jax.ShapeDtypeStruct
+    return pl.pallas_call(
+        functools.partial(finish_kernel, sources=len(sources), widths=widths),
+        grid=(steps,),
+        in_specs=[pl.BlockSpec(memory_space=pltpu.SMEM), *[by_rows(row_tile, width)] * 4, *specs],
+        out_specs=[*[by_pairs(row_tile, width)] * 2, *[by_rows(tile, 2 * w) for w in widths]],
+        out_shape=[
+            like((2, n_rows, width), BF16),
+            like((2, n_rows, width), F32),
+            *[like((f, 2 * w), F32) for w in widths],
+        ],
+        compiler_params=pltpu.CompilerParams(vmem_limit_bytes=60 * MIB),
+        cost_estimate=TINY_COST,
+    )(places.astype(jnp.int32), *rows, *flat)
 
 
 def local(
@@ -1801,6 +2152,7 @@
     inverse_freq = THETA ** (-jnp.arange(head_size // 2, dtype=F32) / (head_size // 2))
     angles = position.astype(F32)[:, None] * inverse_freq[None, :]
     cosine, sine = jnp.cos(angles), jnp.sin(angles)
+    table = jnp.concatenate([cosine, sine], axis=1)
     cosine = jnp.concatenate([cosine, cosine], axis=1)
     sine = jnp.concatenate([-sine, sine], axis=1)
 
@@ -1823,85 +2175,114 @@
             [lax.dynamic_slice_in_dim(w, which * (w.shape[1] // 2), w.shape[1] // 2, 1) for w in weights], axis=1
         )
 
-    mine, theirs = split_batch(hidden_in)
-    other = over_blk(theirs, b_mask)
-    a_own, a_other = halves(a_weights, tensor), halves(a_weights, 1 - tensor)
-    a_by_t = over_blk(a_other, t_mask)
-    a_by_b = over_blk(a_own, b_mask)
-    early = over_blk(jnp.concatenate([a_own, halves((down_weight,), tensor)], axis=1), x_mask)
-    (mine, other, cosine, sine, start_lanes, meta) = pin((mine, other, cosine, sine, start_lanes, meta))
-    if aligned:
-        x_low, xa, gains_in = enter(blk, bit_order, mine, other, gains_in)
-        gain_a, gain_m = gains_in[0], gains_in[1]
+    if extra_bits:
+        mine, theirs = split_batch(hidden_in)
+        other = over_blk(theirs, b_mask)
+        a_own, a_other = halves(a_weights, tensor), halves(a_weights, 1 - tensor)
+        a_by_t = over_blk(a_other, t_mask)
+        a_by_b = over_blk(a_own, b_mask)
+        early = over_blk(jnp.concatenate([a_own, halves((down_weight,), tensor)], axis=1), x_mask)
+        (mine, other, cosine, sine, start_lanes, meta) = pin((mine, other, cosine, sine, start_lanes, meta))
+        if aligned:
+            x_low, xa, gains_in = enter(blk, bit_order, mine, other, gains_in)
+            gain_a, gain_m = gains_in[0], gains_in[1]
+        else:
+            gains_in = regroup(gains_in)
+            gain_a, gain_m = gains_in[0], gains_in[1]
+            x_low = regroup(jnp.concatenate([mine, other], axis=0))
+            x_wide = x_low.astype(F32)
+            xa = (x_wide * rms(x_wide) * gain_a).astype(BF16)
+
+        plan = Plan()
+        a_columns = a_own.shape[1]
+        w_a = fresh_for(plan, a_weights)
+        by_tb = plan.copy((plan.read(a_other), everything), (w_a, rows_at(3)), b_mask | t_mask)
+        lay(plan, a_by_t, w_a, 2, onward=True)
+        lay(plan, a_by_b, w_a, 1, onward=True)
+        lay(plan, a_own, w_a, 0)
+        lay(plan, early, w_a, 4, columns=(0, a_columns))
+        here, cot_out = plan.read(cotangent), plan.fresh((2, local_rows, width), BF16)
+        plan.copy(
+            (here, lambda ref: ref.at[1 - bit_of(lax.axis_index("blk"), batch_bit)]),
+            (cot_out, lambda ref: ref.at[1]),
+            b_mask,
+            point=1,
+        )
+        plan.local(
+            (here, lambda ref: ref.at[bit_of(lax.axis_index("blk"), batch_bit)]),
+            (cot_out, lambda ref: ref.at[0]),
+            (local_rows, width),
+        )
+        w_out = fresh_for(plan, (out_weight,))
+        send_over(plan, out_weight, w_out, 1, 1)
+        send_over(plan, out_weight, w_out, 3, 1)
+        send_over(plan, out_weight, w_out, 2, 1)
+        keep_own(plan, out_weight, w_out, 0)
+        w_down = fresh_for(plan, (down_weight,))
+        send_over(plan, down_weight, w_down, 2, 1)
+        keep_own(plan, down_weight, w_down, 0, onward=False)
+        lay(plan, early, w_down, 4, columns=(a_columns, ff))
+        w_gate = fresh_for(plan, (gate_weight,))
+        keep_own(plan, gate_weight, w_gate, 1)
+        send_on(plan, w_a, (3,), 2, after=by_tb)
+        xa, (w_qkv, cot, w_out, w_down, w_gate) = spread(xa, plan, limit=56 * MIB)
+        w_qkv = whole_weight(w_qkv)
+        cot = cot.reshape(2 * local_rows, width)
+        cot = enter(blk, bit_order, cot)[0] if aligned else regroup(cot)
+        query, key_value, raw = prepare(xa, w_qkv, cosine, sine, gain_q, gain_k, heads)
+
+        plan = Plan()
+        kv_out = plan.fresh(key_value.shape, BF16)
+        plan.copy((plan.read(key_value), everything), (kv_out, everything), x_mask)
+        w_out = plan.through(w_out)
+        send_on(plan, w_out, (1, 2, 3), 0)
+        w_down = plan.through(w_down)
+        send_over(plan, down_weight, w_down, 1, 0)
+        send_over(plan, down_weight, w_down, 3, 0)
+        send_on(plan, w_down, (2,), 1)
+        w_gate = plan.through(w_gate)
+        send_over(plan, gate_weight, w_gate, 2, 1)
+        cot_all, (kv_x, w_out, w_down, w_gate) = spread(cot, plan)
+        w_out = whole_weight(w_out)
+        key_value = [key_value, kv_x]
+        for b in extra_bits:
+            key_value = key_value + [over_blk(c, 1 << b) for c in key_value]
+        key_value = jnp.stack(key_value)
+        keys = key_value[..., :head_size].reshape(parts, 2, 4, half, head_size)
+        values = key_value[..., head_size:].reshape(parts, 2, 4, half, head_size)
+        query = query.reshape(2, 4, half, q_columns)
+        attn, attn_t, total_e = attend(meta, query, keys, values, start_lanes, scaling)
+        attn = attn.reshape(tokens, q_columns)
+
+        x_low = x_low.reshape(share)
     else:
-        gains_in = regroup(gains_in)
-        gain_a, gain_m = gains_in[0], gains_in[1]
-        x_low = regroup(jnp.concatenate([mine, other], axis=0))
-        x_wide = x_low.astype(F32)
-        xa = (x_wide * rms(x_wide) * gain_a).astype(BF16)
-
-    plan = Plan()
-    a_columns = a_own.shape[1]
-    w_a = fresh_for(plan, a_weights)
-    by_tb = plan.copy((plan.read(a_other), everything), (w_a, rows_at(3)), b_mask | t_mask)
-    lay(plan, a_by_t, w_a, 2, onward=True)
-    lay(plan, a_by_b, w_a, 1, onward=True)
-    lay(plan, a_own, w_a, 0)
-    lay(plan, early, w_a, 4, columns=(0, a_columns))
-    here, cot_out = plan.read(cotangent), plan.fresh((2, local_rows, width), BF16)
-    plan.copy(
-        (here, lambda ref: ref.at[1 - bit_of(lax.axis_index("blk"), batch_bit)]),
-        (cot_out, lambda ref: ref.at[1]),
-        b_mask,
-        point=1,
-    )
-    plan.local(
-        (here, lambda ref: ref.at[bit_of(lax.axis_index("blk"), batch_bit)]),
-        (cot_out, lambda ref: ref.at[0]),
-        (local_rows, width),
-    )
-    w_out = fresh_for(plan, (out_weight,))
-    send_over(plan, out_weight, w_out, 1, 1)
-    send_over(plan, out_weight, w_out, 3, 1)
-    send_over(plan, out_weight, w_out, 2, 1)
-    keep_own(plan, out_weight, w_out, 0)
-    w_down = fresh_for(plan, (down_weight,))
-    send_over(plan, down_weight, w_down, 2, 1)
-    keep_own(plan, down_weight, w_down, 0, onward=False)
-    lay(plan, early, w_down, 4, columns=(a_columns, ff))
-    w_gate = fresh_for(plan, (gate_weight,))
-    keep_own(plan, gate_weight, w_gate, 1)
-    send_on(plan, w_a, (3,), 2, after=by_tb)
-    xa, (w_qkv, cot, w_out, w_down, w_gate) = spread(xa, plan, limit=56 * MIB)
-    w_qkv = whole_weight(w_qkv)
-    cot = cot.reshape(2 * local_rows, width)
-    cot = enter(blk, bit_order, cot)[0] if aligned else regroup(cot)
-    query, key_value, raw = prepare(xa, w_qkv, cosine, sine, gain_q, gain_k, heads)
-
-    plan = Plan()
-    kv_out = plan.fresh(key_value.shape, BF16)
-    plan.copy((plan.read(key_value), everything), (kv_out, everything), x_mask)
-    w_out = plan.through(w_out)
-    send_on(plan, w_out, (1, 2, 3), 0)
-    w_down = plan.through(w_down)
-    send_over(plan, down_weight, w_down, 1, 0)
-    send_over(plan, down_weight, w_down, 3, 0)
-    send_on(plan, w_down, (2,), 1)
-    w_gate = plan.through(w_gate)
-    send_over(plan, gate_weight, w_gate, 2, 1)
-    cot_all, (kv_x, w_out, w_down, w_gate) = spread(cot, plan)
-    w_out = whole_weight(w_out)
-    key_value = [key_value, kv_x]
-    for b in extra_bits:
-        key_value = key_value + [over_blk(c, 1 << b) for c in key_value]
-    key_value = jnp.stack(key_value)
-    keys = key_value[..., :head_size].reshape(parts, 2, 4, half, head_size)
-    values = key_value[..., head_size:].reshape(parts, 2, 4, half, head_size)
-    query = query.reshape(2, 4, half, q_columns)
-    attn, attn_t, total_e = attend(meta, query, keys, values, start_lanes, scaling)
-    attn = attn.reshape(tokens, q_columns)
-
-    x_low = x_low.reshape(share)
+        (
+            x_low, cot, gains_group, total_e, xa, cot_all, w_qkv, w_out, w_down, w_gate, query, keys, values, raw, attn, attn_t,
+        ) = first_call(
+            b_mask,
+            bit_order,
+            scaling,
+            dict(
+                gains=gains_in,
+                gain_q=gain_q,
+                gain_k=gain_k,
+                table=table,
+                start=start_lanes,
+                hidden=hidden_in,
+                cotangent=cotangent,
+                wq=query_weight,
+                wk=key_matrix,
+                wv=value_matrix,
+                wo=out_weight,
+                wd=down_weight,
+                wg=gate_weight,
+            ),
+            next(ids),
+        )
+        gain_a, gain_m = gains_group[0], gains_group[1]
+        xa, cot_all = xa.reshape(tokens, width), cot_all.reshape(tokens, width)
+        attn = attn.reshape(tokens, q_columns)
+
     if extra_bits:
         plan = Plan()
         w_down = plan.through(w_down)
@@ -1986,13 +2367,12 @@
         own_gate, away_gate = to_settle(keep_gate, gate_x)
     else:
         (
-            middle, d_middle, gain_m_grad, d_mid_all, mixed_partial, own_down, got_down, own_gate, away_gate, keep_up, away_up,
+            middle, d_middle, gain_m_grad, d_mid_all, mixed_partial, own_down, down_b, down_o, gate_b, send_gate, keep_gate, away_gate, keep_up, away_up,
         ) = middle_call(
-            b_mask, x_low, cot.reshape(share), gain_m[None], attn, w_out, cot_all, w_down, w_gate, gate_weight, up_weight, next(ids)
+            b_mask, x_low, cot.reshape(share), gain_m[None], attn, w_out, cot_all, w_down, w_gate, (down_weight, gate_weight, up_weight), next(ids)
         )
         d_mid_all = d_mid_all.reshape(tokens, width)
         mixed_partial = mixed_partial.reshape(tokens, width)
-        (g_down,) = settled([(own_down, got_down)], (ff,))
         up_x = None
     if extra_bits:
         d_attn = nn(d_mid_all, w_out).astype(BF16).reshape(2, 4, half, q_columns)
@@ -2073,7 +2453,7 @@
         gains = jnp.split(sums.reshape(-1), [width, width + head_size, width + 2 * head_size])
     else:
         (
-            mixed_own, mixed_got, input_own, input_got, sums, got_gate, own_up, got_up, own_qkv, got_a, own_out, got_o,
+            mixed_own, mixed_got, input_own, input_got, sums, own_gate, gate_o, own_up, up_b, up_o, own_qkv, a_b, a_o, own_out, out_b, out_o,
         ) = last_call(
             b_mask,
             bit_order,
@@ -2096,23 +2476,30 @@
                 v=values,
                 ot=attn_t,
                 raw=raw,
-                cos=cosine,
-                sin=sine,
+                table=table,
                 wa=w_qkv,
                 xa=xa,
                 mixed=mixed_partial.reshape(2, 2, 2, 2, local_rows, width),
-                send_g=away_gate,
+                send_g=send_gate,
+                keep_g=keep_gate,
+                away_g=away_gate,
                 keep_u=keep_up,
                 away_u=away_up,
             ),
             next(ids),
         )
-        g_gate, g_up, g_query, g_key, g_value, g_out = settled(
-            [(own_gate, got_gate), (own_up, got_up), (own_qkv, got_a), (own_out, got_o)],
-            (ff, ff, q_columns, k_columns, k_columns, q_columns),
+        mixed, input_grad, g_down, g_gate, g_up, g_query, g_key, g_value, g_out = finish_call(
+            jnp.stack([tensor, batch]),
+            (mixed_own, mixed_got, input_own, input_got),
+            [
+                (own_down, down_b, down_o),
+                (own_gate, gate_b, gate_o),
+                (own_up, up_b, up_o),
+                (own_qkv, a_b, a_o),
+                (own_out, out_b, out_o),
+            ],
+            (ff, ff, ff, q_columns, k_columns, k_columns, q_columns),
         )
-        mixed = in_order(batch, mixed_own[None], mixed_got[None], 0)
-        input_grad = in_order(batch, input_own[None], input_got.astype(F32)[None], 0)
         gains = jnp.split(sums.reshape(-1), [width, width + head_size, width + 2 * head_size])
     return (
         mixed,

time: 476 us -> 438 us (0.920)
  local copies, waits for them, and re-layouts: 19 us -> 4.65 us
  waiting for transfers between devices: 14.2 us -> 0 us
  starting transfers between devices: 7.7 us -> 0 us
  Pallas kernels: 420 us -> 425 us
  other arithmetic: 10.7 us -> 5.89 us
    pallas_call x8 -> x2, Pallas kernels: 102 us -> 123 us  [the longest x1 116 us: first_call(): pl.pallas_call(functools.partial(first_kernel, batch_mask=batch_mask, bit...]
    ppermute x4 -> x0, waiting for transfers between devices: 14.2 us -> none  [over_blk(): return lax.ppermute(value, 'blk', [(i, i ^ mask) for i in range(count)])]
    unnamed x98 -> x4, local copies, waits for them, and re-layouts: 13.5 us -> 0.01 us
    pallas_call x1, Pallas kernels: 142 us -> 133 us  [last_call(): pl.pallas_call(functools.partial(last_kernel, batch_mask=batch_mask, bit_...]
    ppermute x4 -> x0, starting transfers between devices: 7.7 us -> none  [over_blk(): return lax.ppermute(value, 'blk', [(i, i ^ mask) for i in range(count)])]
    pallas_call x1, Pallas kernels: 175 us -> 169 us  [middle_call(): pl.pallas_call(functools.partial(middle_kernel, batch_mask=batch_mask, ch...]
  transfers between devices with their start and end apart: 4 -> 0, of which waited for: 1 -> 0; matrix products, arithmetic and copies ran while one was open for 1% -> 0% of each run, Pallas kernels for 0% -> 0%
where the time goes in v7:
time: 438 us; the launch traced here: 437 us
  Pallas kernels  425 us (97%)
  other arithmetic  5.89 us (1%)
  local copies, waits for them, and re-layouts  4.65 us (1%)
    pallas_call x1, Pallas kernels, middle_call(): pl.pallas_call(functools.partial(middle_kernel, batch_mask=batch_mask, ch...  169 us
    pallas_call x1, Pallas kernels, last_call(): pl.pallas_call(functools.partial(last_kernel, batch_mask=batch_mask, bit_...  133 us
    pallas_call x1, Pallas kernels, first_call(): pl.pallas_call(functools.partial(first_kernel, batch_mask=batch_mask, bit...  116 us

profile of v7, /device:TPU:0, one launch (start us, length us, event | category | flops | bytes accessed | tf_op | source)
XLA Modules:
  0.0 436.6 jit_solution(10805300548781469977)
XLA Ops:
  0.6 0.0 copy-start
  0.7 0.7 pad_add_fusion.place_ref
  1.3 0.0 copy-done
  1.3 0.2 reduce-window.8
  1.6 0.1 xor_multiply_fusion
  1.7 0.1 mul.41
  1.7 1.2 bitcast_convert_fusion
  2.9 0.1 broadcast_add_fusion
  3.0 0.1 select_reduce_fusion
  3.1 0.1 subtract_convert_fusion
  3.2 0.6 tile.12.start_ref
  3.8 0.7 stack.21
  4.5 0.7 stack.22
  5.2 0.6 maximum_convert_fusion.gains_ref
  5.8 1.9 multiply_cosine_fusion
  7.7 1.0 pad_maximum_fusion.table_ref
  8.7 116.1 %shard_map.237 = (bf16[2,64,2048]{2,1,0:T(8,128)(2,1)}, bf16[2,64,2048]{2,1,0:T(8,128)(2,1)}, f32[2,2048]{1,0:T(2,128)}, f32[4,1,512]{2,1,0:T(1,128)}, bf16[2,2,...) custom-call(f32[2,2048]{1,0:T(2,128)} %maximum_convert_fusion.gains_, ...), custom_call_target="tpu_custom_call" | custom-call | tf_op jit(solution)/shard_map/pallas_call | solution.py:1863
  124.8 1.4 fusion.6
  126.2 169.2 %shard_map.238 = (f32[2,64,2048]{2,1,0:T(8,128)}, f32[2,64,2048]{2,1,0:T(8,128)}, f32[1,2048]{1,0:T(1,128)}, bf16[2,2,2,2,64,2048]{5,4,3,2,1,0:T(8,128)(2,1)}, b...) custom-call(bf16[2,64,2048]{2,1,0:T(8,128)(2,1)} %get-tuple-element., ...), custom_call_target="tpu_custom_call" | custom-call | tf_op jit(solution)/shard_map/pallas_call | solution.py:1287
  295.4 133.1 %shard_map.239 = (bf16[64,2048]{1,0:T(8,128)(2,1)}, bf16[64,2048]{1,0:T(8,128)(2,1)}, f32[64,2048]{1,0:T(8,128)}, bf16[64,2048]{1,0:T(8,128)(2,1)}, f32[1,4352]{...) custom-call(bf16[2,64,2048]{2,1,0:T(8,128)(2,1)} %get-tuple-element., ...), custom_call_target="tpu_custom_call" | custom-call | tf_op jit(solution)/shard_map/pallas_call | solution.py:1597
  428.5 0.0 copy-start.1
  428.5 7.0 %shard_map.240 = (bf16[2,64,2048]{2,1,0:T(8,128)(2,1)}, f32[2,64,2048]{2,1,0:T(8,128)}, f32[256,1536]{1,0:T(8,128)}, f32[256,1536]{1,0:T(8,128)}, f32[256,1536]{...) custom-call(s32[2]{0:T(128)} %pad_add_fusion.place_ref, ...), custom_call_target="tpu_custom_call" | custom-call | tf_op jit(solution)/shard_map/pallas_call | solution.py:1942
  435.5 0.5 slice_bitcast_fusion
  436.0 0.6 fusion.5
  (6 shorter events, 0.1 us)
Async XLA Ops:
  0.6 0.7 copy-start
  428.5 7.0 %copy-start.1 = (f32[1,4352]{1,0:T(1,128)S(1)}, f32[1,4352]{1,0:T(1,128)}, u32[]{:S(2)}) copy-start(f32[1,4352]{1,0:T(1,128)} %get-tuple-element.122) | copy-start | bytes 52228

commit v8 on v7

--- a/solution.py
+++ b/solution.py
@@ -1080,9 +1080,9 @@
 
 def middle_kernel(
     low_ref, cot_ref, gain_ref, attn_ref, wo_ref, c_ref, wd_ref, wg_ref, down_ref, gate_ref, up_ref,
-    middle_ref, dmid_ref, gain_grad_ref, dall_ref, mixed_ref, own_d_ref, got_d_b_ref, got_d_o_ref, got_g_b_ref, send_g_ref, keep_g_ref, away_g_ref, keep_u_ref, away_u_ref,
+    middle_ref, dmid_ref, gain_grad_ref, dall_ref, mixed_ref, own_d_ref, got_d_b_ref, got_d_o_ref, got_g_b_ref, send_g_ref, own_g_ref, keep_u_ref, away_u_ref,
     attn, wo, p, core_in, out_y, in_y, out_t, in_t, hold, xm_s, xm, c, wd, wg, wu, dact, gate, act, dg, du,
-    away_d, fold_d, away_g, fold_g, own_d, send_d, keep_g, send_g, up_tile, send, recv, *, batch_mask, chunk,
+    away_d, fold_d, away_g, fold_g, own_d, send_d, send_g, up_tile, send, recv, *, batch_mask, chunk,
 ):
     links = Links(send, recv, batch_mask)
     f, ff = own_d.shape[0], act.shape[1]
@@ -1225,9 +1225,8 @@
             compute_away(xm_cols, dg, away_g, 1, 3)
             folds_g.update(fold(away_g, fold_g, 1))
         if stage == 2:
+            folds_g.update(fold(away_g, fold_g, 3))
             compute_away(xm_cols, dg, away_g, 0, 2)
-            folds_g.update(fold(away_g, fold_g, 3))
-            load(away_g, away_g_ref)
 
     sum_in(links, bufs, chunk, back_partial, while_back)
     for m in range(2):
@@ -1236,19 +1235,20 @@
         dmid_ref[m] = grad
         xm_s[m] = grad.astype(BF16)
 
+    later = []
+
     def while_mid(stage):
         if stage == 0:
             folds_d[0].arrive()
             own_d[...] = total(c_cols, act, fold_d, 0)
-            load(own_d, own_d_ref)
+            own_load = load(own_d, own_d_ref)
+            later.append(own_load)
         if stage == 1:
             settle_d(2, links.across, rows(got_d_o_ref, 0))
             folds_g[1].arrive()
             send_g[pl.ds(0, f), :] = total(xm_cols, dg, fold_g, 1).astype(BF16)
             to(links.batch, rows(send_g, 0), got_g_b_ref)
-            keep_g[pl.ds(0, f), :] = tn(xm_cols(0, f), dg[...])
-            keep_g[pl.ds(f, f), :] = tn(xm_cols(2 * f, f), dg[...])
-            load(keep_g, keep_g_ref)
+            folds_g.update(fold(away_g, fold_g, 2, 0))
 
             def step(i):
                 at = pl.ds(pl.multiple_of(i * 512, 512), 512)
@@ -1269,10 +1269,16 @@
             load(p, mixed_ref)
         if stage == 2:
             folds_g[3].arrive()
-            send_g[pl.ds(f, f), :] = total(xm_cols, dg, fold_g, 3).astype(BF16)
-            load(rows(send_g, 1), send_g_ref)
+            send_g[pl.ds(2 * f, f), :] = total(xm_cols, dg, fold_g, 3).astype(BF16)
 
     spread_in(links, xm_s, dall_ref, chunk, while_mid, in_vmem=False)
+    folds_g[2].arrive()
+    send_g[pl.ds(f, f), :] = total(xm_cols, dg, fold_g, 2).astype(BF16)
+    load(send_g.at[pl.ds(f, 2 * f), :], send_g_ref)
+    folds_g[0].arrive()
+    later[0].arrive()
+    own_d[...] = total(xm_cols, dg, fold_g, 0)
+    load(own_d, own_g_ref)
     links.finish()
 
 
@@ -1287,7 +1293,7 @@
     return pl.pallas_call(
         functools.partial(middle_kernel, batch_mask=batch_mask, chunk=2 * width // 8),
         in_specs=[vmem] * 3 + [hbm] * 8,
-        out_specs=[vmem] * 3 + [hbm] * 11,
+        out_specs=[vmem] * 3 + [hbm] * 10,
         out_shape=[
             like(share, F32),
             like(share, F32),
@@ -1298,9 +1304,8 @@
             like((f, ff), BF16),
             like((2 * f, ff), BF16),
             like((f, ff), BF16),
-            like((f, ff), BF16),
-            like((2 * f, ff), F32),
-            like((4 * f, ff), BF16),
+            like((2 * f, ff), BF16),
+            like((f, ff), F32),
             like((4 * f, ff), F32),
             like((4 * f, ff), BF16),
         ],
@@ -1323,8 +1328,7 @@
             *[pltpu.VMEM((4 * f, ff), BF16)] * 4,
             pltpu.VMEM((f, ff), F32),
             pltpu.VMEM((3 * f, ff), BF16),
-            pltpu.VMEM((2 * f, ff), F32),
-            pltpu.VMEM((2 * f, ff), BF16),
+            pltpu.VMEM((3 * f, ff), BF16),
             pltpu.VMEM((256, ff), F32),
             pltpu.SemaphoreType.DMA((96,)),
             pltpu.SemaphoreType.DMA((96,)),
@@ -1417,12 +1421,12 @@
 def last_kernel(
     low_ref, middle_ref, dmid_ref, gain_ref, gain_m_grad_ref, gain_q_ref, gain_k_ref, start_ref, l_ref,
     dall_ref, wo_ref, attn_ref, q_ref, k_ref, v_ref, ot_ref, raw_ref, table_ref, wa_ref, xa_ref, mixed_ref,
-    send_g_ref, keep_g_ref, away_g_ref, keep_u_ref, away_u_ref,
+    send_g_ref, keep_u_ref, away_u_ref,
     mixed_own_ref, mixed_got_ref, input_own_ref, input_got_ref, sums_ref,
-    own_g_ref, got_g_o_ref, own_u_ref, got_u_b_ref, got_u_o_ref, own_a_ref, got_a_b_ref, got_a_o_ref, own_o_ref, got_o_b_ref, got_o_o_ref,
+    got_g_o_ref, own_u_ref, got_u_b_ref, got_u_o_ref, own_a_ref, got_a_b_ref, got_a_o_ref, own_o_ref, got_o_b_ref, got_o_o_ref,
     dall, wo, attn, q, do, k, v, ot, raw, table, wa, xa, dq, dk, dv, kt, acc, kv_out, kv_in, d_qkv,
-    p, core_in, out_y, in_y, out_t, in_t, hold, m_near, m_core_in, m_in_y, m_in_t,
-    swap_m, swap_i, keep_g, fold_g, own_g, send_g, keep_u, fold_u, own_u, send_u, away_o, fold_o, own_o, send_o, away_a, fold_a, own_a, send_a,
+    p, core_in, out_y, in_y, out_t, in_t, hold, m_near, m_core_in, m_out_y, m_in_y, m_out_t, m_in_t, m_hold,
+    swap_m, swap_i, keep_u, fold_u, own_u, send_u, away_o, fold_o, own_o, send_o, away_a, fold_a, own_a, send_a,
     gains_qk, gain_a_grad, ring_out, ring_in, send, recv, *, batch_mask, bit_order, scaling, chunk,
 ):
     links = Links(send, recv, batch_mask)
@@ -1437,7 +1441,7 @@
     first = [load(dall_ref, dall), load(wo_ref, wo), load(attn_ref, attn)]
     second = [load(a, b) for a, b in ((q_ref, q), (k_ref, k), (v_ref, v), (ot_ref, ot))]
     third = [load(a, b) for a, b in ((raw_ref, raw), (table_ref, table), (wa_ref, wa), (xa_ref, xa))]
-    mixed_near, keep_load, keep_g_load = load(mixed_ref.at[0], m_near.at[0]), load(keep_u_ref, keep_u), load(keep_g_ref, keep_g)
+    mixed_near, keep_load = load(mixed_ref.at[0], m_near.at[0]), load(keep_u_ref, keep_u)
     links.greet()
 
     def settle(src, dst_b, dst_o):
@@ -1445,9 +1449,9 @@
         to(links.both, rows(src, 2), rows(dst_o, 1))
         to(links.across, rows(src, 1), rows(dst_o, 0))
 
-    to(links.both, send_g_ref, rows(got_g_o_ref, 1))
+    to(links.both, rows(send_g_ref, 1), rows(got_g_o_ref, 1))
+    to(links.across, rows(send_g_ref, 0), rows(got_g_o_ref, 0))
     folds_u = {i: to(links.seq, rows(away_u_ref, i), rows(fold_u, i)) for i in (1, 3)}
-    folds_g = {i: to(links.seq, rows(away_g_ref, i), rows(fold_g, i // 2)) for i in (0, 2)}
     for copy in (*first, *second):
         copy.arrive()
 
@@ -1469,35 +1473,6 @@
 
     def xa_cols(at, n):
         return xa[:, pl.ds(at, n)]
-
-    folds = []
-
-    def while_mixed(stage):
-        if stage == 0:
-            loop(4, d_attn)
-            attention_back(q, do, k, v, start_ref, ot, l_ref, dq, dk, dv, kt, acc, batch_mask, scaling)
-            kv_out[:, :width] = dk[1].reshape(-1, width).astype(BF16)
-            kv_out[:, width:] = dv[1].reshape(-1, width).astype(BF16)
-            folds.extend(to(links.seq, kv_out.at[pl.ds(i, 128), :], kv_in.at[pl.ds(i, 128), :]) for i in range(0, kv_out.shape[0], 128))
-            keep_load.arrive()
-            settle_u(1, links.batch, got_u_b_ref)
-            settle_u(3, links.both, rows(got_u_o_ref, 1))
-            away_rows(dall_cols, attn, away_o)
-        if stage == 1:
-            for copy in folds:
-                copy.arrive()
-            folds[:] = [to(links.seq, away_o, fold_o)]
-
-    mixed_near.arrive()
-    sum_in(links, (m_near, m_core_in, out_y, m_in_y, out_t, m_in_t, hold), chunk, None, while_mixed, mixed_ref.at[1])
-    blk = lax.axis_index("blk")
-    store_ungrouped(middle_ref[0] + hold[0], mixed_own_ref, blk, bit_order)
-    store_ungrouped(middle_ref[1] + hold[1], swap_m, blk, bit_order)
-    to(links.batch, swap_m, mixed_got_ref)
-
-    for copy in third:
-        copy.arrive()
-    gains_qk[...] = jnp.zeros_like(gains_qk)
 
     def input_partial(c):
         def step(m):
@@ -1531,35 +1506,56 @@
         if stage == 0:
             away_rows(xa_cols, d_qkv, away_a)
             folds.extend(to(links.seq, rows(away_a, i), rows(fold_a, i)) for i in (1, 3, 0, 2))
+        if stage == 1:
             folds[0].arrive()
             keep_rows(dall_cols, attn, fold_o, own_o, send_o)
             settle(send_o, got_o_b_ref, got_o_o_ref)
             load(own_o, own_o_ref)
+            folds_u.update({i: to(links.seq, rows(away_u_ref, i), rows(fold_u, i)) for i in (2, 0)})
+
+    folds = []
+
+    def while_mixed(stage):
+        if stage == 0:
+            loop(4, d_attn)
+            attention_back(q, do, k, v, start_ref, ot, l_ref, dq, dk, dv, kt, acc, batch_mask, scaling)
+            kv_out[:, :width] = dk[1].reshape(-1, width).astype(BF16)
+            kv_out[:, width:] = dv[1].reshape(-1, width).astype(BF16)
+            folds.extend(
+                to(links.seq, kv_out.at[pl.ds(i, 128), :], kv_in.at[pl.ds(i, 128), :])
+                for i in range(0, kv_out.shape[0], 128)
+            )
+            keep_load.arrive()
+            settle_u(1, links.batch, got_u_b_ref)
+            settle_u(3, links.both, rows(got_u_o_ref, 1))
         if stage == 1:
-            folds_u.update({i: to(links.seq, rows(away_u_ref, i), rows(fold_u, i)) for i in (2, 0)})
-            for copy in (*folds_g.values(), keep_g_load):
+            away_rows(dall_cols, attn, away_o)
+            out_fold = to(links.seq, away_o, fold_o)
+            for copy in (*folds, *third):
                 copy.arrive()
-            for i, ref in ((0, own_g), (1, send_g)):
-                here = pl.ds(i * f, f)
-                ref[...] = (keep_g[here, :] + fold_g[here, :].astype(F32)).astype(ref.dtype)
-            load(own_g, own_g_ref)
-            to(links.across, send_g, rows(got_g_o_ref, 0))
-        if stage == 2:
+            folds[:] = [out_fold]
+            gains_qk[...] = jnp.zeros_like(gains_qk)
+            sum_in(links, (p, core_in, out_y, in_y, out_t, in_t, hold), chunk, input_partial, while_input)
+            for m in range(2):
+                grad = dmid_ref[m] + norm_grad(hold[m], low_ref[m].astype(F32), gain_ref[...], gain_a_grad, m)
+                store_ungrouped(grad, input_own_ref if m == 0 else swap_i, blk, bit_order)
+            to(links.batch, swap_i, input_got_ref)
             for copy in folds:
                 copy.arrive()
             keep_rows(xa_cols, d_qkv, fold_a, own_a, send_a)
             settle(send_a, got_a_b_ref, got_a_o_ref)
             load(own_a, own_a_ref)
-            settle_u(2, links.across, rows(got_u_o_ref, 0))
-            folds_u[0].arrive()
-            own_u[...] = total_u(0)
-            load(own_u, own_u_ref)
-
-    sum_in(links, (p, core_in, out_y, in_y, out_t, in_t, hold), chunk, input_partial, while_input)
-    for m in range(2):
-        grad = dmid_ref[m] + norm_grad(hold[m], low_ref[m].astype(F32), gain_ref[...], gain_a_grad, m)
-        store_ungrouped(grad, input_own_ref if m == 0 else swap_i, blk, bit_order)
-    to(links.batch, swap_i, input_got_ref)
+
+    mixed_near.arrive()
+    blk = lax.axis_index("blk")
+    sum_in(links, (m_near, m_core_in, m_out_y, m_in_y, m_out_t, m_in_t, m_hold), chunk, None, while_mixed, mixed_ref.at[1])
+    store_ungrouped(middle_ref[0] + m_hold[0], mixed_own_ref, blk, bit_order)
+    store_ungrouped(middle_ref[1] + m_hold[1], swap_m, blk, bit_order)
+    to(links.batch, swap_m, mixed_got_ref)
+    settle_u(2, links.across, rows(got_u_o_ref, 0))
+    folds_u[0].arrive()
+    own_u[...] = total_u(0)
+    load(own_u, own_u_ref)
     n = gain_a_grad.shape[1]
     store_ungrouped(gain_a_grad[...], sums_ref.at[:, pl.ds(0, n)], blk, bit_order)
     sums_ref[:, n : n + width] = gains_qk[0:1, :]
@@ -1584,8 +1580,7 @@
     like, held = jax.ShapeDtypeStruct, pltpu.VMEM
     in_vmem = ("low", "middle", "d_middle", "gain", "gain_m_grad", "gain_q", "gain_k", "start", "l")
     in_hbm = (
-        "dall", "w_out", "attn", "q", "k", "v", "ot", "raw", "table", "wa", "xa", "mixed", "send_g", "keep_g", "away_g", "keep_u",
-        "away_u",
+        "dall", "w_out", "attn", "q", "k", "v", "ot", "raw", "table", "wa", "xa", "mixed", "send_g", "keep_u", "away_u",
     )
     total = 2 * width + 2 * head_size
     lanes = 2 * 2 * 128
@@ -1597,14 +1592,13 @@
     return pl.pallas_call(
         functools.partial(last_kernel, batch_mask=batch_mask, bit_order=bit_order, scaling=scaling, chunk=2 * width // 8),
         in_specs=[vmem] * len(in_vmem) + [hbm] * len(in_hbm),
-        out_specs=[vmem, hbm, vmem, hbm, vmem] + [hbm] * 11,
+        out_specs=[vmem, hbm, vmem, hbm, vmem] + [hbm] * 10,
         out_shape=[
             like((rows, width), BF16),
             like((rows, width), BF16),
             like((rows, width), F32),
             like((rows, width), BF16),
             like(sums, F32),
-            like((f, ff), F32),
             like((2 * f, ff), BF16),
             *[
                 like((m * f, n), dtype)
@@ -1637,13 +1631,10 @@
             *sum_bufs,
             held(share, F32),
             held(half_full, BF16),
-            *[sum_bufs[i] for i in (0, 2, 4)],
+            *sum_bufs,
+            held(share, F32),
             held((rows, width), BF16),
             held((rows, width), BF16),
-            held((2 * f, ff), F32),
-            held((2 * f, ff), BF16),
-            held((f, ff), F32),
-            held((f, ff), BF16),
             held((4 * f, ff), F32),
             held((4 * f, ff), BF16),
             *own_and_send(ff),
@@ -1756,8 +1747,7 @@
     load(links.half(wo_ref, 0), rows(wo_out, 0))
     to(links.seq, links.half(wd_ref, 0), rows(wd_out, 4))
     to(links.seq, links.half(wg_ref, 0), rows(wg_out, 4))
-    down_t = to(links.across, links.half(wd_ref, 1), rows(wd_out, 2))
-    out_rows = [to(links.across, links.half(wo_ref, 1), rows(wo_out, 2))]
+    down_t, out_rows = [], []
     n_blocks = 1 << len(bit_order)
     n = x_in.shape[-1] // n_blocks
 
@@ -1772,7 +1762,6 @@
     x_far.arrive()
     a_far = {1: to(links.batch, rows(wa, 0), rows(wa, 1)), 3: to(links.both, wb, rows(wa, 3))}
     c_far = to(links.batch, cot_ref.at[1 - batch], c_in.at[1])
-    to(links.batch, links.half(wd_ref, 0), rows(wd_out, 1))
     regroup(x_in, low_ref, all_rows)
     for m in range(2):
         value = low_ref[m].astype(F32)
@@ -1783,12 +1772,15 @@
             a_t.arrive()
             a_rest.append(to(links.seq, rows(wa, 2), rows(wa, 6)))
         if stage == 1:
+            down_t.append(to(links.across, links.half(wd_ref, 1), rows(wd_out, 2)))
+            out_rows.append(to(links.across, links.half(wo_ref, 1), rows(wo_out, 2)))
             for i, copy in a_far.items():
                 copy.arrive()
                 a_rest.append(to(links.seq, rows(wa, i), rows(wa, i + 4)))
             out_rows.append(to(links.batch, links.half(wo_ref, 0), rows(wo_out, 1)))
             out_rows.append(to(links.both, links.half(wo_ref, 1), rows(wo_out, 3)))
             to(links.both, links.half(wd_ref, 1), rows(wd_out, 3))
+            to(links.batch, links.half(wd_ref, 0), rows(wd_out, 1))
             c_own.arrive()
             c_far.arrive()
             regroup(c_in, cot_low_ref, all_rows)
@@ -1827,7 +1819,7 @@
             load(wa, wa_out)
             load(raw, raw_ref)
             load(q, q_ref)
-            down_t.arrive()
+            down_t[0].arrive()
             to(links.seq, rows(wd_out, 2), rows(wd_out, 6))
         if stage == 1:
             to(links.across, links.half(wg_ref, 1), rows(wg_out, 2))
@@ -2367,7 +2359,7 @@
         own_gate, away_gate = to_settle(keep_gate, gate_x)
     else:
         (
-            middle, d_middle, gain_m_grad, d_mid_all, mixed_partial, own_down, down_b, down_o, gate_b, send_gate, keep_gate, away_gate, keep_up, away_up,
+            middle, d_middle, gain_m_grad, d_mid_all, mixed_partial, own_down, down_b, down_o, gate_b, send_gate, own_gate, keep_up, away_up,
         ) = middle_call(
             b_mask, x_low, cot.reshape(share), gain_m[None], attn, w_out, cot_all, w_down, w_gate, (down_weight, gate_weight, up_weight), next(ids)
         )
@@ -2453,7 +2445,7 @@
         gains = jnp.split(sums.reshape(-1), [width, width + head_size, width + 2 * head_size])
     else:
         (
-            mixed_own, mixed_got, input_own, input_got, sums, own_gate, gate_o, own_up, up_b, up_o, own_qkv, a_b, a_o, own_out, out_b, out_o,
+            mixed_own, mixed_got, input_own, input_got, sums, gate_o, own_up, up_b, up_o, own_qkv, a_b, a_o, own_out, out_b, out_o,
         ) = last_call(
             b_mask,
             bit_order,
@@ -2481,8 +2473,6 @@
                 xa=xa,
                 mixed=mixed_partial.reshape(2, 2, 2, 2, local_rows, width),
                 send_g=send_gate,
-                keep_g=keep_gate,
-                away_g=away_gate,
                 keep_u=keep_up,
                 away_u=away_up,
             ),

time: 438 us -> 426 us (0.973)
  Pallas kernels: 425 us -> 411 us
    pallas_call x1, Pallas kernels: 133 us -> 124 us  [last_call(): pl.pallas_call(functools.partial(last_kernel, batch_mask=batch_mask, bit_...]
    pallas_call x1, Pallas kernels: 116 us -> 109 us  [first_call(): pl.pallas_call(functools.partial(first_kernel, batch_mask=batch_mask, bit...]
where the time goes in v8:
time: 426 us; the launch traced here: 423 us
  Pallas kernels  411 us (96%)
  other arithmetic  5.81 us (1%)
  local copies, waits for them, and re-layouts  4.71 us (1%)
    pallas_call x1, Pallas kernels, middle_call(): pl.pallas_call(functools.partial(middle_kernel, batch_mask=batch_mask, ch...  172 us
    pallas_call x1, Pallas kernels, last_call(): pl.pallas_call(functools.partial(last_kernel, batch_mask=batch_mask, bit_...  124 us
    pallas_call x1, Pallas kernels, first_call(): pl.pallas_call(functools.partial(first_kernel, batch_mask=batch_mask, bit...  109 us

profile of v8, /device:TPU:0, one launch (start us, length us, event | category | flops | bytes accessed | tf_op | source)
XLA Modules:
  0.0 422.6 jit_solution(16508857785029318885)
XLA Ops:
  0.6 0.0 copy-start
  0.7 0.6 pad_add_fusion.place_ref
  1.3 0.1 copy-done
  1.3 0.2 reduce-window.8
  1.6 0.1 xor_multiply_fusion
  1.6 0.1 mul.41
  1.7 1.2 bitcast_convert_fusion
  2.9 0.1 broadcast_add_fusion
  3.0 0.1 select_reduce_fusion
  3.1 0.1 subtract_convert_fusion
  3.2 0.6 tile.12.start_ref
  3.8 0.7 stack.21
  4.5 0.7 stack.22
  5.2 0.6 maximum_convert_fusion.gains_ref
  5.8 1.9 multiply_cosine_fusion
  7.7 1.0 pad_maximum_fusion.table_ref
  8.7 108.5 %shard_map.237 = (bf16[2,64,2048]{2,1,0:T(8,128)(2,1)}, bf16[2,64,2048]{2,1,0:T(8,128)(2,1)}, f32[2,2048]{1,0:T(2,128)}, f32[4,1,512]{2,1,0:T(1,128)}, bf16[2,2,...) custom-call(f32[2,2048]{1,0:T(2,128)} %maximum_convert_fusion.gains_, ...), custom_call_target="tpu_custom_call" | custom-call | tf_op jit(solution)/shard_map/pallas_call | solution.py:1855
  117.2 1.4 fusion.6
  118.6 171.6 %shard_map.238 = (f32[2,64,2048]{2,1,0:T(8,128)}, f32[2,64,2048]{2,1,0:T(8,128)}, f32[1,2048]{1,0:T(1,128)}, bf16[2,2,2,2,64,2048]{5,4,3,2,1,0:T(8,128)(2,1)}, b...) custom-call(bf16[2,64,2048]{2,1,0:T(8,128)(2,1)} %get-tuple-element., ...), custom_call_target="tpu_custom_call" | custom-call | tf_op jit(solution)/shard_map/pallas_call | solution.py:1293
  290.2 124.0 %shard_map.239 = (bf16[64,2048]{1,0:T(8,128)(2,1)}, bf16[64,2048]{1,0:T(8,128)(2,1)}, f32[64,2048]{1,0:T(8,128)}, bf16[64,2048]{1,0:T(8,128)(2,1)}, f32[1,4352]{...) custom-call(bf16[2,64,2048]{2,1,0:T(8,128)(2,1)} %get-tuple-element., ...), custom_call_target="tpu_custom_call" | custom-call | tf_op jit(solution)/shard_map/pallas_call | solution.py:1592
  414.2 0.0 copy-start.1
  414.2 7.0 %shard_map.240 = (bf16[2,64,2048]{2,1,0:T(8,128)(2,1)}, f32[2,64,2048]{2,1,0:T(8,128)}, f32[256,1536]{1,0:T(8,128)}, f32[256,1536]{1,0:T(8,128)}, f32[256,1536]{...) custom-call(s32[2]{0:T(128)} %pad_add_fusion.place_ref, ...), custom_call_target="tpu_custom_call" | custom-call | tf_op jit(solution)/shard_map/pallas_call | solution.py:1934
  421.2 0.5 slice_bitcast_fusion
  421.7 0.6 fusion.5
  (6 shorter events, 0.1 us)
Async XLA Ops:
  0.6 0.7 copy-start
  414.2 7.0 %copy-start.1 = (f32[1,4352]{1,0:T(1,128)S(1)}, f32[1,4352]{1,0:T(1,128)}, u32[]{:S(2)}) copy-start(f32[1,4352]{1,0:T(1,128)} %get-tuple-element.118) | copy-start | bytes 52228

commit v9 on v8

--- a/solution.py
+++ b/solution.py
@@ -966,37 +966,54 @@
     pass
 
 
+class Spread:
+    def __init__(self, links, s_ref, o_ref, chunk, in_vmem=True):
+        self.links, self.s_ref, self.o_ref, self.chunk, self.in_vmem = links, s_ref, o_ref, chunk, in_vmem
+
+    def begin(self):
+        links, s_ref, o_ref, chunk = self.links, self.s_ref, self.o_ref, self.chunk
+        self.across = [
+            links.to(
+                links.across,
+                s_ref.at[:, :, pl.ds(i * chunk, chunk)],
+                o_ref.at[0, :, 1, 0, :, pl.ds((i ^ 1) * chunk, chunk)],
+            )
+            for i in range(s_ref.shape[-1] // chunk)
+        ]
+        self.near = links.to(links.near, s_ref, o_ref.at[0, :, 0, 1])
+        self.core = [links.to(links.core, s_ref, o_ref.at[1, :, 0, 0])]
+        if self.in_vmem:
+            o_ref[0, :, 0, 0] = s_ref[...]
+        else:
+            links.load(s_ref, o_ref.at[0, :, 0, 0])
+
+    def pass_on(self):
+        links, o_ref = self.links, self.o_ref
+        for copy in self.across:
+            copy.arrive()
+        self.onward = links.to(links.near, o_ref.at[0, :, 1, 0], o_ref.at[0, :, 1, 1])
+        self.core.append(links.to(links.core, o_ref.at[0, :, 1, 0], o_ref.at[1, :, 1, 0]))
+        self.near.arrive()
+        self.core.append(links.to(links.core, o_ref.at[0, :, 0, 1], o_ref.at[1, :, 0, 1]))
+
+    def end(self, between=nothing):
+        links, o_ref = self.links, self.o_ref
+        self.onward.arrive()
+        self.core.append(links.to(links.core, o_ref.at[0, :, 1, 1], o_ref.at[1, :, 1, 1]))
+        between(2)
+        for copy in self.core:
+            copy.arrive()
+        for copy in (*self.across, self.near, self.core[0]):
+            copy.sent()
+
+
 def spread_in(links, s_ref, o_ref, chunk, between=nothing, in_vmem=True):
-    pieces = s_ref.shape[-1] // chunk
-    across = [
-        links.to(
-            links.across,
-            s_ref.at[:, :, pl.ds(i * chunk, chunk)],
-            o_ref.at[0, :, 1, 0, :, pl.ds((i ^ 1) * chunk, chunk)],
-        )
-        for i in range(pieces)
-    ]
-    near = links.to(links.near, s_ref, o_ref.at[0, :, 0, 1])
-    core = [links.to(links.core, s_ref, o_ref.at[1, :, 0, 0])]
-    if in_vmem:
-        o_ref[0, :, 0, 0] = s_ref[...]
-    else:
-        links.load(s_ref, o_ref.at[0, :, 0, 0])
+    spread = Spread(links, s_ref, o_ref, chunk, in_vmem)
+    spread.begin()
     between(0)
-    for copy in across:
-        copy.arrive()
-    onward = links.to(links.near, o_ref.at[0, :, 1, 0], o_ref.at[0, :, 1, 1])
-    core.append(links.to(links.core, o_ref.at[0, :, 1, 0], o_ref.at[1, :, 1, 0]))
-    near.arrive()
-    core.append(links.to(links.core, o_ref.at[0, :, 0, 1], o_ref.at[1, :, 0, 1]))
+    spread.pass_on()
     between(1)
-    onward.arrive()
-    core.append(links.to(links.core, o_ref.at[0, :, 1, 1], o_ref.at[1, :, 1, 1]))
-    between(2)
-    for copy in core:
-        copy.arrive()
-    for copy in (*across, near, core[0]):
-        copy.sent()
+    spread.end(between)
 
 
 def sum_in(links, bufs, chunk, partial, between=nothing, far=None):
@@ -1126,7 +1143,7 @@
     for m in range(2):
         middle = low_ref[m].astype(F32) + hold[m]
         middle_ref[m] = middle
-        xm_s[m] = (middle * inverse_rms(middle) * gain_ref[...]).astype(BF16)
+        xm_s[m] = (middle * inverse_rms(middle) * gain_ref[1:2, :]).astype(BF16)
 
     def while_xm(stage):
         if stage == 0:
@@ -1231,7 +1248,7 @@
     sum_in(links, bufs, chunk, back_partial, while_back)
     for m in range(2):
         middle = middle_ref[m]
-        grad = cot_ref[m].astype(F32) + norm_grad(hold[m], middle, gain_ref[...], gain_grad_ref, m)
+        grad = cot_ref[m].astype(F32) + norm_grad(hold[m], middle, gain_ref[1:2, :], gain_grad_ref, m)
         dmid_ref[m] = grad
         xm_s[m] = grad.astype(BF16)
 
@@ -1487,7 +1504,7 @@
                     grad = dq[c, pair, :, cut].reshape(256, width)
                 else:
                     grad = dk[0, c, pair].reshape(256, width) + got[:, :width]
-                gain = (gain_q_ref if h < heads else gain_k_ref)[...]
+                gain = (gain_q_ref if h < heads else gain_k_ref)[...].astype(F32)
                 values = raw[at, cut]
                 inverse = inverse_rms(values)
                 normed = values * inverse
@@ -1537,7 +1554,7 @@
             gains_qk[...] = jnp.zeros_like(gains_qk)
             sum_in(links, (p, core_in, out_y, in_y, out_t, in_t, hold), chunk, input_partial, while_input)
             for m in range(2):
-                grad = dmid_ref[m] + norm_grad(hold[m], low_ref[m].astype(F32), gain_ref[...], gain_a_grad, m)
+                grad = dmid_ref[m] + norm_grad(hold[m], low_ref[m].astype(F32), gain_ref[0:1, :], gain_a_grad, m)
                 store_ungrouped(grad, input_own_ref if m == 0 else swap_i, blk, bit_order)
             to(links.batch, swap_i, input_got_ref)
             for copy in folds:
@@ -1711,8 +1728,8 @@
 
 
 def first_kernel(
-    gains_ref, gain_q_ref, gain_k_ref, table_ref, start_ref,
-    hid_ref, cot_ref, wq_ref, wk_ref, wv_ref, wo_ref, wd_ref, wg_ref,
+    gain_a_ref, gain_m_ref, gain_q_ref, gain_k_ref, table_ref, start_ref,
+    hid_ref, far_ref, cot_ref, wq_ref, wk_ref, wv_ref, wo_ref, wd_ref, wg_ref,
     low_ref, cot_low_ref, gains_out_ref, l_ref,
     xa_ref, call_ref, wa_out, wo_out, wd_out, wg_out, q_ref, k_ref, v_ref, raw_ref, attn_ref, ot_ref,
     x_in, c_in, xa_s, xa, wa, wb, q, k, v, raw, out, ot, vt, acc, total, send, recv, *, batch_mask, bit_order, scaling, chunk,
@@ -1733,12 +1750,11 @@
     def rows(ref, i):
         return ref.at[pl.ds(i * f, f), :]
 
-    x_own = load(hid_ref.at[batch], x_in.at[0])
+    x_own, x_far = load(hid_ref.at[batch], x_in.at[0]), load(far_ref, x_in.at[1])
     c_own = load(cot_ref.at[batch], c_in.at[0])
     a_own = [load(links.half(ref, 0), wa.at[pl.ds(0, f), pl.ds(start, n)]) for ref, start, n in a_params]
     a_other = [load(links.half(ref, 1), wb.at[:, pl.ds(start, n)]) for ref, start, n in a_params]
     links.greet()
-    x_far = to(links.batch, hid_ref.at[1 - batch], x_in.at[1])
     for copy in (*a_own, *a_other):
         copy.arrive()
     a_t = to(links.across, wb, rows(wa, 2))
@@ -1747,7 +1763,6 @@
     load(links.half(wo_ref, 0), rows(wo_out, 0))
     to(links.seq, links.half(wd_ref, 0), rows(wd_out, 4))
     to(links.seq, links.half(wg_ref, 0), rows(wg_out, 4))
-    down_t, out_rows = [], []
     n_blocks = 1 << len(bit_order)
     n = x_in.shape[-1] // n_blocks
 
@@ -1757,7 +1772,10 @@
             dst[(*lead, pl.ds(p * n, n))] = src[(*lead, cut)]
 
     all_rows = (slice(None), slice(None))
-    regroup(gains_ref, gains_out_ref, (slice(None),))
+    for p in range(n_blocks):
+        cut = pl.ds(pl.multiple_of(place_of_block(blk, bit_order, p) * n, n), n)
+        gains_out_ref[0:1, p * n : (p + 1) * n] = gain_a_ref[:, cut].astype(F32)
+        gains_out_ref[1:2, p * n : (p + 1) * n] = gain_m_ref[:, cut].astype(F32)
     x_own.arrive()
     x_far.arrive()
     a_far = {1: to(links.batch, rows(wa, 0), rows(wa, 1)), 3: to(links.both, wb, rows(wa, 3))}
@@ -1767,25 +1785,25 @@
         value = low_ref[m].astype(F32)
         xa_s[m] = (value * inverse_rms(value) * gains_out_ref[0:1, :]).astype(BF16)
 
-    def while_xa(stage):
-        if stage == 0:
-            a_t.arrive()
-            a_rest.append(to(links.seq, rows(wa, 2), rows(wa, 6)))
-        if stage == 1:
-            down_t.append(to(links.across, links.half(wd_ref, 1), rows(wd_out, 2)))
-            out_rows.append(to(links.across, links.half(wo_ref, 1), rows(wo_out, 2)))
-            for i, copy in a_far.items():
-                copy.arrive()
-                a_rest.append(to(links.seq, rows(wa, i), rows(wa, i + 4)))
-            out_rows.append(to(links.batch, links.half(wo_ref, 0), rows(wo_out, 1)))
-            out_rows.append(to(links.both, links.half(wo_ref, 1), rows(wo_out, 3)))
-            to(links.both, links.half(wd_ref, 1), rows(wd_out, 3))
-            to(links.batch, links.half(wd_ref, 0), rows(wd_out, 1))
-            c_own.arrive()
-            c_far.arrive()
-            regroup(c_in, cot_low_ref, all_rows)
-
-    spread_in(links, xa_s, xa, chunk, while_xa)
+    by_rows = Spread(links, xa_s, xa, chunk)
+    by_rows.begin()
+    a_t.arrive()
+    a_rest.append(to(links.seq, rows(wa, 2), rows(wa, 6)))
+    by_rows.pass_on()
+    down_t = to(links.across, links.half(wd_ref, 1), rows(wd_out, 2))
+    out_rows = [to(links.across, links.half(wo_ref, 1), rows(wo_out, 2))]
+    for i, copy in a_far.items():
+        copy.arrive()
+        a_rest.append(to(links.seq, rows(wa, i), rows(wa, i + 4)))
+    c_own.arrive()
+    c_far.arrive()
+    regroup(c_in, cot_low_ref, all_rows)
+    by_cot = Spread(links, cot_low_ref, call_ref, chunk, in_vmem=False)
+    by_cot.begin()
+    out_rows.append(to(links.batch, links.half(wo_ref, 0), rows(wo_out, 1)))
+    out_rows.append(to(links.both, links.half(wo_ref, 1), rows(wo_out, 3)))
+    to(links.both, links.half(wd_ref, 1), rows(wd_out, 3))
+    by_rows.end()
     load(xa, xa_ref)
 
     def prepare_rows(i):
@@ -1798,7 +1816,7 @@
         cos, sin = jnp.concatenate([cos, cos], axis=1), jnp.concatenate([-sin, sin], axis=1)
         for h in range(heads + 1):
             part = acc_rows[:, h * width : (h + 1) * width]
-            scaled = part * inverse_rms(part) * (gain_q_ref if h < heads else gain_k_ref)[...]
+            scaled = part * inverse_rms(part) * (gain_q_ref if h < heads else gain_k_ref)[...].astype(F32)
             turned = (scaled * cos + pltpu.roll(scaled, width // 2, 1) * sin).astype(BF16).reshape(2, 128, width)
             if h < heads:
                 q[c, pair, :, h * width : (h + 1) * width] = turned
@@ -1806,35 +1824,29 @@
                 k[0, c, pair] = turned
         v[0, c, pair] = acc_rows[:, (heads + 1) * width :].astype(BF16).reshape(2, 128, width)
 
-    kv = []
-
-    def while_cot(stage):
-        if stage == 0:
-            for copy in a_rest:
-                copy.arrive()
-            loop(4, prepare_rows)
-            kv.extend(
-                to(links.seq, ref.at[0, c, i], ref.at[1, c, i]) for ref in (k, v) for c in range(2) for i in range(4)
-            )
-            load(wa, wa_out)
-            load(raw, raw_ref)
-            load(q, q_ref)
-            down_t[0].arrive()
-            to(links.seq, rows(wd_out, 2), rows(wd_out, 6))
-        if stage == 1:
-            to(links.across, links.half(wg_ref, 1), rows(wg_out, 2))
-            for i, copy in zip((2, 1, 3), out_rows):
-                copy.arrive()
-                to(links.seq, rows(wo_out, i), rows(wo_out, i + 4))
-            for copy in kv:
-                copy.arrive()
-            load(k, k_ref)
-            load(v, v_ref)
-            attention(q, k, v, start_ref, out, ot, l_ref, vt, acc, total, batch_mask, scaling)
-            load(out, attn_ref)
-            load(ot, ot_ref)
-
-    spread_in(links, cot_low_ref, call_ref, chunk, while_cot, in_vmem=False)
+    for copy in a_rest:
+        copy.arrive()
+    loop(4, prepare_rows)
+    kv = [to(links.seq, ref.at[0, c, i], ref.at[1, c, i]) for ref in (k, v) for c in range(2) for i in range(4)]
+    to(links.batch, links.half(wd_ref, 0), rows(wd_out, 1))
+    load(wa, wa_out)
+    load(raw, raw_ref)
+    load(q, q_ref)
+    down_t.arrive()
+    to(links.seq, rows(wd_out, 2), rows(wd_out, 6))
+    by_cot.pass_on()
+    to(links.across, links.half(wg_ref, 1), rows(wg_out, 2))
+    for i, copy in zip((2, 1, 3), out_rows):
+        copy.arrive()
+        to(links.seq, rows(wo_out, i), rows(wo_out, i + 4))
+    for copy in kv:
+        copy.arrive()
+    load(k, k_ref)
+    load(v, v_ref)
+    attention(q, k, v, start_ref, out, ot, l_ref, vt, acc, total, batch_mask, scaling)
+    load(out, attn_ref)
+    load(ot, ot_ref)
+    by_cot.end()
     links.finish()
 
 
@@ -1848,8 +1860,8 @@
     share, full = (2, rows, width), (2, 2, 2, 2, rows, width)
     vmem, hbm = pl.BlockSpec(memory_space=pltpu.VMEM), pl.BlockSpec(memory_space=pltpu.HBM)
     like, held = jax.ShapeDtypeStruct, pltpu.VMEM
-    in_vmem = ("gains", "gain_q", "gain_k", "table", "start")
-    in_hbm = ("hidden", "cotangent", "wq", "wk", "wv", "wo", "wd", "wg")
+    in_vmem = ("gain_a", "gain_m", "gain_q", "gain_k", "table", "start")
+    in_hbm = ("hidden", "far", "cotangent", "wq", "wk", "wv", "wo", "wd", "wg")
     q_shape, k_shape = (2, 4, half, columns), (2, 2, 4, half, head_size)
     ot_shape, raw_shape = (4, head_size, lanes), (tokens, (heads + 1) * head_size)
     return pl.pallas_call(
@@ -1900,9 +1912,10 @@
     )(*[arrays[n] for n in (*in_vmem, *in_hbm)])
 
 
-def finish_kernel(place_ref, mixed_own, mixed_got, input_own, input_got, *refs, sources, widths):
+def finish_kernel(mixed_own, mixed_got, input_own, input_got, *refs, sources, widths, batch_bit):
     ins, (mixed_ref, input_ref, *outs) = refs[: 3 * sources], refs[3 * sources :]
-    place, batch, k = place_ref[0], place_ref[1], 0
+    blk = lax.axis_index("blk")
+    place, batch, k = bit_of(blk, TENSOR_BIT), bit_of(blk, batch_bit), 0
     mixed_ref[batch] = mixed_own[...]
     mixed_ref[1 - batch] = mixed_got[...]
     input_ref[batch] = input_own[...]
@@ -1919,7 +1932,7 @@
             k += 1
 
 
-def finish_call(places, rows, sources, widths):
+def finish_call(batch_bit, rows, sources, widths):
     steps = 4
     f, (n_rows, width) = sources[0][0].shape[0], rows[0].shape
     tile, row_tile = f // steps, n_rows // steps
@@ -1932,9 +1945,9 @@
         specs += [by_rows(tile, n), by_rows(tile, n), by_pairs(tile, n)]
     like = jax.ShapeDtypeStruct
     return pl.pallas_call(
-        functools.partial(finish_kernel, sources=len(sources), widths=widths),
+        functools.partial(finish_kernel, sources=len(sources), widths=widths, batch_bit=batch_bit),
         grid=(steps,),
-        in_specs=[pl.BlockSpec(memory_space=pltpu.SMEM), *[by_rows(row_tile, width)] * 4, *specs],
+        in_specs=[*[by_rows(row_tile, width)] * 4, *specs],
         out_specs=[*[by_pairs(row_tile, width)] * 2, *[by_rows(tile, 2 * w) for w in widths]],
         out_shape=[
             like((2, n_rows, width), BF16),
@@ -1943,7 +1956,7 @@
         ],
         compiler_params=pltpu.CompilerParams(vmem_limit_bytes=60 * MIB),
         cost_estimate=TINY_COST,
-    )(places.astype(jnp.int32), *rows, *flat)
+    )(*rows, *flat)
 
 
 def local(
@@ -2255,12 +2268,14 @@
             bit_order,
             scaling,
             dict(
-                gains=gains_in,
-                gain_q=gain_q,
-                gain_k=gain_k,
+                gain_a=attn_gain[None],
+                gain_m=mlp_gain[None],
+                gain_q=query_gain[None],
+                gain_k=key_gain[None],
                 table=table,
                 start=start_lanes,
                 hidden=hidden_in,
+                far=over_blk(lax.dynamic_index_in_dim(hidden_in, 1 - batch, 0, keepdims=False), b_mask),
                 cotangent=cotangent,
                 wq=query_weight,
                 wk=key_matrix,
@@ -2271,7 +2286,6 @@
             ),
             next(ids),
         )
-        gain_a, gain_m = gains_group[0], gains_group[1]
         xa, cot_all = xa.reshape(tokens, width), cot_all.reshape(tokens, width)
         attn = attn.reshape(tokens, q_columns)
 
@@ -2361,7 +2375,7 @@
         (
             middle, d_middle, gain_m_grad, d_mid_all, mixed_partial, own_down, down_b, down_o, gate_b, send_gate, own_gate, keep_up, away_up,
         ) = middle_call(
-            b_mask, x_low, cot.reshape(share), gain_m[None], attn, w_out, cot_all, w_down, w_gate, (down_weight, gate_weight, up_weight), next(ids)
+            b_mask, x_low, cot.reshape(share), gains_group, attn, w_out, cot_all, w_down, w_gate, (down_weight, gate_weight, up_weight), next(ids)
         )
         d_mid_all = d_mid_all.reshape(tokens, width)
         mixed_partial = mixed_partial.reshape(tokens, width)
@@ -2454,10 +2468,10 @@
                 low=x_low,
                 middle=middle,
                 d_middle=d_middle,
-                gain=gain_a[None],
+                gain=gains_group,
                 gain_m_grad=gain_m_grad,
-                gain_q=gain_q,
-                gain_k=gain_k,
+                gain_q=query_gain[None],
+                gain_k=key_gain[None],
                 start=start_lanes,
                 l=total_e,
                 dall=d_mid_all,
@@ -2479,7 +2493,7 @@
             next(ids),
         )
         mixed, input_grad, g_down, g_gate, g_up, g_query, g_key, g_value, g_out = finish_call(
-            jnp.stack([tensor, batch]),
+            batch_bit,
             (mixed_own, mixed_got, input_own, input_got),
             [
                 (own_down, down_b, down_o),

time: 426 us -> 427 us (level)
  Pallas kernels: 411 us -> 402 us
  waiting for transfers between devices: 0 us -> 5.18 us
    pallas_call x1, Pallas kernels: 109 us -> 97.5 us  [first_call(): pl.pallas_call(functools.partial(first_kernel, batch_mask=batch_mask, bit...]
    ppermute x0 -> x1, waiting for transfers between devices: none -> 5.18 us  [over_blk(): return lax.ppermute(value, 'blk', [(i, i ^ mask) for i in range(count)])]
  transfers between devices with their start and end apart: 0 -> 1, of which waited for: 0 -> 1; matrix products, arithmetic and copies ran while one was open for 0% -> 2% of each run, Pallas kernels for 0% -> 0%
where the time goes in v9:
time: 427 us; the launch traced here: 423 us
  Pallas kernels  402 us (94%)
  local copies, waits for them, and re-layouts  7.48 us (2%)
  waiting for transfers between devices  5.18 us (1%)
    pallas_call x1, Pallas kernels, middle_call(): pl.pallas_call(functools.partial(middle_kernel, batch_mask=batch_mask, ch...  172 us
    pallas_call x1, Pallas kernels, last_call(): pl.pallas_call(functools.partial(last_kernel, batch_mask=batch_mask, bit_...  126 us
    pallas_call x1, Pallas kernels, first_call(): pl.pallas_call(functools.partial(first_kernel, batch_mask=batch_mask, bit...  97.5 us
  transfers between devices with their start and end apart: 1, of which 1 were waited for; matrix products, arithmetic and copies ran while one was open for 2% of the time, Pallas kernels for 0%

profile of v9, /device:TPU:0, one launch (start us, length us, event | category | flops | bytes accessed | tf_op | source)
XLA Modules:
  0.0 423.3 jit_solution(12970895973819501862)
XLA Ops:
  0.6 0.0 copy-start
  0.7 1.0 dynamic-slice_bitcast_fusion
  1.6 4.1 collective-permute-start
  5.8 0.0 copy-done
  5.8 0.2 reduce-window.8
  6.0 0.1 xor_multiply_fusion
  6.1 0.1 mul.41
  6.1 0.1 broadcast_add_fusion
  6.2 0.1 select_reduce_fusion
  6.3 0.1 subtract_convert_fusion
  6.4 0.6 tile.12.start_ref
  7.0 1.3 broadcast_in_dim.14.gain_a_ref
  8.3 1.3 broadcast_in_dim.15.gain_m_ref
  9.6 1.9 multiply_cosine_fusion
  11.5 1.0 pad_maximum_fusion.table_ref
  12.5 5.2 %collective-permute-done.far_ref = bf16[64,2048]{1,0:T(8,128)(2,1)S(1)} collective-permute-done((bf16[64,2048]{1,0:T(8,128)(2,1)S(1)}, bf16[64,2048]{1,0:T(8,128)(2,1)S(1)}, u32[]{:S(2)}, u32[]{:S(2)}) %collective-permute-start) | collective-permute-done | bytes 262176 | tf_op jit(solution)/shard_map/ppermute | solution.py:42
  17.7 0.0 copy-start.1
  17.7 0.7 copy-done.1
  18.4 97.5 %shard_map.237 = (bf16[2,64,2048]{2,1,0:T(8,128)(2,1)}, bf16[2,64,2048]{2,1,0:T(8,128)(2,1)}, f32[2,2048]{1,0:T(2,128)}, f32[4,1,512]{2,1,0:T(1,128)}, bf16[2,2,...) custom-call(bf16[1,2048]{1,0:T(2,128)(2,1)} %broadcast_in_dim.14.gai, ...), custom_call_target="tpu_custom_call" | custom-call | tf_op jit(solution)/shard_map/pallas_call | solution.py:1867
  115.9 171.8 %shard_map.238 = (f32[2,64,2048]{2,1,0:T(8,128)}, f32[2,64,2048]{2,1,0:T(8,128)}, f32[1,2048]{1,0:T(1,128)}, bf16[2,2,2,2,64,2048]{5,4,3,2,1,0:T(8,128)(2,1)}, b...) custom-call(bf16[2,64,2048]{2,1,0:T(8,128)(2,1)} %get-tuple-element., ...), custom_call_target="tpu_custom_call" | custom-call | tf_op jit(solution)/shard_map/pallas_call | solution.py:1310
  287.6 126.0 %shard_map.239 = (bf16[64,2048]{1,0:T(8,128)(2,1)}, bf16[64,2048]{1,0:T(8,128)(2,1)}, f32[64,2048]{1,0:T(8,128)}, bf16[64,2048]{1,0:T(8,128)(2,1)}, f32[1,4352]{...) custom-call(bf16[2,64,2048]{2,1,0:T(8,128)(2,1)} %get-tuple-element., ...), custom_call_target="tpu_custom_call" | custom-call | tf_op jit(solution)/shard_map/pallas_call | solution.py:1609
  413.6 1.2 slice_bitcast_fusion
  414.8 1.3 fusion.5
  416.1 6.9 %shard_map.240 = (bf16[2,64,2048]{2,1,0:T(8,128)(2,1)}, f32[2,64,2048]{2,1,0:T(8,128)}, f32[256,1536]{1,0:T(8,128)}, f32[256,1536]{1,0:T(8,128)}, f32[256,1536]{...) custom-call(bf16[64,2048]{1,0:T(8,128)(2,1)} %get-tuple-element.90.mixed_own, ...), custom_call_target="tpu_custom_call" | custom-call | tf_op jit(solution)/shard_map/pallas_call | solution.py:1947
  (5 shorter events, 0.1 us)
Async XLA Ops:
  0.6 5.1 %copy-start = (s32[2,9]{1,0:T(2,128)S(1)}, s32[2,9]{1,0:T(2,128)}, u32[]{:S(2)}) copy-start(s32[2,9]{1,0:T(2,128)} %param.15) | copy-start | bytes 220
  1.6 16.0 %collective-permute-start = (bf16[64,2048]{1,0:T(8,128)(2,1)S(1)}, bf16[64,2048]{1,0:T(8,128)(2,1)S(1)}, u32[]{:S(2)}, u32[]{:S(2)}) collective-permute-start(bf16[64,2048]{1,0:T(8,128)(2,1)S(1)} %dynamic-slice_bitcast_fusion), channel_id=1, source_target_pairs={{0,16},{4,20},{8,24},{12,28},{16,0},{20,4},{24,8},{28,12},{1,17},{... | collective-permute-start | bytes 786440 | tf_op jit(solution)/shard_map/ppermute | solution.py:42
  17.7 0.7 copy-start.1

commit v10 on v9

--- a/solution.py
+++ b/solution.py
@@ -1096,10 +1096,10 @@
 
 
 def middle_kernel(
-    low_ref, cot_ref, gain_ref, attn_ref, wo_ref, c_ref, wd_ref, wg_ref, down_ref, gate_ref, up_ref,
-    middle_ref, dmid_ref, gain_grad_ref, dall_ref, mixed_ref, own_d_ref, got_d_b_ref, got_d_o_ref, got_g_b_ref, send_g_ref, own_g_ref, keep_u_ref, away_u_ref,
-    attn, wo, p, core_in, out_y, in_y, out_t, in_t, hold, xm_s, xm, c, wd, wg, wu, dact, gate, act, dg, du,
-    away_d, fold_d, away_g, fold_g, own_d, send_d, send_g, up_tile, send, recv, *, batch_mask, chunk,
+    gain_ref, low_in, cot_in, attn_ref, wo_ref, c_ref, wd_ref, wg_ref, down_ref, gate_ref, up_ref,
+    gain_grad_ref, middle_out, dmid_out, dall_ref, mixed_ref, own_d_ref, got_d_b_ref, got_d_o_ref, got_g_b_ref, send_g_ref, own_g_ref, keep_u_ref, away_u_ref,
+    low_ref, cot_ref, middle_ref, dmid_ref, attn, wo, p, core_in, out_y, in_y, out_t, in_t, hold, xm_s, xm, c, wd, wg, wu, dact, gate, act, dg, du,
+    away_d, fold_d, away_g, fold_g, own_d, send_d, send_g, up_all, up_tile, send, recv, *, batch_mask, chunk,
 ):
     links = Links(send, recv, batch_mask)
     f, ff = own_d.shape[0], act.shape[1]
@@ -1122,6 +1122,7 @@
     down.append(load(links.half(down_ref, 0), rows(wd, 0)))
     gates.append(load(links.half(gate_ref, 0), rows(wg, 0)))
     c_load = load(c_ref, c)
+    low_load, cot_load = load(low_in, low_ref), load(cot_in, cot_ref)
     up_own = load(links.half(up_ref, 0), rows(wu, 0))
     bufs = (p, core_in, out_y, in_y, out_t, in_t, hold)
 
@@ -1140,10 +1141,12 @@
 
     up_z = []
     sum_in(links, bufs, chunk, out_partial, while_out)
+    low_load.arrive()
     for m in range(2):
         middle = low_ref[m].astype(F32) + hold[m]
         middle_ref[m] = middle
         xm_s[m] = (middle * inverse_rms(middle) * gain_ref[1:2, :]).astype(BF16)
+    load(middle_ref, middle_out)
 
     def while_xm(stage):
         if stage == 0:
@@ -1176,12 +1179,20 @@
 
     loop(4, gate_step)
     up_own.arrive()
-    for copy in ups:
+    for copy in ups[:-1]:
         copy.arrive()
+    most = 7 * f
+
+    def most_step(i):
+        at = pl.ds(pl.multiple_of(i * 256, 256), 256)
+        up_all[at, :] = nn(rows_of(xm, i)[:, :most], wu[:most, :])
+
+    loop(4, most_step)
+    ups[-1].arrive()
 
     def up_step(i):
         base = pl.multiple_of(i * 256, 256)
-        up_tile[...] = nn(rows_of(xm, i), wu[...])
+        up_tile[...] = up_all[pl.ds(base, 256), :] + nn(rows_of(xm, i)[:, most:], wu[most:, :])
 
         def part(j):
             at, here = pl.ds(pl.multiple_of(base + j * 32, 32), 32), pl.ds(pl.multiple_of(j * 32, 32), 32)
@@ -1246,12 +1257,13 @@
             compute_away(xm_cols, dg, away_g, 0, 2)
 
     sum_in(links, bufs, chunk, back_partial, while_back)
+    cot_load.arrive()
     for m in range(2):
         middle = middle_ref[m]
         grad = cot_ref[m].astype(F32) + norm_grad(hold[m], middle, gain_ref[1:2, :], gain_grad_ref, m)
         dmid_ref[m] = grad
         xm_s[m] = grad.astype(BF16)
-
+    load(dmid_ref, dmid_out)
     later = []
 
     def while_mid(stage):
@@ -1309,12 +1321,12 @@
     like = jax.ShapeDtypeStruct
     return pl.pallas_call(
         functools.partial(middle_kernel, batch_mask=batch_mask, chunk=2 * width // 8),
-        in_specs=[vmem] * 3 + [hbm] * 8,
-        out_specs=[vmem] * 3 + [hbm] * 10,
+        in_specs=[vmem] + [hbm] * 10,
+        out_specs=[vmem] + [hbm] * 12,
         out_shape=[
+            like((1, width), F32),
             like(share, F32),
             like(share, F32),
-            like((1, width), F32),
             like(full, BF16),
             like(full, BF16),
             like((f, ff), F32),
@@ -1327,6 +1339,10 @@
             like((4 * f, ff), BF16),
         ],
         scratch_shapes=[
+            pltpu.VMEM(share, BF16),
+            pltpu.VMEM(share, BF16),
+            pltpu.VMEM(share, F32),
+            pltpu.VMEM(share, F32),
             pltpu.VMEM((tokens, columns), BF16),
             pltpu.VMEM((width, columns), BF16),
             pltpu.VMEM(full, BF16),
@@ -1346,6 +1362,7 @@
             pltpu.VMEM((f, ff), F32),
             pltpu.VMEM((3 * f, ff), BF16),
             pltpu.VMEM((3 * f, ff), BF16),
+            pltpu.VMEM((tokens, ff), F32),
             pltpu.VMEM((256, ff), F32),
             pltpu.SemaphoreType.DMA((96,)),
             pltpu.SemaphoreType.DMA((96,)),
@@ -1354,7 +1371,7 @@
             collective_id=collective_id, has_side_effects=True, vmem_limit_bytes=60 * MIB
         ),
         cost_estimate=TINY_COST,
-    )(low, cot, gain, attn, w_out, cot_all, w_down, w_gate, *params)
+    )(gain, low, cot, attn, w_out, cot_all, w_down, w_gate, *params)
 
 
 def block_of(n, batch_mask):
@@ -1436,12 +1453,12 @@
 
 
 def last_kernel(
-    low_ref, middle_ref, dmid_ref, gain_ref, gain_m_grad_ref, gain_q_ref, gain_k_ref, start_ref, l_ref,
+    gain_ref, gain_m_grad_ref, gain_q_ref, gain_k_ref, start_ref, l_ref, low_in, middle_in, dmid_in,
     dall_ref, wo_ref, attn_ref, q_ref, k_ref, v_ref, ot_ref, raw_ref, table_ref, wa_ref, xa_ref, mixed_ref,
     send_g_ref, keep_u_ref, away_u_ref,
     mixed_own_ref, mixed_got_ref, input_own_ref, input_got_ref, sums_ref,
     got_g_o_ref, own_u_ref, got_u_b_ref, got_u_o_ref, own_a_ref, got_a_b_ref, got_a_o_ref, own_o_ref, got_o_b_ref, got_o_o_ref,
-    dall, wo, attn, q, do, k, v, ot, raw, table, wa, xa, dq, dk, dv, kt, acc, kv_out, kv_in, d_qkv,
+    low_ref, middle_ref, dmid_ref, dall, wo, attn, q, do, k, v, ot, raw, table, wa, xa, dq, dk, dv, kt, acc, kv_out, kv_in, d_qkv,
     p, core_in, out_y, in_y, out_t, in_t, hold, m_near, m_core_in, m_out_y, m_in_y, m_out_t, m_in_t, m_hold,
     swap_m, swap_i, keep_u, fold_u, own_u, send_u, away_o, fold_o, own_o, send_o, away_a, fold_a, own_a, send_a,
     gains_qk, gain_a_grad, ring_out, ring_in, send, recv, *, batch_mask, bit_order, scaling, chunk,
@@ -1458,6 +1475,7 @@
     first = [load(dall_ref, dall), load(wo_ref, wo), load(attn_ref, attn)]
     second = [load(a, b) for a, b in ((q_ref, q), (k_ref, k), (v_ref, v), (ot_ref, ot))]
     third = [load(a, b) for a, b in ((raw_ref, raw), (table_ref, table), (wa_ref, wa), (xa_ref, xa))]
+    third += [load(a, b) for a, b in ((low_in, low_ref), (middle_in, middle_ref), (dmid_in, dmid_ref))]
     mixed_near, keep_load = load(mixed_ref.at[0], m_near.at[0]), load(keep_u_ref, keep_u)
     links.greet()
 
@@ -1595,9 +1613,9 @@
     share, full, half_full = (2, rows, width), (2, 2, 2, 2, rows, width), (1, 2, 2, 2, rows, width)
     vmem, hbm = pl.BlockSpec(memory_space=pltpu.VMEM), pl.BlockSpec(memory_space=pltpu.HBM)
     like, held = jax.ShapeDtypeStruct, pltpu.VMEM
-    in_vmem = ("low", "middle", "d_middle", "gain", "gain_m_grad", "gain_q", "gain_k", "start", "l")
+    in_vmem = ("gain", "gain_m_grad", "gain_q", "gain_k", "start", "l")
     in_hbm = (
-        "dall", "w_out", "attn", "q", "k", "v", "ot", "raw", "table", "wa", "xa", "mixed", "send_g", "keep_u", "away_u",
+        "low", "middle", "d_middle", "dall", "w_out", "attn", "q", "k", "v", "ot", "raw", "table", "wa", "xa", "mixed", "send_g", "keep_u", "away_u",
     )
     total = 2 * width + 2 * head_size
     lanes = 2 * 2 * 128
@@ -1624,6 +1642,9 @@
             ],
         ],
         scratch_shapes=[
+            held(share, BF16),
+            held(share, F32),
+            held(share, F32),
             held((tokens, width), BF16),
             held((width, columns), BF16),
             held((tokens, columns), BF16),
@@ -1912,8 +1933,13 @@
     )(*[arrays[n] for n in (*in_vmem, *in_hbm)])
 
 
-def finish_kernel(mixed_own, mixed_got, input_own, input_got, *refs, sources, widths, batch_bit):
-    ins, (mixed_ref, input_ref, *outs) = refs[: 3 * sources], refs[3 * sources :]
+def finish_kernel(sums, mixed_own, mixed_got, input_own, input_got, *refs, sources, widths, gains, batch_bit):
+    ins, outs = refs[: 3 * sources], refs[3 * sources :]
+    gain_refs, (mixed_ref, input_ref, *outs) = outs[: len(gains)], outs[len(gains) :]
+    at = 0
+    for ref, n in zip(gain_refs, gains):
+        ref[...] = sums[0, at : at + n]
+        at += n
     blk = lax.axis_index("blk")
     place, batch, k = bit_of(blk, TENSOR_BIT), bit_of(blk, batch_bit), 0
     mixed_ref[batch] = mixed_own[...]
@@ -1932,7 +1958,7 @@
             k += 1
 
 
-def finish_call(batch_bit, rows, sources, widths):
+def finish_call(batch_bit, sums, gains, rows, sources, widths):
     steps = 4
     f, (n_rows, width) = sources[0][0].shape[0], rows[0].shape
     tile, row_tile = f // steps, n_rows // steps
@@ -1945,18 +1971,19 @@
         specs += [by_rows(tile, n), by_rows(tile, n), by_pairs(tile, n)]
     like = jax.ShapeDtypeStruct
     return pl.pallas_call(
-        functools.partial(finish_kernel, sources=len(sources), widths=widths, batch_bit=batch_bit),
+        functools.partial(finish_kernel, sources=len(sources), widths=widths, gains=gains, batch_bit=batch_bit),
         grid=(steps,),
-        in_specs=[*[by_rows(row_tile, width)] * 4, *specs],
-        out_specs=[*[by_pairs(row_tile, width)] * 2, *[by_rows(tile, 2 * w) for w in widths]],
+        in_specs=[pl.BlockSpec(sums.shape, lambda i: (0, 0)), *[by_rows(row_tile, width)] * 4, *specs],
+        out_specs=[*[pl.BlockSpec((n,), lambda i: (0,)) for n in gains], *[by_pairs(row_tile, width)] * 2, *[by_rows(tile, 2 * w) for w in widths]],
         out_shape=[
+            *[like((n,), F32) for n in gains],
             like((2, n_rows, width), BF16),
             like((2, n_rows, width), F32),
             *[like((f, 2 * w), F32) for w in widths],
         ],
         compiler_params=pltpu.CompilerParams(vmem_limit_bytes=60 * MIB),
         cost_estimate=TINY_COST,
-    )(*rows, *flat)
+    )(sums, *rows, *flat)
 
 
 def local(
@@ -2373,7 +2400,7 @@
         own_gate, away_gate = to_settle(keep_gate, gate_x)
     else:
         (
-            middle, d_middle, gain_m_grad, d_mid_all, mixed_partial, own_down, down_b, down_o, gate_b, send_gate, own_gate, keep_up, away_up,
+            gain_m_grad, middle, d_middle, d_mid_all, mixed_partial, own_down, down_b, down_o, gate_b, send_gate, own_gate, keep_up, away_up,
         ) = middle_call(
             b_mask, x_low, cot.reshape(share), gains_group, attn, w_out, cot_all, w_down, w_gate, (down_weight, gate_weight, up_weight), next(ids)
         )
@@ -2492,8 +2519,10 @@
             ),
             next(ids),
         )
-        mixed, input_grad, g_down, g_gate, g_up, g_query, g_key, g_value, g_out = finish_call(
+        *gains, mixed, input_grad, g_down, g_gate, g_up, g_query, g_key, g_value, g_out = finish_call(
             batch_bit,
+            sums,
+            (width, head_size, head_size, width),
             (mixed_own, mixed_got, input_own, input_got),
             [
                 (own_down, down_b, down_o),
@@ -2504,7 +2533,6 @@
             ],
             (ff, ff, ff, q_columns, k_columns, k_columns, q_columns),
         )
-        gains = jnp.split(sums.reshape(-1), [width, width + head_size, width + 2 * head_size])
     return (
         mixed,
         input_grad,

time: 427 us -> 421 us (0.986)
  no operation moved by 1% of the time
where the time goes in v10:
time: 421 us; the launch traced here: 417 us
  Pallas kernels  398 us (95%)
  waiting for transfers between devices  5.18 us (1%)
  local copies, waits for them, and re-layouts  4.98 us (1%)
    pallas_call x1, Pallas kernels, middle_call(): pl.pallas_call(functools.partial(middle_kernel, batch_mask=batch_mask, ch...  171 us
    pallas_call x1, Pallas kernels, last_call(): pl.pallas_call(functools.partial(last_kernel, batch_mask=batch_mask, bit_...  122 us
    pallas_call x1, Pallas kernels, first_call(): pl.pallas_call(functools.partial(first_kernel, batch_mask=batch_mask, bit...  97.5 us
  transfers between devices with their start and end apart: 1, of which 1 were waited for; matrix products, arithmetic and copies ran while one was open for 2% of the time, Pallas kernels for 0%

profile of v10, /device:TPU:0, one launch (start us, length us, event | category | flops | bytes accessed | tf_op | source)
XLA Modules:
  0.0 416.7 jit_solution(16055487802760520501)
XLA Ops:
  0.6 0.0 copy-start
  0.7 1.0 dynamic-slice_bitcast_fusion
  1.6 4.1 collective-permute-start
  5.8 0.0 copy-done
  5.8 0.2 reduce-window.8
  6.0 0.1 xor_multiply_fusion
  6.1 0.1 mul.41
  6.1 0.1 broadcast_add_fusion
  6.2 0.1 select_reduce_fusion
  6.3 0.1 subtract_convert_fusion
  6.4 0.6 tile.12.start_ref
  7.0 1.3 broadcast_in_dim.14.gain_a_ref
  8.3 1.3 broadcast_in_dim.15.gain_m_ref
  9.6 1.9 multiply_cosine_fusion
  11.5 1.0 pad_maximum_fusion.table_ref
  12.5 5.2 %collective-permute-done.far_ref = bf16[64,2048]{1,0:T(8,128)(2,1)S(1)} collective-permute-done((bf16[64,2048]{1,0:T(8,128)(2,1)S(1)}, bf16[64,2048]{1,0:T(8,128)(2,1)S(1)}, u32[]{:S(2)}, u32[]{:S(2)}) %collective-permute-start) | collective-permute-done | bytes 262176 | tf_op jit(solution)/shard_map/ppermute | solution.py:42
  17.7 0.0 copy-start.1
  17.7 0.7 copy-done.1
  18.4 97.5 %shard_map.237 = (bf16[2,64,2048]{2,1,0:T(8,128)(2,1)}, bf16[2,64,2048]{2,1,0:T(8,128)(2,1)}, f32[2,2048]{1,0:T(2,128)}, f32[4,1,512]{2,1,0:T(1,128)}, bf16[2,2,...) custom-call(bf16[1,2048]{1,0:T(2,128)(2,1)} %broadcast_in_dim.14.gai, ...), custom_call_target="tpu_custom_call" | custom-call | tf_op jit(solution)/shard_map/pallas_call | solution.py:1888
  115.9 170.9 %shard_map.238 = (f32[1,2048]{1,0:T(1,128)}, f32[2,64,2048]{2,1,0:T(8,128)}, f32[2,64,2048]{2,1,0:T(8,128)}, bf16[2,2,2,2,64,2048]{5,4,3,2,1,0:T(8,128)(2,1)}, b...) custom-call(f32[2,2048]{1,0:T(2,128)} %get-tuple-element.70.gain_ref, ...), custom_call_target="tpu_custom_call" | custom-call | tf_op jit(solution)/shard_map/pallas_call | solution.py:1322
  286.8 122.4 %shard_map.239 = (bf16[64,2048]{1,0:T(8,128)(2,1)}, bf16[64,2048]{1,0:T(8,128)(2,1)}, f32[64,2048]{1,0:T(8,128)}, bf16[64,2048]{1,0:T(8,128)(2,1)}, f32[1,4352]{...) custom-call(f32[2,2048]{1,0:T(2,128)} %get-tuple-element.70.gain_ref, ...), custom_call_target="tpu_custom_call" | custom-call | tf_op jit(solution)/shard_map/pallas_call | solution.py:1627
  409.2 7.0 %shard_map.240 = (f32[2048]{0:T(1024)}, f32[128]{0:T(128)}, f32[128]{0:T(128)}, f32[2048]{0:T(1024)}, bf16[2,64,2048]{2,1,0:T(8,128)(2,1)}, /*index=5*/f32[2,64,...) custom-call(f32[1,4352]{1,0:T(1,128)} %get-tuple-element.94.sums, ...), custom_call_target="tpu_custom_call" | custom-call | tf_op jit(solution)/shard_map/pallas_call | solution.py:1973
  (5 shorter events, 0.1 us)
Async XLA Ops:
  0.6 5.1 %copy-start = (s32[2,9]{1,0:T(2,128)S(1)}, s32[2,9]{1,0:T(2,128)}, u32[]{:S(2)}) copy-start(s32[2,9]{1,0:T(2,128)} %param.15) | copy-start | bytes 220
  1.6 16.0 %collective-permute-start = (bf16[64,2048]{1,0:T(8,128)(2,1)S(1)}, bf16[64,2048]{1,0:T(8,128)(2,1)S(1)}, u32[]{:S(2)}, u32[]{:S(2)}) collective-permute-start(bf16[64,2048]{1,0:T(8,128)(2,1)S(1)} %dynamic-slice_bitcast_fusion), channel_id=1, source_target_pairs={{0,16},{4,20},{8,24},{12,28},{16,0},{20,4},{24,8},{28,12},{1,17},{... | collective-permute-start | bytes 786440 | tf_op jit(solution)/shard_map/ppermute | solution.py:42
  17.7 0.7 copy-start.1
